TPU v7x, 32 devices: a whole 2x2x4 slice. The times are simulated.
32 devices in a mesh: grp: 2 (over y), ex: 4 (over z), feat: 2 (over x), pb: 2 (over core).
Axes of the slice: x: 2, y: 2, z: 4, core: 2. Of those that a mesh axis runs over, the one named last changes fastest.
Arguments:
- train_grads: bfloat16 [1024, 256, 256], P(('grp', 'ex'), 'feat'), parts along dimension 0, may hold values from -0.029907227 to 0.029907227
- queries: bfloat16 [2, 96, 256, 256], P('pb', ('grp', 'ex'), 'feat'), parts along dimension 1, may hold values from -6 to 6
- left_factor: float32 [512, 256], P('grp'), parts along dimension 0
- right_factor: float32 [512, 256], P('grp'), parts along dimension 0
- block_order: int32 [8], P('grp'), parts along dimension 0, may hold values from 0 to 3, each once
Outputs:
- scores: float32 [1024, 2, 48], P(('grp', 'ex'), 'pb', 'feat'), parts along dimension 0
There are 2 independent parts, one for each index of `grp`. A program takes and returns all parts, laid end to end along the dimension named above; each array names one. Nothing has to cross between parts.
Inputs may be any that keep to these rules, and one draw needn't show every extreme that they name: `block_order`: a permutation of the query blocks.
All inputs are finite; a program needn't handle non-finite values.
Results may differ from a plain program's by a relative error of at most 0.0029.
Values may be sent and summed in bfloat16 or wider, within the bound.
No kernel may reach another device: no remote copies, remote signals or barrier semaphores. Data moves between devices by JAX's collectives and lax.ppermute only.
A program may use at most 128 MiB of HBM per device.

v0:
```python
import jax
import jax.numpy as jnp
from jax import lax
from jax.sharding import PartitionSpec as P


def per_device(train_grads, queries, left_factor, right_factor, block_order):
    row_count = train_grads.shape[0]
    part_rows = train_grads.shape[1]
    right_width = train_grads.shape[2]
    flat_grads = train_grads.reshape(row_count, part_rows * right_width)
    local_queries = queries[0]
    block_size = local_queries.shape[0]
    regrouped = lax.all_to_all(local_queries, "feat", split_axis=0, concat_axis=1, tiled=True)
    whole_mix = jnp.einsum(
        "ik,qkj->qij", left_factor, regrouped.astype(jnp.float32), precision=lax.Precision.HIGHEST
    )
    whole_cond = jnp.einsum(
        "qij,jl->qil", whole_mix, right_factor, precision=lax.Precision.HIGHEST
    ).astype(jnp.bfloat16)
    conditioned = lax.all_to_all(whole_cond, "feat", split_axis=1, concat_axis=0, tiled=True)
    conditioned = conditioned.reshape(block_size, part_rows * right_width)
    partials = lax.dot_general(
        flat_grads,
        lax.all_gather(conditioned, "ex", axis=0, tiled=True),
        (((1,), (1,)), ((), ())),
        preferred_element_type=jnp.float32,
    )
    block_count = lax.axis_size("ex")
    partials = jnp.take(partials.reshape(row_count, block_count, block_size), block_order, axis=1)
    partials = partials.reshape(row_count, block_count * block_size)
    owned_scores = lax.psum_scatter(partials, "feat", scatter_dimension=1, tiled=True)
    return owned_scores.reshape(row_count, 1, owned_scores.shape[1])


def solution(mesh):
    return jax.shard_map(
        per_device,
        mesh=mesh,
        in_specs=(
            P(("grp", "ex"), "feat", None),
            P("pb", ("grp", "ex"), "feat", None),
            P("grp", None),
            P("grp", None),
            P("grp"),
        ),
        out_specs=P(("grp", "ex"), "pb", "feat"),
        check_vma=False,
    )
```

profile of v0, /device:TPU:0, one launch (start us, length us, event | category | flops | bytes accessed | tf_op | source)
XLA Modules:
  0.0 150.9 jit_solution(6405728201377483824)
XLA Ops:
  6.5 0.0 copy-start
  6.5 0.0 copy-start.1
  6.5 0.0 all-gather.3.cloned.1.call-start
  6.5 15.9 %all_to_all.33 = bf16[12,128,256]{2,1,0:T(8,128)(2,1)S(1)} all-to-all(bf16[12,128,256]{2,1,0:T(8,128)(2,1)} %bitcast.43), channel_id=1, replica_groups=mesh['grp'=2,'ex'=4,'feat'=2,'pb'=2] {'feat'}, dimensions={0} | all-to-all | bytes 1572864 | tf_op jit(solution)/shard_map/all_to_all | solution.py:14
  22.5 0.1 copy.11
  22.5 0.0 copy-done
  22.5 0.9 fusion.6
  23.5 0.0 copy-done.1
  23.5 2.6 %fusion.2 = bf16[6,256,256]{2,1,0:T(8,128)(2,1)S(1)} fusion(f32[6,256,256]{2,1,0:T(8,128)S(1)} %fusion.6, f32[256,256]{1,0:T(8,128)S(1)} %copy-done.1), kind=kOutput, calls=%fused_computation.3 | convolution fusion | flops 1208352768 | bytes 2621440 | tf_op jit(solution)/shard_map/qij,jl->qil/dot_general | solution.py:18
  26.1 0.5 copy.14
  26.6 15.8 %all_to_all.34 = bf16[6,256,256]{2,0,1:T(8,128)(2,1)S(1)} all-to-all(bf16[6,256,256]{2,0,1:T(8,128)(2,1)S(1)} %copy.14), channel_id=1, replica_groups=mesh['grp'=2,'ex'=4,'feat'=2,'pb'=2] {'feat'}, dimensions={1} | all-to-all | bytes 1572864 | tf_op jit(solution)/shard_map/all_to_all | solution.py:21
  42.4 0.2 copy.20
  42.5 1.6 %reshape.34 = bf16[1,12,32768]{2,1,0:T(8,128)(2,1)} reshape(bf16[2,6,128,256]{3,2,1,0:T(8,128)(2,1)S(1)} %bitcast.39) | data formatting | bytes 1572864
  44.1 0.0 all-gather.3.cloned.1.call-update
  44.1 0.2 reduce-scatter.4.cloned.1.call-start
  44.3 0.0 copy-start.2
  44.4 12.3 %copy.18 = bf16[16,8,128,256]{3,1,2,0:T(8,128)(2,1)} copy(bf16[16,8,128,256]{3,2,1,0:T(8,128)(2,1)} %bitcast.37) | data formatting | bytes 16777216
  56.7 0.0 copy-done.2
  56.7 0.1 broadcast_in_dim.16
  56.8 0.1 broadcast_in_dim.17
  56.9 68.4 %all-gather.3.cloned.1.call-done = bf16[4,12,32768]{2,1,0:T(8,128)(2,1)} async-done(((bf16[1,12,32768]{2,1,0:T(8,128)(2,1)}), bf16[4,12,32768]{2,1,0:T(8,128)(2,1)}) %all-gather.3.cloned.1.call-update) | async-done | bytes 3145744 | tf_op jit(solution)/shard_map/all_gather | solution.py:25
  125.3 2.6 %reshape.35 = bf16[48,32768]{1,0:T(8,128)(2,1)S(1)} reshape(bf16[4,12,32768]{2,1,0:T(8,128)(2,1)} %all-gather.3.cloned.1.call-done) | data formatting | bytes 6291456
  127.9 6.4 %convolution_bitcast_fusion = f32[128,48]{0,1:T(8,128)S(1)} fusion(bf16[48,32768]{1,0:T(8,128)(2,1)S(1)} %reshape.35, bf16[128,32768]{1,0:T(8,128)(2,1)} %bitcast.36), kind=kOutput, calls=%fused_computation.4 | convolution fusion | flops 402653184 | bytes 11558912 | tf_op jit(solution)/shard_map/dot_general | solution.py:23
  134.3 0.6 gather_fusion
  134.9 0.7 broadcast_select_fusion
  135.6 0.0 reduce-scatter.4.cloned.1.call-update
  135.6 8.5 %reduce-scatter.4.cloned.1.call-done = f32[128,24]{0,1:T(8,128)} async-done(((f32[128,48]{0,1:T(8,128)}), f32[128,24]{0,1:T(8,128)}) %reduce-scatter.4.cloned.1.call-update) | async-done | bytes 12304
  (5 shorter events, 0.0 us)
Async XLA Ops:
  6.5 16.0 %copy-start = (f32[256,256]{1,0:T(8,128)S(1)}, f32[256,256]{1,0:T(8,128)}, u32[]{:S(2)}) copy-start(f32[256,256]{1,0:T(8,128)} %param.7) | copy-start | bytes 786436
  6.5 16.9 %copy-start.1 = (f32[256,256]{1,0:T(8,128)S(1)}, f32[256,256]{1,0:T(8,128)}, u32[]{:S(2)}) copy-start(f32[256,256]{1,0:T(8,128)} %param.8) | copy-start | bytes 786436
  6.5 118.7 %all-gather.3.cloned.1.call-start = ((), (), s32[]{:S(2)}) async-start(), calls=%async_computation.3 | async-start | bytes 5242880 | tf_op jit(solution)/shard_map/all_gather | solution.py:25
  44.1 100.0 %reduce-scatter.4.cloned.1.call-start = ((), (), s32[]{:S(2)}) async-start(), calls=%async_computation.4 | async-start | bytes 36864
  44.3 12.4 %copy-start.2 = (s32[4]{0:T(128)S(1)}, s32[4]{0:T(128)}, u32[]{:S(2)}) copy-start(s32[4]{0:T(128)} %param.9) | copy-start | bytes 52
Sparse Core Ops, SparseCore 0:
  44.2 81.0 all-gather.2
  135.7 8.3 reduce-scatter.3
where the time goes:
time: 151 us
  waiting for transfers between devices  76.9 us (51%)
  blocking collectives  31.7 us (21%)
  local copies, waits for them, and re-layouts  18 us (12%)
  between operations  13.5 us (9%)
  matrix products  9.94 us (7%)
    all_gather x1, waiting for transfers between devices, per_device(): lax.all_gather(conditioned, 'ex', axis=0, tiled=True)  68.4 us
    unnamed x9, local copies, waits for them, and re-layouts  16.6 us
    all_to_all x1, blocking collectives, per_device(): lax.all_to_all(local_queries, 'feat', split_axis=0, concat_axis=1, tiled=...  15.9 us
    all_to_all x1, blocking collectives, per_device(): lax.all_to_all(whole_cond, 'feat', split_axis=1, concat_axis=0, tiled=True)  15.8 us
    unnamed x3, waiting for transfers between devices  8.52 us
    dot_general x1, matrix products, per_device(): lax.dot_general(flat_grads, lax.all_gather(conditioned, 'ex', axis=0, til...  6.37 us
  transfers between devices with their start and end apart: 2, of which 2 were waited for; matrix products, arithmetic and copies ran while one was open for 8% of the time, Pallas kernels for 0%

commit v1 on v0

v1 whole, which is shorter than its diff:
```python
import jax
import jax.numpy as jnp
from jax import lax
from jax.experimental import pallas as pl
from jax.experimental.pallas import tpu as pltpu
from jax.sharding import PartitionSpec as P

F32 = jnp.float32
BF16 = jnp.bfloat16
EARLY = 4
PIECES = 4
VMEM = pl.BlockSpec(memory_space=pltpu.VMEM)
SMEM = pl.BlockSpec(memory_space=pltpu.SMEM)


def parts_of(x, count):
    terms = []
    for _ in range(count):
        top = x.astype(BF16)
        terms.append(top)
        x = x - top.astype(F32)
    return terms


def condition_kernel(own_ref, far_ref, left_ref, right_ref, out_ref, wide_ref):
    count, rows, _ = own_ref.shape
    side = lax.axis_index("feat")
    here = pl.ds(pl.multiple_of(side * rows, rows), rows)
    there = pl.ds(pl.multiple_of((1 - side) * rows, rows), rows)
    left = jnp.concatenate([left_ref[here, here], left_ref[here, there]], axis=1)
    left_terms = jnp.concatenate(parts_of(left, 3), axis=0)
    right_0, right_1 = parts_of(right_ref[...], 2)
    for q in range(count):
        query = jnp.concatenate([own_ref[q], far_ref[q]], axis=0)
        mixed = jnp.dot(left_terms, query, preferred_element_type=F32)
        mixed = mixed[:rows] + (mixed[rows : 2 * rows] + mixed[2 * rows :])
        mixed_0, mixed_1 = parts_of(mixed, 2)
        both = jnp.dot(jnp.concatenate([mixed_0, mixed_1], axis=0), right_0, preferred_element_type=F32)
        cross = jnp.dot(mixed_0, right_1, preferred_element_type=F32)
        wide_ref[:, q, :] = both[:rows] + (both[rows:] + cross)
    out_ref[...] = wide_ref[...].astype(BF16)


def condition(own, far, left, right):
    count, rows, width = own.shape
    return pl.pallas_call(
        condition_kernel,
        out_shape=jax.ShapeDtypeStruct((rows, count, width), BF16),
        in_specs=[VMEM] * 4,
        out_specs=VMEM,
        scratch_shapes=[pltpu.VMEM((rows, count, width), F32)],
        compiler_params=pltpu.CompilerParams(vmem_limit_bytes=24 << 20),
        cost_estimate=pl.CostEstimate(flops=count * 3_000_000 * 40, bytes_accessed=8 * count * rows * width, transcendentals=0),
    )(own, far, left, right)


def inner_products(query_refs, grad_refs):
    total = sum(ref.shape[1] for ref in query_refs)
    acc = jnp.zeros((total, grad_refs[0].shape[1]), F32)
    first = 0
    for grad_ref in grad_refs:
        count = grad_ref.shape[0]
        unroll = 16

        def body(i, acc, grad_ref=grad_ref, first=first):
            for j in range(unroll):
                r = i * unroll + j
                queries = jnp.concatenate([ref[first + r] for ref in query_refs], axis=0)
                acc = acc + lax.dot_general(
                    queries, grad_ref[r], (((1,), (1,)), ((), ())), preferred_element_type=F32
                )
            return acc

        acc = lax.fori_loop(0, count // unroll, body, acc)
        first += count
    return acc


def first_pass_kernel(ex, early_ref, own_ref, up0, down0, up1, down1, *rest):
    *grad_refs, order_ref, out_ref = rest
    late = own_ref.shape[1]
    acc = inner_products((early_ref, own_ref, up0, down0, up1, down1), grad_refs)
    me = lax.axis_index("ex")
    early = [acc[EARLY * s : EARLY * (s + 1)] for s in range(ex)]
    base = EARLY * ex
    slots = [acc[base + late * s : base + late * (s + 1)] for s in range(5)]
    sources = [me, me - 1, me + 1, me - 2, me + 2]
    for b in range(ex):
        block = order_ref[b]
        low = jnp.zeros_like(early[0])
        for s in range(ex):
            low = low + jnp.where(lax.rem(me - s + ex, ex) == block, early[s], 0.0)
        high = jnp.zeros_like(slots[0])
        for slot, source in zip(slots, sources):
            high = high + jnp.where(source == block, slot, 0.0)
        at = b * (EARLY + late)
        out_ref[at : at + EARLY, :] = low
        out_ref[at + EARLY : at + EARLY + late, :] = high


def last_pass_kernel(ex, base_ref, up2, down2, *rest):
    *grad_refs, order_ref, mine_ref, send_ref, full_ref = rest
    late = up2.shape[1]
    acc = inner_products((up2, down2), grad_refs)
    me = lax.axis_index("ex")
    full_ref[...] = base_ref[...]
    for b in range(ex):
        block = order_ref[b]
        at = b * (EARLY + late) + EARLY
        high = jnp.where(block == me - 3, acc[:late], 0.0) + jnp.where(block == me + 3, acc[late:], 0.0)
        full_ref[at : at + late, :] = full_ref[at : at + late, :] + high
    half = mine_ref.shape[0]
    side = lax.axis_index("feat")
    mine_ref[...] = full_ref[pl.ds(pl.multiple_of(side * half, half), half), :]
    send_ref[...] = full_ref[pl.ds(pl.multiple_of((1 - side) * half, half), half), :]


def score_call(kernel, ex, arrays, pieces, order, out_shape, scratch=()):
    count = len(arrays) + len(pieces)
    return pl.pallas_call(
        lambda *refs: kernel(ex, *refs),
        out_shape=out_shape,
        in_specs=[VMEM] * count + [SMEM],
        out_specs=jax.tree.map(lambda _: VMEM, out_shape),
        scratch_shapes=scratch,
        compiler_params=pltpu.CompilerParams(vmem_limit_bytes=32 << 20),
        cost_estimate=pl.CostEstimate(flops=3_000_000_000, bytes_accessed=12_000_000, transcendentals=0),
    )(*arrays, *pieces, order)


def line_step(x, y, step, ex):
    up = [(i, i + 1) for i in range(step, ex - 1)]
    down = [(i + 1, i) for i in range(ex - 1 - step)]
    return lax.ppermute(x, "ex", up), lax.ppermute(y, "ex", down)


def per_device_line(train_grads, queries, left_factor, right_factor, block_order):
    ex = lax.axis_size("ex")
    swap = [(0, 1), (1, 0)]
    rows = train_grads.shape[1]
    count = queries.shape[1]
    raw = queries[0, :EARLY]
    late_raw = queries[0, EARLY:]
    ups, downs = [raw], [raw]
    u, d = line_step(raw, raw, 0, ex)
    ups.append(u)
    downs.append(d)
    late_far = lax.ppermute(late_raw, "feat", swap)
    for s in (1, 2):
        u, d = line_step(ups[-1], downs[-1], s, ex)
        ups.append(u)
        downs.append(d)
    late = condition(late_raw, late_far, left_factor, right_factor)
    up0, down0 = line_step(late, late, 0, ex)
    up1, down1 = line_step(up0, down0, 1, ex)
    up2, down2 = line_step(up1, down1, 2, ex)
    early = jnp.concatenate([raw] + [ups[s] + downs[ex - s] for s in range(1, ex)], axis=0)
    early_far = lax.ppermute(early, "feat", swap)
    early_cond = condition(early, early_far, left_factor, right_factor)
    step = rows // PIECES
    pieces = [train_grads[:, p * step : (p + 1) * step].transpose(1, 0, 2) for p in range(PIECES)]
    n = train_grads.shape[0]
    base = score_call(
        first_pass_kernel, ex, (early_cond, late, up0, down0, up1, down1), pieces, block_order,
        jax.ShapeDtypeStruct((ex * count, n), F32),
    )
    half = jax.ShapeDtypeStruct((ex * count // 2, n), F32)
    mine, send = score_call(
        last_pass_kernel, ex, (base, up2, down2), pieces, block_order, (half, half),
        [pltpu.VMEM((ex * count, n), F32)],
    )
    scores = mine + lax.ppermute(send, "feat", swap)
    return scores.T[:, None, :]


def per_device_gather(train_grads, queries, left_factor, right_factor, block_order):
    row_count = train_grads.shape[0]
    part_rows = train_grads.shape[1]
    right_width = train_grads.shape[2]
    flat_grads = train_grads.reshape(row_count, part_rows * right_width)
    local_queries = queries[0]
    block_size = local_queries.shape[0]
    regrouped = lax.all_to_all(local_queries, "feat", split_axis=0, concat_axis=1, tiled=True)
    whole_mix = jnp.einsum(
        "ik,qkj->qij", left_factor, regrouped.astype(F32), precision=lax.Precision.HIGHEST
    )
    whole_cond = jnp.einsum(
        "qij,jl->qil", whole_mix, right_factor, precision=lax.Precision.HIGHEST
    ).astype(BF16)
    conditioned = lax.all_to_all(whole_cond, "feat", split_axis=1, concat_axis=0, tiled=True)
    conditioned = conditioned.reshape(block_size, part_rows * right_width)
    partials = lax.dot_general(
        flat_grads,
        lax.all_gather(conditioned, "ex", axis=0, tiled=True),
        (((1,), (1,)), ((), ())),
        preferred_element_type=F32,
    )
    block_count = lax.axis_size("ex")
    partials = jnp.take(partials.reshape(row_count, block_count, block_size), block_order, axis=1)
    partials = partials.reshape(row_count, block_count * block_size)
    owned_scores = lax.psum_scatter(partials, "feat", scatter_dimension=1, tiled=True)
    return owned_scores.reshape(row_count, 1, owned_scores.shape[1])


def solution(mesh):
    short_line = mesh.shape["ex"] == 4 and mesh.shape["feat"] == 2
    return jax.shard_map(
        per_device_line if short_line else per_device_gather,
        mesh=mesh,
        in_specs=(
            P(("grp", "ex"), "feat", None),
            P("pb", ("grp", "ex"), "feat", None),
            P("grp", None),
            P("grp", None),
            P("grp"),
        ),
        out_specs=P(("grp", "ex"), "pb", "feat"),
        check_vma=False,
    )
```

time: 151 us -> 84.4 us (0.56)
  waiting for transfers between devices: 76.9 us -> 31.3 us
  blocking collectives: 31.7 us -> 0 us
  starting transfers between devices: 0.22 us -> 26.6 us
  between operations: 13.5 us -> 0.29 us
  Pallas kernels: 0 us -> 12 us
  matrix products: 9.94 us -> 0 us
  local copies, waits for them, and re-layouts: 18 us -> 12.8 us
    all_gather x1 -> x0, waiting for transfers between devices: 68.4 us -> none  [per_device(): lax.all_gather(conditioned, 'ex', axis=0, tiled=True)]
    all_to_all x2 -> x0, blocking collectives: 31.7 us -> none  [the longest x1 15.9 us: per_device(): lax.all_to_all(local_queries, 'feat', split_axis=0, concat_axis=1, tiled=...]
    ppermute x0 -> x15, waiting for transfers between devices: none -> 31.3 us  [the longest x12 23.5 us: line_step(): return (lax.ppermute(x, 'ex', up), lax.ppermute(y, 'ex', down))]
    ppermute x0 -> x15, starting transfers between devices: none -> 26.6 us  [the longest x12 22.4 us: line_step(): return (lax.ppermute(x, 'ex', up), lax.ppermute(y, 'ex', down))]
    unnamed x9 -> x10, local copies, waits for them, and re-layouts: 16.6 us -> 1.91 us
    pallas_call x0 -> x4, Pallas kernels: none -> 12 us  [the longest x2 8.06 us: score_call(): pl.pallas_call(lambda *refs: kernel(ex, *refs), out_shape=out_shape, in_s...]
    dot_general x3 -> x0, matrix products: 9.94 us -> none  [the longest x1 6.37 us: per_device(): lax.dot_general(flat_grads, lax.all_gather(conditioned, 'ex', axis=0, til...]
    unnamed x3 -> x0, waiting for transfers between devices: 8.52 us -> none
  transfers between devices with their start and end apart: 2 -> 15, of which waited for: 2 -> 5; matrix products, arithmetic and copies ran while one was open for 8% -> 12% of each run, Pallas kernels for 0% -> 10%
where the time goes in v1:
time: 84.4 us; the launch traced here: 83.9 us
  waiting for transfers between devices  31.3 us (37%)
  starting transfers between devices  26.6 us (32%)
  local copies, waits for them, and re-layouts  12.8 us (15%)
  Pallas kernels  12 us (14%)
  other arithmetic  0.93 us (1%)
    ppermute x12, waiting for transfers between devices, line_step(): return (lax.ppermute(x, 'ex', up), lax.ppermute(y, 'ex', down))  23.5 us
    ppermute x12, starting transfers between devices, line_step(): return (lax.ppermute(x, 'ex', up), lax.ppermute(y, 'ex', down))  22.4 us
    pallas_call x2, Pallas kernels, score_call(): pl.pallas_call(lambda *refs: kernel(ex, *refs), out_shape=out_shape, in_s...  8.06 us
    transpose x2, local copies, waits for them, and re-layouts, per_device_line(): train_grads[:, p * step:(p + 1) * step].transpose(1, 0, 2)  4.82 us
    ppermute x1, waiting for transfers between devices, per_device_line(): early_far = lax.ppermute(early, 'feat', swap)  4.62 us
    slice x1, local copies, waits for them, and re-layouts, per_device_line(): train_grads[:, p * step:(p + 1) * step].transpose(1, 0, 2)  3.98 us
    pallas_call x2, Pallas kernels, condition(): pl.pallas_call(condition_kernel, out_shape=jax.ShapeDtypeStruct((rows, co...  3.95 us
    ppermute x1, waiting for transfers between devices, per_device_line(): scores = mine + lax.ppermute(send, 'feat', swap)  3.17 us
  transfers between devices with their start and end apart: 15, of which 5 were waited for; matrix products, arithmetic and copies ran while one was open for 12% of the time, Pallas kernels for 10%

profile of v1, /device:TPU:0, one launch (start us, length us, event | category | flops | bytes accessed | tf_op | source)
XLA Modules:
  0.0 83.9 jit_solution(7379422076690418117)
XLA Ops:
  0.0 1.1 %slice_bitcast_fusion.own_ref = bf16[8,128,256]{2,1,0:T(8,128)(2,1)S(1)} fusion(bf16[1,12,128,256]{3,2,1,0:T(8,128)(2,1)} %param.6), kind=kLoop, calls=%fused_computation.5 | loop fusion | bytes 1048576 | tf_op jit(solution)/shard_map/squeeze | solution.py:143
  1.1 3.0 %collective-permute-start.7 = (bf16[8,128,256]{2,1,0:T(8,128)(2,1)S(1)}, bf16[8,128,256]{2,1,0:T(8,128)(2,1)S(1)}, u32[]{:S(2)}, u32[]{:S(2)}) collective-permute-start(bf16[8,128,256]{2,1,0:T(8,128)(2,1)S(1)} %slice_bitcast_fusion.own_ref), channel_id=1, source_target_pairs={{0,2},{2,0},{1,3},{3,1},{4,6},{6,4},{5,7},{7,5},{8,10},{10,8},{9,1... | collective-permute-start | bytes 1572872 | tf_op jit(solution)/shard_map/ppermute | solution.py:148
  4.1 1.0 %slice_bitcast_fusion.1 = bf16[4,128,256]{2,1,0:T(8,128)(2,1)S(1)} fusion(bf16[1,12,128,256]{3,2,1,0:T(8,128)(2,1)} %param.6), kind=kLoop, calls=%fused_computation.6 | loop fusion | bytes 524288 | tf_op jit(solution)/shard_map/squeeze | solution.py:142
  5.1 1.3 %collective-permute-start.1 = (bf16[4,128,256]{2,1,0:T(8,128)(2,1)S(1)}, bf16[4,128,256]{2,1,0:T(8,128)(2,1)S(1)}, u32[]{:S(2)}, u32[]{:S(2)}) collective-permute-start(bf16[4,128,256]{2,1,0:T(8,128)(2,1)S(1)} %slice_bitcast_fusion.1), channel_id=1, source_target_pairs={{4,0},{8,4},{12,8},{5,1},{9,5},{13,9},{6,2},{10,6},{14,10},{7,3},{... | collective-permute-start | bytes 786440 | tf_op jit(solution)/shard_map/ppermute | solution.py:134
  6.4 4.6 %collective-permute-start = (bf16[4,128,256]{2,1,0:T(8,128)(2,1)S(1)}, bf16[4,128,256]{2,1,0:T(8,128)(2,1)S(1)}, u32[]{:S(2)}, u32[]{:S(2)}) collective-permute-start(bf16[4,128,256]{2,1,0:T(8,128)(2,1)S(1)} %slice_bitcast_fusion.1), channel_id=1, source_target_pairs={{0,4},{4,8},{8,12},{1,5},{5,9},{9,13},{2,6},{6,10},{10,14},{3,7},{... | collective-permute-start | bytes 786440 | tf_op jit(solution)/shard_map/ppermute | solution.py:134
  10.9 3.8 %collective-permute-done.1 = bf16[4,128,256]{2,1,0:T(8,128)(2,1)S(1)} collective-permute-done((bf16[4,128,256]{2,1,0:T(8,128)(2,1)S(1)}, bf16[4,128,256]{2,1,0:T(8,128)(2,1)S(1)}, u32[]{:S(2)}, u32[]{:S(2)}) %collective-permute-start.1) | collective-permute-done | bytes 262176 | tf_op jit(solution)/shard_map/ppermute | solution.py:134
  14.7 1.3 %collective-permute-start.2 = (bf16[4,128,256]{2,1,0:T(8,128)(2,1)S(1)}, bf16[4,128,256]{2,1,0:T(8,128)(2,1)S(1)}, u32[]{:S(2)}, u32[]{:S(2)}) collective-permute-start(bf16[4,128,256]{2,1,0:T(8,128)(2,1)S(1)} %collective-permute-done.1), channel_id=1, source_target_pairs={{4,0},{8,4},{5,1},{9,5},{6,2},{10,6},{7,3},{11,7},{20,16},{24,20},... | collective-permute-start | bytes 786440 | tf_op jit(solution)/shard_map/ppermute | solution.py:134
  16.0 0.7 collective-permute-start.4
  16.7 0.9 %copy-done.1 = f32[256,256]{1,0:T(8,128)S(1)} copy-done((f32[256,256]{1,0:T(8,128)S(1)}, f32[256,256]{1,0:T(8,128)}, u32[]{:S(2)}) %copy-start.1) | copy-done | bytes 262168
  17.7 0.9 %copy-done.3 = f32[256,256]{1,0:T(8,128)S(1)} copy-done((f32[256,256]{1,0:T(8,128)S(1)}, f32[256,256]{1,0:T(8,128)}, u32[]{:S(2)}) %copy-start.3) | copy-done | bytes 262168
  18.6 1.3 %shard_map.56.refs_1_ = bf16[128,8,256]{2,1,0:T(8,128)(2,1)S(1)} custom-call(bf16[8,128,256]{2,1,0:T(8,128)(2,1)S(1)} %slice_bitcast_fusion.own_ref, bf16[8,128,256]{2,1,0:T(8,128)(2,1)S(1)} %collective-permute-done.7.far_ref, f32[256,256]{1,0:T(8,128)S(1)} %copy-done.1, f32[256,256]{1,0:T(8,128)S(1)} %copy-done.3), custom_call_target="tpu_custom_call" | custom-call | flops 960000000 | bytes 2097152 | tf_op jit(solution)/shard_map/pallas_call | solution.py:46
  19.9 7.4 %collective-permute-start.8 = (bf16[128,8,256]{2,1,0:T(8,128)(2,1)S(1)}, bf16[128,8,256]{2,1,0:T(8,128)(2,1)S(1)}, u32[]{:S(2)}, u32[]{:S(2)}) collective-permute-start(bf16[128,8,256]{2,1,0:T(8,128)(2,1)S(1)} %shard_map.56.refs_1_), channel_id=1, source_target_pairs={{0,4},{4,8},{8,12},{1,5},{5,9},{9,13},{2,6},{6,10},{10,14},{3,7},{... | collective-permute-start | bytes 1572872 | tf_op jit(solution)/shard_map/ppermute | solution.py:134
  27.3 1.3 %collective-permute-start.9 = (bf16[128,8,256]{2,1,0:T(8,128)(2,1)S(1)}, bf16[128,8,256]{2,1,0:T(8,128)(2,1)S(1)}, u32[]{:S(2)}, u32[]{:S(2)}) collective-permute-start(bf16[128,8,256]{2,1,0:T(8,128)(2,1)S(1)} %shard_map.56.refs_1_), channel_id=1, source_target_pairs={{4,0},{8,4},{12,8},{5,1},{9,5},{13,9},{6,2},{10,6},{14,10},{7,3},{... | collective-permute-start | bytes 1572872 | tf_op jit(solution)/shard_map/ppermute | solution.py:134
  28.6 1.3 %collective-permute-start.3 = (bf16[4,128,256]{2,1,0:T(8,128)(2,1)S(1)}, bf16[4,128,256]{2,1,0:T(8,128)(2,1)S(1)}, u32[]{:S(2)}, u32[]{:S(2)}) collective-permute-start(bf16[4,128,256]{2,1,0:T(8,128)(2,1)S(1)} %collective-permute-done.2), channel_id=1, source_target_pairs={{4,0},{5,1},{6,2},{7,3},{20,16},{21,17},{22,18},{23,19}} | collective-permute-start | bytes 786440 | tf_op jit(solution)/shard_map/ppermute | solution.py:134
  29.9 0.7 collective-permute-start.5
  30.7 15.8 %collective-permute-done.3 = bf16[4,128,256]{2,1,0:T(8,128)(2,1)S(1)} collective-permute-done((bf16[4,128,256]{2,1,0:T(8,128)(2,1)S(1)}, bf16[4,128,256]{2,1,0:T(8,128)(2,1)S(1)}, u32[]{:S(2)}, u32[]{:S(2)}) %collective-permute-start.3) | collective-permute-done | bytes 262176 | tf_op jit(solution)/shard_map/ppermute | solution.py:134
  46.7 0.6 collective-permute-start.6
  47.3 0.7 collective-permute-start.10
  48.0 1.3 %collective-permute-start.11 = (bf16[128,8,256]{2,1,0:T(8,128)(2,1)S(1)}, bf16[128,8,256]{2,1,0:T(8,128)(2,1)S(1)}, u32[]{:S(2)}, u32[]{:S(2)}) collective-permute-start(bf16[128,8,256]{2,1,0:T(8,128)(2,1)S(1)} %collective-permute-done.9.refs_3_), channel_id=1, source_target_pairs={{4,0},{8,4},{5,1},{9,5},{6,2},{10,6},{7,3},{11,7},{20,16},{24,20},... | collective-permute-start | bytes 1572872 | tf_op jit(solution)/shard_map/ppermute | solution.py:134
  49.3 4.0 %fusion = (bf16[128,32,256]{2,1,0:T(8,128)(2,1)S(1)}, bf16[128,32,256]{2,1,0:T(8,128)(2,1)S(1)}, bf16[128,32,256]{2,1,0:T(8,128)(2,1)S(1)}, bf16[128,32,256]{2,1,0:T(8,128)(2,1)S(1)}) fusion(bf16[128,128,256]{2,1,0:T(8,128)(2,1)} %param.5), kind=kLoop, calls=%fused_computation.8 | loop fusion | bytes 16777216 | tf_op jit(solution)/shard_map/slice | solution.py:161
  53.3 2.4 %copy_bitcast_fusion = (bf16[32,128,256]{2,1,0:T(8,128)(2,1)S(1)}, bf16[32,128,256]{2,1,0:T(8,128)(2,1)S(1)}) fusion(bf16[128,32,256]{2,1,0:T(8,128)(2,1)S(1)} %get-tuple-element.9, bf16[128,32,256]{2,1,0:T(8,128)(2,1)S(1)} %get-tuple-element.10), kind=kLoop, calls=%fused_computation | loop fusion | bytes 8388608 | tf_op jit(solution)/shard_map/transpose | solution.py:161
  55.7 0.7 collective-permute-start.12
  56.4 3.9 %collective-permute-done.11.refs_5_ = bf16[128,8,256]{2,1,0:T(8,128)(2,1)S(1)} collective-permute-done((bf16[128,8,256]{2,1,0:T(8,128)(2,1)S(1)}, bf16[128,8,256]{2,1,0:T(8,128)(2,1)S(1)}, u32[]{:S(2)}, u32[]{:S(2)}) %collective-permute-start.11) | collective-permute-done | bytes 524320 | tf_op jit(solution)/shard_map/ppermute | solution.py:134
  60.4 1.3 %collective-permute-start.13 = (bf16[128,8,256]{2,1,0:T(8,128)(2,1)S(1)}, bf16[128,8,256]{2,1,0:T(8,128)(2,1)S(1)}, u32[]{:S(2)}, u32[]{:S(2)}) collective-permute-start(bf16[128,8,256]{2,1,0:T(8,128)(2,1)S(1)} %collective-permute-done.11.refs_5_), channel_id=1, source_target_pairs={{4,0},{5,1},{6,2},{7,3},{20,16},{21,17},{22,18},{23,19}} | collective-permute-start | bytes 1572872 | tf_op jit(solution)/shard_map/ppermute | solution.py:134
  61.7 2.4 %copy_bitcast_fusion.2 = (bf16[32,128,256]{2,1,0:T(8,128)(2,1)S(1)}, bf16[32,128,256]{2,1,0:T(8,128)(2,1)S(1)}) fusion(bf16[128,32,256]{2,1,0:T(8,128)(2,1)S(1)} %get-tuple-element.11, bf16[128,32,256]{2,1,0:T(8,128)(2,1)S(1)} %get-tuple-element.12), kind=kLoop, calls=%fused_computation.2 | loop fusion | bytes 8388608 | tf_op jit(solution)/shard_map/transpose | solution.py:161
  64.1 4.6 %collective-permute-done.6.far_ref = bf16[16,128,256]{2,1,0:T(8,128)(2,1)S(1)} collective-permute-done((bf16[16,128,256]{2,1,0:T(8,128)(2,1)S(1)}, bf16[16,128,256]{2,1,0:T(8,128)(2,1)S(1)}, u32[]{:S(2)}, u32[]{:S(2)}) %collective-permute-start.6) | collective-permute-done | bytes 1048608 | tf_op jit(solution)/shard_map/ppermute | solution.py:158
  68.7 2.7 %shard_map.55.refs_0_ = bf16[128,16,256]{2,1,0:T(8,128)(2,1)S(1)} custom-call(bf16[16,128,256]{2,1,0:T(8,128)(2,1)S(1)} %pad_maximum_fusion.own_ref, bf16[16,128,256]{2,1,0:T(8,128)(2,1)S(1)} %collective-permute-done.6.far_ref, f32[256,256]{1,0:T(8,128)S(1)} %copy-done.2, f32[256,256]{1,0:T(8,128)S(1)} %copy-done.4), custom_call_target="tpu_custom_call" | custom-call | flops 1920000000 | bytes 4194304 | tf_op jit(solution)/shard_map/pallas_call | solution.py:46
  71.5 4.4 %shard_map.57.refs_0_ = f32[48,128]{1,0:T(8,128)S(1)} custom-call(bf16[128,16,256]{2,1,0:T(8,128)(2,1)S(1)} %shard_map.55.refs_0_, bf16[128,8,256]{2,1,0:T(8,128)(2,1)S(1)} %shard_map.56.refs_1_, bf16[128,8,256]{2,1,0:T(8,128)(2,1)S(1)} %collective-permute-done.8.refs_2_, bf16[128,8,256]{2,1,0:T(8,128)(2,1)S(1)} %collective-permute-done.9.refs_3_, ...), custom_call_target="tpu_custom_call" | custom-call | flops 3000000000 | bytes 12000000 | tf_op jit(solution)/shard_map/pallas_call | solution.py:120
  75.9 3.7 %shard_map.58 = (f32[24,128]{1,0:T(8,128)S(1)}, f32[24,128]{1,0:T(8,128)S(1)}) custom-call(f32[48,128]{1,0:T(8,128)S(1)} %shard_map.57.refs_0_, bf16[128,8,256]{2,1,0:T(8,128)(2,1)S(1)} %collective-permute-done.12.refs_1_, bf16[128,8,256]{2,1,0:T(8,128)(2,1)S(1)} %collective-permute-done.13.refs_2_, ...), custom_call_target="tpu_custom_call" | custom-call | flops 3000000000 | bytes 12000000 | tf_op jit(solution)/shard_map/pallas_call | solution.py:120
  79.6 0.6 collective-permute-start.14
  80.2 3.2 %collective-permute-done.14 = f32[24,128]{1,0:T(8,128)S(1)} collective-permute-done((f32[24,128]{1,0:T(8,128)S(1)}, f32[24,128]{1,0:T(8,128)S(1)}, u32[]{:S(2)}, u32[]{:S(2)}) %collective-permute-start.14) | collective-permute-done | bytes 12320 | tf_op jit(solution)/shard_map/ppermute | solution.py:172
  83.3 0.6 add_bitcast_fusion
  (22 shorter events, 0.4 us)
Async XLA Ops:
  1.1 15.6 %collective-permute-start.7 = (bf16[8,128,256]{2,1,0:T(8,128)(2,1)S(1)}, bf16[8,128,256]{2,1,0:T(8,128)(2,1)S(1)}, u32[]{:S(2)}, u32[]{:S(2)}) collective-permute-start(bf16[8,128,256]{2,1,0:T(8,128)(2,1)S(1)} %slice_bitcast_fusion.own_ref), channel_id=1, source_target_pairs={{0,2},{2,0},{1,3},{3,1},{4,6},{6,4},{5,7},{7,5},{8,10},{10,8},{9,1... | collective-permute-start | bytes 1572872 | tf_op jit(solution)/shard_map/ppermute | solution.py:148
  5.1 9.7 %collective-permute-start.1 = (bf16[4,128,256]{2,1,0:T(8,128)(2,1)S(1)}, bf16[4,128,256]{2,1,0:T(8,128)(2,1)S(1)}, u32[]{:S(2)}, u32[]{:S(2)}) collective-permute-start(bf16[4,128,256]{2,1,0:T(8,128)(2,1)S(1)} %slice_bitcast_fusion.1), channel_id=1, source_target_pairs={{4,0},{8,4},{12,8},{5,1},{9,5},{13,9},{6,2},{10,6},{14,10},{7,3},{... | collective-permute-start | bytes 786440 | tf_op jit(solution)/shard_map/ppermute | solution.py:134
  6.4 9.7 %collective-permute-start = (bf16[4,128,256]{2,1,0:T(8,128)(2,1)S(1)}, bf16[4,128,256]{2,1,0:T(8,128)(2,1)S(1)}, u32[]{:S(2)}, u32[]{:S(2)}) collective-permute-start(bf16[4,128,256]{2,1,0:T(8,128)(2,1)S(1)} %slice_bitcast_fusion.1), channel_id=1, source_target_pairs={{0,4},{4,8},{8,12},{1,5},{5,9},{9,13},{2,6},{6,10},{10,14},{3,7},{... | collective-permute-start | bytes 786440 | tf_op jit(solution)/shard_map/ppermute | solution.py:134
  14.7 13.9 %collective-permute-start.2 = (bf16[4,128,256]{2,1,0:T(8,128)(2,1)S(1)}, bf16[4,128,256]{2,1,0:T(8,128)(2,1)S(1)}, u32[]{:S(2)}, u32[]{:S(2)}) collective-permute-start(bf16[4,128,256]{2,1,0:T(8,128)(2,1)S(1)} %collective-permute-done.1), channel_id=1, source_target_pairs={{4,0},{8,4},{5,1},{9,5},{6,2},{10,6},{7,3},{11,7},{20,16},{24,20},... | collective-permute-start | bytes 786440 | tf_op jit(solution)/shard_map/ppermute | solution.py:134
  16.0 13.9 %collective-permute-start.4 = (bf16[4,128,256]{2,1,0:T(8,128)(2,1)S(1)}, bf16[4,128,256]{2,1,0:T(8,128)(2,1)S(1)}, u32[]{:S(2)}, u32[]{:S(2)}) collective-permute-start(bf16[4,128,256]{2,1,0:T(8,128)(2,1)S(1)} %collective-permute-done), channel_id=1, source_target_pairs={{4,8},{8,12},{5,9},{9,13},{6,10},{10,14},{7,11},{11,15},{20,24},{2... | collective-permute-start | bytes 786440 | tf_op jit(solution)/shard_map/ppermute | solution.py:134
  16.7 1.0 %copy-start.1 = (f32[256,256]{1,0:T(8,128)S(1)}, f32[256,256]{1,0:T(8,128)}, u32[]{:S(2)}) copy-start(f32[256,256]{1,0:T(8,128)} %left_ref.3) | copy-start | bytes 786436
  17.7 0.9 %copy-start.3 = (f32[256,256]{1,0:T(8,128)S(1)}, f32[256,256]{1,0:T(8,128)}, u32[]{:S(2)}) copy-start(f32[256,256]{1,0:T(8,128)} %right_ref.3) | copy-start | bytes 786436
  19.9 27.5 %collective-permute-start.8 = (bf16[128,8,256]{2,1,0:T(8,128)(2,1)S(1)}, bf16[128,8,256]{2,1,0:T(8,128)(2,1)S(1)}, u32[]{:S(2)}, u32[]{:S(2)}) collective-permute-start(bf16[128,8,256]{2,1,0:T(8,128)(2,1)S(1)} %shard_map.56.refs_1_), channel_id=1, source_target_pairs={{0,4},{4,8},{8,12},{1,5},{5,9},{9,13},{2,6},{6,10},{10,14},{3,7},{... | collective-permute-start | bytes 1572872 | tf_op jit(solution)/shard_map/ppermute | solution.py:134
  27.3 20.7 %collective-permute-start.9 = (bf16[128,8,256]{2,1,0:T(8,128)(2,1)S(1)}, bf16[128,8,256]{2,1,0:T(8,128)(2,1)S(1)}, u32[]{:S(2)}, u32[]{:S(2)}) collective-permute-start(bf16[128,8,256]{2,1,0:T(8,128)(2,1)S(1)} %shard_map.56.refs_1_), channel_id=1, source_target_pairs={{4,0},{8,4},{12,8},{5,1},{9,5},{13,9},{6,2},{10,6},{14,10},{7,3},{... | collective-permute-start | bytes 1572872 | tf_op jit(solution)/shard_map/ppermute | solution.py:134
  28.6 17.8 %collective-permute-start.3 = (bf16[4,128,256]{2,1,0:T(8,128)(2,1)S(1)}, bf16[4,128,256]{2,1,0:T(8,128)(2,1)S(1)}, u32[]{:S(2)}, u32[]{:S(2)}) collective-permute-start(bf16[4,128,256]{2,1,0:T(8,128)(2,1)S(1)} %collective-permute-done.2), channel_id=1, source_target_pairs={{4,0},{5,1},{6,2},{7,3},{20,16},{21,17},{22,18},{23,19}} | collective-permute-start | bytes 786440 | tf_op jit(solution)/shard_map/ppermute | solution.py:134
  29.9 16.6 %collective-permute-start.5 = (bf16[4,128,256]{2,1,0:T(8,128)(2,1)S(1)}, bf16[4,128,256]{2,1,0:T(8,128)(2,1)S(1)}, u32[]{:S(2)}, u32[]{:S(2)}) collective-permute-start(bf16[4,128,256]{2,1,0:T(8,128)(2,1)S(1)} %collective-permute-done.4), channel_id=1, source_target_pairs={{8,12},{9,13},{10,14},{11,15},{24,28},{25,29},{26,30},{27,31}} | collective-permute-start | bytes 786440 | tf_op jit(solution)/shard_map/ppermute | solution.py:134
  46.7 22.0 %collective-permute-start.6 = (bf16[16,128,256]{2,1,0:T(8,128)(2,1)S(1)}, bf16[16,128,256]{2,1,0:T(8,128)(2,1)S(1)}, u32[]{:S(2)}, u32[]{:S(2)}) collective-permute-start(bf16[16,128,256]{2,1,0:T(8,128)(2,1)S(1)} %pad_maximum_fusion.own_ref), channel_id=1, source_target_pairs={{0,2},{2,0},{1,3},{3,1},{4,6},{6,4},{5,7},{7,5},{8,10},{10,8},{9,1... | collective-permute-start | bytes 3145736 | tf_op jit(solution)/shard_map/ppermute | solution.py:158
  47.3 8.4 %collective-permute-start.10 = (bf16[128,8,256]{2,1,0:T(8,128)(2,1)S(1)}, bf16[128,8,256]{2,1,0:T(8,128)(2,1)S(1)}, u32[]{:S(2)}, u32[]{:S(2)}) collective-permute-start(bf16[128,8,256]{2,1,0:T(8,128)(2,1)S(1)} %collective-permute-done.8.refs_2_), channel_id=1, source_target_pairs={{4,8},{8,12},{5,9},{9,13},{6,10},{10,14},{7,11},{11,15},{20,24},{2... | collective-permute-start | bytes 1572872 | tf_op jit(solution)/shard_map/ppermute | solution.py:134
  48.0 12.3 %collective-permute-start.11 = (bf16[128,8,256]{2,1,0:T(8,128)(2,1)S(1)}, bf16[128,8,256]{2,1,0:T(8,128)(2,1)S(1)}, u32[]{:S(2)}, u32[]{:S(2)}) collective-permute-start(bf16[128,8,256]{2,1,0:T(8,128)(2,1)S(1)} %collective-permute-done.9.refs_3_), channel_id=1, source_target_pairs={{4,0},{8,4},{5,1},{9,5},{6,2},{10,6},{7,3},{11,7},{20,16},{24,20},... | collective-permute-start | bytes 1572872 | tf_op jit(solution)/shard_map/ppermute | solution.py:134
  55.7 20.2 %collective-permute-start.12 = (bf16[128,8,256]{2,1,0:T(8,128)(2,1)S(1)}, bf16[128,8,256]{2,1,0:T(8,128)(2,1)S(1)}, u32[]{:S(2)}, u32[]{:S(2)}) collective-permute-start(bf16[128,8,256]{2,1,0:T(8,128)(2,1)S(1)} %collective-permute-done.10.refs_4_), channel_id=1, source_target_pairs={{8,12},{9,13},{10,14},{11,15},{24,28},{25,29},{26,30},{27,31}} | collective-permute-start | bytes 1572872 | tf_op jit(solution)/shard_map/ppermute | solution.py:134
  60.4 15.5 %collective-permute-start.13 = (bf16[128,8,256]{2,1,0:T(8,128)(2,1)S(1)}, bf16[128,8,256]{2,1,0:T(8,128)(2,1)S(1)}, u32[]{:S(2)}, u32[]{:S(2)}) collective-permute-start(bf16[128,8,256]{2,1,0:T(8,128)(2,1)S(1)} %collective-permute-done.11.refs_5_), channel_id=1, source_target_pairs={{4,0},{5,1},{6,2},{7,3},{20,16},{21,17},{22,18},{23,19}} | collective-permute-start | bytes 1572872 | tf_op jit(solution)/shard_map/ppermute | solution.py:134
  61.6 7.1 %copy-start.2 = (f32[256,256]{1,0:T(8,128)S(1)}, f32[256,256]{1,0:T(8,128)}, u32[]{:S(2)}) copy-start(f32[256,256]{1,0:T(8,128)} %left_ref.3) | copy-start | bytes 786436
  61.7 7.1 %copy-start.4 = (f32[256,256]{1,0:T(8,128)S(1)}, f32[256,256]{1,0:T(8,128)}, u32[]{:S(2)}) copy-start(f32[256,256]{1,0:T(8,128)} %right_ref.3) | copy-start | bytes 786436
  64.1 7.3 %copy-start = (s32[4]{0:T(128)S(1)}, s32[4]{0:T(128)}, u32[]{:S(2)}) copy-start(s32[4]{0:T(128)} %refs_7_.1) | copy-start | bytes 52
  79.6 3.8 %collective-permute-start.14 = (f32[24,128]{1,0:T(8,128)S(1)}, f32[24,128]{1,0:T(8,128)S(1)}, u32[]{:S(2)}, u32[]{:S(2)}) collective-permute-start(f32[24,128]{1,0:T(8,128)S(1)} %get-tuple-element.8), channel_id=1, source_target_pairs={{0,2},{2,0},{1,3},{3,1},{4,6},{6,4},{5,7},{7,5},{8,10},{10,8},{9,1... | collective-permute-start | bytes 36872 | tf_op jit(solution)/shard_map/ppermute | solution.py:172

commit v2 on v1

--- a/solution.py
+++ b/solution.py
@@ -8,7 +8,6 @@
 F32 = jnp.float32
 BF16 = jnp.bfloat16
 EARLY = 4
-PIECES = 4
 VMEM = pl.BlockSpec(memory_space=pltpu.VMEM)
 SMEM = pl.BlockSpec(memory_space=pltpu.SMEM)
 
@@ -22,14 +21,34 @@
     return terms
 
 
-def condition_kernel(own_ref, far_ref, left_ref, right_ref, out_ref, wide_ref):
-    count, rows, _ = own_ref.shape
+def factor_kernel(left_ref, right_ref, left_out, right_out):
+    rows = left_out.shape[0] // 3
     side = lax.axis_index("feat")
     here = pl.ds(pl.multiple_of(side * rows, rows), rows)
     there = pl.ds(pl.multiple_of((1 - side) * rows, rows), rows)
     left = jnp.concatenate([left_ref[here, here], left_ref[here, there]], axis=1)
-    left_terms = jnp.concatenate(parts_of(left, 3), axis=0)
-    right_0, right_1 = parts_of(right_ref[...], 2)
+    left_out[...] = jnp.concatenate(parts_of(left, 3), axis=0)
+    right_out[...] = jnp.concatenate(parts_of(right_ref[...], 2), axis=0)
+
+
+def factor_terms(left, right, rows):
+    wide, width = left.shape[1], right.shape[1]
+    return pl.pallas_call(
+        factor_kernel,
+        out_shape=(
+            jax.ShapeDtypeStruct((3 * rows, wide), BF16),
+            jax.ShapeDtypeStruct((2 * width, width), BF16),
+        ),
+        in_specs=[VMEM] * 2,
+        out_specs=(VMEM, VMEM),
+        compiler_params=pltpu.CompilerParams(vmem_limit_bytes=16 << 20),
+    )(left, right)
+
+
+def condition_kernel(own_ref, far_ref, left_ref, right_ref, out_ref, wide_ref):
+    count, rows, width = own_ref.shape
+    left_terms = left_ref[...]
+    right_0, right_1 = right_ref[:width], right_ref[width:]
     for q in range(count):
         query = jnp.concatenate([own_ref[q], far_ref[q]], axis=0)
         mixed = jnp.dot(left_terms, query, preferred_element_type=F32)
@@ -41,7 +60,7 @@
     out_ref[...] = wide_ref[...].astype(BF16)
 
 
-def condition(own, far, left, right):
+def condition(own, far, left_terms, right_terms):
     count, rows, width = own.shape
     return pl.pallas_call(
         condition_kernel,
@@ -51,7 +70,7 @@
         scratch_shapes=[pltpu.VMEM((rows, count, width), F32)],
         compiler_params=pltpu.CompilerParams(vmem_limit_bytes=24 << 20),
         cost_estimate=pl.CostEstimate(flops=count * 3_000_000 * 40, bytes_accessed=8 * count * rows * width, transcendentals=0),
-    )(own, far, left, right)
+    )(own, far, left_terms, right_terms)
 
 
 def inner_products(query_refs, grad_refs):
@@ -76,39 +95,43 @@
     return acc
 
 
-def first_pass_kernel(ex, early_ref, own_ref, up0, down0, up1, down1, *rest):
+def first_pass_kernel(ex, early_0, early_1, own_ref, near, mid, far_in, *rest):
     *grad_refs, order_ref, out_ref = rest
     late = own_ref.shape[1]
-    acc = inner_products((early_ref, own_ref, up0, down0, up1, down1), grad_refs)
+    acc = inner_products((early_0, early_1, own_ref, near, mid, far_in), grad_refs)
     me = lax.axis_index("ex")
+    sources = slot_sources(me)
     early = [acc[EARLY * s : EARLY * (s + 1)] for s in range(ex)]
     base = EARLY * ex
-    slots = [acc[base + late * s : base + late * (s + 1)] for s in range(5)]
-    sources = [me, me - 1, me + 1, me - 2, me + 2]
+    slots = [acc[base + late * s : base + late * (s + 1)] for s in range(4)]
     for b in range(ex):
         block = order_ref[b]
         low = jnp.zeros_like(early[0])
+        high = jnp.zeros_like(slots[0])
         for s in range(ex):
-            low = low + jnp.where(lax.rem(me - s + ex, ex) == block, early[s], 0.0)
-        high = jnp.zeros_like(slots[0])
-        for slot, source in zip(slots, sources):
-            high = high + jnp.where(source == block, slot, 0.0)
+            hit = sources[s] == block
+            low = low + jnp.where(hit, early[s], 0.0)
+            high = high + jnp.where(hit, slots[s], 0.0)
         at = b * (EARLY + late)
         out_ref[at : at + EARLY, :] = low
         out_ref[at + EARLY : at + EARLY + late, :] = high
 
 
-def last_pass_kernel(ex, base_ref, up2, down2, *rest):
+def slot_sources(me):
+    low_pair = me < 2
+    near = jnp.where(low_pair, 1 - me, 5 - me)
+    return [me, near, jnp.where(low_pair, 2, 1), jnp.where(low_pair, 3, 0)]
+
+
+def last_pass_kernel(ex, base_ref, far_out, *rest):
     *grad_refs, order_ref, mine_ref, send_ref, full_ref = rest
-    late = up2.shape[1]
-    acc = inner_products((up2, down2), grad_refs)
-    me = lax.axis_index("ex")
+    late = far_out.shape[1]
+    acc = inner_products((far_out,), grad_refs)
+    far = slot_sources(lax.axis_index("ex"))[3]
     full_ref[...] = base_ref[...]
     for b in range(ex):
-        block = order_ref[b]
         at = b * (EARLY + late) + EARLY
-        high = jnp.where(block == me - 3, acc[:late], 0.0) + jnp.where(block == me + 3, acc[late:], 0.0)
-        full_ref[at : at + late, :] = full_ref[at : at + late, :] + high
+        full_ref[at : at + late, :] = full_ref[at : at + late, :] + jnp.where(order_ref[b] == far, acc, 0.0)
     half = mine_ref.shape[0]
     side = lax.axis_index("feat")
     mine_ref[...] = full_ref[pl.ds(pl.multiple_of(side * half, half), half), :]
@@ -128,45 +151,51 @@
     )(*arrays, *pieces, order)
 
 
-def line_step(x, y, step, ex):
-    up = [(i, i + 1) for i in range(step, ex - 1)]
-    down = [(i + 1, i) for i in range(ex - 1 - step)]
-    return lax.ppermute(x, "ex", up), lax.ppermute(y, "ex", down)
+def after(x, *others):
+    return lax.optimization_barrier((x, *others))[0]
+
+
+PAIRS = [(0, 1), (1, 0), (2, 3), (3, 2)]
+MIDDLE = [(1, 2), (2, 1)]
+OUTWARD = [(1, 0), (2, 3)]
 
 
 def per_device_line(train_grads, queries, left_factor, right_factor, block_order):
     ex = lax.axis_size("ex")
     swap = [(0, 1), (1, 0)]
-    rows = train_grads.shape[1]
     count = queries.shape[1]
+    n = train_grads.shape[0]
     raw = queries[0, :EARLY]
-    late_raw = queries[0, EARLY:]
-    ups, downs = [raw], [raw]
-    u, d = line_step(raw, raw, 0, ex)
-    ups.append(u)
-    downs.append(d)
-    late_far = lax.ppermute(late_raw, "feat", swap)
-    for s in (1, 2):
-        u, d = line_step(ups[-1], downs[-1], s, ex)
-        ups.append(u)
-        downs.append(d)
-    late = condition(late_raw, late_far, left_factor, right_factor)
-    up0, down0 = line_step(late, late, 0, ex)
-    up1, down1 = line_step(up0, down0, 1, ex)
-    up2, down2 = line_step(up1, down1, 2, ex)
-    early = jnp.concatenate([raw] + [ups[s] + downs[ex - s] for s in range(1, ex)], axis=0)
-    early_far = lax.ppermute(early, "feat", swap)
-    early_cond = condition(early, early_far, left_factor, right_factor)
-    step = rows // PIECES
-    pieces = [train_grads[:, p * step : (p + 1) * step].transpose(1, 0, 2) for p in range(PIECES)]
-    n = train_grads.shape[0]
+    late_raw = after(queries, raw)[0, EARLY:]
+    raw_near = lax.ppermute(raw, "ex", PAIRS)
+    raw_mid = lax.ppermute(raw, "ex", MIDDLE)
+    late_other = lax.ppermute(late_raw, "feat", swap)
+    terms = factor_terms(left_factor, after(right_factor, late_raw), train_grads.shape[1])
+    raw_far_mid = lax.ppermute(after(raw_near, *terms), "ex", MIDDLE)
+    raw_mid_out = lax.ppermute(after(raw_mid, *terms), "ex", OUTWARD)
+    early_0 = jnp.concatenate([raw, raw_near], axis=0)
+    early_0_other = lax.ppermute(early_0, "feat", swap)
+
+    late = condition(after(late_raw, raw_far_mid, raw_mid_out), late_other, *terms)
+    raw_far_out = lax.ppermute(raw_far_mid, "ex", OUTWARD)
+    near = lax.ppermute(late, "ex", PAIRS)
+    mid = lax.ppermute(late, "ex", MIDDLE)
+    grads = after(train_grads, late).transpose(1, 0, 2)
+    early_1 = jnp.concatenate([raw_mid + raw_mid_out, raw_far_mid + raw_far_out], axis=0)
+    early_1_other = lax.ppermute(early_1, "feat", swap)
+    far_mid = lax.ppermute(after(near, grads, early_0_other), "ex", MIDDLE)
+    mid_out = lax.ppermute(after(mid, grads), "ex", OUTWARD)
+    cond_0 = condition(after(early_0, far_mid, mid_out), early_0_other, *terms)
+    cond_1 = condition(after(early_1, cond_0), early_1_other, *terms)
+    far_out = lax.ppermute(far_mid, "ex", OUTWARD)
+    pieces = [grads]
     base = score_call(
-        first_pass_kernel, ex, (early_cond, late, up0, down0, up1, down1), pieces, block_order,
+        first_pass_kernel, ex, (cond_0, cond_1, late, near, mid + mid_out, far_mid), pieces, block_order,
         jax.ShapeDtypeStruct((ex * count, n), F32),
     )
     half = jax.ShapeDtypeStruct((ex * count // 2, n), F32)
     mine, send = score_call(
-        last_pass_kernel, ex, (base, up2, down2), pieces, block_order, (half, half),
+        last_pass_kernel, ex, (base, far_out), pieces, block_order, (half, half),
         [pltpu.VMEM((ex * count, n), F32)],
     )
     scores = mine + lax.ppermute(send, "feat", swap)

time: 84.4 us -> 75.4 us (0.89)
  starting transfers between devices: 26.6 us -> 19.1 us
  waiting for transfers between devices: 31.3 us -> 27.7 us
  local copies, waits for them, and re-layouts: 12.8 us -> 15.3 us
    optimization_barrier x0 -> x1, local copies, waits for them, and re-layouts: none -> 11.4 us  [after(): return lax.optimization_barrier((x, *others))[0]]
    ppermute x14 -> x13, starting transfers between devices: 26 us -> 18.2 us  [the longest x1 3.09 us: per_device_line(): raw_near = lax.ppermute(raw, 'ex', PAIRS)]
    transpose x2 -> x0, local copies, waits for them, and re-layouts: 4.82 us -> none  [per_device_line(): train_grads[:, p * step:(p + 1) * step].transpose(1, 0, 2)]
    slice x1 -> x0, local copies, waits for them, and re-layouts: 3.98 us -> none  [per_device_line(): train_grads[:, p * step:(p + 1) * step].transpose(1, 0, 2)]
    ppermute x14 -> x13, waiting for transfers between devices: 28.1 us -> 24.8 us  [the longest x1 12.1 us: per_device_line(): mid_out = lax.ppermute(after(mid, grads), 'ex', OUTWARD)]
    pallas_call x2 -> x3, Pallas kernels: 3.95 us -> 3.75 us  [condition(): pl.pallas_call(condition_kernel, out_shape=jax.ShapeDtypeStruct((rows, co...]
    unnamed x10 -> x8, local copies, waits for them, and re-layouts: 1.91 us -> 1.91 us
  transfers between devices with their start and end apart: 15 -> 14, of which waited for: 5 -> 6; matrix products, arithmetic and copies ran while one was open for 12% -> 17% of each run, Pallas kernels for 10% -> 11%
where the time goes in v2:
time: 75.4 us; the launch traced here: 75 us
  waiting for transfers between devices  27.7 us (37%)
  starting transfers between devices  19.1 us (25%)
  local copies, waits for them, and re-layouts  15.3 us (20%)
  Pallas kernels  11.7 us (16%)
  other arithmetic  0.98 us (1%)
    ppermute x1, waiting for transfers between devices, per_device_line(): mid_out = lax.ppermute(after(mid, grads), 'ex', OUTWARD)  12.1 us
    optimization_barrier x1, local copies, waits for them, and re-layouts, after(): return lax.optimization_barrier((x, *others))[0]  11.4 us
    ppermute x1, waiting for transfers between devices, per_device_line(): raw_mid_out = lax.ppermute(after(raw_mid, *terms), 'ex', OUTWARD)  8.29 us
    pallas_call x2, Pallas kernels, score_call(): pl.pallas_call(lambda *refs: kernel(ex, *refs), out_shape=out_shape, in_s...  7.92 us
    pallas_call x3, Pallas kernels, condition(): pl.pallas_call(condition_kernel, out_shape=jax.ShapeDtypeStruct((rows, co...  3.75 us
    ppermute x1, starting transfers between devices, per_device_line(): raw_near = lax.ppermute(raw, 'ex', PAIRS)  3.09 us
    ppermute x1, waiting for transfers between devices, per_device_line(): scores = mine + lax.ppermute(send, 'feat', swap)  2.91 us
    ppermute x1, starting transfers between devices, per_device_line(): near = lax.ppermute(late, 'ex', PAIRS)  2.77 us
  transfers between devices with their start and end apart: 14, of which 6 were waited for; matrix products, arithmetic and copies ran while one was open for 17% of the time, Pallas kernels for 11%

profile of v2, /device:TPU:0, one launch (start us, length us, event | category | flops | bytes accessed | tf_op | source)
XLA Modules:
  0.0 75.0 jit_solution(13080498882323946681)
XLA Ops:
  0.0 1.0 %slice_bitcast_fusion.1 = bf16[4,128,256]{2,1,0:T(8,128)(2,1)S(1)} fusion(bf16[1,12,128,256]{3,2,1,0:T(8,128)(2,1)} %param.6), kind=kLoop, calls=%fused_computation.4 | loop fusion | bytes 524288 | tf_op jit(solution)/shard_map/squeeze | solution.py:168
  1.0 3.1 %collective-permute-start = (bf16[4,128,256]{2,1,0:T(8,128)(2,1)S(1)}, bf16[4,128,256]{2,1,0:T(8,128)(2,1)S(1)}, u32[]{:S(2)}, u32[]{:S(2)}) collective-permute-start(bf16[4,128,256]{2,1,0:T(8,128)(2,1)S(1)} %slice_bitcast_fusion.1), channel_id=1, source_target_pairs={{0,4},{4,0},{8,12},{12,8},{1,5},{5,1},{9,13},{13,9},{2,6},{6,2},{1... | collective-permute-start | bytes 786440 | tf_op jit(solution)/shard_map/ppermute | solution.py:170
  4.1 0.7 collective-permute-start.2
  4.7 1.1 %slice_bitcast_fusion.own_ref = bf16[8,128,256]{2,1,0:T(8,128)(2,1)S(1)} fusion(bf16[1,12,128,256]{3,2,1,0:T(8,128)(2,1)} %param.6), kind=kLoop, calls=%fused_computation.3 | loop fusion | bytes 1048576 | tf_op jit(solution)/shard_map/squeeze | solution.py:169
  5.8 1.6 %collective-permute-start.4 = (bf16[8,128,256]{2,1,0:T(8,128)(2,1)S(1)}, bf16[8,128,256]{2,1,0:T(8,128)(2,1)S(1)}, u32[]{:S(2)}, u32[]{:S(2)}) collective-permute-start(bf16[8,128,256]{2,1,0:T(8,128)(2,1)S(1)} %slice_bitcast_fusion.own_ref), channel_id=1, source_target_pairs={{0,2},{2,0},{1,3},{3,1},{4,6},{6,4},{5,7},{7,5},{8,10},{10,8},{9,1... | collective-permute-start | bytes 1572872 | tf_op jit(solution)/shard_map/ppermute | solution.py:172
  7.4 0.9 %copy-done.1 = f32[256,256]{1,0:T(8,128)S(1)} copy-done((f32[256,256]{1,0:T(8,128)S(1)}, f32[256,256]{1,0:T(8,128)}, u32[]{:S(2)}) %copy-start.1) | copy-done | bytes 262168
  8.3 0.9 %copy-done.2 = f32[256,256]{1,0:T(8,128)S(1)} copy-done((f32[256,256]{1,0:T(8,128)S(1)}, f32[256,256]{1,0:T(8,128)}, u32[]{:S(2)}) %copy-start.2) | copy-done | bytes 262168
  9.4 1.0 %collective-permute-done = bf16[4,128,256]{2,1,0:T(8,128)(2,1)S(1)} collective-permute-done((bf16[4,128,256]{2,1,0:T(8,128)(2,1)S(1)}, bf16[4,128,256]{2,1,0:T(8,128)(2,1)S(1)}, u32[]{:S(2)}, u32[]{:S(2)}) %collective-permute-start) | collective-permute-done | bytes 262176 | tf_op jit(solution)/shard_map/ppermute | solution.py:170
  10.4 0.7 collective-permute-start.1
  11.1 1.3 %collective-permute-start.3 = (bf16[4,128,256]{2,1,0:T(8,128)(2,1)S(1)}, bf16[4,128,256]{2,1,0:T(8,128)(2,1)S(1)}, u32[]{:S(2)}, u32[]{:S(2)}) collective-permute-start(bf16[4,128,256]{2,1,0:T(8,128)(2,1)S(1)} %collective-permute-done.2), channel_id=1, source_target_pairs={{4,0},{8,12},{5,1},{9,13},{6,2},{10,14},{7,3},{11,15},{20,16},{24,... | collective-permute-start | bytes 786440 | tf_op jit(solution)/shard_map/ppermute | solution.py:175
  12.4 1.7 %collective-permute-start.6 = (bf16[8,128,256]{2,1,0:T(8,128)(2,1)S(1)}, bf16[8,128,256]{2,1,0:T(8,128)(2,1)S(1)}, u32[]{:S(2)}, u32[]{:S(2)}) collective-permute-start(bf16[8,128,256]{2,1,0:T(8,128)(2,1)S(1)} %pad_maximum_fusion.own_ref), channel_id=1, source_target_pairs={{0,2},{2,0},{1,3},{3,1},{4,6},{6,4},{5,7},{7,5},{8,10},{10,8},{9,1... | collective-permute-start | bytes 1572872 | tf_op jit(solution)/shard_map/ppermute | solution.py:177
  14.1 8.3 %collective-permute-done.3 = bf16[4,128,256]{2,1,0:T(8,128)(2,1)S(1)} collective-permute-done((bf16[4,128,256]{2,1,0:T(8,128)(2,1)S(1)}, bf16[4,128,256]{2,1,0:T(8,128)(2,1)S(1)}, u32[]{:S(2)}, u32[]{:S(2)}) %collective-permute-start.3) | collective-permute-done | bytes 262176 | tf_op jit(solution)/shard_map/ppermute | solution.py:175
  22.4 1.2 %shard_map.56.refs_2_ = bf16[128,8,256]{2,1,0:T(8,128)(2,1)S(1)} custom-call(bf16[8,128,256]{2,1,0:T(8,128)(2,1)S(1)} %slice_bitcast_fusion.own_ref, bf16[8,128,256]{2,1,0:T(8,128)(2,1)S(1)} %collective-permute-done.4.far_ref, bf16[384,256]{1,0:T(8,128)(2,1)S(1)} %get-tuple-element.21.left_ref, bf16[512,256]{1,0:T(8,128)(2,1)S(1)} %get-tuple-element.22.right_ref), custom_call_target="tpu_custom_call" | custom-call | flops 960000000 | bytes 2097152 | tf_op jit(solution)/shard_map/pallas_call | solution.py:65
  23.7 2.8 %collective-permute-start.5 = (bf16[128,8,256]{2,1,0:T(8,128)(2,1)S(1)}, bf16[128,8,256]{2,1,0:T(8,128)(2,1)S(1)}, u32[]{:S(2)}, u32[]{:S(2)}) collective-permute-start(bf16[128,8,256]{2,1,0:T(8,128)(2,1)S(1)} %shard_map.56.refs_2_), channel_id=1, source_target_pairs={{0,4},{4,0},{8,12},{12,8},{1,5},{5,1},{9,13},{13,9},{2,6},{6,2},{1... | collective-permute-start | bytes 1572872 | tf_op jit(solution)/shard_map/ppermute | solution.py:181
  26.4 0.7 collective-permute-start.8
  27.1 1.3 %collective-permute-start.10 = (bf16[4,128,256]{2,1,0:T(8,128)(2,1)S(1)}, bf16[4,128,256]{2,1,0:T(8,128)(2,1)S(1)}, u32[]{:S(2)}, u32[]{:S(2)}) collective-permute-start(bf16[4,128,256]{2,1,0:T(8,128)(2,1)S(1)} %collective-permute-done.1), channel_id=1, source_target_pairs={{4,0},{8,12},{5,1},{9,13},{6,2},{10,14},{7,3},{11,15},{20,16},{24,... | collective-permute-start | bytes 786440 | tf_op jit(solution)/shard_map/ppermute | solution.py:180
  28.4 11.4 %copy.8 = bf16[128,128,256]{2,0,1:T(8,128)(2,1)} copy(bf16[128,128,256]{2,1,0:T(8,128)(2,1)} %param.5) | data formatting | bytes 16777216 | tf_op jit(solution)/shard_map/optimization_barrier | solution.py:155
  39.8 0.8 %collective-permute-start.7 = (bf16[128,8,256]{2,1,0:T(8,128)(2,1)S(1)}, bf16[128,8,256]{2,1,0:T(8,128)(2,1)S(1)}, u32[]{:S(2)}, u32[]{:S(2)}) collective-permute-start(bf16[128,8,256]{2,1,0:T(8,128)(2,1)S(1)} %collective-permute-done.5.refs_3_), channel_id=1, source_target_pairs={{4,8},{8,4},{5,9},{9,5},{6,10},{10,6},{7,11},{11,7},{20,24},{24,20... | collective-permute-start | bytes 1572872 | tf_op jit(solution)/shard_map/ppermute | solution.py:186
  40.7 0.8 %collective-permute-done.10 = bf16[4,128,256]{2,1,0:T(8,128)(2,1)S(1)} collective-permute-done((bf16[4,128,256]{2,1,0:T(8,128)(2,1)S(1)}, bf16[4,128,256]{2,1,0:T(8,128)(2,1)S(1)}, u32[]{:S(2)}, u32[]{:S(2)}) %collective-permute-start.10) | collective-permute-done | bytes 262176 | tf_op jit(solution)/shard_map/ppermute | solution.py:180
  41.6 1.4 %collective-permute-start.9 = (bf16[128,8,256]{2,1,0:T(8,128)(2,1)S(1)}, bf16[128,8,256]{2,1,0:T(8,128)(2,1)S(1)}, u32[]{:S(2)}, u32[]{:S(2)}) collective-permute-start(bf16[128,8,256]{2,1,0:T(8,128)(2,1)S(1)} %collective-permute-done.8), channel_id=1, source_target_pairs={{4,0},{8,12},{5,1},{9,13},{6,2},{10,14},{7,3},{11,15},{20,16},{24,... | collective-permute-start | bytes 1572872 | tf_op jit(solution)/shard_map/ppermute | solution.py:187
  43.1 1.0 %collective-permute-start.11 = (bf16[8,128,256]{2,1,0:T(8,128)(2,1)S(1)}, bf16[8,128,256]{2,1,0:T(8,128)(2,1)S(1)}, u32[]{:S(2)}, u32[]{:S(2)}) collective-permute-start(bf16[8,128,256]{2,1,0:T(8,128)(2,1)S(1)} %pad_maximum_fusion.1.own_ref), channel_id=1, source_target_pairs={{0,2},{2,0},{1,3},{3,1},{4,6},{6,4},{5,7},{7,5},{8,10},{10,8},{9,1... | collective-permute-start | bytes 1572872 | tf_op jit(solution)/shard_map/ppermute | solution.py:185
  44.1 1.3 %collective-permute-start.12 = (bf16[128,8,256]{2,1,0:T(8,128)(2,1)S(1)}, bf16[128,8,256]{2,1,0:T(8,128)(2,1)S(1)}, u32[]{:S(2)}, u32[]{:S(2)}) collective-permute-start(bf16[128,8,256]{2,1,0:T(8,128)(2,1)S(1)} %collective-permute-done.7.refs_5_), channel_id=1, source_target_pairs={{4,0},{8,12},{5,1},{9,13},{6,2},{10,14},{7,3},{11,15},{20,16},{24,... | collective-permute-start | bytes 1572872 | tf_op jit(solution)/shard_map/ppermute | solution.py:190
  45.4 12.1 %collective-permute-done.9 = bf16[128,8,256]{2,1,0:T(8,128)(2,1)S(1)} collective-permute-done((bf16[128,8,256]{2,1,0:T(8,128)(2,1)S(1)}, bf16[128,8,256]{2,1,0:T(8,128)(2,1)S(1)}, u32[]{:S(2)}, u32[]{:S(2)}) %collective-permute-start.9) | collective-permute-done | bytes 524320 | tf_op jit(solution)/shard_map/ppermute | solution.py:187
  57.5 1.3 %shard_map.57.refs_0_ = bf16[128,8,256]{2,1,0:T(8,128)(2,1)S(1)} custom-call(bf16[8,128,256]{2,1,0:T(8,128)(2,1)S(1)} %pad_maximum_fusion.own_ref, bf16[8,128,256]{2,1,0:T(8,128)(2,1)S(1)} %collective-permute-done.6.far_ref, bf16[384,256]{1,0:T(8,128)(2,1)S(1)} %get-tuple-element.21.left_ref, bf16[512,256]{1,0:T(8,128)(2,1)S(1)} %get-tuple-element.22.right_ref), custom_call_target="tpu_custom_call" | custom-call | flops 960000000 | bytes 2097152 | tf_op jit(solution)/shard_map/pallas_call | solution.py:65
  58.8 0.1 add.14.refs_4_
  58.9 1.2 %shard_map.58.refs_1_ = bf16[128,8,256]{2,1,0:T(8,128)(2,1)S(1)} custom-call(bf16[8,128,256]{2,1,0:T(8,128)(2,1)S(1)} %pad_maximum_fusion.1.own_ref, bf16[8,128,256]{2,1,0:T(8,128)(2,1)S(1)} %collective-permute-done.11.far_ref, bf16[384,256]{1,0:T(8,128)(2,1)S(1)} %get-tuple-element.21.left_ref, bf16[512,256]{1,0:T(8,128)(2,1)S(1)} %get-tuple-element.22.right_ref), custom_call_target="tpu_custom_call" | custom-call | flops 960000000 | bytes 2097152 | tf_op jit(solution)/shard_map/pallas_call | solution.py:65
  60.2 4.3 %shard_map.59.refs_0_ = f32[48,128]{1,0:T(8,128)S(1)} custom-call(bf16[128,8,256]{2,1,0:T(8,128)(2,1)S(1)} %shard_map.57.refs_0_, bf16[128,8,256]{2,1,0:T(8,128)(2,1)S(1)} %shard_map.58.refs_1_, bf16[128,8,256]{2,1,0:T(8,128)(2,1)S(1)} %shard_map.56.refs_2_, bf16[128,8,256]{2,1,0:T(8,128)(2,1)S(1)} %collective-permute-done.5.refs_3_, ...), custom_call_target="tpu_custom_call" | custom-call | flops 3000000000 | bytes 12000000 | tf_op jit(solution)/shard_map/pallas_call | solution.py:143
  64.5 2.5 %collective-permute-done.12.refs_1_ = bf16[128,8,256]{2,1,0:T(8,128)(2,1)S(1)} collective-permute-done((bf16[128,8,256]{2,1,0:T(8,128)(2,1)S(1)}, bf16[128,8,256]{2,1,0:T(8,128)(2,1)S(1)}, u32[]{:S(2)}, u32[]{:S(2)}) %collective-permute-start.12) | collective-permute-done | bytes 524320 | tf_op jit(solution)/shard_map/ppermute | solution.py:190
  67.0 3.6 %shard_map.60 = (f32[24,128]{1,0:T(8,128)S(1)}, f32[24,128]{1,0:T(8,128)S(1)}) custom-call(f32[48,128]{1,0:T(8,128)S(1)} %shard_map.59.refs_0_, bf16[128,8,256]{2,1,0:T(8,128)(2,1)S(1)} %collective-permute-done.12.refs_1_, bf16[128,128,256]{2,1,0:T(8,128)(2,1)S(1)} %bitcast.12, s32[4]{0:T(128)S(1)} %copy-done.3), custom_call_target="tpu_custom_call" | custom-call | flops 3000000000 | bytes 12000000 | tf_op jit(solution)/shard_map/pallas_call | solution.py:143
  70.7 0.8 %collective-permute-start.13 = (f32[24,128]{1,0:T(8,128)S(1)}, f32[24,128]{1,0:T(8,128)S(1)}, u32[]{:S(2)}, u32[]{:S(2)}) collective-permute-start(f32[24,128]{1,0:T(8,128)S(1)} %get-tuple-element.32), channel_id=1, source_target_pairs={{0,2},{2,0},{1,3},{3,1},{4,6},{6,4},{5,7},{7,5},{8,10},{10,8},{9,1... | collective-permute-start | bytes 36872 | tf_op jit(solution)/shard_map/ppermute | solution.py:201
  71.5 2.9 %collective-permute-done.13 = f32[24,128]{1,0:T(8,128)S(1)} collective-permute-done((f32[24,128]{1,0:T(8,128)S(1)}, f32[24,128]{1,0:T(8,128)S(1)}, u32[]{:S(2)}, u32[]{:S(2)}) %collective-permute-start.13) | collective-permute-done | bytes 12320 | tf_op jit(solution)/shard_map/ppermute | solution.py:201
  74.4 0.6 add_bitcast_fusion
  (19 shorter events, 0.3 us)
Async XLA Ops:
  1.0 9.4 %collective-permute-start = (bf16[4,128,256]{2,1,0:T(8,128)(2,1)S(1)}, bf16[4,128,256]{2,1,0:T(8,128)(2,1)S(1)}, u32[]{:S(2)}, u32[]{:S(2)}) collective-permute-start(bf16[4,128,256]{2,1,0:T(8,128)(2,1)S(1)} %slice_bitcast_fusion.1), channel_id=1, source_target_pairs={{0,4},{4,0},{8,12},{12,8},{1,5},{5,1},{9,13},{13,9},{2,6},{6,2},{1... | collective-permute-start | bytes 786440 | tf_op jit(solution)/shard_map/ppermute | solution.py:170
  4.1 7.0 %collective-permute-start.2 = (bf16[4,128,256]{2,1,0:T(8,128)(2,1)S(1)}, bf16[4,128,256]{2,1,0:T(8,128)(2,1)S(1)}, u32[]{:S(2)}, u32[]{:S(2)}) collective-permute-start(bf16[4,128,256]{2,1,0:T(8,128)(2,1)S(1)} %slice_bitcast_fusion.1), channel_id=1, source_target_pairs={{4,8},{8,4},{5,9},{9,5},{6,10},{10,6},{7,11},{11,7},{20,24},{24,20... | collective-permute-start | bytes 786440 | tf_op jit(solution)/shard_map/ppermute | solution.py:171
  5.8 16.6 %collective-permute-start.4 = (bf16[8,128,256]{2,1,0:T(8,128)(2,1)S(1)}, bf16[8,128,256]{2,1,0:T(8,128)(2,1)S(1)}, u32[]{:S(2)}, u32[]{:S(2)}) collective-permute-start(bf16[8,128,256]{2,1,0:T(8,128)(2,1)S(1)} %slice_bitcast_fusion.own_ref), channel_id=1, source_target_pairs={{0,2},{2,0},{1,3},{3,1},{4,6},{6,4},{5,7},{7,5},{8,10},{10,8},{9,1... | collective-permute-start | bytes 1572872 | tf_op jit(solution)/shard_map/ppermute | solution.py:172
  7.4 0.9 %copy-start.1 = (f32[256,256]{1,0:T(8,128)S(1)}, f32[256,256]{1,0:T(8,128)}, u32[]{:S(2)}) copy-start(f32[256,256]{1,0:T(8,128)} %left_ref.1) | copy-start | bytes 786436
  8.3 0.9 %copy-start.2 = (f32[256,256]{1,0:T(8,128)S(1)}, f32[256,256]{1,0:T(8,128)}, u32[]{:S(2)}) copy-start(f32[256,256]{1,0:T(8,128)} %right_ref) | copy-start | bytes 786436
  10.4 3.8 %collective-permute-start.1 = (bf16[4,128,256]{2,1,0:T(8,128)(2,1)S(1)}, bf16[4,128,256]{2,1,0:T(8,128)(2,1)S(1)}, u32[]{:S(2)}, u32[]{:S(2)}) collective-permute-start(bf16[4,128,256]{2,1,0:T(8,128)(2,1)S(1)} %collective-permute-done), channel_id=1, source_target_pairs={{4,8},{8,4},{5,9},{9,5},{6,10},{10,6},{7,11},{11,7},{20,24},{24,20... | collective-permute-start | bytes 786440 | tf_op jit(solution)/shard_map/ppermute | solution.py:174
  11.1 11.4 %collective-permute-start.3 = (bf16[4,128,256]{2,1,0:T(8,128)(2,1)S(1)}, bf16[4,128,256]{2,1,0:T(8,128)(2,1)S(1)}, u32[]{:S(2)}, u32[]{:S(2)}) collective-permute-start(bf16[4,128,256]{2,1,0:T(8,128)(2,1)S(1)} %collective-permute-done.2), channel_id=1, source_target_pairs={{4,0},{8,12},{5,1},{9,13},{6,2},{10,14},{7,3},{11,15},{20,16},{24,... | collective-permute-start | bytes 786440 | tf_op jit(solution)/shard_map/ppermute | solution.py:175
  12.4 27.4 %collective-permute-start.6 = (bf16[8,128,256]{2,1,0:T(8,128)(2,1)S(1)}, bf16[8,128,256]{2,1,0:T(8,128)(2,1)S(1)}, u32[]{:S(2)}, u32[]{:S(2)}) collective-permute-start(bf16[8,128,256]{2,1,0:T(8,128)(2,1)S(1)} %pad_maximum_fusion.own_ref), channel_id=1, source_target_pairs={{0,2},{2,0},{1,3},{3,1},{4,6},{6,4},{5,7},{7,5},{8,10},{10,8},{9,1... | collective-permute-start | bytes 1572872 | tf_op jit(solution)/shard_map/ppermute | solution.py:177
  23.7 16.2 %collective-permute-start.5 = (bf16[128,8,256]{2,1,0:T(8,128)(2,1)S(1)}, bf16[128,8,256]{2,1,0:T(8,128)(2,1)S(1)}, u32[]{:S(2)}, u32[]{:S(2)}) collective-permute-start(bf16[128,8,256]{2,1,0:T(8,128)(2,1)S(1)} %shard_map.56.refs_2_), channel_id=1, source_target_pairs={{0,4},{4,0},{8,12},{12,8},{1,5},{5,1},{9,13},{13,9},{2,6},{6,2},{1... | collective-permute-start | bytes 1572872 | tf_op jit(solution)/shard_map/ppermute | solution.py:181
  26.4 15.2 %collective-permute-start.8 = (bf16[128,8,256]{2,1,0:T(8,128)(2,1)S(1)}, bf16[128,8,256]{2,1,0:T(8,128)(2,1)S(1)}, u32[]{:S(2)}, u32[]{:S(2)}) collective-permute-start(bf16[128,8,256]{2,1,0:T(8,128)(2,1)S(1)} %shard_map.56.refs_2_), channel_id=1, source_target_pairs={{4,8},{8,4},{5,9},{9,5},{6,10},{10,6},{7,11},{11,7},{20,24},{24,20... | collective-permute-start | bytes 1572872 | tf_op jit(solution)/shard_map/ppermute | solution.py:182
  27.1 14.4 %collective-permute-start.10 = (bf16[4,128,256]{2,1,0:T(8,128)(2,1)S(1)}, bf16[4,128,256]{2,1,0:T(8,128)(2,1)S(1)}, u32[]{:S(2)}, u32[]{:S(2)}) collective-permute-start(bf16[4,128,256]{2,1,0:T(8,128)(2,1)S(1)} %collective-permute-done.1), channel_id=1, source_target_pairs={{4,0},{8,12},{5,1},{9,13},{6,2},{10,14},{7,3},{11,15},{20,16},{24,... | collective-permute-start | bytes 786440 | tf_op jit(solution)/shard_map/ppermute | solution.py:180
  39.8 20.4 %copy-start = (bf16[128,128,256]{2,0,1:T(8,128)(2,1)S(1)}, bf16[128,128,256]{2,0,1:T(8,128)(2,1)}, u32[]{:S(2)}) copy-start(bf16[128,128,256]{2,0,1:T(8,128)(2,1)} %copy.8) | copy-start | bytes 25165828
  39.8 20.4 %copy-start.3 = (s32[4]{0:T(128)S(1)}, s32[4]{0:T(128)}, u32[]{:S(2)}) copy-start(s32[4]{0:T(128)} %refs_3_.1) | copy-start | bytes 52
  39.8 4.3 %collective-permute-start.7 = (bf16[128,8,256]{2,1,0:T(8,128)(2,1)S(1)}, bf16[128,8,256]{2,1,0:T(8,128)(2,1)S(1)}, u32[]{:S(2)}, u32[]{:S(2)}) collective-permute-start(bf16[128,8,256]{2,1,0:T(8,128)(2,1)S(1)} %collective-permute-done.5.refs_3_), channel_id=1, source_target_pairs={{4,8},{8,4},{5,9},{9,5},{6,10},{10,6},{7,11},{11,7},{20,24},{24,20... | collective-permute-start | bytes 1572872 | tf_op jit(solution)/shard_map/ppermute | solution.py:186
  41.6 15.9 %collective-permute-start.9 = (bf16[128,8,256]{2,1,0:T(8,128)(2,1)S(1)}, bf16[128,8,256]{2,1,0:T(8,128)(2,1)S(1)}, u32[]{:S(2)}, u32[]{:S(2)}) collective-permute-start(bf16[128,8,256]{2,1,0:T(8,128)(2,1)S(1)} %collective-permute-done.8), channel_id=1, source_target_pairs={{4,0},{8,12},{5,1},{9,13},{6,2},{10,14},{7,3},{11,15},{20,16},{24,... | collective-permute-start | bytes 1572872 | tf_op jit(solution)/shard_map/ppermute | solution.py:187
  43.1 15.8 %collective-permute-start.11 = (bf16[8,128,256]{2,1,0:T(8,128)(2,1)S(1)}, bf16[8,128,256]{2,1,0:T(8,128)(2,1)S(1)}, u32[]{:S(2)}, u32[]{:S(2)}) collective-permute-start(bf16[8,128,256]{2,1,0:T(8,128)(2,1)S(1)} %pad_maximum_fusion.1.own_ref), channel_id=1, source_target_pairs={{0,2},{2,0},{1,3},{3,1},{4,6},{6,4},{5,7},{7,5},{8,10},{10,8},{9,1... | collective-permute-start | bytes 1572872 | tf_op jit(solution)/shard_map/ppermute | solution.py:185
  44.1 22.9 %collective-permute-start.12 = (bf16[128,8,256]{2,1,0:T(8,128)(2,1)S(1)}, bf16[128,8,256]{2,1,0:T(8,128)(2,1)S(1)}, u32[]{:S(2)}, u32[]{:S(2)}) collective-permute-start(bf16[128,8,256]{2,1,0:T(8,128)(2,1)S(1)} %collective-permute-done.7.refs_5_), channel_id=1, source_target_pairs={{4,0},{8,12},{5,1},{9,13},{6,2},{10,14},{7,3},{11,15},{20,16},{24,... | collective-permute-start | bytes 1572872 | tf_op jit(solution)/shard_map/ppermute | solution.py:190
  70.7 3.8 %collective-permute-start.13 = (f32[24,128]{1,0:T(8,128)S(1)}, f32[24,128]{1,0:T(8,128)S(1)}, u32[]{:S(2)}, u32[]{:S(2)}) collective-permute-start(f32[24,128]{1,0:T(8,128)S(1)} %get-tuple-element.32), channel_id=1, source_target_pairs={{0,2},{2,0},{1,3},{3,1},{4,6},{6,4},{5,7},{7,5},{8,10},{10,8},{9,1... | collective-permute-start | bytes 36872 | tf_op jit(solution)/shard_map/ppermute | solution.py:201

commit v3 on v2

--- a/solution.py
+++ b/solution.py
@@ -1,3 +1,5 @@
+import functools
+
 import jax
 import jax.numpy as jnp
 from jax import lax
@@ -8,6 +10,9 @@
 F32 = jnp.float32
 BF16 = jnp.bfloat16
 EARLY = 4
+TILE = 16
+EXAMPLES = 32
+DEEP = 32
 VMEM = pl.BlockSpec(memory_space=pltpu.VMEM)
 SMEM = pl.BlockSpec(memory_space=pltpu.SMEM)
 
@@ -73,32 +78,62 @@
     )(own, far, left_terms, right_terms)
 
 
-def inner_products(query_refs, grad_refs):
+def regroup_kernel(grads_ref, out_ref, held_ref, sems):
+    examples, rows, width = held_ref.shape
+    blocks = examples // EXAMPLES
+    copies = []
+    for b in range(blocks):
+        part = pl.ds(b * EXAMPLES, EXAMPLES)
+        copies.append(pltpu.make_async_copy(grads_ref.at[part], held_ref.at[part], sems.at[b]))
+        copies[-1].start()
+    i = lax.broadcasted_iota(jnp.int32, (TILE * TILE, TILE * TILE), 0)
+    j = lax.broadcasted_iota(jnp.int32, (TILE * TILE, TILE * TILE), 1)
+    swap = jnp.where((i // TILE == j % TILE) & (i % TILE == j // TILE), 1.0, 0.0).astype(BF16)
+    for b in range(blocks):
+        copies[b].wait()
+
+        @pl.loop(b * EXAMPLES // TILE, (b + 1) * EXAMPLES // TILE)
+        def _(step):
+            n = pl.ds(pl.multiple_of(step * TILE, TILE), TILE)
+            for r in range(0, rows, TILE):
+                tile = held_ref[n, r : r + TILE, :].reshape(TILE * TILE, width)
+                turned = jnp.dot(swap, tile, preferred_element_type=F32).astype(BF16)
+                out_ref[r : r + TILE, n, :] = turned.reshape(TILE, TILE, width)
+
+
+def regroup(grads):
+    n, rows, width = grads.shape
+    return pl.pallas_call(
+        regroup_kernel,
+        out_shape=jax.ShapeDtypeStruct((rows, n, width), BF16),
+        in_specs=[pl.BlockSpec(memory_space=pltpu.HBM)],
+        out_specs=VMEM,
+        scratch_shapes=[pltpu.VMEM((n, rows, width), BF16), pltpu.SemaphoreType.DMA((n // EXAMPLES,))],
+        compiler_params=pltpu.CompilerParams(vmem_limit_bytes=48 << 20),
+        cost_estimate=pl.CostEstimate(flops=6_000_000_000, bytes_accessed=16_000_000, transcendentals=0),
+    )(grads)
+
+
+def inner_products(query_refs, grad_ref):
     total = sum(ref.shape[1] for ref in query_refs)
-    acc = jnp.zeros((total, grad_refs[0].shape[1]), F32)
-    first = 0
-    for grad_ref in grad_refs:
-        count = grad_ref.shape[0]
-        unroll = 16
-
-        def body(i, acc, grad_ref=grad_ref, first=first):
-            for j in range(unroll):
-                r = i * unroll + j
-                queries = jnp.concatenate([ref[first + r] for ref in query_refs], axis=0)
-                acc = acc + lax.dot_general(
-                    queries, grad_ref[r], (((1,), (1,)), ((), ())), preferred_element_type=F32
-                )
-            return acc
-
-        acc = lax.fori_loop(0, count // unroll, body, acc)
-        first += count
-    return acc
-
-
-def first_pass_kernel(ex, early_0, early_1, own_ref, near, mid, far_in, *rest):
-    *grad_refs, order_ref, out_ref = rest
+
+    def body(i, acc):
+        at = [i * DEEP + j for j in range(DEEP)]
+        queries = [jnp.concatenate([ref[r] for ref in query_refs], axis=0) for r in at]
+        return acc + lax.dot_general(
+            jnp.concatenate(queries, axis=1),
+            jnp.concatenate([grad_ref[r] for r in at], axis=1),
+            (((1,), (1,)), ((), ())),
+            preferred_element_type=F32,
+        )
+
+    start = jnp.zeros((total, grad_ref.shape[1]), F32)
+    return lax.fori_loop(0, grad_ref.shape[0] // DEEP, body, start)
+
+
+def first_pass_kernel(ex, early_0, early_1, own_ref, near, mid, far_in, grad_ref, order_ref, out_ref):
     late = own_ref.shape[1]
-    acc = inner_products((early_0, early_1, own_ref, near, mid, far_in), grad_refs)
+    acc = inner_products((early_0, early_1, own_ref, near, mid, far_in), grad_ref)
     me = lax.axis_index("ex")
     sources = slot_sources(me)
     early = [acc[EARLY * s : EARLY * (s + 1)] for s in range(ex)]
@@ -123,10 +158,9 @@
     return [me, near, jnp.where(low_pair, 2, 1), jnp.where(low_pair, 3, 0)]
 
 
-def last_pass_kernel(ex, base_ref, far_out, *rest):
-    *grad_refs, order_ref, mine_ref, send_ref, full_ref = rest
+def last_pass_kernel(ex, base_ref, far_out, grad_ref, order_ref, mine_ref, send_ref, full_ref):
     late = far_out.shape[1]
-    acc = inner_products((far_out,), grad_refs)
+    acc = inner_products((far_out,), grad_ref)
     far = slot_sources(lax.axis_index("ex"))[3]
     full_ref[...] = base_ref[...]
     for b in range(ex):
@@ -138,17 +172,16 @@
     send_ref[...] = full_ref[pl.ds(pl.multiple_of((1 - side) * half, half), half), :]
 
 
-def score_call(kernel, ex, arrays, pieces, order, out_shape, scratch=()):
-    count = len(arrays) + len(pieces)
-    return pl.pallas_call(
-        lambda *refs: kernel(ex, *refs),
+def score_call(kernel, ex, arrays, order, out_shape, scratch=()):
+    return pl.pallas_call(
+        functools.partial(kernel, ex),
         out_shape=out_shape,
-        in_specs=[VMEM] * count + [SMEM],
+        in_specs=[VMEM] * len(arrays) + [SMEM],
         out_specs=jax.tree.map(lambda _: VMEM, out_shape),
         scratch_shapes=scratch,
-        compiler_params=pltpu.CompilerParams(vmem_limit_bytes=32 << 20),
+        compiler_params=pltpu.CompilerParams(vmem_limit_bytes=40 << 20),
         cost_estimate=pl.CostEstimate(flops=3_000_000_000, bytes_accessed=12_000_000, transcendentals=0),
-    )(*arrays, *pieces, order)
+    )(*arrays, order)
 
 
 def after(x, *others):
@@ -165,37 +198,37 @@
     swap = [(0, 1), (1, 0)]
     count = queries.shape[1]
     n = train_grads.shape[0]
-    raw = queries[0, :EARLY]
-    late_raw = after(queries, raw)[0, EARLY:]
+    late_raw = queries[0, EARLY:]
+    late_other = lax.ppermute(late_raw, "feat", swap)
+    raw = after(queries, late_raw)[0, :EARLY]
+    terms = factor_terms(left_factor, after(right_factor, raw), train_grads.shape[1])
     raw_near = lax.ppermute(raw, "ex", PAIRS)
     raw_mid = lax.ppermute(raw, "ex", MIDDLE)
-    late_other = lax.ppermute(late_raw, "feat", swap)
-    terms = factor_terms(left_factor, after(right_factor, late_raw), train_grads.shape[1])
+    grads = regroup(after(train_grads, late_other))
     raw_far_mid = lax.ppermute(after(raw_near, *terms), "ex", MIDDLE)
-    raw_mid_out = lax.ppermute(after(raw_mid, *terms), "ex", OUTWARD)
-    early_0 = jnp.concatenate([raw, raw_near], axis=0)
-    early_0_other = lax.ppermute(early_0, "feat", swap)
-
-    late = condition(after(late_raw, raw_far_mid, raw_mid_out), late_other, *terms)
-    raw_far_out = lax.ppermute(raw_far_mid, "ex", OUTWARD)
+    raw_mid_out = lax.ppermute(raw_mid, "ex", OUTWARD)
+
+    late = condition(after(late_raw, raw_far_mid, raw_mid_out, grads), late_other, *terms)
     near = lax.ppermute(late, "ex", PAIRS)
     mid = lax.ppermute(late, "ex", MIDDLE)
-    grads = after(train_grads, late).transpose(1, 0, 2)
+    early_0 = jnp.concatenate([raw, after(raw_near, late)], axis=0)
+    early_0_other = lax.ppermute(early_0, "feat", swap)
+    raw_far_out = lax.ppermute(after(raw_far_mid, near), "ex", OUTWARD)
+    far_mid = lax.ppermute(near, "ex", MIDDLE)
+    mid_out = lax.ppermute(after(mid, near), "ex", OUTWARD)
+    cond_0 = condition(after(early_0, near, mid), early_0_other, *terms)
     early_1 = jnp.concatenate([raw_mid + raw_mid_out, raw_far_mid + raw_far_out], axis=0)
-    early_1_other = lax.ppermute(early_1, "feat", swap)
-    far_mid = lax.ppermute(after(near, grads, early_0_other), "ex", MIDDLE)
-    mid_out = lax.ppermute(after(mid, grads), "ex", OUTWARD)
-    cond_0 = condition(after(early_0, far_mid, mid_out), early_0_other, *terms)
-    cond_1 = condition(after(early_1, cond_0), early_1_other, *terms)
+    early_1_other = lax.ppermute(after(early_1, cond_0), "feat", swap)
     far_out = lax.ppermute(far_mid, "ex", OUTWARD)
-    pieces = [grads]
+    cond_1 = condition(after(early_1, far_mid), early_1_other, *terms)
+
     base = score_call(
-        first_pass_kernel, ex, (cond_0, cond_1, late, near, mid + mid_out, far_mid), pieces, block_order,
+        first_pass_kernel, ex, (cond_0, cond_1, late, near, mid + mid_out, far_mid, grads), block_order,
         jax.ShapeDtypeStruct((ex * count, n), F32),
     )
     half = jax.ShapeDtypeStruct((ex * count // 2, n), F32)
     mine, send = score_call(
-        last_pass_kernel, ex, (base, far_out), pieces, block_order, (half, half),
+        last_pass_kernel, ex, (base, far_out, grads), block_order, (half, half),
         [pltpu.VMEM((ex * count, n), F32)],
     )
     scores = mine + lax.ppermute(send, "feat", swap)

time: 75.4 us -> 77.7 us (1.031)
  local copies, waits for them, and re-layouts: 15.3 us -> 3.95 us
  Pallas kernels: 11.7 us -> 19.4 us
  waiting for transfers between devices: 27.7 us -> 33.9 us
    optimization_barrier x1 -> x0, local copies, waits for them, and re-layouts: 11.4 us -> none  [after(): return lax.optimization_barrier((x, *others))[0]]
    ppermute x1, waiting for transfers between devices: 0.01 us -> 9.1 us  [per_device_line(): near = lax.ppermute(late, 'ex', PAIRS)]
    ppermute x5, waiting for transfers between devices: 21.2 us -> 13.1 us  [the longest x1 6.2 us: per_device_line(): raw_far_out = lax.ppermute(after(raw_far_mid, near), 'ex', OUTWARD)]
    pallas_call x2 -> x3, Pallas kernels: 7.92 us -> 15.6 us  [the longest x1 8.42 us: regroup(): pl.pallas_call(regroup_kernel, out_shape=jax.ShapeDtypeStruct((rows, n, w...]
    ppermute x1, waiting for transfers between devices: 1.01 us -> 3.53 us  [per_device_line(): raw_near = lax.ppermute(raw, 'ex', PAIRS)]
    ppermute x1, waiting for transfers between devices: 2.52 us -> 4.5 us  [per_device_line(): far_out = lax.ppermute(far_mid, 'ex', OUTWARD)]
    ppermute x1, starting transfers between devices: 1.56 us -> 3 us  [per_device_line(): late_other = lax.ppermute(late_raw, 'feat', swap)]
    ppermute x1, starting transfers between devices: 3.09 us -> 1.64 us  [per_device_line(): raw_near = lax.ppermute(raw, 'ex', PAIRS)]
  transfers between devices with their start and end apart: 14 -> 14, of which waited for: 6 -> 8; matrix products, arithmetic and copies ran while one was open for 17% -> 2% of each run, Pallas kernels for 11% -> 19%
where the time goes in v3:
time: 77.7 us; the launch traced here: 77.4 us
  waiting for transfers between devices  33.9 us (44%)
  Pallas kernels  19.4 us (25%)
  starting transfers between devices  18.8 us (24%)
  local copies, waits for them, and re-layouts  3.95 us (5%)
  other arithmetic  0.98 us (1%)
    ppermute x1, waiting for transfers between devices, per_device_line(): near = lax.ppermute(late, 'ex', PAIRS)  9.1 us
    pallas_call x1, Pallas kernels, regroup(): pl.pallas_call(regroup_kernel, out_shape=jax.ShapeDtypeStruct((rows, n, w...  8.42 us
    pallas_call x2, Pallas kernels, score_call(): pl.pallas_call(functools.partial(kernel, ex), out_shape=out_shape, in_spe...  7.16 us
    ppermute x1, waiting for transfers between devices, per_device_line(): raw_far_out = lax.ppermute(after(raw_far_mid, near), 'ex', OUTWARD)  6.2 us
    ppermute x1, waiting for transfers between devices, per_device_line(): mid_out = lax.ppermute(after(mid, near), 'ex', OUTWARD)  5.85 us
    ppermute x1, waiting for transfers between devices, per_device_line(): far_out = lax.ppermute(far_mid, 'ex', OUTWARD)  4.5 us
    pallas_call x3, Pallas kernels, condition(): pl.pallas_call(condition_kernel, out_shape=jax.ShapeDtypeStruct((rows, co...  3.79 us
    ppermute x1, waiting for transfers between devices, per_device_line(): raw_near = lax.ppermute(raw, 'ex', PAIRS)  3.53 us
  transfers between devices with their start and end apart: 14, of which 8 were waited for; matrix products, arithmetic and copies ran while one was open for 2% of the time, Pallas kernels for 19%

profile of v3, /device:TPU:0, one launch (start us, length us, event | category | flops | bytes accessed | tf_op | source)
XLA Modules:
  0.0 77.4 jit_solution(13779341578004960608)
XLA Ops:
  0.0 1.1 %slice_bitcast_fusion.own_ref = bf16[8,128,256]{2,1,0:T(8,128)(2,1)S(1)} fusion(bf16[1,12,128,256]{3,2,1,0:T(8,128)(2,1)} %param.6), kind=kLoop, calls=%fused_computation.2 | loop fusion | bytes 1048576 | tf_op jit(solution)/shard_map/squeeze | solution.py:201
  1.1 3.0 %collective-permute-start.4 = (bf16[8,128,256]{2,1,0:T(8,128)(2,1)S(1)}, bf16[8,128,256]{2,1,0:T(8,128)(2,1)S(1)}, u32[]{:S(2)}, u32[]{:S(2)}) collective-permute-start(bf16[8,128,256]{2,1,0:T(8,128)(2,1)S(1)} %slice_bitcast_fusion.own_ref), channel_id=1, source_target_pairs={{0,2},{2,0},{1,3},{3,1},{4,6},{6,4},{5,7},{7,5},{8,10},{10,8},{9,1... | collective-permute-start | bytes 1572872 | tf_op jit(solution)/shard_map/ppermute | solution.py:202
  4.1 1.0 %slice_bitcast_fusion.1 = bf16[4,128,256]{2,1,0:T(8,128)(2,1)S(1)} fusion(bf16[1,12,128,256]{3,2,1,0:T(8,128)(2,1)} %param.6), kind=kLoop, calls=%fused_computation.3 | loop fusion | bytes 524288 | tf_op jit(solution)/shard_map/squeeze | solution.py:203
  5.1 1.6 %collective-permute-start = (bf16[4,128,256]{2,1,0:T(8,128)(2,1)S(1)}, bf16[4,128,256]{2,1,0:T(8,128)(2,1)S(1)}, u32[]{:S(2)}, u32[]{:S(2)}) collective-permute-start(bf16[4,128,256]{2,1,0:T(8,128)(2,1)S(1)} %slice_bitcast_fusion.1), channel_id=1, source_target_pairs={{0,4},{4,0},{8,12},{12,8},{1,5},{5,1},{9,13},{13,9},{2,6},{6,2},{1... | collective-permute-start | bytes 786440 | tf_op jit(solution)/shard_map/ppermute | solution.py:205
  6.7 0.7 collective-permute-start.2
  7.4 0.9 %copy-done = f32[256,256]{1,0:T(8,128)S(1)} copy-done((f32[256,256]{1,0:T(8,128)S(1)}, f32[256,256]{1,0:T(8,128)}, u32[]{:S(2)}) %copy-start) | copy-done | bytes 262168
  8.3 0.9 %copy-done.1 = f32[256,256]{1,0:T(8,128)S(1)} copy-done((f32[256,256]{1,0:T(8,128)S(1)}, f32[256,256]{1,0:T(8,128)}, u32[]{:S(2)}) %copy-start.1) | copy-done | bytes 262168
  9.4 3.5 %collective-permute-done = bf16[4,128,256]{2,1,0:T(8,128)(2,1)S(1)} collective-permute-done((bf16[4,128,256]{2,1,0:T(8,128)(2,1)S(1)}, bf16[4,128,256]{2,1,0:T(8,128)(2,1)S(1)}, u32[]{:S(2)}, u32[]{:S(2)}) %collective-permute-start) | collective-permute-done | bytes 262176 | tf_op jit(solution)/shard_map/ppermute | solution.py:205
  12.9 0.7 collective-permute-start.1
  13.6 1.3 %collective-permute-start.3 = (bf16[4,128,256]{2,1,0:T(8,128)(2,1)S(1)}, bf16[4,128,256]{2,1,0:T(8,128)(2,1)S(1)}, u32[]{:S(2)}, u32[]{:S(2)}) collective-permute-start(bf16[4,128,256]{2,1,0:T(8,128)(2,1)S(1)} %collective-permute-done.2), channel_id=1, source_target_pairs={{4,0},{8,12},{5,1},{9,13},{6,2},{10,14},{7,3},{11,15},{20,16},{24,... | collective-permute-start | bytes 786440 | tf_op jit(solution)/shard_map/ppermute | solution.py:209
  14.9 1.1 %collective-permute-done.4.far_ref = bf16[8,128,256]{2,1,0:T(8,128)(2,1)S(1)} collective-permute-done((bf16[8,128,256]{2,1,0:T(8,128)(2,1)S(1)}, bf16[8,128,256]{2,1,0:T(8,128)(2,1)S(1)}, u32[]{:S(2)}, u32[]{:S(2)}) %collective-permute-start.4) | collective-permute-done | bytes 524320 | tf_op jit(solution)/shard_map/ppermute | solution.py:202
  16.0 8.4 %shard_map.56.grad_ref = bf16[128,128,256]{2,1,0:T(8,128)(2,1)} custom-call(bf16[128,128,256]{2,1,0:T(8,128)(2,1)} %grads_ref), custom_call_target="tpu_custom_call" | custom-call | flops 6000000000 | bytes 16000000 | tf_op jit(solution)/shard_map/pallas_call | solution.py:106
  24.5 1.3 %shard_map.57.own_ref = bf16[128,8,256]{2,1,0:T(8,128)(2,1)S(1)} custom-call(bf16[8,128,256]{2,1,0:T(8,128)(2,1)S(1)} %slice_bitcast_fusion.own_ref, bf16[8,128,256]{2,1,0:T(8,128)(2,1)S(1)} %collective-permute-done.4.far_ref, bf16[384,256]{1,0:T(8,128)(2,1)S(1)} %get-tuple-element.22.left_ref, bf16[512,256]{1,0:T(8,128)(2,1)S(1)} %get-tuple-element.23.right_ref), custom_call_target="tpu_custom_call" | custom-call | flops 960000000 | bytes 2097152 | tf_op jit(solution)/shard_map/pallas_call | solution.py:70
  25.8 3.3 %collective-permute-start.5 = (bf16[128,8,256]{2,1,0:T(8,128)(2,1)S(1)}, bf16[128,8,256]{2,1,0:T(8,128)(2,1)S(1)}, u32[]{:S(2)}, u32[]{:S(2)}) collective-permute-start(bf16[128,8,256]{2,1,0:T(8,128)(2,1)S(1)} %shard_map.57.own_ref), channel_id=1, source_target_pairs={{0,4},{4,0},{8,12},{12,8},{1,5},{5,1},{9,13},{13,9},{2,6},{6,2},{1... | collective-permute-start | bytes 1572872 | tf_op jit(solution)/shard_map/ppermute | solution.py:212
  29.1 0.7 collective-permute-start.6
  30.4 9.1 %collective-permute-done.5.near = bf16[128,8,256]{2,1,0:T(8,128)(2,1)S(1)} collective-permute-done((bf16[128,8,256]{2,1,0:T(8,128)(2,1)S(1)}, bf16[128,8,256]{2,1,0:T(8,128)(2,1)S(1)}, u32[]{:S(2)}, u32[]{:S(2)}) %collective-permute-start.5) | collective-permute-done | bytes 524320 | tf_op jit(solution)/shard_map/ppermute | solution.py:212
  39.5 1.3 %collective-permute-start.8 = (bf16[4,128,256]{2,1,0:T(8,128)(2,1)S(1)}, bf16[4,128,256]{2,1,0:T(8,128)(2,1)S(1)}, u32[]{:S(2)}, u32[]{:S(2)}) collective-permute-start(bf16[4,128,256]{2,1,0:T(8,128)(2,1)S(1)} %collective-permute-done.1), channel_id=1, source_target_pairs={{4,0},{8,12},{5,1},{9,13},{6,2},{10,14},{7,3},{11,15},{20,16},{24,... | collective-permute-start | bytes 786440 | tf_op jit(solution)/shard_map/ppermute | solution.py:216
  40.9 1.6 %collective-permute-start.11 = (bf16[128,8,256]{2,1,0:T(8,128)(2,1)S(1)}, bf16[128,8,256]{2,1,0:T(8,128)(2,1)S(1)}, u32[]{:S(2)}, u32[]{:S(2)}) collective-permute-start(bf16[128,8,256]{2,1,0:T(8,128)(2,1)S(1)} %collective-permute-done.6), channel_id=1, source_target_pairs={{4,0},{8,12},{5,1},{9,13},{6,2},{10,14},{7,3},{11,15},{20,16},{24,... | collective-permute-start | bytes 1572872 | tf_op jit(solution)/shard_map/ppermute | solution.py:218
  42.5 0.7 collective-permute-start.9
  43.2 1.3 %shard_map.58.early_0 = bf16[128,8,256]{2,1,0:T(8,128)(2,1)S(1)} custom-call(bf16[8,128,256]{2,1,0:T(8,128)(2,1)S(1)} %pad_maximum_fusion.own_ref, bf16[8,128,256]{2,1,0:T(8,128)(2,1)S(1)} %collective-permute-done.7.far_ref, bf16[384,256]{1,0:T(8,128)(2,1)S(1)} %get-tuple-element.22.left_ref, bf16[512,256]{1,0:T(8,128)(2,1)S(1)} %get-tuple-element.23.right_ref), custom_call_target="tpu_custom_call" | custom-call | flops 960000000 | bytes 2097152 | tf_op jit(solution)/shard_map/pallas_call | solution.py:70
  44.5 6.2 %collective-permute-done.8 = bf16[4,128,256]{2,1,0:T(8,128)(2,1)S(1)} collective-permute-done((bf16[4,128,256]{2,1,0:T(8,128)(2,1)S(1)}, bf16[4,128,256]{2,1,0:T(8,128)(2,1)S(1)}, u32[]{:S(2)}, u32[]{:S(2)}) %collective-permute-start.8) | collective-permute-done | bytes 262176 | tf_op jit(solution)/shard_map/ppermute | solution.py:216
  50.8 0.9 %collective-permute-start.10 = (bf16[8,128,256]{2,1,0:T(8,128)(2,1)S(1)}, bf16[8,128,256]{2,1,0:T(8,128)(2,1)S(1)}, u32[]{:S(2)}, u32[]{:S(2)}) collective-permute-start(bf16[8,128,256]{2,1,0:T(8,128)(2,1)S(1)} %pad_maximum_fusion.1.own_ref), channel_id=1, source_target_pairs={{0,2},{2,0},{1,3},{3,1},{4,6},{6,4},{5,7},{7,5},{8,10},{10,8},{9,1... | collective-permute-start | bytes 1572872 | tf_op jit(solution)/shard_map/ppermute | solution.py:221
  51.7 1.3 %collective-permute-start.12 = (bf16[128,8,256]{2,1,0:T(8,128)(2,1)S(1)}, bf16[128,8,256]{2,1,0:T(8,128)(2,1)S(1)}, u32[]{:S(2)}, u32[]{:S(2)}) collective-permute-start(bf16[128,8,256]{2,1,0:T(8,128)(2,1)S(1)} %collective-permute-done.9.far_in), channel_id=1, source_target_pairs={{4,0},{8,12},{5,1},{9,13},{6,2},{10,14},{7,3},{11,15},{20,16},{24,... | collective-permute-start | bytes 1572872 | tf_op jit(solution)/shard_map/ppermute | solution.py:222
  53.0 5.8 %collective-permute-done.11 = bf16[128,8,256]{2,1,0:T(8,128)(2,1)S(1)} collective-permute-done((bf16[128,8,256]{2,1,0:T(8,128)(2,1)S(1)}, bf16[128,8,256]{2,1,0:T(8,128)(2,1)S(1)}, u32[]{:S(2)}, u32[]{:S(2)}) %collective-permute-start.11) | collective-permute-done | bytes 524320 | tf_op jit(solution)/shard_map/ppermute | solution.py:218
  59.0 1.1 %collective-permute-done.10.far_ref = bf16[8,128,256]{2,1,0:T(8,128)(2,1)S(1)} collective-permute-done((bf16[8,128,256]{2,1,0:T(8,128)(2,1)S(1)}, bf16[8,128,256]{2,1,0:T(8,128)(2,1)S(1)}, u32[]{:S(2)}, u32[]{:S(2)}) %collective-permute-start.10) | collective-permute-done | bytes 524320 | tf_op jit(solution)/shard_map/ppermute | solution.py:221
  60.0 1.3 %shard_map.59.early_1 = bf16[128,8,256]{2,1,0:T(8,128)(2,1)S(1)} custom-call(bf16[8,128,256]{2,1,0:T(8,128)(2,1)S(1)} %pad_maximum_fusion.1.own_ref, bf16[8,128,256]{2,1,0:T(8,128)(2,1)S(1)} %collective-permute-done.10.far_ref, bf16[384,256]{1,0:T(8,128)(2,1)S(1)} %get-tuple-element.22.left_ref, bf16[512,256]{1,0:T(8,128)(2,1)S(1)} %get-tuple-element.23.right_ref), custom_call_target="tpu_custom_call" | custom-call | flops 960000000 | bytes 2097152 | tf_op jit(solution)/shard_map/pallas_call | solution.py:70
  61.3 4.0 %shard_map.60.base_ref = f32[48,128]{1,0:T(8,128)S(1)} custom-call(bf16[128,8,256]{2,1,0:T(8,128)(2,1)S(1)} %shard_map.58.early_0, bf16[128,8,256]{2,1,0:T(8,128)(2,1)S(1)} %shard_map.59.early_1, bf16[128,8,256]{2,1,0:T(8,128)(2,1)S(1)} %shard_map.57.own_ref, bf16[128,8,256]{2,1,0:T(8,128)(2,1)S(1)} %collective-permute-done.5.near, ...), custom_call_target="tpu_custom_call" | custom-call | flops 3000000000 | bytes 12000000 | tf_op jit(solution)/shard_map/pallas_call | solution.py:176
  65.3 4.5 %collective-permute-done.12.far_out = bf16[128,8,256]{2,1,0:T(8,128)(2,1)S(1)} collective-permute-done((bf16[128,8,256]{2,1,0:T(8,128)(2,1)S(1)}, bf16[128,8,256]{2,1,0:T(8,128)(2,1)S(1)}, u32[]{:S(2)}, u32[]{:S(2)}) %collective-permute-start.12) | collective-permute-done | bytes 524320 | tf_op jit(solution)/shard_map/ppermute | solution.py:222
  69.8 3.2 %shard_map.61 = (f32[24,128]{1,0:T(8,128)S(1)}, f32[24,128]{1,0:T(8,128)S(1)}) custom-call(f32[48,128]{1,0:T(8,128)S(1)} %shard_map.60.base_ref, bf16[128,8,256]{2,1,0:T(8,128)(2,1)S(1)} %collective-permute-done.12.far_out, bf16[128,128,256]{2,1,0:T(8,128)(2,1)S(1)} %bitcast.9, s32[4]{0:T(128)S(1)} %copy-done.2), custom_call_target="tpu_custom_call" | custom-call | flops 3000000000 | bytes 12000000 | tf_op jit(solution)/shard_map/pallas_call | solution.py:176
  73.0 1.3 %collective-permute-start.13 = (f32[24,128]{1,0:T(8,128)S(1)}, f32[24,128]{1,0:T(8,128)S(1)}, u32[]{:S(2)}, u32[]{:S(2)}) collective-permute-start(f32[24,128]{1,0:T(8,128)S(1)} %get-tuple-element.34), channel_id=1, source_target_pairs={{0,2},{2,0},{1,3},{3,1},{4,6},{6,4},{5,7},{7,5},{8,10},{10,8},{9,1... | collective-permute-start | bytes 36872 | tf_op jit(solution)/shard_map/ppermute | solution.py:234
  74.3 2.5 %collective-permute-done.13 = f32[24,128]{1,0:T(8,128)S(1)} collective-permute-done((f32[24,128]{1,0:T(8,128)S(1)}, f32[24,128]{1,0:T(8,128)S(1)}, u32[]{:S(2)}, u32[]{:S(2)}) %collective-permute-start.13) | collective-permute-done | bytes 12320 | tf_op jit(solution)/shard_map/ppermute | solution.py:234
  76.8 0.6 add_bitcast_fusion
  (22 shorter events, 1.1 us)
Async XLA Ops:
  1.1 14.9 %collective-permute-start.4 = (bf16[8,128,256]{2,1,0:T(8,128)(2,1)S(1)}, bf16[8,128,256]{2,1,0:T(8,128)(2,1)S(1)}, u32[]{:S(2)}, u32[]{:S(2)}) collective-permute-start(bf16[8,128,256]{2,1,0:T(8,128)(2,1)S(1)} %slice_bitcast_fusion.own_ref), channel_id=1, source_target_pairs={{0,2},{2,0},{1,3},{3,1},{4,6},{6,4},{5,7},{7,5},{8,10},{10,8},{9,1... | collective-permute-start | bytes 1572872 | tf_op jit(solution)/shard_map/ppermute | solution.py:202
  5.1 7.8 %collective-permute-start = (bf16[4,128,256]{2,1,0:T(8,128)(2,1)S(1)}, bf16[4,128,256]{2,1,0:T(8,128)(2,1)S(1)}, u32[]{:S(2)}, u32[]{:S(2)}) collective-permute-start(bf16[4,128,256]{2,1,0:T(8,128)(2,1)S(1)} %slice_bitcast_fusion.1), channel_id=1, source_target_pairs={{0,4},{4,0},{8,12},{12,8},{1,5},{5,1},{9,13},{13,9},{2,6},{6,2},{1... | collective-permute-start | bytes 786440 | tf_op jit(solution)/shard_map/ppermute | solution.py:205
  6.7 6.9 %collective-permute-start.2 = (bf16[4,128,256]{2,1,0:T(8,128)(2,1)S(1)}, bf16[4,128,256]{2,1,0:T(8,128)(2,1)S(1)}, u32[]{:S(2)}, u32[]{:S(2)}) collective-permute-start(bf16[4,128,256]{2,1,0:T(8,128)(2,1)S(1)} %slice_bitcast_fusion.1), channel_id=1, source_target_pairs={{4,8},{8,4},{5,9},{9,5},{6,10},{10,6},{7,11},{11,7},{20,24},{24,20... | collective-permute-start | bytes 786440 | tf_op jit(solution)/shard_map/ppermute | solution.py:206
  7.4 1.0 %copy-start = (f32[256,256]{1,0:T(8,128)S(1)}, f32[256,256]{1,0:T(8,128)}, u32[]{:S(2)}) copy-start(f32[256,256]{1,0:T(8,128)} %left_ref.1) | copy-start | bytes 786436
  8.3 0.9 %copy-start.1 = (f32[256,256]{1,0:T(8,128)S(1)}, f32[256,256]{1,0:T(8,128)}, u32[]{:S(2)}) copy-start(f32[256,256]{1,0:T(8,128)} %right_ref) | copy-start | bytes 786436
  12.9 11.6 %collective-permute-start.1 = (bf16[4,128,256]{2,1,0:T(8,128)(2,1)S(1)}, bf16[4,128,256]{2,1,0:T(8,128)(2,1)S(1)}, u32[]{:S(2)}, u32[]{:S(2)}) collective-permute-start(bf16[4,128,256]{2,1,0:T(8,128)(2,1)S(1)} %collective-permute-done), channel_id=1, source_target_pairs={{4,8},{8,4},{5,9},{9,5},{6,10},{10,6},{7,11},{11,7},{20,24},{24,20... | collective-permute-start | bytes 786440 | tf_op jit(solution)/shard_map/ppermute | solution.py:208
  13.6 10.9 %collective-permute-start.3 = (bf16[4,128,256]{2,1,0:T(8,128)(2,1)S(1)}, bf16[4,128,256]{2,1,0:T(8,128)(2,1)S(1)}, u32[]{:S(2)}, u32[]{:S(2)}) collective-permute-start(bf16[4,128,256]{2,1,0:T(8,128)(2,1)S(1)} %collective-permute-done.2), channel_id=1, source_target_pairs={{4,0},{8,12},{5,1},{9,13},{6,2},{10,14},{7,3},{11,15},{20,16},{24,... | collective-permute-start | bytes 786440 | tf_op jit(solution)/shard_map/ppermute | solution.py:209
  24.4 36.9 %slice-start = ((s8[8388608]{0:T(1024)(128)(4,1)}), s8[4194304]{0:T(1024)(128)(4,1)S(1)}, s32[]{:S(2)}) async-start(s8[8388608]{0:T(1024)(128)(4,1)} %bitcast.8), calls=%async_computation | async-start | bytes 8388608
  24.4 36.9 %copy-start.2 = (s32[4]{0:T(128)S(1)}, s32[4]{0:T(128)}, u32[]{:S(2)}) copy-start(s32[4]{0:T(128)} %order_ref.3) | copy-start | bytes 52
  25.8 13.8 %collective-permute-start.5 = (bf16[128,8,256]{2,1,0:T(8,128)(2,1)S(1)}, bf16[128,8,256]{2,1,0:T(8,128)(2,1)S(1)}, u32[]{:S(2)}, u32[]{:S(2)}) collective-permute-start(bf16[128,8,256]{2,1,0:T(8,128)(2,1)S(1)} %shard_map.57.own_ref), channel_id=1, source_target_pairs={{0,4},{4,0},{8,12},{12,8},{1,5},{5,1},{9,13},{13,9},{2,6},{6,2},{1... | collective-permute-start | bytes 1572872 | tf_op jit(solution)/shard_map/ppermute | solution.py:212
  29.1 11.8 %collective-permute-start.6 = (bf16[128,8,256]{2,1,0:T(8,128)(2,1)S(1)}, bf16[128,8,256]{2,1,0:T(8,128)(2,1)S(1)}, u32[]{:S(2)}, u32[]{:S(2)}) collective-permute-start(bf16[128,8,256]{2,1,0:T(8,128)(2,1)S(1)} %shard_map.57.own_ref), channel_id=1, source_target_pairs={{4,8},{8,4},{5,9},{9,5},{6,10},{10,6},{7,11},{11,7},{20,24},{24,20... | collective-permute-start | bytes 1572872 | tf_op jit(solution)/shard_map/ppermute | solution.py:213
  29.8 13.3 %collective-permute-start.7 = (bf16[8,128,256]{2,1,0:T(8,128)(2,1)S(1)}, bf16[8,128,256]{2,1,0:T(8,128)(2,1)S(1)}, u32[]{:S(2)}, u32[]{:S(2)}) collective-permute-start(bf16[8,128,256]{2,1,0:T(8,128)(2,1)S(1)} %pad_maximum_fusion.own_ref), channel_id=1, source_target_pairs={{0,2},{2,0},{1,3},{3,1},{4,6},{6,4},{5,7},{7,5},{8,10},{10,8},{9,1... | collective-permute-start | bytes 1572872 | tf_op jit(solution)/shard_map/ppermute | solution.py:215
  39.5 11.1 %collective-permute-start.8 = (bf16[4,128,256]{2,1,0:T(8,128)(2,1)S(1)}, bf16[4,128,256]{2,1,0:T(8,128)(2,1)S(1)}, u32[]{:S(2)}, u32[]{:S(2)}) collective-permute-start(bf16[4,128,256]{2,1,0:T(8,128)(2,1)S(1)} %collective-permute-done.1), channel_id=1, source_target_pairs={{4,0},{8,12},{5,1},{9,13},{6,2},{10,14},{7,3},{11,15},{20,16},{24,... | collective-permute-start | bytes 786440 | tf_op jit(solution)/shard_map/ppermute | solution.py:216
  40.9 20.4 %slice-start.1 = ((s8[8388608]{0:T(1024)(128)(4,1)}), s8[4194304]{0:T(1024)(128)(4,1)S(1)}, s32[]{:S(2)}) async-start(s8[8388608]{0:T(1024)(128)(4,1)} %bitcast.8), calls=%async_computation.1 | async-start | bytes 8388608
  40.9 17.9 %collective-permute-start.11 = (bf16[128,8,256]{2,1,0:T(8,128)(2,1)S(1)}, bf16[128,8,256]{2,1,0:T(8,128)(2,1)S(1)}, u32[]{:S(2)}, u32[]{:S(2)}) collective-permute-start(bf16[128,8,256]{2,1,0:T(8,128)(2,1)S(1)} %collective-permute-done.6), channel_id=1, source_target_pairs={{4,0},{8,12},{5,1},{9,13},{6,2},{10,14},{7,3},{11,15},{20,16},{24,... | collective-permute-start | bytes 1572872 | tf_op jit(solution)/shard_map/ppermute | solution.py:218
  42.5 9.2 %collective-permute-start.9 = (bf16[128,8,256]{2,1,0:T(8,128)(2,1)S(1)}, bf16[128,8,256]{2,1,0:T(8,128)(2,1)S(1)}, u32[]{:S(2)}, u32[]{:S(2)}) collective-permute-start(bf16[128,8,256]{2,1,0:T(8,128)(2,1)S(1)} %collective-permute-done.5.near), channel_id=1, source_target_pairs={{4,8},{8,4},{5,9},{9,5},{6,10},{10,6},{7,11},{11,7},{20,24},{24,20... | collective-permute-start | bytes 1572872 | tf_op jit(solution)/shard_map/ppermute | solution.py:217
  50.8 9.2 %collective-permute-start.10 = (bf16[8,128,256]{2,1,0:T(8,128)(2,1)S(1)}, bf16[8,128,256]{2,1,0:T(8,128)(2,1)S(1)}, u32[]{:S(2)}, u32[]{:S(2)}) collective-permute-start(bf16[8,128,256]{2,1,0:T(8,128)(2,1)S(1)} %pad_maximum_fusion.1.own_ref), channel_id=1, source_target_pairs={{0,2},{2,0},{1,3},{3,1},{4,6},{6,4},{5,7},{7,5},{8,10},{10,8},{9,1... | collective-permute-start | bytes 1572872 | tf_op jit(solution)/shard_map/ppermute | solution.py:221
  51.7 18.1 %collective-permute-start.12 = (bf16[128,8,256]{2,1,0:T(8,128)(2,1)S(1)}, bf16[128,8,256]{2,1,0:T(8,128)(2,1)S(1)}, u32[]{:S(2)}, u32[]{:S(2)}) collective-permute-start(bf16[128,8,256]{2,1,0:T(8,128)(2,1)S(1)} %collective-permute-done.9.far_in), channel_id=1, source_target_pairs={{4,0},{8,12},{5,1},{9,13},{6,2},{10,14},{7,3},{11,15},{20,16},{24,... | collective-permute-start | bytes 1572872 | tf_op jit(solution)/shard_map/ppermute | solution.py:222
  73.0 3.8 %collective-permute-start.13 = (f32[24,128]{1,0:T(8,128)S(1)}, f32[24,128]{1,0:T(8,128)S(1)}, u32[]{:S(2)}, u32[]{:S(2)}) collective-permute-start(f32[24,128]{1,0:T(8,128)S(1)} %get-tuple-element.34), channel_id=1, source_target_pairs={{0,2},{2,0},{1,3},{3,1},{4,6},{6,4},{5,7},{7,5},{8,10},{10,8},{9,1... | collective-permute-start | bytes 36872 | tf_op jit(solution)/shard_map/ppermute | solution.py:234

commit v4 on v3

--- a/solution.py
+++ b/solution.py
@@ -204,20 +204,20 @@
     terms = factor_terms(left_factor, after(right_factor, raw), train_grads.shape[1])
     raw_near = lax.ppermute(raw, "ex", PAIRS)
     raw_mid = lax.ppermute(raw, "ex", MIDDLE)
-    grads = regroup(after(train_grads, late_other))
     raw_far_mid = lax.ppermute(after(raw_near, *terms), "ex", MIDDLE)
     raw_mid_out = lax.ppermute(raw_mid, "ex", OUTWARD)
 
-    late = condition(after(late_raw, raw_far_mid, raw_mid_out, grads), late_other, *terms)
+    late = condition(after(late_raw, raw_near, raw_mid), late_other, *terms)
     near = lax.ppermute(late, "ex", PAIRS)
     mid = lax.ppermute(late, "ex", MIDDLE)
+    grads = regroup(after(train_grads, late))
     early_0 = jnp.concatenate([raw, after(raw_near, late)], axis=0)
     early_0_other = lax.ppermute(early_0, "feat", swap)
-    raw_far_out = lax.ppermute(after(raw_far_mid, near), "ex", OUTWARD)
-    far_mid = lax.ppermute(near, "ex", MIDDLE)
-    mid_out = lax.ppermute(after(mid, near), "ex", OUTWARD)
+    raw_far_out = lax.ppermute(after(raw_far_mid, grads), "ex", OUTWARD)
+    far_mid = lax.ppermute(after(near, grads), "ex", MIDDLE)
+    mid_out = lax.ppermute(after(mid, near, grads), "ex", OUTWARD)
     cond_0 = condition(after(early_0, near, mid), early_0_other, *terms)
-    early_1 = jnp.concatenate([raw_mid + raw_mid_out, raw_far_mid + raw_far_out], axis=0)
+    early_1 = jnp.concatenate([raw_mid + raw_mid_out, after(raw_far_mid, near, mid) + raw_far_out], axis=0)
     early_1_other = lax.ppermute(after(early_1, cond_0), "feat", swap)
     far_out = lax.ppermute(far_mid, "ex", OUTWARD)
     cond_1 = condition(after(early_1, far_mid), early_1_other, *terms)

time: 77.7 us -> 74.2 us (0.955)
  waiting for transfers between devices: 33.9 us -> 28.1 us
  starting transfers between devices: 18.8 us -> 21.2 us
    ppermute x1, waiting for transfers between devices: 9.1 us -> 5.1 us  [per_device_line(): near = lax.ppermute(late, 'ex', PAIRS)]
    ppermute x1, starting transfers between devices: 3.34 us -> 6.51 us  [per_device_line(): near = lax.ppermute(late, 'ex', PAIRS)]
    ppermute x1, waiting for transfers between devices: 1.07 us -> 0.01 us  [per_device_line(): early_1_other = lax.ppermute(after(early_1, cond_0), 'feat', swap)]
    ppermute x1, waiting for transfers between devices: 4.5 us -> 3.68 us  [per_device_line(): far_out = lax.ppermute(far_mid, 'ex', OUTWARD)]
    unnamed x10 -> x8, local copies, waits for them, and re-layouts: 1.91 us -> 1.91 us
  transfers between devices with their start and end apart: 14 -> 14, of which waited for: 8 -> 7; matrix products, arithmetic and copies ran while one was open for 2% -> 2% of each run, Pallas kernels for 19% -> 22%
where the time goes in v4:
time: 74.2 us; the launch traced here: 73.8 us
  waiting for transfers between devices  28.1 us (38%)
  starting transfers between devices  21.2 us (29%)
  Pallas kernels  19.4 us (26%)
  local copies, waits for them, and re-layouts  3.95 us (5%)
  other arithmetic  0.97 us (1%)
    ppermute x1, waiting for transfers between devices, per_device_line(): mid_out = lax.ppermute(after(mid, near, grads), 'ex', OUTWARD)  9.08 us
    pallas_call x1, Pallas kernels, regroup(): pl.pallas_call(regroup_kernel, out_shape=jax.ShapeDtypeStruct((rows, n, w...  8.39 us
    pallas_call x2, Pallas kernels, score_call(): pl.pallas_call(functools.partial(kernel, ex), out_shape=out_shape, in_spe...  7.16 us
    ppermute x1, starting transfers between devices, per_device_line(): near = lax.ppermute(late, 'ex', PAIRS)  6.51 us
    ppermute x1, waiting for transfers between devices, per_device_line(): near = lax.ppermute(late, 'ex', PAIRS)  5.1 us
    pallas_call x3, Pallas kernels, condition(): pl.pallas_call(condition_kernel, out_shape=jax.ShapeDtypeStruct((rows, co...  3.78 us
    ppermute x1, waiting for transfers between devices, per_device_line(): far_out = lax.ppermute(far_mid, 'ex', OUTWARD)  3.68 us
    ppermute x1, waiting for transfers between devices, per_device_line(): raw_near = lax.ppermute(raw, 'ex', PAIRS)  3.53 us
  transfers between devices with their start and end apart: 14, of which 7 were waited for; matrix products, arithmetic and copies ran while one was open for 2% of the time, Pallas kernels for 22%

profile of v4, /device:TPU:0, one launch (start us, length us, event | category | flops | bytes accessed | tf_op | source)
XLA Modules:
  0.0 73.8 jit_solution(1237872815234049424)
XLA Ops:
  0.0 1.1 %slice_bitcast_fusion.own_ref = bf16[8,128,256]{2,1,0:T(8,128)(2,1)S(1)} fusion(bf16[1,12,128,256]{3,2,1,0:T(8,128)(2,1)} %param.6), kind=kLoop, calls=%fused_computation.2 | loop fusion | bytes 1048576 | tf_op jit(solution)/shard_map/squeeze | solution.py:201
  1.1 3.0 %collective-permute-start.2 = (bf16[8,128,256]{2,1,0:T(8,128)(2,1)S(1)}, bf16[8,128,256]{2,1,0:T(8,128)(2,1)S(1)}, u32[]{:S(2)}, u32[]{:S(2)}) collective-permute-start(bf16[8,128,256]{2,1,0:T(8,128)(2,1)S(1)} %slice_bitcast_fusion.own_ref), channel_id=1, source_target_pairs={{0,2},{2,0},{1,3},{3,1},{4,6},{6,4},{5,7},{7,5},{8,10},{10,8},{9,1... | collective-permute-start | bytes 1572872 | tf_op jit(solution)/shard_map/ppermute | solution.py:202
  4.1 1.0 %slice_bitcast_fusion.1 = bf16[4,128,256]{2,1,0:T(8,128)(2,1)S(1)} fusion(bf16[1,12,128,256]{3,2,1,0:T(8,128)(2,1)} %param.6), kind=kLoop, calls=%fused_computation.3 | loop fusion | bytes 524288 | tf_op jit(solution)/shard_map/squeeze | solution.py:203
  5.1 1.6 %collective-permute-start = (bf16[4,128,256]{2,1,0:T(8,128)(2,1)S(1)}, bf16[4,128,256]{2,1,0:T(8,128)(2,1)S(1)}, u32[]{:S(2)}, u32[]{:S(2)}) collective-permute-start(bf16[4,128,256]{2,1,0:T(8,128)(2,1)S(1)} %slice_bitcast_fusion.1), channel_id=1, source_target_pairs={{0,4},{4,0},{8,12},{12,8},{1,5},{5,1},{9,13},{13,9},{2,6},{6,2},{1... | collective-permute-start | bytes 786440 | tf_op jit(solution)/shard_map/ppermute | solution.py:205
  6.7 0.7 collective-permute-start.1
  7.4 0.9 %copy-done.1 = f32[256,256]{1,0:T(8,128)S(1)} copy-done((f32[256,256]{1,0:T(8,128)S(1)}, f32[256,256]{1,0:T(8,128)}, u32[]{:S(2)}) %copy-start.1) | copy-done | bytes 262168
  8.3 0.9 %copy-done.2 = f32[256,256]{1,0:T(8,128)S(1)} copy-done((f32[256,256]{1,0:T(8,128)S(1)}, f32[256,256]{1,0:T(8,128)}, u32[]{:S(2)}) %copy-start.2) | copy-done | bytes 262168
  9.4 3.5 %collective-permute-done = bf16[4,128,256]{2,1,0:T(8,128)(2,1)S(1)} collective-permute-done((bf16[4,128,256]{2,1,0:T(8,128)(2,1)S(1)}, bf16[4,128,256]{2,1,0:T(8,128)(2,1)S(1)}, u32[]{:S(2)}, u32[]{:S(2)}) %collective-permute-start) | collective-permute-done | bytes 262176 | tf_op jit(solution)/shard_map/ppermute | solution.py:205
  12.9 0.7 collective-permute-start.7
  13.6 1.3 %collective-permute-start.6 = (bf16[4,128,256]{2,1,0:T(8,128)(2,1)S(1)}, bf16[4,128,256]{2,1,0:T(8,128)(2,1)S(1)}, u32[]{:S(2)}, u32[]{:S(2)}) collective-permute-start(bf16[4,128,256]{2,1,0:T(8,128)(2,1)S(1)} %collective-permute-done.1), channel_id=1, source_target_pairs={{4,0},{8,12},{5,1},{9,13},{6,2},{10,14},{7,3},{11,15},{20,16},{24,... | collective-permute-start | bytes 786440 | tf_op jit(solution)/shard_map/ppermute | solution.py:208
  14.9 1.1 %collective-permute-done.2.far_ref = bf16[8,128,256]{2,1,0:T(8,128)(2,1)S(1)} collective-permute-done((bf16[8,128,256]{2,1,0:T(8,128)(2,1)S(1)}, bf16[8,128,256]{2,1,0:T(8,128)(2,1)S(1)}, u32[]{:S(2)}, u32[]{:S(2)}) %collective-permute-start.2) | collective-permute-done | bytes 524320 | tf_op jit(solution)/shard_map/ppermute | solution.py:202
  16.0 1.3 %shard_map.56.own_ref = bf16[128,8,256]{2,1,0:T(8,128)(2,1)S(1)} custom-call(bf16[8,128,256]{2,1,0:T(8,128)(2,1)S(1)} %slice_bitcast_fusion.own_ref, bf16[8,128,256]{2,1,0:T(8,128)(2,1)S(1)} %collective-permute-done.2.far_ref, bf16[384,256]{1,0:T(8,128)(2,1)S(1)} %get-tuple-element.25.left_ref, bf16[512,256]{1,0:T(8,128)(2,1)S(1)} %get-tuple-element.26.right_ref), custom_call_target="tpu_custom_call" | custom-call | flops 960000000 | bytes 2097152 | tf_op jit(solution)/shard_map/pallas_call | solution.py:70
  17.3 6.5 %collective-permute-start.3 = (bf16[128,8,256]{2,1,0:T(8,128)(2,1)S(1)}, bf16[128,8,256]{2,1,0:T(8,128)(2,1)S(1)}, u32[]{:S(2)}, u32[]{:S(2)}) collective-permute-start(bf16[128,8,256]{2,1,0:T(8,128)(2,1)S(1)} %shard_map.56.own_ref), channel_id=1, source_target_pairs={{0,4},{4,0},{8,12},{12,8},{1,5},{5,1},{9,13},{13,9},{2,6},{6,2},{1... | collective-permute-start | bytes 1572872 | tf_op jit(solution)/shard_map/ppermute | solution.py:211
  23.8 0.7 collective-permute-start.4
  24.5 0.6 collective-permute-start.5
  25.1 8.4 %shard_map.58.grad_ref = bf16[128,128,256]{2,1,0:T(8,128)(2,1)} custom-call(bf16[128,128,256]{2,1,0:T(8,128)(2,1)} %grads_ref), custom_call_target="tpu_custom_call" | custom-call | flops 6000000000 | bytes 16000000 | tf_op jit(solution)/shard_map/pallas_call | solution.py:106
  33.6 1.6 %collective-permute-start.8 = (bf16[4,128,256]{2,1,0:T(8,128)(2,1)S(1)}, bf16[4,128,256]{2,1,0:T(8,128)(2,1)S(1)}, u32[]{:S(2)}, u32[]{:S(2)}) collective-permute-start(bf16[4,128,256]{2,1,0:T(8,128)(2,1)S(1)} %collective-permute-done.7), channel_id=1, source_target_pairs={{4,0},{8,12},{5,1},{9,13},{6,2},{10,14},{7,3},{11,15},{20,16},{24,... | collective-permute-start | bytes 786440 | tf_op jit(solution)/shard_map/ppermute | solution.py:216
  35.2 5.1 %collective-permute-done.3.near = bf16[128,8,256]{2,1,0:T(8,128)(2,1)S(1)} collective-permute-done((bf16[128,8,256]{2,1,0:T(8,128)(2,1)S(1)}, bf16[128,8,256]{2,1,0:T(8,128)(2,1)S(1)}, u32[]{:S(2)}, u32[]{:S(2)}) %collective-permute-start.3) | collective-permute-done | bytes 524320 | tf_op jit(solution)/shard_map/ppermute | solution.py:211
  40.3 1.3 %collective-permute-start.11 = (bf16[128,8,256]{2,1,0:T(8,128)(2,1)S(1)}, bf16[128,8,256]{2,1,0:T(8,128)(2,1)S(1)}, u32[]{:S(2)}, u32[]{:S(2)}) collective-permute-start(bf16[128,8,256]{2,1,0:T(8,128)(2,1)S(1)} %collective-permute-done.4), channel_id=1, source_target_pairs={{4,0},{8,12},{5,1},{9,13},{6,2},{10,14},{7,3},{11,15},{20,16},{24,... | collective-permute-start | bytes 1572872 | tf_op jit(solution)/shard_map/ppermute | solution.py:218
  41.6 0.7 collective-permute-start.9
  42.3 1.3 %shard_map.57.early_0 = bf16[128,8,256]{2,1,0:T(8,128)(2,1)S(1)} custom-call(bf16[8,128,256]{2,1,0:T(8,128)(2,1)S(1)} %pad_maximum_fusion.own_ref, bf16[8,128,256]{2,1,0:T(8,128)(2,1)S(1)} %collective-permute-done.5.far_ref, bf16[384,256]{1,0:T(8,128)(2,1)S(1)} %get-tuple-element.25.left_ref, bf16[512,256]{1,0:T(8,128)(2,1)S(1)} %get-tuple-element.26.right_ref), custom_call_target="tpu_custom_call" | custom-call | flops 960000000 | bytes 2097152 | tf_op jit(solution)/shard_map/pallas_call | solution.py:70
  43.6 2.3 %collective-permute-done.8 = bf16[4,128,256]{2,1,0:T(8,128)(2,1)S(1)} collective-permute-done((bf16[4,128,256]{2,1,0:T(8,128)(2,1)S(1)}, bf16[4,128,256]{2,1,0:T(8,128)(2,1)S(1)}, u32[]{:S(2)}, u32[]{:S(2)}) %collective-permute-start.8) | collective-permute-done | bytes 262176 | tf_op jit(solution)/shard_map/ppermute | solution.py:216
  46.1 0.7 collective-permute-start.10
  46.8 1.3 %collective-permute-start.12 = (bf16[128,8,256]{2,1,0:T(8,128)(2,1)S(1)}, bf16[128,8,256]{2,1,0:T(8,128)(2,1)S(1)}, u32[]{:S(2)}, u32[]{:S(2)}) collective-permute-start(bf16[128,8,256]{2,1,0:T(8,128)(2,1)S(1)} %collective-permute-done.9.far_in), channel_id=1, source_target_pairs={{4,0},{8,12},{5,1},{9,13},{6,2},{10,14},{7,3},{11,15},{20,16},{24,... | collective-permute-start | bytes 1572872 | tf_op jit(solution)/shard_map/ppermute | solution.py:222
  48.1 9.1 %collective-permute-done.11 = bf16[128,8,256]{2,1,0:T(8,128)(2,1)S(1)} collective-permute-done((bf16[128,8,256]{2,1,0:T(8,128)(2,1)S(1)}, bf16[128,8,256]{2,1,0:T(8,128)(2,1)S(1)}, u32[]{:S(2)}, u32[]{:S(2)}) %collective-permute-start.11) | collective-permute-done | bytes 524320 | tf_op jit(solution)/shard_map/ppermute | solution.py:218
  57.3 1.3 %shard_map.59.early_1 = bf16[128,8,256]{2,1,0:T(8,128)(2,1)S(1)} custom-call(bf16[8,128,256]{2,1,0:T(8,128)(2,1)S(1)} %pad_maximum_fusion.1.own_ref, bf16[8,128,256]{2,1,0:T(8,128)(2,1)S(1)} %collective-permute-done.10.far_ref, bf16[384,256]{1,0:T(8,128)(2,1)S(1)} %get-tuple-element.25.left_ref, bf16[512,256]{1,0:T(8,128)(2,1)S(1)} %get-tuple-element.26.right_ref), custom_call_target="tpu_custom_call" | custom-call | flops 960000000 | bytes 2097152 | tf_op jit(solution)/shard_map/pallas_call | solution.py:70
  58.6 4.0 %shard_map.60.base_ref = f32[48,128]{1,0:T(8,128)S(1)} custom-call(bf16[128,8,256]{2,1,0:T(8,128)(2,1)S(1)} %shard_map.57.early_0, bf16[128,8,256]{2,1,0:T(8,128)(2,1)S(1)} %shard_map.59.early_1, bf16[128,8,256]{2,1,0:T(8,128)(2,1)S(1)} %shard_map.56.own_ref, bf16[128,8,256]{2,1,0:T(8,128)(2,1)S(1)} %collective-permute-done.3.near, ...), custom_call_target="tpu_custom_call" | custom-call | flops 3000000000 | bytes 12000000 | tf_op jit(solution)/shard_map/pallas_call | solution.py:176
  62.6 3.7 %collective-permute-done.12.far_out = bf16[128,8,256]{2,1,0:T(8,128)(2,1)S(1)} collective-permute-done((bf16[128,8,256]{2,1,0:T(8,128)(2,1)S(1)}, bf16[128,8,256]{2,1,0:T(8,128)(2,1)S(1)}, u32[]{:S(2)}, u32[]{:S(2)}) %collective-permute-start.12) | collective-permute-done | bytes 524320 | tf_op jit(solution)/shard_map/ppermute | solution.py:222
  66.3 3.2 %shard_map.61 = (f32[24,128]{1,0:T(8,128)S(1)}, f32[24,128]{1,0:T(8,128)S(1)}) custom-call(f32[48,128]{1,0:T(8,128)S(1)} %shard_map.60.base_ref, bf16[128,8,256]{2,1,0:T(8,128)(2,1)S(1)} %collective-permute-done.12.far_out, bf16[128,128,256]{2,1,0:T(8,128)(2,1)S(1)} %copy-done, s32[4]{0:T(128)S(1)} %copy-done.3), custom_call_target="tpu_custom_call" | custom-call | flops 3000000000 | bytes 12000000 | tf_op jit(solution)/shard_map/pallas_call | solution.py:176
  69.5 0.6 collective-permute-start.13
  70.1 3.2 %collective-permute-done.13 = f32[24,128]{1,0:T(8,128)S(1)} collective-permute-done((f32[24,128]{1,0:T(8,128)S(1)}, f32[24,128]{1,0:T(8,128)S(1)}, u32[]{:S(2)}, u32[]{:S(2)}) %collective-permute-start.13) | collective-permute-done | bytes 12320 | tf_op jit(solution)/shard_map/ppermute | solution.py:234
  73.2 0.6 add_bitcast_fusion
  (19 shorter events, 0.5 us)
Async XLA Ops:
  1.1 14.9 %collective-permute-start.2 = (bf16[8,128,256]{2,1,0:T(8,128)(2,1)S(1)}, bf16[8,128,256]{2,1,0:T(8,128)(2,1)S(1)}, u32[]{:S(2)}, u32[]{:S(2)}) collective-permute-start(bf16[8,128,256]{2,1,0:T(8,128)(2,1)S(1)} %slice_bitcast_fusion.own_ref), channel_id=1, source_target_pairs={{0,2},{2,0},{1,3},{3,1},{4,6},{6,4},{5,7},{7,5},{8,10},{10,8},{9,1... | collective-permute-start | bytes 1572872 | tf_op jit(solution)/shard_map/ppermute | solution.py:202
  5.1 7.8 %collective-permute-start = (bf16[4,128,256]{2,1,0:T(8,128)(2,1)S(1)}, bf16[4,128,256]{2,1,0:T(8,128)(2,1)S(1)}, u32[]{:S(2)}, u32[]{:S(2)}) collective-permute-start(bf16[4,128,256]{2,1,0:T(8,128)(2,1)S(1)} %slice_bitcast_fusion.1), channel_id=1, source_target_pairs={{0,4},{4,0},{8,12},{12,8},{1,5},{5,1},{9,13},{13,9},{2,6},{6,2},{1... | collective-permute-start | bytes 786440 | tf_op jit(solution)/shard_map/ppermute | solution.py:205
  6.7 6.2 %collective-permute-start.1 = (bf16[4,128,256]{2,1,0:T(8,128)(2,1)S(1)}, bf16[4,128,256]{2,1,0:T(8,128)(2,1)S(1)}, u32[]{:S(2)}, u32[]{:S(2)}) collective-permute-start(bf16[4,128,256]{2,1,0:T(8,128)(2,1)S(1)} %slice_bitcast_fusion.1), channel_id=1, source_target_pairs={{4,8},{8,4},{5,9},{9,5},{6,10},{10,6},{7,11},{11,7},{20,24},{24,20... | collective-permute-start | bytes 786440 | tf_op jit(solution)/shard_map/ppermute | solution.py:206
  7.4 1.0 %copy-start.1 = (f32[256,256]{1,0:T(8,128)S(1)}, f32[256,256]{1,0:T(8,128)}, u32[]{:S(2)}) copy-start(f32[256,256]{1,0:T(8,128)} %left_ref.1) | copy-start | bytes 786436
  8.3 0.9 %copy-start.2 = (f32[256,256]{1,0:T(8,128)S(1)}, f32[256,256]{1,0:T(8,128)}, u32[]{:S(2)}) copy-start(f32[256,256]{1,0:T(8,128)} %right_ref) | copy-start | bytes 786436
  12.9 20.7 %collective-permute-start.7 = (bf16[4,128,256]{2,1,0:T(8,128)(2,1)S(1)}, bf16[4,128,256]{2,1,0:T(8,128)(2,1)S(1)}, u32[]{:S(2)}, u32[]{:S(2)}) collective-permute-start(bf16[4,128,256]{2,1,0:T(8,128)(2,1)S(1)} %collective-permute-done), channel_id=1, source_target_pairs={{4,8},{8,4},{5,9},{9,5},{6,10},{10,6},{7,11},{11,7},{20,24},{24,20... | collective-permute-start | bytes 786440 | tf_op jit(solution)/shard_map/ppermute | solution.py:207
  13.6 21.6 %collective-permute-start.6 = (bf16[4,128,256]{2,1,0:T(8,128)(2,1)S(1)}, bf16[4,128,256]{2,1,0:T(8,128)(2,1)S(1)}, u32[]{:S(2)}, u32[]{:S(2)}) collective-permute-start(bf16[4,128,256]{2,1,0:T(8,128)(2,1)S(1)} %collective-permute-done.1), channel_id=1, source_target_pairs={{4,0},{8,12},{5,1},{9,13},{6,2},{10,14},{7,3},{11,15},{20,16},{24,... | collective-permute-start | bytes 786440 | tf_op jit(solution)/shard_map/ppermute | solution.py:208
  17.3 23.0 %collective-permute-start.3 = (bf16[128,8,256]{2,1,0:T(8,128)(2,1)S(1)}, bf16[128,8,256]{2,1,0:T(8,128)(2,1)S(1)}, u32[]{:S(2)}, u32[]{:S(2)}) collective-permute-start(bf16[128,8,256]{2,1,0:T(8,128)(2,1)S(1)} %shard_map.56.own_ref), channel_id=1, source_target_pairs={{0,4},{4,0},{8,12},{12,8},{1,5},{5,1},{9,13},{13,9},{2,6},{6,2},{1... | collective-permute-start | bytes 1572872 | tf_op jit(solution)/shard_map/ppermute | solution.py:211
  23.8 16.5 %collective-permute-start.4 = (bf16[128,8,256]{2,1,0:T(8,128)(2,1)S(1)}, bf16[128,8,256]{2,1,0:T(8,128)(2,1)S(1)}, u32[]{:S(2)}, u32[]{:S(2)}) collective-permute-start(bf16[128,8,256]{2,1,0:T(8,128)(2,1)S(1)} %shard_map.56.own_ref), channel_id=1, source_target_pairs={{4,8},{8,4},{5,9},{9,5},{6,10},{10,6},{7,11},{11,7},{20,24},{24,20... | collective-permute-start | bytes 1572872 | tf_op jit(solution)/shard_map/ppermute | solution.py:212
  24.5 17.8 %collective-permute-start.5 = (bf16[8,128,256]{2,1,0:T(8,128)(2,1)S(1)}, bf16[8,128,256]{2,1,0:T(8,128)(2,1)S(1)}, u32[]{:S(2)}, u32[]{:S(2)}) collective-permute-start(bf16[8,128,256]{2,1,0:T(8,128)(2,1)S(1)} %pad_maximum_fusion.own_ref), channel_id=1, source_target_pairs={{0,2},{2,0},{1,3},{3,1},{4,6},{6,4},{5,7},{7,5},{8,10},{10,8},{9,1... | collective-permute-start | bytes 1572872 | tf_op jit(solution)/shard_map/ppermute | solution.py:215
  33.5 25.1 %copy-start = (bf16[128,128,256]{2,1,0:T(8,128)(2,1)S(1)}, bf16[128,128,256]{2,1,0:T(8,128)(2,1)}, u32[]{:S(2)}) copy-start(bf16[128,128,256]{2,1,0:T(8,128)(2,1)} %shard_map.58.grad_ref) | copy-start | bytes 25165828
  33.5 25.1 %copy-start.3 = (s32[4]{0:T(128)S(1)}, s32[4]{0:T(128)}, u32[]{:S(2)}) copy-start(s32[4]{0:T(128)} %order_ref.3) | copy-start | bytes 52
  33.6 12.4 %collective-permute-start.8 = (bf16[4,128,256]{2,1,0:T(8,128)(2,1)S(1)}, bf16[4,128,256]{2,1,0:T(8,128)(2,1)S(1)}, u32[]{:S(2)}, u32[]{:S(2)}) collective-permute-start(bf16[4,128,256]{2,1,0:T(8,128)(2,1)S(1)} %collective-permute-done.7), channel_id=1, source_target_pairs={{4,0},{8,12},{5,1},{9,13},{6,2},{10,14},{7,3},{11,15},{20,16},{24,... | collective-permute-start | bytes 786440 | tf_op jit(solution)/shard_map/ppermute | solution.py:216
  40.3 16.8 %collective-permute-start.11 = (bf16[128,8,256]{2,1,0:T(8,128)(2,1)S(1)}, bf16[128,8,256]{2,1,0:T(8,128)(2,1)S(1)}, u32[]{:S(2)}, u32[]{:S(2)}) collective-permute-start(bf16[128,8,256]{2,1,0:T(8,128)(2,1)S(1)} %collective-permute-done.4), channel_id=1, source_target_pairs={{4,0},{8,12},{5,1},{9,13},{6,2},{10,14},{7,3},{11,15},{20,16},{24,... | collective-permute-start | bytes 1572872 | tf_op jit(solution)/shard_map/ppermute | solution.py:218
  41.6 5.2 %collective-permute-start.9 = (bf16[128,8,256]{2,1,0:T(8,128)(2,1)S(1)}, bf16[128,8,256]{2,1,0:T(8,128)(2,1)S(1)}, u32[]{:S(2)}, u32[]{:S(2)}) collective-permute-start(bf16[128,8,256]{2,1,0:T(8,128)(2,1)S(1)} %collective-permute-done.3.near), channel_id=1, source_target_pairs={{4,8},{8,4},{5,9},{9,5},{6,10},{10,6},{7,11},{11,7},{20,24},{24,20... | collective-permute-start | bytes 1572872 | tf_op jit(solution)/shard_map/ppermute | solution.py:217
  46.1 11.3 %collective-permute-start.10 = (bf16[8,128,256]{2,1,0:T(8,128)(2,1)S(1)}, bf16[8,128,256]{2,1,0:T(8,128)(2,1)S(1)}, u32[]{:S(2)}, u32[]{:S(2)}) collective-permute-start(bf16[8,128,256]{2,1,0:T(8,128)(2,1)S(1)} %pad_maximum_fusion.1.own_ref), channel_id=1, source_target_pairs={{0,2},{2,0},{1,3},{3,1},{4,6},{6,4},{5,7},{7,5},{8,10},{10,8},{9,1... | collective-permute-start | bytes 1572872 | tf_op jit(solution)/shard_map/ppermute | solution.py:221
  46.8 19.5 %collective-permute-start.12 = (bf16[128,8,256]{2,1,0:T(8,128)(2,1)S(1)}, bf16[128,8,256]{2,1,0:T(8,128)(2,1)S(1)}, u32[]{:S(2)}, u32[]{:S(2)}) collective-permute-start(bf16[128,8,256]{2,1,0:T(8,128)(2,1)S(1)} %collective-permute-done.9.far_in), channel_id=1, source_target_pairs={{4,0},{8,12},{5,1},{9,13},{6,2},{10,14},{7,3},{11,15},{20,16},{24,... | collective-permute-start | bytes 1572872 | tf_op jit(solution)/shard_map/ppermute | solution.py:222
  69.5 3.8 %collective-permute-start.13 = (f32[24,128]{1,0:T(8,128)S(1)}, f32[24,128]{1,0:T(8,128)S(1)}, u32[]{:S(2)}, u32[]{:S(2)}) collective-permute-start(f32[24,128]{1,0:T(8,128)S(1)} %get-tuple-element.38), channel_id=1, source_target_pairs={{0,2},{2,0},{1,3},{3,1},{4,6},{6,4},{5,7},{7,5},{8,10},{10,8},{9,1... | collective-permute-start | bytes 36872 | tf_op jit(solution)/shard_map/ppermute | solution.py:234

commit v5 on v4

--- a/solution.py
+++ b/solution.py
@@ -202,10 +202,10 @@
     late_other = lax.ppermute(late_raw, "feat", swap)
     raw = after(queries, late_raw)[0, :EARLY]
     terms = factor_terms(left_factor, after(right_factor, raw), train_grads.shape[1])
+    raw_mid = lax.ppermute(raw, "ex", MIDDLE)
     raw_near = lax.ppermute(raw, "ex", PAIRS)
-    raw_mid = lax.ppermute(raw, "ex", MIDDLE)
-    raw_far_mid = lax.ppermute(after(raw_near, *terms), "ex", MIDDLE)
-    raw_mid_out = lax.ppermute(raw_mid, "ex", OUTWARD)
+    raw_far_mid = lax.ppermute(after(raw_near, late_other), "ex", MIDDLE)
+    raw_mid_out = lax.ppermute(after(raw_mid, *terms), "ex", OUTWARD)
 
     late = condition(after(late_raw, raw_near, raw_mid), late_other, *terms)
     near = lax.ppermute(late, "ex", PAIRS)

time: 74.2 us -> 76.8 us (1.035)
  waiting for transfers between devices: 28.1 us -> 32.5 us
  starting transfers between devices: 21.2 us -> 19.3 us
    ppermute x1, waiting for transfers between devices: 2.35 us -> 10.7 us  [per_device_line(): raw_far_out = lax.ppermute(after(raw_far_mid, grads), 'ex', OUTWARD)]
    ppermute x1, starting transfers between devices: 6.51 us -> 2.86 us  [per_device_line(): near = lax.ppermute(late, 'ex', PAIRS)]
    ppermute x1, waiting for transfers between devices: 9.08 us -> 6.75 us  [per_device_line(): mid_out = lax.ppermute(after(mid, near, grads), 'ex', OUTWARD)]
    ppermute x1, waiting for transfers between devices: 5.1 us -> 2.85 us  [per_device_line(): near = lax.ppermute(late, 'ex', PAIRS)]
    ppermute x1, waiting for transfers between devices: 3.16 us -> 2.2 us  [per_device_line(): scores = mine + lax.ppermute(send, 'feat', swap)]
    ppermute x1, starting transfers between devices: 0.6 us -> 1.56 us  [per_device_line(): scores = mine + lax.ppermute(send, 'feat', swap)]
    ppermute x1, waiting for transfers between devices: 3.68 us -> 4.61 us  [per_device_line(): far_out = lax.ppermute(far_mid, 'ex', OUTWARD)]
    ppermute x1, starting transfers between devices: 0.74 us -> 1.56 us  [per_device_line(): early_1_other = lax.ppermute(after(early_1, cond_0), 'feat', swap)]
  transfers between devices with their start and end apart: 14 -> 14, of which waited for: 7 -> 7; matrix products, arithmetic and copies ran while one was open for 2% -> 2% of each run, Pallas kernels for 22% -> 21%
where the time goes in v5:
time: 76.8 us; the launch traced here: 76.4 us
  waiting for transfers between devices  32.5 us (42%)
  Pallas kernels  19.4 us (25%)
  starting transfers between devices  19.3 us (25%)
  local copies, waits for them, and re-layouts  3.95 us (5%)
  other arithmetic  0.97 us (1%)
    ppermute x1, waiting for transfers between devices, per_device_line(): raw_far_out = lax.ppermute(after(raw_far_mid, grads), 'ex', OUTWARD)  10.7 us
    pallas_call x1, Pallas kernels, regroup(): pl.pallas_call(regroup_kernel, out_shape=jax.ShapeDtypeStruct((rows, n, w...  8.39 us
    pallas_call x2, Pallas kernels, score_call(): pl.pallas_call(functools.partial(kernel, ex), out_shape=out_shape, in_spe...  7.17 us
    ppermute x1, waiting for transfers between devices, per_device_line(): mid_out = lax.ppermute(after(mid, near, grads), 'ex', OUTWARD)  6.75 us
    ppermute x1, waiting for transfers between devices, per_device_line(): far_out = lax.ppermute(far_mid, 'ex', OUTWARD)  4.61 us
    pallas_call x3, Pallas kernels, condition(): pl.pallas_call(condition_kernel, out_shape=jax.ShapeDtypeStruct((rows, co...  3.78 us
    ppermute x1, waiting for transfers between devices, per_device_line(): raw_near = lax.ppermute(raw, 'ex', PAIRS)  3.53 us
    ppermute x1, starting transfers between devices, per_device_line(): late_other = lax.ppermute(late_raw, 'feat', swap)  3 us
  transfers between devices with their start and end apart: 14, of which 7 were waited for; matrix products, arithmetic and copies ran while one was open for 2% of the time, Pallas kernels for 21%

profile of v5, /device:TPU:0, one launch (start us, length us, event | category | flops | bytes accessed | tf_op | source)
XLA Modules:
  0.0 76.4 jit_solution(17706133262202306923)
XLA Ops:
  0.0 1.1 %slice_bitcast_fusion.own_ref = bf16[8,128,256]{2,1,0:T(8,128)(2,1)S(1)} fusion(bf16[1,12,128,256]{3,2,1,0:T(8,128)(2,1)} %param.6), kind=kLoop, calls=%fused_computation.2 | loop fusion | bytes 1048576 | tf_op jit(solution)/shard_map/squeeze | solution.py:201
  1.1 3.0 %collective-permute-start.2 = (bf16[8,128,256]{2,1,0:T(8,128)(2,1)S(1)}, bf16[8,128,256]{2,1,0:T(8,128)(2,1)S(1)}, u32[]{:S(2)}, u32[]{:S(2)}) collective-permute-start(bf16[8,128,256]{2,1,0:T(8,128)(2,1)S(1)} %slice_bitcast_fusion.own_ref), channel_id=1, source_target_pairs={{0,2},{2,0},{1,3},{3,1},{4,6},{6,4},{5,7},{7,5},{8,10},{10,8},{9,1... | collective-permute-start | bytes 1572872 | tf_op jit(solution)/shard_map/ppermute | solution.py:202
  4.1 1.0 %slice_bitcast_fusion.1 = bf16[4,128,256]{2,1,0:T(8,128)(2,1)S(1)} fusion(bf16[1,12,128,256]{3,2,1,0:T(8,128)(2,1)} %param.6), kind=kLoop, calls=%fused_computation.3 | loop fusion | bytes 524288 | tf_op jit(solution)/shard_map/squeeze | solution.py:203
  5.1 1.6 %collective-permute-start = (bf16[4,128,256]{2,1,0:T(8,128)(2,1)S(1)}, bf16[4,128,256]{2,1,0:T(8,128)(2,1)S(1)}, u32[]{:S(2)}, u32[]{:S(2)}) collective-permute-start(bf16[4,128,256]{2,1,0:T(8,128)(2,1)S(1)} %slice_bitcast_fusion.1), channel_id=1, source_target_pairs={{0,4},{4,0},{8,12},{12,8},{1,5},{5,1},{9,13},{13,9},{2,6},{6,2},{1... | collective-permute-start | bytes 786440 | tf_op jit(solution)/shard_map/ppermute | solution.py:206
  6.7 0.7 collective-permute-start.1
  7.4 0.9 %copy-done.1 = f32[256,256]{1,0:T(8,128)S(1)} copy-done((f32[256,256]{1,0:T(8,128)S(1)}, f32[256,256]{1,0:T(8,128)}, u32[]{:S(2)}) %copy-start.1) | copy-done | bytes 262168
  8.3 0.9 %copy-done.2 = f32[256,256]{1,0:T(8,128)S(1)} copy-done((f32[256,256]{1,0:T(8,128)S(1)}, f32[256,256]{1,0:T(8,128)}, u32[]{:S(2)}) %copy-start.2) | copy-done | bytes 262168
  9.4 3.5 %collective-permute-done = bf16[4,128,256]{2,1,0:T(8,128)(2,1)S(1)} collective-permute-done((bf16[4,128,256]{2,1,0:T(8,128)(2,1)S(1)}, bf16[4,128,256]{2,1,0:T(8,128)(2,1)S(1)}, u32[]{:S(2)}, u32[]{:S(2)}) %collective-permute-start) | collective-permute-done | bytes 262176 | tf_op jit(solution)/shard_map/ppermute | solution.py:206
  12.9 1.3 %collective-permute-start.6 = (bf16[4,128,256]{2,1,0:T(8,128)(2,1)S(1)}, bf16[4,128,256]{2,1,0:T(8,128)(2,1)S(1)}, u32[]{:S(2)}, u32[]{:S(2)}) collective-permute-start(bf16[4,128,256]{2,1,0:T(8,128)(2,1)S(1)} %collective-permute-done.1), channel_id=1, source_target_pairs={{4,0},{8,12},{5,1},{9,13},{6,2},{10,14},{7,3},{11,15},{20,16},{24,... | collective-permute-start | bytes 786440 | tf_op jit(solution)/shard_map/ppermute | solution.py:208
  14.2 1.8 %collective-permute-done.2.far_ref = bf16[8,128,256]{2,1,0:T(8,128)(2,1)S(1)} collective-permute-done((bf16[8,128,256]{2,1,0:T(8,128)(2,1)S(1)}, bf16[8,128,256]{2,1,0:T(8,128)(2,1)S(1)}, u32[]{:S(2)}, u32[]{:S(2)}) %collective-permute-start.2) | collective-permute-done | bytes 524320 | tf_op jit(solution)/shard_map/ppermute | solution.py:202
  16.0 1.3 %shard_map.56.own_ref = bf16[128,8,256]{2,1,0:T(8,128)(2,1)S(1)} custom-call(bf16[8,128,256]{2,1,0:T(8,128)(2,1)S(1)} %slice_bitcast_fusion.own_ref, bf16[8,128,256]{2,1,0:T(8,128)(2,1)S(1)} %collective-permute-done.2.far_ref, bf16[384,256]{1,0:T(8,128)(2,1)S(1)} %get-tuple-element.26.left_ref, bf16[512,256]{1,0:T(8,128)(2,1)S(1)} %get-tuple-element.27.right_ref), custom_call_target="tpu_custom_call" | custom-call | flops 960000000 | bytes 2097152 | tf_op jit(solution)/shard_map/pallas_call | solution.py:70
  17.3 2.9 %collective-permute-start.3 = (bf16[128,8,256]{2,1,0:T(8,128)(2,1)S(1)}, bf16[128,8,256]{2,1,0:T(8,128)(2,1)S(1)}, u32[]{:S(2)}, u32[]{:S(2)}) collective-permute-start(bf16[128,8,256]{2,1,0:T(8,128)(2,1)S(1)} %shard_map.56.own_ref), channel_id=1, source_target_pairs={{0,4},{4,0},{8,12},{12,8},{1,5},{5,1},{9,13},{13,9},{2,6},{6,2},{1... | collective-permute-start | bytes 1572872 | tf_op jit(solution)/shard_map/ppermute | solution.py:211
  20.1 0.7 collective-permute-start.4
  20.8 0.7 collective-permute-start.7
  21.6 0.6 collective-permute-start.5
  22.2 8.4 %shard_map.58.grad_ref = bf16[128,128,256]{2,1,0:T(8,128)(2,1)} custom-call(bf16[128,128,256]{2,1,0:T(8,128)(2,1)} %grads_ref), custom_call_target="tpu_custom_call" | custom-call | flops 6000000000 | bytes 16000000 | tf_op jit(solution)/shard_map/pallas_call | solution.py:106
  30.6 1.6 %collective-permute-start.8 = (bf16[4,128,256]{2,1,0:T(8,128)(2,1)S(1)}, bf16[4,128,256]{2,1,0:T(8,128)(2,1)S(1)}, u32[]{:S(2)}, u32[]{:S(2)}) collective-permute-start(bf16[4,128,256]{2,1,0:T(8,128)(2,1)S(1)} %collective-permute-done.7), channel_id=1, source_target_pairs={{4,0},{8,12},{5,1},{9,13},{6,2},{10,14},{7,3},{11,15},{20,16},{24,... | collective-permute-start | bytes 786440 | tf_op jit(solution)/shard_map/ppermute | solution.py:216
  32.2 2.9 %collective-permute-done.3.near = bf16[128,8,256]{2,1,0:T(8,128)(2,1)S(1)} collective-permute-done((bf16[128,8,256]{2,1,0:T(8,128)(2,1)S(1)}, bf16[128,8,256]{2,1,0:T(8,128)(2,1)S(1)}, u32[]{:S(2)}, u32[]{:S(2)}) %collective-permute-start.3) | collective-permute-done | bytes 524320 | tf_op jit(solution)/shard_map/ppermute | solution.py:211
  35.1 1.3 %collective-permute-start.11 = (bf16[128,8,256]{2,1,0:T(8,128)(2,1)S(1)}, bf16[128,8,256]{2,1,0:T(8,128)(2,1)S(1)}, u32[]{:S(2)}, u32[]{:S(2)}) collective-permute-start(bf16[128,8,256]{2,1,0:T(8,128)(2,1)S(1)} %collective-permute-done.4), channel_id=1, source_target_pairs={{4,0},{8,12},{5,1},{9,13},{6,2},{10,14},{7,3},{11,15},{20,16},{24,... | collective-permute-start | bytes 1572872 | tf_op jit(solution)/shard_map/ppermute | solution.py:218
  36.4 0.7 collective-permute-start.9
  37.1 1.3 %shard_map.57.early_0 = bf16[128,8,256]{2,1,0:T(8,128)(2,1)S(1)} custom-call(bf16[8,128,256]{2,1,0:T(8,128)(2,1)S(1)} %pad_maximum_fusion.own_ref, bf16[8,128,256]{2,1,0:T(8,128)(2,1)S(1)} %collective-permute-done.5.far_ref, bf16[384,256]{1,0:T(8,128)(2,1)S(1)} %get-tuple-element.26.left_ref, bf16[512,256]{1,0:T(8,128)(2,1)S(1)} %get-tuple-element.27.right_ref), custom_call_target="tpu_custom_call" | custom-call | flops 960000000 | bytes 2097152 | tf_op jit(solution)/shard_map/pallas_call | solution.py:70
  38.4 10.7 %collective-permute-done.8 = bf16[4,128,256]{2,1,0:T(8,128)(2,1)S(1)} collective-permute-done((bf16[4,128,256]{2,1,0:T(8,128)(2,1)S(1)}, bf16[4,128,256]{2,1,0:T(8,128)(2,1)S(1)}, u32[]{:S(2)}, u32[]{:S(2)}) %collective-permute-start.8) | collective-permute-done | bytes 262176 | tf_op jit(solution)/shard_map/ppermute | solution.py:216
  49.2 1.6 %collective-permute-start.10 = (bf16[8,128,256]{2,1,0:T(8,128)(2,1)S(1)}, bf16[8,128,256]{2,1,0:T(8,128)(2,1)S(1)}, u32[]{:S(2)}, u32[]{:S(2)}) collective-permute-start(bf16[8,128,256]{2,1,0:T(8,128)(2,1)S(1)} %pad_maximum_fusion.1.own_ref), channel_id=1, source_target_pairs={{0,2},{2,0},{1,3},{3,1},{4,6},{6,4},{5,7},{7,5},{8,10},{10,8},{9,1... | collective-permute-start | bytes 1572872 | tf_op jit(solution)/shard_map/ppermute | solution.py:221
  50.8 1.3 %collective-permute-start.12 = (bf16[128,8,256]{2,1,0:T(8,128)(2,1)S(1)}, bf16[128,8,256]{2,1,0:T(8,128)(2,1)S(1)}, u32[]{:S(2)}, u32[]{:S(2)}) collective-permute-start(bf16[128,8,256]{2,1,0:T(8,128)(2,1)S(1)} %collective-permute-done.9.far_in), channel_id=1, source_target_pairs={{4,0},{8,12},{5,1},{9,13},{6,2},{10,14},{7,3},{11,15},{20,16},{24,... | collective-permute-start | bytes 1572872 | tf_op jit(solution)/shard_map/ppermute | solution.py:222
  52.1 6.8 %collective-permute-done.11 = bf16[128,8,256]{2,1,0:T(8,128)(2,1)S(1)} collective-permute-done((bf16[128,8,256]{2,1,0:T(8,128)(2,1)S(1)}, bf16[128,8,256]{2,1,0:T(8,128)(2,1)S(1)}, u32[]{:S(2)}, u32[]{:S(2)}) %collective-permute-start.11) | collective-permute-done | bytes 524320 | tf_op jit(solution)/shard_map/ppermute | solution.py:218
  59.0 1.3 %shard_map.59.early_1 = bf16[128,8,256]{2,1,0:T(8,128)(2,1)S(1)} custom-call(bf16[8,128,256]{2,1,0:T(8,128)(2,1)S(1)} %pad_maximum_fusion.1.own_ref, bf16[8,128,256]{2,1,0:T(8,128)(2,1)S(1)} %collective-permute-done.10.far_ref, bf16[384,256]{1,0:T(8,128)(2,1)S(1)} %get-tuple-element.26.left_ref, bf16[512,256]{1,0:T(8,128)(2,1)S(1)} %get-tuple-element.27.right_ref), custom_call_target="tpu_custom_call" | custom-call | flops 960000000 | bytes 2097152 | tf_op jit(solution)/shard_map/pallas_call | solution.py:70
  60.3 4.0 %shard_map.60.base_ref = f32[48,128]{1,0:T(8,128)S(1)} custom-call(bf16[128,8,256]{2,1,0:T(8,128)(2,1)S(1)} %shard_map.57.early_0, bf16[128,8,256]{2,1,0:T(8,128)(2,1)S(1)} %shard_map.59.early_1, bf16[128,8,256]{2,1,0:T(8,128)(2,1)S(1)} %shard_map.56.own_ref, bf16[128,8,256]{2,1,0:T(8,128)(2,1)S(1)} %collective-permute-done.3.near, ...), custom_call_target="tpu_custom_call" | custom-call | flops 3000000000 | bytes 12000000 | tf_op jit(solution)/shard_map/pallas_call | solution.py:176
  64.2 4.6 %collective-permute-done.12.far_out = bf16[128,8,256]{2,1,0:T(8,128)(2,1)S(1)} collective-permute-done((bf16[128,8,256]{2,1,0:T(8,128)(2,1)S(1)}, bf16[128,8,256]{2,1,0:T(8,128)(2,1)S(1)}, u32[]{:S(2)}, u32[]{:S(2)}) %collective-permute-start.12) | collective-permute-done | bytes 524320 | tf_op jit(solution)/shard_map/ppermute | solution.py:222
  68.8 3.2 %shard_map.61 = (f32[24,128]{1,0:T(8,128)S(1)}, f32[24,128]{1,0:T(8,128)S(1)}) custom-call(f32[48,128]{1,0:T(8,128)S(1)} %shard_map.60.base_ref, bf16[128,8,256]{2,1,0:T(8,128)(2,1)S(1)} %collective-permute-done.12.far_out, bf16[128,128,256]{2,1,0:T(8,128)(2,1)S(1)} %copy-done, s32[4]{0:T(128)S(1)} %copy-done.3), custom_call_target="tpu_custom_call" | custom-call | flops 3000000000 | bytes 12000000 | tf_op jit(solution)/shard_map/pallas_call | solution.py:176
  72.0 1.6 %collective-permute-start.13 = (f32[24,128]{1,0:T(8,128)S(1)}, f32[24,128]{1,0:T(8,128)S(1)}, u32[]{:S(2)}, u32[]{:S(2)}) collective-permute-start(f32[24,128]{1,0:T(8,128)S(1)} %get-tuple-element.40), channel_id=1, source_target_pairs={{0,2},{2,0},{1,3},{3,1},{4,6},{6,4},{5,7},{7,5},{8,10},{10,8},{9,1... | collective-permute-start | bytes 36872 | tf_op jit(solution)/shard_map/ppermute | solution.py:234
  73.6 2.2 %collective-permute-done.13 = f32[24,128]{1,0:T(8,128)S(1)} collective-permute-done((f32[24,128]{1,0:T(8,128)S(1)}, f32[24,128]{1,0:T(8,128)S(1)}, u32[]{:S(2)}, u32[]{:S(2)}) %collective-permute-start.13) | collective-permute-done | bytes 12320 | tf_op jit(solution)/shard_map/ppermute | solution.py:234
  75.8 0.6 add_bitcast_fusion
  (19 shorter events, 0.5 us)
Async XLA Ops:
  1.1 14.9 %collective-permute-start.2 = (bf16[8,128,256]{2,1,0:T(8,128)(2,1)S(1)}, bf16[8,128,256]{2,1,0:T(8,128)(2,1)S(1)}, u32[]{:S(2)}, u32[]{:S(2)}) collective-permute-start(bf16[8,128,256]{2,1,0:T(8,128)(2,1)S(1)} %slice_bitcast_fusion.own_ref), channel_id=1, source_target_pairs={{0,2},{2,0},{1,3},{3,1},{4,6},{6,4},{5,7},{7,5},{8,10},{10,8},{9,1... | collective-permute-start | bytes 1572872 | tf_op jit(solution)/shard_map/ppermute | solution.py:202
  5.1 7.8 %collective-permute-start = (bf16[4,128,256]{2,1,0:T(8,128)(2,1)S(1)}, bf16[4,128,256]{2,1,0:T(8,128)(2,1)S(1)}, u32[]{:S(2)}, u32[]{:S(2)}) collective-permute-start(bf16[4,128,256]{2,1,0:T(8,128)(2,1)S(1)} %slice_bitcast_fusion.1), channel_id=1, source_target_pairs={{0,4},{4,0},{8,12},{12,8},{1,5},{5,1},{9,13},{13,9},{2,6},{6,2},{1... | collective-permute-start | bytes 786440 | tf_op jit(solution)/shard_map/ppermute | solution.py:206
  6.7 6.2 %collective-permute-start.1 = (bf16[4,128,256]{2,1,0:T(8,128)(2,1)S(1)}, bf16[4,128,256]{2,1,0:T(8,128)(2,1)S(1)}, u32[]{:S(2)}, u32[]{:S(2)}) collective-permute-start(bf16[4,128,256]{2,1,0:T(8,128)(2,1)S(1)} %slice_bitcast_fusion.1), channel_id=1, source_target_pairs={{4,8},{8,4},{5,9},{9,5},{6,10},{10,6},{7,11},{11,7},{20,24},{24,20... | collective-permute-start | bytes 786440 | tf_op jit(solution)/shard_map/ppermute | solution.py:205
  7.4 1.0 %copy-start.1 = (f32[256,256]{1,0:T(8,128)S(1)}, f32[256,256]{1,0:T(8,128)}, u32[]{:S(2)}) copy-start(f32[256,256]{1,0:T(8,128)} %left_ref.1) | copy-start | bytes 786436
  8.3 0.9 %copy-start.2 = (f32[256,256]{1,0:T(8,128)S(1)}, f32[256,256]{1,0:T(8,128)}, u32[]{:S(2)}) copy-start(f32[256,256]{1,0:T(8,128)} %right_ref) | copy-start | bytes 786436
  12.9 19.3 %collective-permute-start.6 = (bf16[4,128,256]{2,1,0:T(8,128)(2,1)S(1)}, bf16[4,128,256]{2,1,0:T(8,128)(2,1)S(1)}, u32[]{:S(2)}, u32[]{:S(2)}) collective-permute-start(bf16[4,128,256]{2,1,0:T(8,128)(2,1)S(1)} %collective-permute-done.1), channel_id=1, source_target_pairs={{4,0},{8,12},{5,1},{9,13},{6,2},{10,14},{7,3},{11,15},{20,16},{24,... | collective-permute-start | bytes 786440 | tf_op jit(solution)/shard_map/ppermute | solution.py:208
  17.3 17.8 %collective-permute-start.3 = (bf16[128,8,256]{2,1,0:T(8,128)(2,1)S(1)}, bf16[128,8,256]{2,1,0:T(8,128)(2,1)S(1)}, u32[]{:S(2)}, u32[]{:S(2)}) collective-permute-start(bf16[128,8,256]{2,1,0:T(8,128)(2,1)S(1)} %shard_map.56.own_ref), channel_id=1, source_target_pairs={{0,4},{4,0},{8,12},{12,8},{1,5},{5,1},{9,13},{13,9},{2,6},{6,2},{1... | collective-permute-start | bytes 1572872 | tf_op jit(solution)/shard_map/ppermute | solution.py:211
  20.1 15.0 %collective-permute-start.4 = (bf16[128,8,256]{2,1,0:T(8,128)(2,1)S(1)}, bf16[128,8,256]{2,1,0:T(8,128)(2,1)S(1)}, u32[]{:S(2)}, u32[]{:S(2)}) collective-permute-start(bf16[128,8,256]{2,1,0:T(8,128)(2,1)S(1)} %shard_map.56.own_ref), channel_id=1, source_target_pairs={{4,8},{8,4},{5,9},{9,5},{6,10},{10,6},{7,11},{11,7},{20,24},{24,20... | collective-permute-start | bytes 1572872 | tf_op jit(solution)/shard_map/ppermute | solution.py:212
  20.8 9.8 %collective-permute-start.7 = (bf16[4,128,256]{2,1,0:T(8,128)(2,1)S(1)}, bf16[4,128,256]{2,1,0:T(8,128)(2,1)S(1)}, u32[]{:S(2)}, u32[]{:S(2)}) collective-permute-start(bf16[4,128,256]{2,1,0:T(8,128)(2,1)S(1)} %collective-permute-done), channel_id=1, source_target_pairs={{4,8},{8,4},{5,9},{9,5},{6,10},{10,6},{7,11},{11,7},{20,24},{24,20... | collective-permute-start | bytes 786440 | tf_op jit(solution)/shard_map/ppermute | solution.py:207
  21.6 15.5 %collective-permute-start.5 = (bf16[8,128,256]{2,1,0:T(8,128)(2,1)S(1)}, bf16[8,128,256]{2,1,0:T(8,128)(2,1)S(1)}, u32[]{:S(2)}, u32[]{:S(2)}) collective-permute-start(bf16[8,128,256]{2,1,0:T(8,128)(2,1)S(1)} %pad_maximum_fusion.own_ref), channel_id=1, source_target_pairs={{0,2},{2,0},{1,3},{3,1},{4,6},{6,4},{5,7},{7,5},{8,10},{10,8},{9,1... | collective-permute-start | bytes 1572872 | tf_op jit(solution)/shard_map/ppermute | solution.py:215
  30.6 29.7 %copy-start = (bf16[128,128,256]{2,1,0:T(8,128)(2,1)S(1)}, bf16[128,128,256]{2,1,0:T(8,128)(2,1)}, u32[]{:S(2)}) copy-start(bf16[128,128,256]{2,1,0:T(8,128)(2,1)} %shard_map.58.grad_ref) | copy-start | bytes 25165828
  30.6 29.7 %copy-start.3 = (s32[4]{0:T(128)S(1)}, s32[4]{0:T(128)}, u32[]{:S(2)}) copy-start(s32[4]{0:T(128)} %order_ref.3) | copy-start | bytes 52
  30.6 18.5 %collective-permute-start.8 = (bf16[4,128,256]{2,1,0:T(8,128)(2,1)S(1)}, bf16[4,128,256]{2,1,0:T(8,128)(2,1)S(1)}, u32[]{:S(2)}, u32[]{:S(2)}) collective-permute-start(bf16[4,128,256]{2,1,0:T(8,128)(2,1)S(1)} %collective-permute-done.7), channel_id=1, source_target_pairs={{4,0},{8,12},{5,1},{9,13},{6,2},{10,14},{7,3},{11,15},{20,16},{24,... | collective-permute-start | bytes 786440 | tf_op jit(solution)/shard_map/ppermute | solution.py:216
  35.1 23.7 %collective-permute-start.11 = (bf16[128,8,256]{2,1,0:T(8,128)(2,1)S(1)}, bf16[128,8,256]{2,1,0:T(8,128)(2,1)S(1)}, u32[]{:S(2)}, u32[]{:S(2)}) collective-permute-start(bf16[128,8,256]{2,1,0:T(8,128)(2,1)S(1)} %collective-permute-done.4), channel_id=1, source_target_pairs={{4,0},{8,12},{5,1},{9,13},{6,2},{10,14},{7,3},{11,15},{20,16},{24,... | collective-permute-start | bytes 1572872 | tf_op jit(solution)/shard_map/ppermute | solution.py:218
  36.4 14.4 %collective-permute-start.9 = (bf16[128,8,256]{2,1,0:T(8,128)(2,1)S(1)}, bf16[128,8,256]{2,1,0:T(8,128)(2,1)S(1)}, u32[]{:S(2)}, u32[]{:S(2)}) collective-permute-start(bf16[128,8,256]{2,1,0:T(8,128)(2,1)S(1)} %collective-permute-done.3.near), channel_id=1, source_target_pairs={{4,8},{8,4},{5,9},{9,5},{6,10},{10,6},{7,11},{11,7},{20,24},{24,20... | collective-permute-start | bytes 1572872 | tf_op jit(solution)/shard_map/ppermute | solution.py:217
  49.2 9.8 %collective-permute-start.10 = (bf16[8,128,256]{2,1,0:T(8,128)(2,1)S(1)}, bf16[8,128,256]{2,1,0:T(8,128)(2,1)S(1)}, u32[]{:S(2)}, u32[]{:S(2)}) collective-permute-start(bf16[8,128,256]{2,1,0:T(8,128)(2,1)S(1)} %pad_maximum_fusion.1.own_ref), channel_id=1, source_target_pairs={{0,2},{2,0},{1,3},{3,1},{4,6},{6,4},{5,7},{7,5},{8,10},{10,8},{9,1... | collective-permute-start | bytes 1572872 | tf_op jit(solution)/shard_map/ppermute | solution.py:221
  50.8 18.1 %collective-permute-start.12 = (bf16[128,8,256]{2,1,0:T(8,128)(2,1)S(1)}, bf16[128,8,256]{2,1,0:T(8,128)(2,1)S(1)}, u32[]{:S(2)}, u32[]{:S(2)}) collective-permute-start(bf16[128,8,256]{2,1,0:T(8,128)(2,1)S(1)} %collective-permute-done.9.far_in), channel_id=1, source_target_pairs={{4,0},{8,12},{5,1},{9,13},{6,2},{10,14},{7,3},{11,15},{20,16},{24,... | collective-permute-start | bytes 1572872 | tf_op jit(solution)/shard_map/ppermute | solution.py:222
  72.0 3.8 %collective-permute-start.13 = (f32[24,128]{1,0:T(8,128)S(1)}, f32[24,128]{1,0:T(8,128)S(1)}, u32[]{:S(2)}, u32[]{:S(2)}) collective-permute-start(f32[24,128]{1,0:T(8,128)S(1)} %get-tuple-element.40), channel_id=1, source_target_pairs={{0,2},{2,0},{1,3},{3,1},{4,6},{6,4},{5,7},{7,5},{8,10},{10,8},{9,1... | collective-permute-start | bytes 36872 | tf_op jit(solution)/shard_map/ppermute | solution.py:234

commit v6 on v5

--- a/solution.py
+++ b/solution.py
@@ -114,7 +114,7 @@
     )(grads)
 
 
-def inner_products(query_refs, grad_ref):
+def inner_products(query_refs, grad_ref, first=0):
     total = sum(ref.shape[1] for ref in query_refs)
 
     def body(i, acc):
@@ -122,13 +122,13 @@
         queries = [jnp.concatenate([ref[r] for ref in query_refs], axis=0) for r in at]
         return acc + lax.dot_general(
             jnp.concatenate(queries, axis=1),
-            jnp.concatenate([grad_ref[r] for r in at], axis=1),
+            jnp.concatenate([grad_ref[first + r] for r in at], axis=1),
             (((1,), (1,)), ((), ())),
             preferred_element_type=F32,
         )
 
     start = jnp.zeros((total, grad_ref.shape[1]), F32)
-    return lax.fori_loop(0, grad_ref.shape[0] // DEEP, body, start)
+    return lax.fori_loop(0, query_refs[0].shape[0] // DEEP, body, start)
 
 
 def first_pass_kernel(ex, early_0, early_1, own_ref, near, mid, far_in, grad_ref, order_ref, out_ref):
@@ -158,9 +158,13 @@
     return [me, near, jnp.where(low_pair, 2, 1), jnp.where(low_pair, 3, 0)]
 
 
-def last_pass_kernel(ex, base_ref, far_out, grad_ref, order_ref, mine_ref, send_ref, full_ref):
+def far_pass_kernel(ex, far_out, grad_ref, order_ref, out_ref):
+    out_ref[...] = inner_products((far_out,), grad_ref)
+
+
+def last_pass_kernel(ex, base_ref, far_ref, far_out, grad_ref, order_ref, mine_ref, send_ref, full_ref):
     late = far_out.shape[1]
-    acc = inner_products((far_out,), grad_ref)
+    acc = far_ref[...] + inner_products((far_out,), grad_ref, far_out.shape[0])
     far = slot_sources(lax.axis_index("ex"))[3]
     full_ref[...] = base_ref[...]
     for b in range(ex):
@@ -202,33 +206,39 @@
     late_other = lax.ppermute(late_raw, "feat", swap)
     raw = after(queries, late_raw)[0, :EARLY]
     terms = factor_terms(left_factor, after(right_factor, raw), train_grads.shape[1])
+    raw_near = lax.ppermute(raw, "ex", PAIRS)
     raw_mid = lax.ppermute(raw, "ex", MIDDLE)
-    raw_near = lax.ppermute(raw, "ex", PAIRS)
-    raw_far_mid = lax.ppermute(after(raw_near, late_other), "ex", MIDDLE)
     raw_mid_out = lax.ppermute(after(raw_mid, *terms), "ex", OUTWARD)
+    early_0 = jnp.concatenate([raw, after(raw_near, raw_mid)], axis=0)
+    raw_far_mid = lax.ppermute(after(raw_near, early_0), "ex", MIDDLE)
 
     late = condition(after(late_raw, raw_near, raw_mid), late_other, *terms)
     near = lax.ppermute(late, "ex", PAIRS)
     mid = lax.ppermute(late, "ex", MIDDLE)
     grads = regroup(after(train_grads, late))
-    early_0 = jnp.concatenate([raw, after(raw_near, late)], axis=0)
-    early_0_other = lax.ppermute(early_0, "feat", swap)
+    early_0_other = lax.ppermute(after(early_0, late), "feat", swap)
     raw_far_out = lax.ppermute(after(raw_far_mid, grads), "ex", OUTWARD)
     far_mid = lax.ppermute(after(near, grads), "ex", MIDDLE)
     mid_out = lax.ppermute(after(mid, near, grads), "ex", OUTWARD)
     cond_0 = condition(after(early_0, near, mid), early_0_other, *terms)
     early_1 = jnp.concatenate([raw_mid + raw_mid_out, after(raw_far_mid, near, mid) + raw_far_out], axis=0)
     early_1_other = lax.ppermute(after(early_1, cond_0), "feat", swap)
-    far_out = lax.ppermute(far_mid, "ex", OUTWARD)
+    part = far_mid.shape[0] // 2
+    far_out_0 = lax.ppermute(far_mid[:part], "ex", OUTWARD)
+    far_out_1 = lax.ppermute(far_mid[part:], "ex", OUTWARD)
     cond_1 = condition(after(early_1, far_mid), early_1_other, *terms)
 
     base = score_call(
         first_pass_kernel, ex, (cond_0, cond_1, late, near, mid + mid_out, far_mid, grads), block_order,
         jax.ShapeDtypeStruct((ex * count, n), F32),
     )
+    far_0 = score_call(
+        far_pass_kernel, ex, (far_out_0, after(grads, base)), block_order,
+        jax.ShapeDtypeStruct((count - EARLY, n), F32),
+    )
     half = jax.ShapeDtypeStruct((ex * count // 2, n), F32)
     mine, send = score_call(
-        last_pass_kernel, ex, (base, far_out, grads), block_order, (half, half),
+        last_pass_kernel, ex, (base, far_0, far_out_1, grads), block_order, (half, half),
         [pltpu.VMEM((ex * count, n), F32)],
     )
     scores = mine + lax.ppermute(send, "feat", swap)

time: 76.8 us -> 76.9 us (level)
  waiting for transfers between devices: 32.5 us -> 29.4 us
  starting transfers between devices: 19.3 us -> 22 us
    ppermute x1, waiting for transfers between devices: 10.7 us -> 3.53 us  [per_device_line(): raw_far_out = lax.ppermute(after(raw_far_mid, grads), 'ex', OUTWARD)]
    ppermute x1, starting transfers between devices: 1.64 us -> 4.45 us  [per_device_line(): raw_near = lax.ppermute(raw, 'ex', PAIRS)]
    ppermute x1, waiting for transfers between devices: 2.85 us -> 5.04 us  [per_device_line(): near = lax.ppermute(late, 'ex', PAIRS)]
    ppermute x1, waiting for transfers between devices: 1.83 us -> 0.01 us  [per_device_line(): late_other = lax.ppermute(late_raw, 'feat', swap)]
    ppermute x1, waiting for transfers between devices: 6.75 us -> 8.32 us  [per_device_line(): mid_out = lax.ppermute(after(mid, near, grads), 'ex', OUTWARD)]
    ppermute x1, waiting for transfers between devices: 2.2 us -> 3.59 us  [per_device_line(): scores = mine + lax.ppermute(send, 'feat', swap)]
    ppermute x1, starting transfers between devices: 1.56 us -> 0.17 us  [per_device_line(): scores = mine + lax.ppermute(send, 'feat', swap)]
    ppermute x3 -> x4, starting transfers between devices: 2.56 us -> 3.86 us  [the longest x1 1.29 us: per_device_line(): far_out_0 = lax.ppermute(far_mid[:part], 'ex', OUTWARD)]
  transfers between devices with their start and end apart: 14 -> 15, of which waited for: 7 -> 6; matrix products, arithmetic and copies ran while one was open for 2% -> 2% of each run, Pallas kernels for 21% -> 24%
where the time goes in v6:
time: 76.9 us; the launch traced here: 76.6 us
  waiting for transfers between devices  29.4 us (38%)
  starting transfers between devices  22 us (29%)
  Pallas kernels  20 us (26%)
  local copies, waits for them, and re-layouts  3.99 us (5%)
  other arithmetic  0.97 us (1%)
    pallas_call x1, Pallas kernels, regroup(): pl.pallas_call(regroup_kernel, out_shape=jax.ShapeDtypeStruct((rows, n, w...  8.41 us
    ppermute x1, waiting for transfers between devices, per_device_line(): mid_out = lax.ppermute(after(mid, near, grads), 'ex', OUTWARD)  8.32 us
    pallas_call x3, Pallas kernels, score_call(): pl.pallas_call(functools.partial(kernel, ex), out_shape=out_shape, in_spe...  7.68 us
    ppermute x1, waiting for transfers between devices, per_device_line(): far_out_1 = lax.ppermute(far_mid[part:], 'ex', OUTWARD)  5.11 us
    ppermute x1, waiting for transfers between devices, per_device_line(): near = lax.ppermute(late, 'ex', PAIRS)  5.04 us
    ppermute x1, starting transfers between devices, per_device_line(): raw_near = lax.ppermute(raw, 'ex', PAIRS)  4.45 us
    pallas_call x3, Pallas kernels, condition(): pl.pallas_call(condition_kernel, out_shape=jax.ShapeDtypeStruct((rows, co...  3.79 us
    ppermute x1, waiting for transfers between devices, per_device_line(): raw_near = lax.ppermute(raw, 'ex', PAIRS)  3.75 us
  transfers between devices with their start and end apart: 15, of which 6 were waited for; matrix products, arithmetic and copies ran while one was open for 2% of the time, Pallas kernels for 24%

profile of v6, /device:TPU:0, one launch (start us, length us, event | category | flops | bytes accessed | tf_op | source)
XLA Modules:
  0.0 76.6 jit_solution(16590347353456435611)
XLA Ops:
  0.0 1.1 %slice_bitcast_fusion.own_ref = bf16[8,128,256]{2,1,0:T(8,128)(2,1)S(1)} fusion(bf16[1,12,128,256]{3,2,1,0:T(8,128)(2,1)} %param.6), kind=kLoop, calls=%fused_computation.2 | loop fusion | bytes 1048576 | tf_op jit(solution)/shard_map/squeeze | solution.py:205
  1.1 3.0 %collective-permute-start.2 = (bf16[8,128,256]{2,1,0:T(8,128)(2,1)S(1)}, bf16[8,128,256]{2,1,0:T(8,128)(2,1)S(1)}, u32[]{:S(2)}, u32[]{:S(2)}) collective-permute-start(bf16[8,128,256]{2,1,0:T(8,128)(2,1)S(1)} %slice_bitcast_fusion.own_ref), channel_id=1, source_target_pairs={{0,2},{2,0},{1,3},{3,1},{4,6},{6,4},{5,7},{7,5},{8,10},{10,8},{9,1... | collective-permute-start | bytes 1572872 | tf_op jit(solution)/shard_map/ppermute | solution.py:206
  4.1 1.0 %slice_bitcast_fusion.1 = bf16[4,128,256]{2,1,0:T(8,128)(2,1)S(1)} fusion(bf16[1,12,128,256]{3,2,1,0:T(8,128)(2,1)} %param.6), kind=kLoop, calls=%fused_computation.3 | loop fusion | bytes 524288 | tf_op jit(solution)/shard_map/squeeze | solution.py:207
  5.1 0.7 collective-permute-start.1
  5.7 4.4 %collective-permute-start = (bf16[4,128,256]{2,1,0:T(8,128)(2,1)S(1)}, bf16[4,128,256]{2,1,0:T(8,128)(2,1)S(1)}, u32[]{:S(2)}, u32[]{:S(2)}) collective-permute-start(bf16[4,128,256]{2,1,0:T(8,128)(2,1)S(1)} %slice_bitcast_fusion.1), channel_id=1, source_target_pairs={{0,4},{4,0},{8,12},{12,8},{1,5},{5,1},{9,13},{13,9},{2,6},{6,2},{1... | collective-permute-start | bytes 786440 | tf_op jit(solution)/shard_map/ppermute | solution.py:209
  10.2 0.9 %copy-done.1 = f32[256,256]{1,0:T(8,128)S(1)} copy-done((f32[256,256]{1,0:T(8,128)S(1)}, f32[256,256]{1,0:T(8,128)}, u32[]{:S(2)}) %copy-start.1) | copy-done | bytes 262168
  11.1 0.9 %copy-done.2 = f32[256,256]{1,0:T(8,128)S(1)} copy-done((f32[256,256]{1,0:T(8,128)S(1)}, f32[256,256]{1,0:T(8,128)}, u32[]{:S(2)}) %copy-start.2) | copy-done | bytes 262168
  12.2 3.8 %collective-permute-done = bf16[4,128,256]{2,1,0:T(8,128)(2,1)S(1)} collective-permute-done((bf16[4,128,256]{2,1,0:T(8,128)(2,1)S(1)}, bf16[4,128,256]{2,1,0:T(8,128)(2,1)S(1)}, u32[]{:S(2)}, u32[]{:S(2)}) %collective-permute-start) | collective-permute-done | bytes 262176 | tf_op jit(solution)/shard_map/ppermute | solution.py:209
  16.0 0.7 collective-permute-start.7
  16.7 1.3 %collective-permute-start.6 = (bf16[4,128,256]{2,1,0:T(8,128)(2,1)S(1)}, bf16[4,128,256]{2,1,0:T(8,128)(2,1)S(1)}, u32[]{:S(2)}, u32[]{:S(2)}) collective-permute-start(bf16[4,128,256]{2,1,0:T(8,128)(2,1)S(1)} %collective-permute-done.1), channel_id=1, source_target_pairs={{4,0},{8,12},{5,1},{9,13},{6,2},{10,14},{7,3},{11,15},{20,16},{24,... | collective-permute-start | bytes 786440 | tf_op jit(solution)/shard_map/ppermute | solution.py:211
  18.0 1.3 %shard_map.56.own_ref = bf16[128,8,256]{2,1,0:T(8,128)(2,1)S(1)} custom-call(bf16[8,128,256]{2,1,0:T(8,128)(2,1)S(1)} %slice_bitcast_fusion.own_ref, bf16[8,128,256]{2,1,0:T(8,128)(2,1)S(1)} %collective-permute-done.2.far_ref, bf16[384,256]{1,0:T(8,128)(2,1)S(1)} %get-tuple-element.29.left_ref, bf16[512,256]{1,0:T(8,128)(2,1)S(1)} %get-tuple-element.30.right_ref), custom_call_target="tpu_custom_call" | custom-call | flops 960000000 | bytes 2097152 | tf_op jit(solution)/shard_map/pallas_call | solution.py:70
  19.3 3.5 %collective-permute-start.3 = (bf16[128,8,256]{2,1,0:T(8,128)(2,1)S(1)}, bf16[128,8,256]{2,1,0:T(8,128)(2,1)S(1)}, u32[]{:S(2)}, u32[]{:S(2)}) collective-permute-start(bf16[128,8,256]{2,1,0:T(8,128)(2,1)S(1)} %shard_map.56.own_ref), channel_id=1, source_target_pairs={{0,4},{4,0},{8,12},{12,8},{1,5},{5,1},{9,13},{13,9},{2,6},{6,2},{1... | collective-permute-start | bytes 1572872 | tf_op jit(solution)/shard_map/ppermute | solution.py:216
  22.8 0.7 collective-permute-start.4
  23.4 0.6 collective-permute-start.5
  24.0 8.4 %shard_map.58.grad_ref = bf16[128,128,256]{2,1,0:T(8,128)(2,1)} custom-call(bf16[128,128,256]{2,1,0:T(8,128)(2,1)} %grads_ref), custom_call_target="tpu_custom_call" | custom-call | flops 6000000000 | bytes 16000000 | tf_op jit(solution)/shard_map/pallas_call | solution.py:106
  32.5 1.6 %collective-permute-start.8 = (bf16[4,128,256]{2,1,0:T(8,128)(2,1)S(1)}, bf16[4,128,256]{2,1,0:T(8,128)(2,1)S(1)}, u32[]{:S(2)}, u32[]{:S(2)}) collective-permute-start(bf16[4,128,256]{2,1,0:T(8,128)(2,1)S(1)} %collective-permute-done.7), channel_id=1, source_target_pairs={{4,0},{8,12},{5,1},{9,13},{6,2},{10,14},{7,3},{11,15},{20,16},{24,... | collective-permute-start | bytes 786440 | tf_op jit(solution)/shard_map/ppermute | solution.py:220
  34.1 5.0 %collective-permute-done.3.near = bf16[128,8,256]{2,1,0:T(8,128)(2,1)S(1)} collective-permute-done((bf16[128,8,256]{2,1,0:T(8,128)(2,1)S(1)}, bf16[128,8,256]{2,1,0:T(8,128)(2,1)S(1)}, u32[]{:S(2)}, u32[]{:S(2)}) %collective-permute-start.3) | collective-permute-done | bytes 524320 | tf_op jit(solution)/shard_map/ppermute | solution.py:216
  39.1 0.7 collective-permute-start.9
  39.9 1.3 %collective-permute-start.11 = (bf16[128,8,256]{2,1,0:T(8,128)(2,1)S(1)}, bf16[128,8,256]{2,1,0:T(8,128)(2,1)S(1)}, u32[]{:S(2)}, u32[]{:S(2)}) collective-permute-start(bf16[128,8,256]{2,1,0:T(8,128)(2,1)S(1)} %collective-permute-done.4), channel_id=1, source_target_pairs={{4,0},{8,12},{5,1},{9,13},{6,2},{10,14},{7,3},{11,15},{20,16},{24,... | collective-permute-start | bytes 1572872 | tf_op jit(solution)/shard_map/ppermute | solution.py:222
  41.2 3.5 %collective-permute-done.8 = bf16[4,128,256]{2,1,0:T(8,128)(2,1)S(1)} collective-permute-done((bf16[4,128,256]{2,1,0:T(8,128)(2,1)S(1)}, bf16[4,128,256]{2,1,0:T(8,128)(2,1)S(1)}, u32[]{:S(2)}, u32[]{:S(2)}) %collective-permute-start.8) | collective-permute-done | bytes 262176 | tf_op jit(solution)/shard_map/ppermute | solution.py:220
  44.8 1.3 %shard_map.57.early_0 = bf16[128,8,256]{2,1,0:T(8,128)(2,1)S(1)} custom-call(bf16[8,128,256]{2,1,0:T(8,128)(2,1)S(1)} %pad_maximum_fusion.own_ref, bf16[8,128,256]{2,1,0:T(8,128)(2,1)S(1)} %collective-permute-done.5.far_ref, bf16[384,256]{1,0:T(8,128)(2,1)S(1)} %get-tuple-element.29.left_ref, bf16[512,256]{1,0:T(8,128)(2,1)S(1)} %get-tuple-element.30.right_ref), custom_call_target="tpu_custom_call" | custom-call | flops 960000000 | bytes 2097152 | tf_op jit(solution)/shard_map/pallas_call | solution.py:70
  46.1 0.9 %collective-permute-start.10 = (bf16[8,128,256]{2,1,0:T(8,128)(2,1)S(1)}, bf16[8,128,256]{2,1,0:T(8,128)(2,1)S(1)}, u32[]{:S(2)}, u32[]{:S(2)}) collective-permute-start(bf16[8,128,256]{2,1,0:T(8,128)(2,1)S(1)} %pad_maximum_fusion.1.own_ref), channel_id=1, source_target_pairs={{0,2},{2,0},{1,3},{3,1},{4,6},{6,4},{5,7},{7,5},{8,10},{10,8},{9,1... | collective-permute-start | bytes 1572872 | tf_op jit(solution)/shard_map/ppermute | solution.py:225
  47.0 1.3 %collective-permute-start.12 = (bf16[64,8,256]{2,1,0:T(8,128)(2,1)S(1)}, bf16[64,8,256]{2,1,0:T(8,128)(2,1)S(1)}, u32[]{:S(2)}, u32[]{:S(2)}) collective-permute-start(bf16[64,8,256]{2,1,0:T(8,128)(2,1)S(1)} %get-tuple-element.46), channel_id=1, source_target_pairs={{4,0},{8,12},{5,1},{9,13},{6,2},{10,14},{7,3},{11,15},{20,16},{24,... | collective-permute-start | bytes 786440 | tf_op jit(solution)/shard_map/ppermute | solution.py:227
  48.3 8.3 %collective-permute-done.11 = bf16[128,8,256]{2,1,0:T(8,128)(2,1)S(1)} collective-permute-done((bf16[128,8,256]{2,1,0:T(8,128)(2,1)S(1)}, bf16[128,8,256]{2,1,0:T(8,128)(2,1)S(1)}, u32[]{:S(2)}, u32[]{:S(2)}) %collective-permute-start.11) | collective-permute-done | bytes 524320 | tf_op jit(solution)/shard_map/ppermute | solution.py:222
  56.8 1.3 %shard_map.59.early_1 = bf16[128,8,256]{2,1,0:T(8,128)(2,1)S(1)} custom-call(bf16[8,128,256]{2,1,0:T(8,128)(2,1)S(1)} %pad_maximum_fusion.1.own_ref, bf16[8,128,256]{2,1,0:T(8,128)(2,1)S(1)} %collective-permute-done.10.far_ref, bf16[384,256]{1,0:T(8,128)(2,1)S(1)} %get-tuple-element.29.left_ref, bf16[512,256]{1,0:T(8,128)(2,1)S(1)} %get-tuple-element.30.right_ref), custom_call_target="tpu_custom_call" | custom-call | flops 960000000 | bytes 2097152 | tf_op jit(solution)/shard_map/pallas_call | solution.py:70
  58.1 4.0 %shard_map.60.base_ref = f32[48,128]{1,0:T(8,128)S(1)} custom-call(bf16[128,8,256]{2,1,0:T(8,128)(2,1)S(1)} %shard_map.57.early_0, bf16[128,8,256]{2,1,0:T(8,128)(2,1)S(1)} %shard_map.59.early_1, bf16[128,8,256]{2,1,0:T(8,128)(2,1)S(1)} %shard_map.56.own_ref, bf16[128,8,256]{2,1,0:T(8,128)(2,1)S(1)} %collective-permute-done.3.near, ...), custom_call_target="tpu_custom_call" | custom-call | flops 3000000000 | bytes 12000000 | tf_op jit(solution)/shard_map/pallas_call | solution.py:180
  62.1 1.3 %collective-permute-start.13 = (bf16[64,8,256]{2,1,0:T(8,128)(2,1)S(1)}, bf16[64,8,256]{2,1,0:T(8,128)(2,1)S(1)}, u32[]{:S(2)}, u32[]{:S(2)}) collective-permute-start(bf16[64,8,256]{2,1,0:T(8,128)(2,1)S(1)} %get-tuple-element.45), channel_id=1, source_target_pairs={{4,0},{8,12},{5,1},{9,13},{6,2},{10,14},{7,3},{11,15},{20,16},{24,... | collective-permute-start | bytes 786440 | tf_op jit(solution)/shard_map/ppermute | solution.py:228
  63.4 1.8 %shard_map.61.far_ref = f32[8,128]{1,0:T(8,128)S(1)} custom-call(bf16[64,8,256]{2,1,0:T(8,128)(2,1)S(1)} %collective-permute-done.12.far_out, bf16[128,128,256]{2,1,0:T(8,128)(2,1)S(1)} %copy-done, s32[4]{0:T(128)S(1)} %copy-done.3), custom_call_target="tpu_custom_call" | custom-call | flops 3000000000 | bytes 12000000 | tf_op jit(solution)/shard_map/pallas_call | solution.py:180
  65.2 5.1 %collective-permute-done.13.far_out = bf16[64,8,256]{2,1,0:T(8,128)(2,1)S(1)} collective-permute-done((bf16[64,8,256]{2,1,0:T(8,128)(2,1)S(1)}, bf16[64,8,256]{2,1,0:T(8,128)(2,1)S(1)}, u32[]{:S(2)}, u32[]{:S(2)}) %collective-permute-start.13) | collective-permute-done | bytes 262176 | tf_op jit(solution)/shard_map/ppermute | solution.py:228
  70.3 1.9 %shard_map.62 = (f32[24,128]{1,0:T(8,128)S(1)}, f32[24,128]{1,0:T(8,128)S(1)}) custom-call(f32[48,128]{1,0:T(8,128)S(1)} %shard_map.60.base_ref, f32[8,128]{1,0:T(8,128)S(1)} %shard_map.61.far_ref, bf16[64,8,256]{2,1,0:T(8,128)(2,1)S(1)} %collective-permute-done.13.far_out, bf16[128,128,256]{2,1,0:T(8,128)(2,1)S(1)} %copy-done, s32[4]{0:T(128)S(1)} %copy-done.3), custom_call_target="tpu_custom_call" | custom-call | flops 3000000000 | bytes 12000000 | tf_op jit(solution)/shard_map/pallas_call | solution.py:180
  72.4 3.6 %collective-permute-done.14 = f32[24,128]{1,0:T(8,128)S(1)} collective-permute-done((f32[24,128]{1,0:T(8,128)S(1)}, f32[24,128]{1,0:T(8,128)S(1)}, u32[]{:S(2)}, u32[]{:S(2)}) %collective-permute-start.14) | collective-permute-done | bytes 12320 | tf_op jit(solution)/shard_map/ppermute | solution.py:244
  76.0 0.6 add_bitcast_fusion
  (23 shorter events, 0.7 us)
Async XLA Ops:
  1.1 16.9 %collective-permute-start.2 = (bf16[8,128,256]{2,1,0:T(8,128)(2,1)S(1)}, bf16[8,128,256]{2,1,0:T(8,128)(2,1)S(1)}, u32[]{:S(2)}, u32[]{:S(2)}) collective-permute-start(bf16[8,128,256]{2,1,0:T(8,128)(2,1)S(1)} %slice_bitcast_fusion.own_ref), channel_id=1, source_target_pairs={{0,2},{2,0},{1,3},{3,1},{4,6},{6,4},{5,7},{7,5},{8,10},{10,8},{9,1... | collective-permute-start | bytes 1572872 | tf_op jit(solution)/shard_map/ppermute | solution.py:206
  5.1 7.1 %collective-permute-start.1 = (bf16[4,128,256]{2,1,0:T(8,128)(2,1)S(1)}, bf16[4,128,256]{2,1,0:T(8,128)(2,1)S(1)}, u32[]{:S(2)}, u32[]{:S(2)}) collective-permute-start(bf16[4,128,256]{2,1,0:T(8,128)(2,1)S(1)} %slice_bitcast_fusion.1), channel_id=1, source_target_pairs={{4,8},{8,4},{5,9},{9,5},{6,10},{10,6},{7,11},{11,7},{20,24},{24,20... | collective-permute-start | bytes 786440 | tf_op jit(solution)/shard_map/ppermute | solution.py:210
  5.7 10.2 %collective-permute-start = (bf16[4,128,256]{2,1,0:T(8,128)(2,1)S(1)}, bf16[4,128,256]{2,1,0:T(8,128)(2,1)S(1)}, u32[]{:S(2)}, u32[]{:S(2)}) collective-permute-start(bf16[4,128,256]{2,1,0:T(8,128)(2,1)S(1)} %slice_bitcast_fusion.1), channel_id=1, source_target_pairs={{0,4},{4,0},{8,12},{12,8},{1,5},{5,1},{9,13},{13,9},{2,6},{6,2},{1... | collective-permute-start | bytes 786440 | tf_op jit(solution)/shard_map/ppermute | solution.py:209
  10.2 0.9 %copy-start.1 = (f32[256,256]{1,0:T(8,128)S(1)}, f32[256,256]{1,0:T(8,128)}, u32[]{:S(2)}) copy-start(f32[256,256]{1,0:T(8,128)} %left_ref.1) | copy-start | bytes 786436
  11.1 0.9 %copy-start.2 = (f32[256,256]{1,0:T(8,128)S(1)}, f32[256,256]{1,0:T(8,128)}, u32[]{:S(2)}) copy-start(f32[256,256]{1,0:T(8,128)} %right_ref) | copy-start | bytes 786436
  16.0 16.5 %collective-permute-start.7 = (bf16[4,128,256]{2,1,0:T(8,128)(2,1)S(1)}, bf16[4,128,256]{2,1,0:T(8,128)(2,1)S(1)}, u32[]{:S(2)}, u32[]{:S(2)}) collective-permute-start(bf16[4,128,256]{2,1,0:T(8,128)(2,1)S(1)} %collective-permute-done), channel_id=1, source_target_pairs={{4,8},{8,4},{5,9},{9,5},{6,10},{10,6},{7,11},{11,7},{20,24},{24,20... | collective-permute-start | bytes 786440 | tf_op jit(solution)/shard_map/ppermute | solution.py:213
  16.7 23.1 %collective-permute-start.6 = (bf16[4,128,256]{2,1,0:T(8,128)(2,1)S(1)}, bf16[4,128,256]{2,1,0:T(8,128)(2,1)S(1)}, u32[]{:S(2)}, u32[]{:S(2)}) collective-permute-start(bf16[4,128,256]{2,1,0:T(8,128)(2,1)S(1)} %collective-permute-done.1), channel_id=1, source_target_pairs={{4,0},{8,12},{5,1},{9,13},{6,2},{10,14},{7,3},{11,15},{20,16},{24,... | collective-permute-start | bytes 786440 | tf_op jit(solution)/shard_map/ppermute | solution.py:211
  19.3 19.8 %collective-permute-start.3 = (bf16[128,8,256]{2,1,0:T(8,128)(2,1)S(1)}, bf16[128,8,256]{2,1,0:T(8,128)(2,1)S(1)}, u32[]{:S(2)}, u32[]{:S(2)}) collective-permute-start(bf16[128,8,256]{2,1,0:T(8,128)(2,1)S(1)} %shard_map.56.own_ref), channel_id=1, source_target_pairs={{0,4},{4,0},{8,12},{12,8},{1,5},{5,1},{9,13},{13,9},{2,6},{6,2},{1... | collective-permute-start | bytes 1572872 | tf_op jit(solution)/shard_map/ppermute | solution.py:216
  22.8 17.1 %collective-permute-start.4 = (bf16[128,8,256]{2,1,0:T(8,128)(2,1)S(1)}, bf16[128,8,256]{2,1,0:T(8,128)(2,1)S(1)}, u32[]{:S(2)}, u32[]{:S(2)}) collective-permute-start(bf16[128,8,256]{2,1,0:T(8,128)(2,1)S(1)} %shard_map.56.own_ref), channel_id=1, source_target_pairs={{4,8},{8,4},{5,9},{9,5},{6,10},{10,6},{7,11},{11,7},{20,24},{24,20... | collective-permute-start | bytes 1572872 | tf_op jit(solution)/shard_map/ppermute | solution.py:217
  23.4 21.3 %collective-permute-start.5 = (bf16[8,128,256]{2,1,0:T(8,128)(2,1)S(1)}, bf16[8,128,256]{2,1,0:T(8,128)(2,1)S(1)}, u32[]{:S(2)}, u32[]{:S(2)}) collective-permute-start(bf16[8,128,256]{2,1,0:T(8,128)(2,1)S(1)} %pad_maximum_fusion.own_ref), channel_id=1, source_target_pairs={{0,2},{2,0},{1,3},{3,1},{4,6},{6,4},{5,7},{7,5},{8,10},{10,8},{9,1... | collective-permute-start | bytes 1572872 | tf_op jit(solution)/shard_map/ppermute | solution.py:219
  32.5 25.6 %copy-start = (bf16[128,128,256]{2,1,0:T(8,128)(2,1)S(1)}, bf16[128,128,256]{2,1,0:T(8,128)(2,1)}, u32[]{:S(2)}) copy-start(bf16[128,128,256]{2,1,0:T(8,128)(2,1)} %shard_map.58.grad_ref) | copy-start | bytes 25165828
  32.5 25.6 %copy-start.3 = (s32[4]{0:T(128)S(1)}, s32[4]{0:T(128)}, u32[]{:S(2)}) copy-start(s32[4]{0:T(128)} %order_ref.5) | copy-start | bytes 52
  32.5 12.2 %collective-permute-start.8 = (bf16[4,128,256]{2,1,0:T(8,128)(2,1)S(1)}, bf16[4,128,256]{2,1,0:T(8,128)(2,1)S(1)}, u32[]{:S(2)}, u32[]{:S(2)}) collective-permute-start(bf16[4,128,256]{2,1,0:T(8,128)(2,1)S(1)} %collective-permute-done.7), channel_id=1, source_target_pairs={{4,0},{8,12},{5,1},{9,13},{6,2},{10,14},{7,3},{11,15},{20,16},{24,... | collective-permute-start | bytes 786440 | tf_op jit(solution)/shard_map/ppermute | solution.py:220
  39.1 7.9 %collective-permute-start.9 = (bf16[128,8,256]{2,1,0:T(8,128)(2,1)S(1)}, bf16[128,8,256]{2,1,0:T(8,128)(2,1)S(1)}, u32[]{:S(2)}, u32[]{:S(2)}) collective-permute-start(bf16[128,8,256]{2,1,0:T(8,128)(2,1)S(1)} %collective-permute-done.3.near), channel_id=1, source_target_pairs={{4,8},{8,4},{5,9},{9,5},{6,10},{10,6},{7,11},{11,7},{20,24},{24,20... | collective-permute-start | bytes 1572872 | tf_op jit(solution)/shard_map/ppermute | solution.py:221
  39.9 16.8 %collective-permute-start.11 = (bf16[128,8,256]{2,1,0:T(8,128)(2,1)S(1)}, bf16[128,8,256]{2,1,0:T(8,128)(2,1)S(1)}, u32[]{:S(2)}, u32[]{:S(2)}) collective-permute-start(bf16[128,8,256]{2,1,0:T(8,128)(2,1)S(1)} %collective-permute-done.4), channel_id=1, source_target_pairs={{4,0},{8,12},{5,1},{9,13},{6,2},{10,14},{7,3},{11,15},{20,16},{24,... | collective-permute-start | bytes 1572872 | tf_op jit(solution)/shard_map/ppermute | solution.py:222
  46.1 10.7 %collective-permute-start.10 = (bf16[8,128,256]{2,1,0:T(8,128)(2,1)S(1)}, bf16[8,128,256]{2,1,0:T(8,128)(2,1)S(1)}, u32[]{:S(2)}, u32[]{:S(2)}) collective-permute-start(bf16[8,128,256]{2,1,0:T(8,128)(2,1)S(1)} %pad_maximum_fusion.1.own_ref), channel_id=1, source_target_pairs={{0,2},{2,0},{1,3},{3,1},{4,6},{6,4},{5,7},{7,5},{8,10},{10,8},{9,1... | collective-permute-start | bytes 1572872 | tf_op jit(solution)/shard_map/ppermute | solution.py:225
  47.0 16.3 %collective-permute-start.12 = (bf16[64,8,256]{2,1,0:T(8,128)(2,1)S(1)}, bf16[64,8,256]{2,1,0:T(8,128)(2,1)S(1)}, u32[]{:S(2)}, u32[]{:S(2)}) collective-permute-start(bf16[64,8,256]{2,1,0:T(8,128)(2,1)S(1)} %get-tuple-element.46), channel_id=1, source_target_pairs={{4,0},{8,12},{5,1},{9,13},{6,2},{10,14},{7,3},{11,15},{20,16},{24,... | collective-permute-start | bytes 786440 | tf_op jit(solution)/shard_map/ppermute | solution.py:227
  62.1 8.3 %collective-permute-start.13 = (bf16[64,8,256]{2,1,0:T(8,128)(2,1)S(1)}, bf16[64,8,256]{2,1,0:T(8,128)(2,1)S(1)}, u32[]{:S(2)}, u32[]{:S(2)}) collective-permute-start(bf16[64,8,256]{2,1,0:T(8,128)(2,1)S(1)} %get-tuple-element.45), channel_id=1, source_target_pairs={{4,0},{8,12},{5,1},{9,13},{6,2},{10,14},{7,3},{11,15},{20,16},{24,... | collective-permute-start | bytes 786440 | tf_op jit(solution)/shard_map/ppermute | solution.py:228
  72.2 3.8 %collective-permute-start.14 = (f32[24,128]{1,0:T(8,128)S(1)}, f32[24,128]{1,0:T(8,128)S(1)}, u32[]{:S(2)}, u32[]{:S(2)}) collective-permute-start(f32[24,128]{1,0:T(8,128)S(1)} %get-tuple-element.44), channel_id=1, source_target_pairs={{0,2},{2,0},{1,3},{3,1},{4,6},{6,4},{5,7},{7,5},{8,10},{10,8},{9,1... | collective-permute-start | bytes 36872 | tf_op jit(solution)/shard_map/ppermute | solution.py:244

commit v7 on v6

--- a/solution.py
+++ b/solution.py
@@ -184,7 +184,7 @@
         out_specs=jax.tree.map(lambda _: VMEM, out_shape),
         scratch_shapes=scratch,
         compiler_params=pltpu.CompilerParams(vmem_limit_bytes=40 << 20),
-        cost_estimate=pl.CostEstimate(flops=3_000_000_000, bytes_accessed=12_000_000, transcendentals=0),
+        cost_estimate=pl.CostEstimate(flops=1000, bytes_accessed=1000, transcendentals=0),
     )(*arrays, order)
 
 

time: 76.9 us -> 71.9 us (0.935)
  waiting for transfers between devices: 29.4 us -> 23.9 us
    ppermute x1, waiting for transfers between devices: 5.11 us -> 1.16 us  [per_device_line(): far_out_1 = lax.ppermute(far_mid[part:], 'ex', OUTWARD)]
    ppermute x1, waiting for transfers between devices: 8.32 us -> 7.02 us  [per_device_line(): mid_out = lax.ppermute(after(mid, near, grads), 'ex', OUTWARD)]
  transfers between devices with their start and end apart: 15 -> 15, of which waited for: 6 -> 7; matrix products, arithmetic and copies ran while one was open for 2% -> 2% of each run, Pallas kernels for 24% -> 25%
where the time goes in v7:
time: 71.9 us; the launch traced here: 71.5 us
  waiting for transfers between devices  23.9 us (33%)
  starting transfers between devices  22.5 us (31%)
  Pallas kernels  19.9 us (28%)
  local copies, waits for them, and re-layouts  3.99 us (6%)
  other arithmetic  0.98 us (1%)
    pallas_call x1, Pallas kernels, regroup(): pl.pallas_call(regroup_kernel, out_shape=jax.ShapeDtypeStruct((rows, n, w...  8.4 us
    pallas_call x3, Pallas kernels, score_call(): pl.pallas_call(functools.partial(kernel, ex), out_shape=out_shape, in_spe...  7.68 us
    ppermute x1, waiting for transfers between devices, per_device_line(): mid_out = lax.ppermute(after(mid, near, grads), 'ex', OUTWARD)  7.02 us
    ppermute x1, waiting for transfers between devices, per_device_line(): near = lax.ppermute(late, 'ex', PAIRS)  5.08 us
    ppermute x1, starting transfers between devices, per_device_line(): raw_near = lax.ppermute(raw, 'ex', PAIRS)  4.45 us
    ppermute x1, waiting for transfers between devices, per_device_line(): raw_near = lax.ppermute(raw, 'ex', PAIRS)  3.75 us
    pallas_call x3, Pallas kernels, condition(): pl.pallas_call(condition_kernel, out_shape=jax.ShapeDtypeStruct((rows, co...  3.73 us
    ppermute x1, waiting for transfers between devices, per_device_line(): raw_far_out = lax.ppermute(after(raw_far_mid, grads), 'ex', OUTWARD)  3.53 us
  transfers between devices with their start and end apart: 15, of which 7 were waited for; matrix products, arithmetic and copies ran while one was open for 2% of the time, Pallas kernels for 25%

profile of v7, /device:TPU:0, one launch (start us, length us, event | category | flops | bytes accessed | tf_op | source)
XLA Modules:
  0.0 71.5 jit_solution(1865575831605323962)
XLA Ops:
  0.0 1.1 %slice_bitcast_fusion.own_ref = bf16[8,128,256]{2,1,0:T(8,128)(2,1)S(1)} fusion(bf16[1,12,128,256]{3,2,1,0:T(8,128)(2,1)} %param.6), kind=kLoop, calls=%fused_computation.2 | loop fusion | bytes 1048576 | tf_op jit(solution)/shard_map/squeeze | solution.py:205
  1.1 3.0 %collective-permute-start.2 = (bf16[8,128,256]{2,1,0:T(8,128)(2,1)S(1)}, bf16[8,128,256]{2,1,0:T(8,128)(2,1)S(1)}, u32[]{:S(2)}, u32[]{:S(2)}) collective-permute-start(bf16[8,128,256]{2,1,0:T(8,128)(2,1)S(1)} %slice_bitcast_fusion.own_ref), channel_id=1, source_target_pairs={{0,2},{2,0},{1,3},{3,1},{4,6},{6,4},{5,7},{7,5},{8,10},{10,8},{9,1... | collective-permute-start | bytes 1572872 | tf_op jit(solution)/shard_map/ppermute | solution.py:206
  4.1 1.0 %slice_bitcast_fusion.1 = bf16[4,128,256]{2,1,0:T(8,128)(2,1)S(1)} fusion(bf16[1,12,128,256]{3,2,1,0:T(8,128)(2,1)} %param.6), kind=kLoop, calls=%fused_computation.3 | loop fusion | bytes 524288 | tf_op jit(solution)/shard_map/squeeze | solution.py:207
  5.1 0.7 collective-permute-start.1
  5.7 4.4 %collective-permute-start = (bf16[4,128,256]{2,1,0:T(8,128)(2,1)S(1)}, bf16[4,128,256]{2,1,0:T(8,128)(2,1)S(1)}, u32[]{:S(2)}, u32[]{:S(2)}) collective-permute-start(bf16[4,128,256]{2,1,0:T(8,128)(2,1)S(1)} %slice_bitcast_fusion.1), channel_id=1, source_target_pairs={{0,4},{4,0},{8,12},{12,8},{1,5},{5,1},{9,13},{13,9},{2,6},{6,2},{1... | collective-permute-start | bytes 786440 | tf_op jit(solution)/shard_map/ppermute | solution.py:209
  10.2 0.9 %copy-done.1 = f32[256,256]{1,0:T(8,128)S(1)} copy-done((f32[256,256]{1,0:T(8,128)S(1)}, f32[256,256]{1,0:T(8,128)}, u32[]{:S(2)}) %copy-start.1) | copy-done | bytes 262168
  11.1 0.9 %copy-done.2 = f32[256,256]{1,0:T(8,128)S(1)} copy-done((f32[256,256]{1,0:T(8,128)S(1)}, f32[256,256]{1,0:T(8,128)}, u32[]{:S(2)}) %copy-start.2) | copy-done | bytes 262168
  12.2 3.8 %collective-permute-done = bf16[4,128,256]{2,1,0:T(8,128)(2,1)S(1)} collective-permute-done((bf16[4,128,256]{2,1,0:T(8,128)(2,1)S(1)}, bf16[4,128,256]{2,1,0:T(8,128)(2,1)S(1)}, u32[]{:S(2)}, u32[]{:S(2)}) %collective-permute-start) | collective-permute-done | bytes 262176 | tf_op jit(solution)/shard_map/ppermute | solution.py:209
  16.0 0.7 collective-permute-start.7
  16.7 1.3 %collective-permute-start.6 = (bf16[4,128,256]{2,1,0:T(8,128)(2,1)S(1)}, bf16[4,128,256]{2,1,0:T(8,128)(2,1)S(1)}, u32[]{:S(2)}, u32[]{:S(2)}) collective-permute-start(bf16[4,128,256]{2,1,0:T(8,128)(2,1)S(1)} %collective-permute-done.1), channel_id=1, source_target_pairs={{4,0},{8,12},{5,1},{9,13},{6,2},{10,14},{7,3},{11,15},{20,16},{24,... | collective-permute-start | bytes 786440 | tf_op jit(solution)/shard_map/ppermute | solution.py:211
  18.0 1.2 %shard_map.56.own_ref = bf16[128,8,256]{2,1,0:T(8,128)(2,1)S(1)} custom-call(bf16[8,128,256]{2,1,0:T(8,128)(2,1)S(1)} %slice_bitcast_fusion.own_ref, bf16[8,128,256]{2,1,0:T(8,128)(2,1)S(1)} %collective-permute-done.2.far_ref, bf16[384,256]{1,0:T(8,128)(2,1)S(1)} %get-tuple-element.29.left_ref, bf16[512,256]{1,0:T(8,128)(2,1)S(1)} %get-tuple-element.30.right_ref), custom_call_target="tpu_custom_call" | custom-call | flops 960000000 | bytes 2097152 | tf_op jit(solution)/shard_map/pallas_call | solution.py:70
  19.2 3.5 %collective-permute-start.3 = (bf16[128,8,256]{2,1,0:T(8,128)(2,1)S(1)}, bf16[128,8,256]{2,1,0:T(8,128)(2,1)S(1)}, u32[]{:S(2)}, u32[]{:S(2)}) collective-permute-start(bf16[128,8,256]{2,1,0:T(8,128)(2,1)S(1)} %shard_map.56.own_ref), channel_id=1, source_target_pairs={{0,4},{4,0},{8,12},{12,8},{1,5},{5,1},{9,13},{13,9},{2,6},{6,2},{1... | collective-permute-start | bytes 1572872 | tf_op jit(solution)/shard_map/ppermute | solution.py:216
  22.7 0.7 collective-permute-start.4
  24.0 8.4 %shard_map.58.grad_ref = bf16[128,128,256]{2,1,0:T(8,128)(2,1)} custom-call(bf16[128,128,256]{2,1,0:T(8,128)(2,1)} %grads_ref), custom_call_target="tpu_custom_call" | custom-call | flops 6000000000 | bytes 16000000 | tf_op jit(solution)/shard_map/pallas_call | solution.py:106
  32.5 1.6 %collective-permute-start.8 = (bf16[4,128,256]{2,1,0:T(8,128)(2,1)S(1)}, bf16[4,128,256]{2,1,0:T(8,128)(2,1)S(1)}, u32[]{:S(2)}, u32[]{:S(2)}) collective-permute-start(bf16[4,128,256]{2,1,0:T(8,128)(2,1)S(1)} %collective-permute-done.7), channel_id=1, source_target_pairs={{4,0},{8,12},{5,1},{9,13},{6,2},{10,14},{7,3},{11,15},{20,16},{24,... | collective-permute-start | bytes 786440 | tf_op jit(solution)/shard_map/ppermute | solution.py:220
  34.0 5.1 %collective-permute-done.3.near = bf16[128,8,256]{2,1,0:T(8,128)(2,1)S(1)} collective-permute-done((bf16[128,8,256]{2,1,0:T(8,128)(2,1)S(1)}, bf16[128,8,256]{2,1,0:T(8,128)(2,1)S(1)}, u32[]{:S(2)}, u32[]{:S(2)}) %collective-permute-start.3) | collective-permute-done | bytes 524320 | tf_op jit(solution)/shard_map/ppermute | solution.py:216
  39.1 0.7 collective-permute-start.9
  39.9 1.3 %collective-permute-start.11 = (bf16[128,8,256]{2,1,0:T(8,128)(2,1)S(1)}, bf16[128,8,256]{2,1,0:T(8,128)(2,1)S(1)}, u32[]{:S(2)}, u32[]{:S(2)}) collective-permute-start(bf16[128,8,256]{2,1,0:T(8,128)(2,1)S(1)} %collective-permute-done.4), channel_id=1, source_target_pairs={{4,0},{8,12},{5,1},{9,13},{6,2},{10,14},{7,3},{11,15},{20,16},{24,... | collective-permute-start | bytes 1572872 | tf_op jit(solution)/shard_map/ppermute | solution.py:222
  41.2 3.5 %collective-permute-done.8 = bf16[4,128,256]{2,1,0:T(8,128)(2,1)S(1)} collective-permute-done((bf16[4,128,256]{2,1,0:T(8,128)(2,1)S(1)}, bf16[4,128,256]{2,1,0:T(8,128)(2,1)S(1)}, u32[]{:S(2)}, u32[]{:S(2)}) %collective-permute-start.8) | collective-permute-done | bytes 262176 | tf_op jit(solution)/shard_map/ppermute | solution.py:220
  44.8 1.2 %shard_map.57.early_0 = bf16[128,8,256]{2,1,0:T(8,128)(2,1)S(1)} custom-call(bf16[8,128,256]{2,1,0:T(8,128)(2,1)S(1)} %pad_maximum_fusion.own_ref, bf16[8,128,256]{2,1,0:T(8,128)(2,1)S(1)} %collective-permute-done.5.far_ref, bf16[384,256]{1,0:T(8,128)(2,1)S(1)} %get-tuple-element.29.left_ref, bf16[512,256]{1,0:T(8,128)(2,1)S(1)} %get-tuple-element.30.right_ref), custom_call_target="tpu_custom_call" | custom-call | flops 960000000 | bytes 2097152 | tf_op jit(solution)/shard_map/pallas_call | solution.py:70
  46.1 0.9 %collective-permute-start.10 = (bf16[8,128,256]{2,1,0:T(8,128)(2,1)S(1)}, bf16[8,128,256]{2,1,0:T(8,128)(2,1)S(1)}, u32[]{:S(2)}, u32[]{:S(2)}) collective-permute-start(bf16[8,128,256]{2,1,0:T(8,128)(2,1)S(1)} %pad_maximum_fusion.1.own_ref), channel_id=1, source_target_pairs={{0,2},{2,0},{1,3},{3,1},{4,6},{6,4},{5,7},{7,5},{8,10},{10,8},{9,1... | collective-permute-start | bytes 1572872 | tf_op jit(solution)/shard_map/ppermute | solution.py:225
  47.0 1.3 %collective-permute-start.12 = (bf16[64,8,256]{2,1,0:T(8,128)(2,1)S(1)}, bf16[64,8,256]{2,1,0:T(8,128)(2,1)S(1)}, u32[]{:S(2)}, u32[]{:S(2)}) collective-permute-start(bf16[64,8,256]{2,1,0:T(8,128)(2,1)S(1)} %get-tuple-element.46), channel_id=1, source_target_pairs={{4,0},{8,12},{5,1},{9,13},{6,2},{10,14},{7,3},{11,15},{20,16},{24,... | collective-permute-start | bytes 786440 | tf_op jit(solution)/shard_map/ppermute | solution.py:227
  48.3 1.3 %collective-permute-start.13 = (bf16[64,8,256]{2,1,0:T(8,128)(2,1)S(1)}, bf16[64,8,256]{2,1,0:T(8,128)(2,1)S(1)}, u32[]{:S(2)}, u32[]{:S(2)}) collective-permute-start(bf16[64,8,256]{2,1,0:T(8,128)(2,1)S(1)} %get-tuple-element.45), channel_id=1, source_target_pairs={{4,0},{8,12},{5,1},{9,13},{6,2},{10,14},{7,3},{11,15},{20,16},{24,... | collective-permute-start | bytes 786440 | tf_op jit(solution)/shard_map/ppermute | solution.py:228
  49.6 7.0 %collective-permute-done.11 = bf16[128,8,256]{2,1,0:T(8,128)(2,1)S(1)} collective-permute-done((bf16[128,8,256]{2,1,0:T(8,128)(2,1)S(1)}, bf16[128,8,256]{2,1,0:T(8,128)(2,1)S(1)}, u32[]{:S(2)}, u32[]{:S(2)}) %collective-permute-start.11) | collective-permute-done | bytes 524320 | tf_op jit(solution)/shard_map/ppermute | solution.py:222
  56.8 1.2 %shard_map.59.early_1 = bf16[128,8,256]{2,1,0:T(8,128)(2,1)S(1)} custom-call(bf16[8,128,256]{2,1,0:T(8,128)(2,1)S(1)} %pad_maximum_fusion.1.own_ref, bf16[8,128,256]{2,1,0:T(8,128)(2,1)S(1)} %collective-permute-done.10.far_ref, bf16[384,256]{1,0:T(8,128)(2,1)S(1)} %get-tuple-element.29.left_ref, bf16[512,256]{1,0:T(8,128)(2,1)S(1)} %get-tuple-element.30.right_ref), custom_call_target="tpu_custom_call" | custom-call | flops 960000000 | bytes 2097152 | tf_op jit(solution)/shard_map/pallas_call | solution.py:70
  58.1 4.0 %shard_map.60.base_ref = f32[48,128]{1,0:T(8,128)S(1)} custom-call(bf16[128,8,256]{2,1,0:T(8,128)(2,1)S(1)} %shard_map.57.early_0, bf16[128,8,256]{2,1,0:T(8,128)(2,1)S(1)} %shard_map.59.early_1, bf16[128,8,256]{2,1,0:T(8,128)(2,1)S(1)} %shard_map.56.own_ref, bf16[128,8,256]{2,1,0:T(8,128)(2,1)S(1)} %collective-permute-done.3.near, ...), custom_call_target="tpu_custom_call" | custom-call | flops 1000 | bytes 1000 | tf_op jit(solution)/shard_map/pallas_call | solution.py:180
  62.3 1.8 %shard_map.61.far_ref = f32[8,128]{1,0:T(8,128)S(1)} custom-call(bf16[64,8,256]{2,1,0:T(8,128)(2,1)S(1)} %collective-permute-done.12.far_out, bf16[128,128,256]{2,1,0:T(8,128)(2,1)S(1)} %copy-done, s32[4]{0:T(128)S(1)} %copy-done.3), custom_call_target="tpu_custom_call" | custom-call | flops 1000 | bytes 1000 | tf_op jit(solution)/shard_map/pallas_call | solution.py:180
  64.1 1.2 %collective-permute-done.13.far_out = bf16[64,8,256]{2,1,0:T(8,128)(2,1)S(1)} collective-permute-done((bf16[64,8,256]{2,1,0:T(8,128)(2,1)S(1)}, bf16[64,8,256]{2,1,0:T(8,128)(2,1)S(1)}, u32[]{:S(2)}, u32[]{:S(2)}) %collective-permute-start.13) | collective-permute-done | bytes 262176 | tf_op jit(solution)/shard_map/ppermute | solution.py:228
  65.3 1.9 %shard_map.62 = (f32[24,128]{1,0:T(8,128)S(1)}, f32[24,128]{1,0:T(8,128)S(1)}) custom-call(f32[48,128]{1,0:T(8,128)S(1)} %shard_map.60.base_ref, f32[8,128]{1,0:T(8,128)S(1)} %shard_map.61.far_ref, bf16[64,8,256]{2,1,0:T(8,128)(2,1)S(1)} %collective-permute-done.13.far_out, bf16[128,128,256]{2,1,0:T(8,128)(2,1)S(1)} %copy-done, s32[4]{0:T(128)S(1)} %copy-done.3), custom_call_target="tpu_custom_call" | custom-call | flops 1000 | bytes 1000 | tf_op jit(solution)/shard_map/pallas_call | solution.py:180
  67.2 0.6 collective-permute-start.14
  67.8 3.2 %collective-permute-done.14 = f32[24,128]{1,0:T(8,128)S(1)} collective-permute-done((f32[24,128]{1,0:T(8,128)S(1)}, f32[24,128]{1,0:T(8,128)S(1)}, u32[]{:S(2)}, u32[]{:S(2)}) %collective-permute-start.14) | collective-permute-done | bytes 12320 | tf_op jit(solution)/shard_map/ppermute | solution.py:244
  70.9 0.6 add_bitcast_fusion
  (23 shorter events, 1.3 us)
Async XLA Ops:
  1.1 16.9 %collective-permute-start.2 = (bf16[8,128,256]{2,1,0:T(8,128)(2,1)S(1)}, bf16[8,128,256]{2,1,0:T(8,128)(2,1)S(1)}, u32[]{:S(2)}, u32[]{:S(2)}) collective-permute-start(bf16[8,128,256]{2,1,0:T(8,128)(2,1)S(1)} %slice_bitcast_fusion.own_ref), channel_id=1, source_target_pairs={{0,2},{2,0},{1,3},{3,1},{4,6},{6,4},{5,7},{7,5},{8,10},{10,8},{9,1... | collective-permute-start | bytes 1572872 | tf_op jit(solution)/shard_map/ppermute | solution.py:206
  5.1 7.1 %collective-permute-start.1 = (bf16[4,128,256]{2,1,0:T(8,128)(2,1)S(1)}, bf16[4,128,256]{2,1,0:T(8,128)(2,1)S(1)}, u32[]{:S(2)}, u32[]{:S(2)}) collective-permute-start(bf16[4,128,256]{2,1,0:T(8,128)(2,1)S(1)} %slice_bitcast_fusion.1), channel_id=1, source_target_pairs={{4,8},{8,4},{5,9},{9,5},{6,10},{10,6},{7,11},{11,7},{20,24},{24,20... | collective-permute-start | bytes 786440 | tf_op jit(solution)/shard_map/ppermute | solution.py:210
  5.7 10.2 %collective-permute-start = (bf16[4,128,256]{2,1,0:T(8,128)(2,1)S(1)}, bf16[4,128,256]{2,1,0:T(8,128)(2,1)S(1)}, u32[]{:S(2)}, u32[]{:S(2)}) collective-permute-start(bf16[4,128,256]{2,1,0:T(8,128)(2,1)S(1)} %slice_bitcast_fusion.1), channel_id=1, source_target_pairs={{0,4},{4,0},{8,12},{12,8},{1,5},{5,1},{9,13},{13,9},{2,6},{6,2},{1... | collective-permute-start | bytes 786440 | tf_op jit(solution)/shard_map/ppermute | solution.py:209
  10.2 0.9 %copy-start.1 = (f32[256,256]{1,0:T(8,128)S(1)}, f32[256,256]{1,0:T(8,128)}, u32[]{:S(2)}) copy-start(f32[256,256]{1,0:T(8,128)} %left_ref.1) | copy-start | bytes 786436
  11.1 0.9 %copy-start.2 = (f32[256,256]{1,0:T(8,128)S(1)}, f32[256,256]{1,0:T(8,128)}, u32[]{:S(2)}) copy-start(f32[256,256]{1,0:T(8,128)} %right_ref) | copy-start | bytes 786436
  16.0 16.5 %collective-permute-start.7 = (bf16[4,128,256]{2,1,0:T(8,128)(2,1)S(1)}, bf16[4,128,256]{2,1,0:T(8,128)(2,1)S(1)}, u32[]{:S(2)}, u32[]{:S(2)}) collective-permute-start(bf16[4,128,256]{2,1,0:T(8,128)(2,1)S(1)} %collective-permute-done), channel_id=1, source_target_pairs={{4,8},{8,4},{5,9},{9,5},{6,10},{10,6},{7,11},{11,7},{20,24},{24,20... | collective-permute-start | bytes 786440 | tf_op jit(solution)/shard_map/ppermute | solution.py:213
  16.7 23.1 %collective-permute-start.6 = (bf16[4,128,256]{2,1,0:T(8,128)(2,1)S(1)}, bf16[4,128,256]{2,1,0:T(8,128)(2,1)S(1)}, u32[]{:S(2)}, u32[]{:S(2)}) collective-permute-start(bf16[4,128,256]{2,1,0:T(8,128)(2,1)S(1)} %collective-permute-done.1), channel_id=1, source_target_pairs={{4,0},{8,12},{5,1},{9,13},{6,2},{10,14},{7,3},{11,15},{20,16},{24,... | collective-permute-start | bytes 786440 | tf_op jit(solution)/shard_map/ppermute | solution.py:211
  19.2 19.9 %collective-permute-start.3 = (bf16[128,8,256]{2,1,0:T(8,128)(2,1)S(1)}, bf16[128,8,256]{2,1,0:T(8,128)(2,1)S(1)}, u32[]{:S(2)}, u32[]{:S(2)}) collective-permute-start(bf16[128,8,256]{2,1,0:T(8,128)(2,1)S(1)} %shard_map.56.own_ref), channel_id=1, source_target_pairs={{0,4},{4,0},{8,12},{12,8},{1,5},{5,1},{9,13},{13,9},{2,6},{6,2},{1... | collective-permute-start | bytes 1572872 | tf_op jit(solution)/shard_map/ppermute | solution.py:216
  22.7 17.1 %collective-permute-start.4 = (bf16[128,8,256]{2,1,0:T(8,128)(2,1)S(1)}, bf16[128,8,256]{2,1,0:T(8,128)(2,1)S(1)}, u32[]{:S(2)}, u32[]{:S(2)}) collective-permute-start(bf16[128,8,256]{2,1,0:T(8,128)(2,1)S(1)} %shard_map.56.own_ref), channel_id=1, source_target_pairs={{4,8},{8,4},{5,9},{9,5},{6,10},{10,6},{7,11},{11,7},{20,24},{24,20... | collective-permute-start | bytes 1572872 | tf_op jit(solution)/shard_map/ppermute | solution.py:217
  23.4 21.4 %collective-permute-start.5 = (bf16[8,128,256]{2,1,0:T(8,128)(2,1)S(1)}, bf16[8,128,256]{2,1,0:T(8,128)(2,1)S(1)}, u32[]{:S(2)}, u32[]{:S(2)}) collective-permute-start(bf16[8,128,256]{2,1,0:T(8,128)(2,1)S(1)} %pad_maximum_fusion.own_ref), channel_id=1, source_target_pairs={{0,2},{2,0},{1,3},{3,1},{4,6},{6,4},{5,7},{7,5},{8,10},{10,8},{9,1... | collective-permute-start | bytes 1572872 | tf_op jit(solution)/shard_map/ppermute | solution.py:219
  32.4 25.6 %copy-start = (bf16[128,128,256]{2,1,0:T(8,128)(2,1)S(1)}, bf16[128,128,256]{2,1,0:T(8,128)(2,1)}, u32[]{:S(2)}) copy-start(bf16[128,128,256]{2,1,0:T(8,128)(2,1)} %shard_map.58.grad_ref) | copy-start | bytes 25165828
  32.4 25.6 %copy-start.3 = (s32[4]{0:T(128)S(1)}, s32[4]{0:T(128)}, u32[]{:S(2)}) copy-start(s32[4]{0:T(128)} %order_ref.5) | copy-start | bytes 52
  32.5 12.3 %collective-permute-start.8 = (bf16[4,128,256]{2,1,0:T(8,128)(2,1)S(1)}, bf16[4,128,256]{2,1,0:T(8,128)(2,1)S(1)}, u32[]{:S(2)}, u32[]{:S(2)}) collective-permute-start(bf16[4,128,256]{2,1,0:T(8,128)(2,1)S(1)} %collective-permute-done.7), channel_id=1, source_target_pairs={{4,0},{8,12},{5,1},{9,13},{6,2},{10,14},{7,3},{11,15},{20,16},{24,... | collective-permute-start | bytes 786440 | tf_op jit(solution)/shard_map/ppermute | solution.py:220
  39.1 7.9 %collective-permute-start.9 = (bf16[128,8,256]{2,1,0:T(8,128)(2,1)S(1)}, bf16[128,8,256]{2,1,0:T(8,128)(2,1)S(1)}, u32[]{:S(2)}, u32[]{:S(2)}) collective-permute-start(bf16[128,8,256]{2,1,0:T(8,128)(2,1)S(1)} %collective-permute-done.3.near), channel_id=1, source_target_pairs={{4,8},{8,4},{5,9},{9,5},{6,10},{10,6},{7,11},{11,7},{20,24},{24,20... | collective-permute-start | bytes 1572872 | tf_op jit(solution)/shard_map/ppermute | solution.py:221
  39.9 16.8 %collective-permute-start.11 = (bf16[128,8,256]{2,1,0:T(8,128)(2,1)S(1)}, bf16[128,8,256]{2,1,0:T(8,128)(2,1)S(1)}, u32[]{:S(2)}, u32[]{:S(2)}) collective-permute-start(bf16[128,8,256]{2,1,0:T(8,128)(2,1)S(1)} %collective-permute-done.4), channel_id=1, source_target_pairs={{4,0},{8,12},{5,1},{9,13},{6,2},{10,14},{7,3},{11,15},{20,16},{24,... | collective-permute-start | bytes 1572872 | tf_op jit(solution)/shard_map/ppermute | solution.py:222
  46.1 10.7 %collective-permute-start.10 = (bf16[8,128,256]{2,1,0:T(8,128)(2,1)S(1)}, bf16[8,128,256]{2,1,0:T(8,128)(2,1)S(1)}, u32[]{:S(2)}, u32[]{:S(2)}) collective-permute-start(bf16[8,128,256]{2,1,0:T(8,128)(2,1)S(1)} %pad_maximum_fusion.1.own_ref), channel_id=1, source_target_pairs={{0,2},{2,0},{1,3},{3,1},{4,6},{6,4},{5,7},{7,5},{8,10},{10,8},{9,1... | collective-permute-start | bytes 1572872 | tf_op jit(solution)/shard_map/ppermute | solution.py:225
  47.0 15.2 %collective-permute-start.12 = (bf16[64,8,256]{2,1,0:T(8,128)(2,1)S(1)}, bf16[64,8,256]{2,1,0:T(8,128)(2,1)S(1)}, u32[]{:S(2)}, u32[]{:S(2)}) collective-permute-start(bf16[64,8,256]{2,1,0:T(8,128)(2,1)S(1)} %get-tuple-element.46), channel_id=1, source_target_pairs={{4,0},{8,12},{5,1},{9,13},{6,2},{10,14},{7,3},{11,15},{20,16},{24,... | collective-permute-start | bytes 786440 | tf_op jit(solution)/shard_map/ppermute | solution.py:227
  48.3 16.9 %collective-permute-start.13 = (bf16[64,8,256]{2,1,0:T(8,128)(2,1)S(1)}, bf16[64,8,256]{2,1,0:T(8,128)(2,1)S(1)}, u32[]{:S(2)}, u32[]{:S(2)}) collective-permute-start(bf16[64,8,256]{2,1,0:T(8,128)(2,1)S(1)} %get-tuple-element.45), channel_id=1, source_target_pairs={{4,0},{8,12},{5,1},{9,13},{6,2},{10,14},{7,3},{11,15},{20,16},{24,... | collective-permute-start | bytes 786440 | tf_op jit(solution)/shard_map/ppermute | solution.py:228
  67.2 3.8 %collective-permute-start.14 = (f32[24,128]{1,0:T(8,128)S(1)}, f32[24,128]{1,0:T(8,128)S(1)}, u32[]{:S(2)}, u32[]{:S(2)}) collective-permute-start(f32[24,128]{1,0:T(8,128)S(1)} %get-tuple-element.44), channel_id=1, source_target_pairs={{0,2},{2,0},{1,3},{3,1},{4,6},{6,4},{5,7},{7,5},{8,10},{10,8},{9,1... | collective-permute-start | bytes 36872 | tf_op jit(solution)/shard_map/ppermute | solution.py:244

commit v8 on v7

--- a/solution.py
+++ b/solution.py
@@ -10,6 +10,7 @@
 F32 = jnp.float32
 BF16 = jnp.bfloat16
 EARLY = 4
+SHARED = 16
 TILE = 16
 EXAMPLES = 32
 DEEP = 32
@@ -114,11 +115,14 @@
     )(grads)
 
 
-def inner_products(query_refs, grad_ref, first=0):
+def inner_products(query_refs, grad_ref, first=0, rows=None):
     total = sum(ref.shape[1] for ref in query_refs)
 
+    rows = rows or query_refs[0].shape[0]
+    deep = next(d for d in range(DEEP, 0, -1) if rows % d == 0)
+
     def body(i, acc):
-        at = [i * DEEP + j for j in range(DEEP)]
+        at = [i * deep + j for j in range(deep)]
         queries = [jnp.concatenate([ref[r] for ref in query_refs], axis=0) for r in at]
         return acc + lax.dot_general(
             jnp.concatenate(queries, axis=1),
@@ -128,7 +132,7 @@
         )
 
     start = jnp.zeros((total, grad_ref.shape[1]), F32)
-    return lax.fori_loop(0, query_refs[0].shape[0] // DEEP, body, start)
+    return lax.fori_loop(0, rows // deep, body, start)
 
 
 def first_pass_kernel(ex, early_0, early_1, own_ref, near, mid, far_in, grad_ref, order_ref, out_ref):
@@ -158,18 +162,41 @@
     return [me, near, jnp.where(low_pair, 2, 1), jnp.where(low_pair, 3, 0)]
 
 
+def shared_kernel(own_ref, mid_ref, far_ref, mine_ref, other_ref, out_ref):
+    queries = (own_ref, mid_ref, far_ref)
+    mine = inner_products(queries, mine_ref, 0, mine_ref.shape[0])
+    other = inner_products(queries, other_ref, 0, mine_ref.shape[0])
+    lower = lax.axis_index("pb") == 0
+    out_ref[...] = jnp.concatenate([jnp.where(lower, mine, other), jnp.where(lower, other, mine)], axis=1)
+
+
+def shared_products(own, mid, far, mine, other):
+    return pl.pallas_call(
+        shared_kernel,
+        out_shape=jax.ShapeDtypeStruct((3 * own.shape[1], 2 * mine.shape[1]), F32),
+        in_specs=[VMEM] * 5,
+        out_specs=VMEM,
+        compiler_params=pltpu.CompilerParams(vmem_limit_bytes=24 << 20),
+        cost_estimate=pl.CostEstimate(flops=1000, bytes_accessed=1000, transcendentals=0),
+    )(own, mid, far, mine, other)
+
+
 def far_pass_kernel(ex, far_out, grad_ref, order_ref, out_ref):
-    out_ref[...] = inner_products((far_out,), grad_ref)
-
-
-def last_pass_kernel(ex, base_ref, far_ref, far_out, grad_ref, order_ref, mine_ref, send_ref, full_ref):
+    out_ref[...] = inner_products((far_out,), grad_ref, SHARED)
+
+
+def last_pass_kernel(ex, base_ref, far_ref, shared_ref, far_out, grad_ref, order_ref, mine_ref, send_ref, full_ref):
     late = far_out.shape[1]
-    acc = far_ref[...] + inner_products((far_out,), grad_ref, far_out.shape[0])
-    far = slot_sources(lax.axis_index("ex"))[3]
+    acc = far_ref[...] + inner_products((far_out,), grad_ref, SHARED + far_out.shape[0])
+    slots = [shared_ref[:late], shared_ref[late : 2 * late], shared_ref[2 * late :] + acc]
+    sources = slot_sources(lax.axis_index("ex"))[1:]
     full_ref[...] = base_ref[...]
     for b in range(ex):
         at = b * (EARLY + late) + EARLY
-        full_ref[at : at + late, :] = full_ref[at : at + late, :] + jnp.where(order_ref[b] == far, acc, 0.0)
+        high = full_ref[at : at + late, :]
+        for source, slot in zip(sources, slots):
+            high = high + jnp.where(order_ref[b] == source, slot, 0.0)
+        full_ref[at : at + late, :] = high
     half = mine_ref.shape[0]
     side = lax.axis_index("feat")
     mine_ref[...] = full_ref[pl.ds(pl.multiple_of(side * half, half), half), :]
@@ -195,6 +222,7 @@
 PAIRS = [(0, 1), (1, 0), (2, 3), (3, 2)]
 MIDDLE = [(1, 2), (2, 1)]
 OUTWARD = [(1, 0), (2, 3)]
+INWARD = [(0, 1), (3, 2)]
 
 
 def per_device_line(train_grads, queries, left_factor, right_factor, block_order):
@@ -213,23 +241,31 @@
     raw_far_mid = lax.ppermute(after(raw_near, early_0), "ex", MIDDLE)
 
     late = condition(after(late_raw, raw_near, raw_mid), late_other, *terms)
-    near = lax.ppermute(late, "ex", PAIRS)
-    mid = lax.ppermute(late, "ex", MIDDLE)
-    grads = regroup(after(train_grads, late))
+    near_in = lax.ppermute(late, "ex", INWARD)
+    near_out = lax.ppermute(late[SHARED:], "ex", OUTWARD)
+    mid_in = lax.ppermute(late, "ex", MIDDLE)
+    grads = regroup(after(train_grads, late, raw_mid_out, raw_far_mid))
     early_0_other = lax.ppermute(after(early_0, late), "feat", swap)
     raw_far_out = lax.ppermute(after(raw_far_mid, grads), "ex", OUTWARD)
-    far_mid = lax.ppermute(after(near, grads), "ex", MIDDLE)
-    mid_out = lax.ppermute(after(mid, near, grads), "ex", OUTWARD)
-    cond_0 = condition(after(early_0, near, mid), early_0_other, *terms)
-    early_1 = jnp.concatenate([raw_mid + raw_mid_out, after(raw_far_mid, near, mid) + raw_far_out], axis=0)
+    far_mid = lax.ppermute(after(near_in, near_out, grads), "ex", MIDDLE)
+    mid_out = lax.ppermute(after(mid_in, grads)[SHARED:], "ex", OUTWARD)
+    lot = n // lax.axis_size("pb")
+    share = lax.dynamic_slice_in_dim(grads[:SHARED], lax.axis_index("pb") * lot, lot, axis=1)
+    cond_0 = condition(after(early_0, near_in, mid_in, near_out), early_0_other, *terms)
+    share_mine = lax.ppermute(after(share, near_in, near_out, mid_in), "ex", INWARD)
+    share_other = lax.ppermute(after(share_mine, mid_out), "pb", swap)
+    early_1 = jnp.concatenate([raw_mid + raw_mid_out, after(raw_far_mid, near_in, mid_in) + raw_far_out], axis=0)
     early_1_other = lax.ppermute(after(early_1, cond_0), "feat", swap)
-    part = far_mid.shape[0] // 2
-    far_out_0 = lax.ppermute(far_mid[:part], "ex", OUTWARD)
-    far_out_1 = lax.ppermute(far_mid[part:], "ex", OUTWARD)
+    part = (far_mid.shape[0] - SHARED) // 2
+    far_out_0 = lax.ppermute(far_mid[SHARED : SHARED + part], "ex", OUTWARD)
+    far_out_1 = lax.ppermute(far_mid[SHARED + part :], "ex", OUTWARD)
+    near = jnp.concatenate([near_in[:SHARED], near_in[SHARED:] + near_out], axis=0)
+    mid = jnp.concatenate([mid_in[:SHARED], mid_in[SHARED:] + mid_out], axis=0)
+    shared = lax.ppermute(shared_products(late, mid_in, far_mid, share_mine, share_other), "ex", OUTWARD)
     cond_1 = condition(after(early_1, far_mid), early_1_other, *terms)
 
     base = score_call(
-        first_pass_kernel, ex, (cond_0, cond_1, late, near, mid + mid_out, far_mid, grads), block_order,
+        first_pass_kernel, ex, (cond_0, cond_1, late, near, mid, far_mid, grads), block_order,
         jax.ShapeDtypeStruct((ex * count, n), F32),
     )
     far_0 = score_call(
@@ -238,7 +274,7 @@
     )
     half = jax.ShapeDtypeStruct((ex * count // 2, n), F32)
     mine, send = score_call(
-        last_pass_kernel, ex, (base, far_0, far_out_1, grads), block_order, (half, half),
+        last_pass_kernel, ex, (base, far_0, shared, far_out_1, grads), block_order, (half, half),
         [pltpu.VMEM((ex * count, n), F32)],
     )
     scores = mine + lax.ppermute(send, "feat", swap)

time: 71.9 us -> 82.8 us (1.15)
  starting transfers between devices: 22.5 us -> 33.7 us
  waiting for transfers between devices: 23.9 us -> 18.5 us
  other arithmetic: 0.98 us -> 4.12 us
  local copies, waits for them, and re-layouts: 3.99 us -> 5.43 us
    ppermute x6 -> x10, starting transfers between devices: 8.74 us -> 21.7 us  [the longest x1 7.57 us: per_device_line(): lax.ppermute(after(share, near_in, near_out, mid_in), 'ex', INWARD)]
    ppermute x6 -> x10, waiting for transfers between devices: 13.5 us -> 8.1 us  [the longest x1 3 us: per_device_line(): far_out_1 = lax.ppermute(far_mid[SHARED + part:], 'ex', OUTWARD)]
    ppermute x1, waiting for transfers between devices: 0.01 us -> 5.1 us  [per_device_line(): late_other = lax.ppermute(late_raw, 'feat', swap)]
    ppermute x1, waiting for transfers between devices: 3.53 us -> 0.01 us  [per_device_line(): raw_far_out = lax.ppermute(after(raw_far_mid, grads), 'ex', OUTWARD)]
    add x2 -> x3, other arithmetic: 0.21 us -> 2.23 us  [the longest x1 1.09 us: per_device_line(): after(raw_far_mid, near_in, mid_in) + raw_far_out]
    ppermute x1, waiting for transfers between devices: 3.75 us -> 2.1 us  [per_device_line(): raw_near = lax.ppermute(raw, 'ex', PAIRS)]
    ppermute x1, starting transfers between devices: 3 us -> 1.56 us  [per_device_line(): late_other = lax.ppermute(late_raw, 'feat', swap)]
    slice x1 -> x6, local copies, waits for them, and re-layouts: 0.03 us -> 1.42 us  [the longest x1 1.31 us: per_device_line(): grads[:SHARED]]
  transfers between devices with their start and end apart: 15 -> 19, of which waited for: 7 -> 8; matrix products, arithmetic and copies ran while one was open for 2% -> 6% of each run, Pallas kernels for 25% -> 22%
where the time goes in v8:
time: 82.8 us; the launch traced here: 82.2 us
  starting transfers between devices  33.7 us (41%)
  Pallas kernels  20.1 us (24%)
  waiting for transfers between devices  18.5 us (22%)
  local copies, waits for them, and re-layouts  5.43 us (7%)
  other arithmetic  4.12 us (5%)
    pallas_call x1, Pallas kernels, regroup(): pl.pallas_call(regroup_kernel, out_shape=jax.ShapeDtypeStruct((rows, n, w...  8.44 us
    ppermute x1, starting transfers between devices, per_device_line(): lax.ppermute(after(share, near_in, near_out, mid_in), 'ex', INWARD)  7.57 us
    pallas_call x3, Pallas kernels, score_call(): pl.pallas_call(functools.partial(kernel, ex), out_shape=out_shape, in_spe...  7.41 us
    ppermute x1, starting transfers between devices, per_device_line(): near_in = lax.ppermute(late, 'ex', INWARD)  6.04 us
    ppermute x1, waiting for transfers between devices, per_device_line(): late_other = lax.ppermute(late_raw, 'feat', swap)  5.1 us
    pallas_call x3, Pallas kernels, condition(): pl.pallas_call(condition_kernel, out_shape=jax.ShapeDtypeStruct((rows, co...  3.75 us
    ppermute x1, waiting for transfers between devices, per_device_line(): scores = mine + lax.ppermute(send, 'feat', swap)  3.17 us
    ppermute x1, starting transfers between devices, per_device_line(): raw_near = lax.ppermute(raw, 'ex', PAIRS)  3.09 us
  transfers between devices with their start and end apart: 19, of which 8 were waited for; matrix products, arithmetic and copies ran while one was open for 6% of the time, Pallas kernels for 22%

profile of v8, /device:TPU:0, one launch (start us, length us, event | category | flops | bytes accessed | tf_op | source)
XLA Modules:
  0.0 82.2 jit_solution(13373536441869302626)
XLA Ops:
  0.0 1.1 %slice_bitcast_fusion.own_ref = bf16[8,128,256]{2,1,0:T(8,128)(2,1)S(1)} fusion(bf16[1,12,128,256]{3,2,1,0:T(8,128)(2,1)} %param.6), kind=kLoop, calls=%fused_computation.4 | loop fusion | bytes 1048576 | tf_op jit(solution)/shard_map/squeeze | solution.py:233
  1.1 1.0 %slice_bitcast_fusion.1 = bf16[4,128,256]{2,1,0:T(8,128)(2,1)S(1)} fusion(bf16[1,12,128,256]{3,2,1,0:T(8,128)(2,1)} %param.6), kind=kLoop, calls=%fused_computation.7 | loop fusion | bytes 524288 | tf_op jit(solution)/shard_map/squeeze | solution.py:235
  2.1 3.1 %collective-permute-start = (bf16[4,128,256]{2,1,0:T(8,128)(2,1)S(1)}, bf16[4,128,256]{2,1,0:T(8,128)(2,1)S(1)}, u32[]{:S(2)}, u32[]{:S(2)}) collective-permute-start(bf16[4,128,256]{2,1,0:T(8,128)(2,1)S(1)} %slice_bitcast_fusion.1), channel_id=1, source_target_pairs={{0,4},{4,0},{8,12},{12,8},{1,5},{5,1},{9,13},{13,9},{2,6},{6,2},{1... | collective-permute-start | bytes 786440 | tf_op jit(solution)/shard_map/ppermute | solution.py:237
  5.8 1.6 %collective-permute-start.2 = (bf16[8,128,256]{2,1,0:T(8,128)(2,1)S(1)}, bf16[8,128,256]{2,1,0:T(8,128)(2,1)S(1)}, u32[]{:S(2)}, u32[]{:S(2)}) collective-permute-start(bf16[8,128,256]{2,1,0:T(8,128)(2,1)S(1)} %slice_bitcast_fusion.own_ref), channel_id=1, source_target_pairs={{0,2},{2,0},{1,3},{3,1},{4,6},{6,4},{5,7},{7,5},{8,10},{10,8},{9,1... | collective-permute-start | bytes 1572872 | tf_op jit(solution)/shard_map/ppermute | solution.py:234
  9.4 2.1 %collective-permute-done = bf16[4,128,256]{2,1,0:T(8,128)(2,1)S(1)} collective-permute-done((bf16[4,128,256]{2,1,0:T(8,128)(2,1)S(1)}, bf16[4,128,256]{2,1,0:T(8,128)(2,1)S(1)}, u32[]{:S(2)}, u32[]{:S(2)}) %collective-permute-start) | collective-permute-done | bytes 262176 | tf_op jit(solution)/shard_map/ppermute | solution.py:237
  11.5 1.4 %collective-permute-start.8 = (bf16[4,128,256]{2,1,0:T(8,128)(2,1)S(1)}, bf16[4,128,256]{2,1,0:T(8,128)(2,1)}, u32[]{:S(2)}, u32[]{:S(2)}) collective-permute-start(bf16[4,128,256]{2,1,0:T(8,128)(2,1)S(1)} %collective-permute-done), channel_id=1, source_target_pairs={{4,8},{8,4},{5,9},{9,5},{6,10},{10,6},{7,11},{11,7},{20,24},{24,20... | collective-permute-start | bytes 786440 | tf_op jit(solution)/shard_map/ppermute | solution.py:241
  12.9 1.3 %collective-permute-start.7 = (bf16[4,128,256]{2,1,0:T(8,128)(2,1)S(1)}, bf16[4,128,256]{2,1,0:T(8,128)(2,1)}, u32[]{:S(2)}, u32[]{:S(2)}) collective-permute-start(bf16[4,128,256]{2,1,0:T(8,128)(2,1)S(1)} %collective-permute-done.1), channel_id=1, source_target_pairs={{4,0},{8,12},{5,1},{9,13},{6,2},{10,14},{7,3},{11,15},{20,16},{24,... | collective-permute-start | bytes 786440 | tf_op jit(solution)/shard_map/ppermute | solution.py:239
  14.2 5.1 %collective-permute-done.2.far_ref = bf16[8,128,256]{2,1,0:T(8,128)(2,1)S(1)} collective-permute-done((bf16[8,128,256]{2,1,0:T(8,128)(2,1)S(1)}, bf16[8,128,256]{2,1,0:T(8,128)(2,1)S(1)}, u32[]{:S(2)}, u32[]{:S(2)}) %collective-permute-start.2) | collective-permute-done | bytes 524320 | tf_op jit(solution)/shard_map/ppermute | solution.py:234
  19.3 1.2 %shard_map.56.own_ref = bf16[128,8,256]{2,1,0:T(8,128)(2,1)S(1)} custom-call(bf16[8,128,256]{2,1,0:T(8,128)(2,1)S(1)} %slice_bitcast_fusion.own_ref, bf16[8,128,256]{2,1,0:T(8,128)(2,1)S(1)} %collective-permute-done.2.far_ref, bf16[384,256]{1,0:T(8,128)(2,1)S(1)} %get-tuple-element.31.left_ref, bf16[512,256]{1,0:T(8,128)(2,1)S(1)} %get-tuple-element.32.right_ref), custom_call_target="tpu_custom_call" | custom-call | flops 960000000 | bytes 2097152 | tf_op jit(solution)/shard_map/pallas_call | solution.py:71
  20.5 6.0 %collective-permute-start.3 = (bf16[128,8,256]{2,1,0:T(8,128)(2,1)S(1)}, bf16[128,8,256]{2,1,0:T(8,128)(2,1)S(1)}, u32[]{:S(2)}, u32[]{:S(2)}) collective-permute-start(bf16[128,8,256]{2,1,0:T(8,128)(2,1)S(1)} %shard_map.56.own_ref), channel_id=1, source_target_pairs={{0,4},{12,8},{1,5},{13,9},{2,6},{14,10},{3,7},{15,11},{16,20},{28,... | collective-permute-start | bytes 1572872 | tf_op jit(solution)/shard_map/ppermute | solution.py:244
  27.3 1.3 %collective-permute-start.5 = (bf16[112,8,256]{2,1,0:T(8,128)(2,1)S(1)}, bf16[112,8,256]{2,1,0:T(8,128)(2,1)}, u32[]{:S(2)}, u32[]{:S(2)}) collective-permute-start(bf16[112,8,256]{2,1,0:T(8,128)(2,1)S(1)} %slice.44), channel_id=1, source_target_pairs={{4,0},{8,12},{5,1},{9,13},{6,2},{10,14},{7,3},{11,15},{20,16},{24,... | collective-permute-start | bytes 1376264 | tf_op jit(solution)/shard_map/ppermute | solution.py:245
  28.6 1.6 %collective-permute-start.6 = (bf16[8,128,256]{2,1,0:T(8,128)(2,1)S(1)}, bf16[8,128,256]{2,1,0:T(8,128)(2,1)S(1)}, u32[]{:S(2)}, u32[]{:S(2)}) collective-permute-start(bf16[8,128,256]{2,1,0:T(8,128)(2,1)S(1)} %pad_maximum_fusion.own_ref), channel_id=1, source_target_pairs={{0,2},{2,0},{1,3},{3,1},{4,6},{6,4},{5,7},{7,5},{8,10},{10,8},{9,1... | collective-permute-start | bytes 1572872 | tf_op jit(solution)/shard_map/ppermute | solution.py:248
  30.2 8.4 %shard_map.58.grad_ref = bf16[128,128,256]{2,1,0:T(8,128)(2,1)} custom-call(bf16[128,128,256]{2,1,0:T(8,128)(2,1)} %grads_ref), custom_call_target="tpu_custom_call" | custom-call | flops 6000000000 | bytes 16000000 | tf_op jit(solution)/shard_map/pallas_call | solution.py:107
  38.6 1.3 %collective-permute-start.9 = (bf16[4,128,256]{2,1,0:T(8,128)(2,1)}, bf16[4,128,256]{2,1,0:T(8,128)(2,1)}, u32[]{:S(2)}, u32[]{:S(2)}) collective-permute-start(bf16[4,128,256]{2,1,0:T(8,128)(2,1)} %collective-permute-done.8), channel_id=1, source_target_pairs={{4,0},{8,12},{5,1},{9,13},{6,2},{10,14},{7,3},{11,15},{20,16},{24,... | collective-permute-start | bytes 786440 | tf_op jit(solution)/shard_map/ppermute | solution.py:249
  39.9 1.3 %slice.50 = bf16[16,128,256]{2,1,0:T(8,128)(2,1)S(1)} slice(bf16[128,128,256]{2,1,0:T(8,128)(2,1)} %shard_map.58.grad_ref), slice={[0:16], [0:128], [0:256]} | slice | bytes 2097152 | tf_op jit(solution)/shard_map/slice | solution.py:253
  41.3 1.1 %add.18 = bf16[4,128,256]{2,1,0:T(8,128)(2,1)S(1)} add(bf16[4,128,256]{2,1,0:T(8,128)(2,1)} %copy-done.3, bf16[4,128,256]{2,1,0:T(8,128)(2,1)} %collective-permute-done.7) | non-fusion elementwise | flops 131072 | bytes 786432 | tf_op jit(solution)/shard_map/add | solution.py:257
  43.2 1.3 %collective-permute-start.12 = (bf16[112,8,256]{2,1,0:T(8,128)(2,1)S(1)}, bf16[112,8,256]{2,1,0:T(8,128)(2,1)S(1)}, u32[]{:S(2)}, u32[]{:S(2)}) collective-permute-start(bf16[112,8,256]{2,1,0:T(8,128)(2,1)S(1)} %slice.40), channel_id=1, source_target_pairs={{4,0},{8,12},{5,1},{9,13},{6,2},{10,14},{7,3},{11,15},{20,16},{24,... | collective-permute-start | bytes 1376264 | tf_op jit(solution)/shard_map/ppermute | solution.py:251
  44.5 7.6 %collective-permute-start.14 = (bf16[16,64,256]{2,1,0:T(8,128)(2,1)S(1)}, bf16[16,64,256]{2,1,0:T(8,128)(2,1)S(1)}, u32[]{:S(2)}, u32[]{:S(2)}) collective-permute-start(bf16[16,64,256]{2,1,0:T(8,128)(2,1)S(1)} %constant_dynamic-slice_fusion), channel_id=1, source_target_pairs={{0,4},{12,8},{1,5},{13,9},{2,6},{14,10},{3,7},{15,11},{16,20},{28,... | collective-permute-start | bytes 1572872 | tf_op jit(solution)/shard_map/ppermute | solution.py:255
  52.1 1.1 %add.19 = bf16[4,128,256]{2,1,0:T(8,128)(2,1)S(1)} add(bf16[4,128,256]{2,1,0:T(8,128)(2,1)} %collective-permute-done.8, bf16[4,128,256]{2,1,0:T(8,128)(2,1)} %collective-permute-done.9) | non-fusion elementwise | flops 131072 | bytes 786432 | tf_op jit(solution)/shard_map/add | solution.py:257
  53.3 1.2 %shard_map.57.early_0 = bf16[128,8,256]{2,1,0:T(8,128)(2,1)S(1)} custom-call(bf16[8,128,256]{2,1,0:T(8,128)(2,1)S(1)} %pad_maximum_fusion.own_ref, bf16[8,128,256]{2,1,0:T(8,128)(2,1)S(1)} %collective-permute-done.6.far_ref, bf16[384,256]{1,0:T(8,128)(2,1)S(1)} %get-tuple-element.31.left_ref, bf16[512,256]{1,0:T(8,128)(2,1)S(1)} %get-tuple-element.32.right_ref), custom_call_target="tpu_custom_call" | custom-call | flops 960000000 | bytes 2097152 | tf_op jit(solution)/shard_map/pallas_call | solution.py:71
  55.1 1.1 %slice_add_fusion.1 = bf16[112,8,256]{2,1,0:T(8,128)(2,1)S(1)} fusion(bf16[112,8,256]{2,1,0:T(8,128)(2,1)} %collective-permute-done.5, bf16[128,8,256]{2,1,0:T(8,128)(2,1)S(1)} %collective-permute-done.3), kind=kLoop, calls=%fused_computation.6 | loop fusion | flops 229376 | bytes 1376256 | tf_op jit(solution)/shard_map/add | solution.py:262
  56.2 2.0 %collective-permute-done.12 = bf16[112,8,256]{2,1,0:T(8,128)(2,1)S(1)} collective-permute-done((bf16[112,8,256]{2,1,0:T(8,128)(2,1)S(1)}, bf16[112,8,256]{2,1,0:T(8,128)(2,1)S(1)}, u32[]{:S(2)}, u32[]{:S(2)}) %collective-permute-start.12) | collective-permute-done | bytes 458784 | tf_op jit(solution)/shard_map/ppermute | solution.py:251
  58.3 2.6 %collective-permute-done.14.mine_ref = bf16[16,64,256]{2,1,0:T(8,128)(2,1)S(1)} collective-permute-done((bf16[16,64,256]{2,1,0:T(8,128)(2,1)S(1)}, bf16[16,64,256]{2,1,0:T(8,128)(2,1)S(1)}, u32[]{:S(2)}, u32[]{:S(2)}) %collective-permute-start.14) | collective-permute-done | bytes 524320 | tf_op jit(solution)/shard_map/ppermute | solution.py:255
  60.9 1.3 %collective-permute-start.13 = (bf16[56,8,256]{2,1,0:T(8,128)(2,1)S(1)}, bf16[56,8,256]{2,1,0:T(8,128)(2,1)S(1)}, u32[]{:S(2)}, u32[]{:S(2)}) collective-permute-start(bf16[56,8,256]{2,1,0:T(8,128)(2,1)S(1)} %get-tuple-element.50), channel_id=1, source_target_pairs={{4,0},{8,12},{5,1},{9,13},{6,2},{10,14},{7,3},{11,15},{20,16},{24,... | collective-permute-start | bytes 688136 | tf_op jit(solution)/shard_map/ppermute | solution.py:260
  62.2 1.6 %collective-permute-start.17 = (bf16[56,8,256]{2,1,0:T(8,128)(2,1)S(1)}, bf16[56,8,256]{2,1,0:T(8,128)(2,1)S(1)}, u32[]{:S(2)}, u32[]{:S(2)}) collective-permute-start(bf16[56,8,256]{2,1,0:T(8,128)(2,1)S(1)} %get-tuple-element.49), channel_id=1, source_target_pairs={{4,0},{8,12},{5,1},{9,13},{6,2},{10,14},{7,3},{11,15},{20,16},{24,... | collective-permute-start | bytes 688136 | tf_op jit(solution)/shard_map/ppermute | solution.py:261
  64.4 1.3 %collective-permute-start.16 = (f32[24,128]{1,0:T(8,128)S(1)}, f32[24,128]{1,0:T(8,128)S(1)}, u32[]{:S(2)}, u32[]{:S(2)}) collective-permute-start(f32[24,128]{1,0:T(8,128)S(1)} %shard_map.62), channel_id=1, source_target_pairs={{4,0},{8,12},{5,1},{9,13},{6,2},{10,14},{7,3},{11,15},{20,16},{24,... | collective-permute-start | bytes 36872 | tf_op jit(solution)/shard_map/ppermute | solution.py:264
  65.7 1.3 %shard_map.59.early_1 = bf16[128,8,256]{2,1,0:T(8,128)(2,1)S(1)} custom-call(bf16[8,128,256]{2,1,0:T(8,128)(2,1)S(1)} %pad_maximum_fusion.1.own_ref, bf16[8,128,256]{2,1,0:T(8,128)(2,1)S(1)} %collective-permute-done.11.far_ref, bf16[384,256]{1,0:T(8,128)(2,1)S(1)} %get-tuple-element.31.left_ref, bf16[512,256]{1,0:T(8,128)(2,1)S(1)} %get-tuple-element.32.right_ref), custom_call_target="tpu_custom_call" | custom-call | flops 960000000 | bytes 2097152 | tf_op jit(solution)/shard_map/pallas_call | solution.py:71
  67.0 3.9 %shard_map.60.base_ref = f32[48,128]{1,0:T(8,128)S(1)} custom-call(bf16[128,8,256]{2,1,0:T(8,128)(2,1)S(1)} %shard_map.57.early_0, bf16[128,8,256]{2,1,0:T(8,128)(2,1)S(1)} %shard_map.59.early_1, bf16[128,8,256]{2,1,0:T(8,128)(2,1)S(1)} %shard_map.56.own_ref, bf16[128,8,256]{2,1,0:T(8,128)(2,1)S(1)} %pad_maximum_fusion.2.near, ...), custom_call_target="tpu_custom_call" | custom-call | flops 1000 | bytes 1000 | tf_op jit(solution)/shard_map/pallas_call | solution.py:207
  71.3 1.7 %shard_map.61.far_ref = f32[8,128]{1,0:T(8,128)S(1)} custom-call(bf16[56,8,256]{2,1,0:T(8,128)(2,1)S(1)} %collective-permute-done.13.far_out, bf16[128,128,256]{2,1,0:T(8,128)(2,1)S(1)} %bitcast.9, s32[4]{0:T(128)S(1)} %copy-done.2), custom_call_target="tpu_custom_call" | custom-call | flops 1000 | bytes 1000 | tf_op jit(solution)/shard_map/pallas_call | solution.py:207
  73.0 3.0 %collective-permute-done.17.far_out = bf16[56,8,256]{2,1,0:T(8,128)(2,1)S(1)} collective-permute-done((bf16[56,8,256]{2,1,0:T(8,128)(2,1)S(1)}, bf16[56,8,256]{2,1,0:T(8,128)(2,1)S(1)}, u32[]{:S(2)}, u32[]{:S(2)}) %collective-permute-start.17) | collective-permute-done | bytes 229408 | tf_op jit(solution)/shard_map/ppermute | solution.py:261
  76.1 1.8 %shard_map.63 = (f32[24,128]{1,0:T(8,128)S(1)}, f32[24,128]{1,0:T(8,128)S(1)}) custom-call(f32[48,128]{1,0:T(8,128)S(1)} %shard_map.60.base_ref, f32[8,128]{1,0:T(8,128)S(1)} %shard_map.61.far_ref, f32[24,128]{1,0:T(8,128)S(1)} %collective-permute-done.16.shared_ref, bf16[56,8,256]{2,1,0:T(8,128)(2,1)S(1)} %collective-permute-done.17.far_out, ...), custom_call_target="tpu_custom_call" | custom-call | flops 1000 | bytes 1000 | tf_op jit(solution)/shard_map/pallas_call | solution.py:207
  78.5 3.2 %collective-permute-done.18 = f32[24,128]{1,0:T(8,128)S(1)} collective-permute-done((f32[24,128]{1,0:T(8,128)S(1)}, f32[24,128]{1,0:T(8,128)S(1)}, u32[]{:S(2)}, u32[]{:S(2)}) %collective-permute-start.18) | collective-permute-done | bytes 12320 | tf_op jit(solution)/shard_map/ppermute | solution.py:280
  (46 shorter events, 7.2 us)
Async XLA Ops:
  2.1 9.4 %collective-permute-start = (bf16[4,128,256]{2,1,0:T(8,128)(2,1)S(1)}, bf16[4,128,256]{2,1,0:T(8,128)(2,1)S(1)}, u32[]{:S(2)}, u32[]{:S(2)}) collective-permute-start(bf16[4,128,256]{2,1,0:T(8,128)(2,1)S(1)} %slice_bitcast_fusion.1), channel_id=1, source_target_pairs={{0,4},{4,0},{8,12},{12,8},{1,5},{5,1},{9,13},{13,9},{2,6},{6,2},{1... | collective-permute-start | bytes 786440 | tf_op jit(solution)/shard_map/ppermute | solution.py:237
  5.1 6.3 %collective-permute-start.1 = (bf16[4,128,256]{2,1,0:T(8,128)(2,1)S(1)}, bf16[4,128,256]{2,1,0:T(8,128)(2,1)S(1)}, u32[]{:S(2)}, u32[]{:S(2)}) collective-permute-start(bf16[4,128,256]{2,1,0:T(8,128)(2,1)S(1)} %slice_bitcast_fusion.1), channel_id=1, source_target_pairs={{4,8},{8,4},{5,9},{9,5},{6,10},{10,6},{7,11},{11,7},{20,24},{24,20... | collective-permute-start | bytes 786440 | tf_op jit(solution)/shard_map/ppermute | solution.py:238
  5.8 13.4 %collective-permute-start.2 = (bf16[8,128,256]{2,1,0:T(8,128)(2,1)S(1)}, bf16[8,128,256]{2,1,0:T(8,128)(2,1)S(1)}, u32[]{:S(2)}, u32[]{:S(2)}) collective-permute-start(bf16[8,128,256]{2,1,0:T(8,128)(2,1)S(1)} %slice_bitcast_fusion.own_ref), channel_id=1, source_target_pairs={{0,2},{2,0},{1,3},{3,1},{4,6},{6,4},{5,7},{7,5},{8,10},{10,8},{9,1... | collective-permute-start | bytes 1572872 | tf_op jit(solution)/shard_map/ppermute | solution.py:234
  7.4 0.9 %copy-start = (f32[256,256]{1,0:T(8,128)S(1)}, f32[256,256]{1,0:T(8,128)}, u32[]{:S(2)}) copy-start(f32[256,256]{1,0:T(8,128)} %left_ref.1) | copy-start | bytes 786436
  8.3 0.9 %copy-start.1 = (f32[256,256]{1,0:T(8,128)S(1)}, f32[256,256]{1,0:T(8,128)}, u32[]{:S(2)}) copy-start(f32[256,256]{1,0:T(8,128)} %right_ref) | copy-start | bytes 786436
  11.5 17.2 %copy-start.3 = (bf16[4,128,256]{2,1,0:T(8,128)(2,1)}, bf16[4,128,256]{2,1,0:T(8,128)(2,1)S(1)}, u32[]{:S(2)}) copy-start(bf16[4,128,256]{2,1,0:T(8,128)(2,1)S(1)} %collective-permute-done.1) | copy-start | bytes 786436
  11.5 17.1 %collective-permute-start.8 = (bf16[4,128,256]{2,1,0:T(8,128)(2,1)S(1)}, bf16[4,128,256]{2,1,0:T(8,128)(2,1)}, u32[]{:S(2)}, u32[]{:S(2)}) collective-permute-start(bf16[4,128,256]{2,1,0:T(8,128)(2,1)S(1)} %collective-permute-done), channel_id=1, source_target_pairs={{4,8},{8,4},{5,9},{9,5},{6,10},{10,6},{7,11},{11,7},{20,24},{24,20... | collective-permute-start | bytes 786440 | tf_op jit(solution)/shard_map/ppermute | solution.py:241
  12.9 17.3 %collective-permute-start.7 = (bf16[4,128,256]{2,1,0:T(8,128)(2,1)S(1)}, bf16[4,128,256]{2,1,0:T(8,128)(2,1)}, u32[]{:S(2)}, u32[]{:S(2)}) collective-permute-start(bf16[4,128,256]{2,1,0:T(8,128)(2,1)S(1)} %collective-permute-done.1), channel_id=1, source_target_pairs={{4,0},{8,12},{5,1},{9,13},{6,2},{10,14},{7,3},{11,15},{20,16},{24,... | collective-permute-start | bytes 786440 | tf_op jit(solution)/shard_map/ppermute | solution.py:239
  20.5 21.9 %collective-permute-start.3 = (bf16[128,8,256]{2,1,0:T(8,128)(2,1)S(1)}, bf16[128,8,256]{2,1,0:T(8,128)(2,1)S(1)}, u32[]{:S(2)}, u32[]{:S(2)}) collective-permute-start(bf16[128,8,256]{2,1,0:T(8,128)(2,1)S(1)} %shard_map.56.own_ref), channel_id=1, source_target_pairs={{0,4},{12,8},{1,5},{13,9},{2,6},{14,10},{3,7},{15,11},{16,20},{28,... | collective-permute-start | bytes 1572872 | tf_op jit(solution)/shard_map/ppermute | solution.py:244
  26.6 15.9 %collective-permute-start.4 = (bf16[128,8,256]{2,1,0:T(8,128)(2,1)S(1)}, bf16[128,8,256]{2,1,0:T(8,128)(2,1)S(1)}, u32[]{:S(2)}, u32[]{:S(2)}) collective-permute-start(bf16[128,8,256]{2,1,0:T(8,128)(2,1)S(1)} %shard_map.56.own_ref), channel_id=1, source_target_pairs={{4,8},{8,4},{5,9},{9,5},{6,10},{10,6},{7,11},{11,7},{20,24},{24,20... | collective-permute-start | bytes 1572872 | tf_op jit(solution)/shard_map/ppermute | solution.py:246
  27.3 15.1 %collective-permute-start.5 = (bf16[112,8,256]{2,1,0:T(8,128)(2,1)S(1)}, bf16[112,8,256]{2,1,0:T(8,128)(2,1)}, u32[]{:S(2)}, u32[]{:S(2)}) collective-permute-start(bf16[112,8,256]{2,1,0:T(8,128)(2,1)S(1)} %slice.44), channel_id=1, source_target_pairs={{4,0},{8,12},{5,1},{9,13},{6,2},{10,14},{7,3},{11,15},{20,16},{24,... | collective-permute-start | bytes 1376264 | tf_op jit(solution)/shard_map/ppermute | solution.py:245
  28.6 24.6 %collective-permute-start.6 = (bf16[8,128,256]{2,1,0:T(8,128)(2,1)S(1)}, bf16[8,128,256]{2,1,0:T(8,128)(2,1)S(1)}, u32[]{:S(2)}, u32[]{:S(2)}) collective-permute-start(bf16[8,128,256]{2,1,0:T(8,128)(2,1)S(1)} %pad_maximum_fusion.own_ref), channel_id=1, source_target_pairs={{0,2},{2,0},{1,3},{3,1},{4,6},{6,4},{5,7},{7,5},{8,10},{10,8},{9,1... | collective-permute-start | bytes 1572872 | tf_op jit(solution)/shard_map/ppermute | solution.py:248
  38.6 13.4 %collective-permute-start.9 = (bf16[4,128,256]{2,1,0:T(8,128)(2,1)}, bf16[4,128,256]{2,1,0:T(8,128)(2,1)}, u32[]{:S(2)}, u32[]{:S(2)}) collective-permute-start(bf16[4,128,256]{2,1,0:T(8,128)(2,1)} %collective-permute-done.8), channel_id=1, source_target_pairs={{4,0},{8,12},{5,1},{9,13},{6,2},{10,14},{7,3},{11,15},{20,16},{24,... | collective-permute-start | bytes 786440 | tf_op jit(solution)/shard_map/ppermute | solution.py:249
  42.4 18.4 %collective-permute-start.10 = (bf16[128,8,256]{2,1,0:T(8,128)(2,1)S(1)}, bf16[128,8,256]{2,1,0:T(8,128)(2,1)S(1)}, u32[]{:S(2)}, u32[]{:S(2)}) collective-permute-start(bf16[128,8,256]{2,1,0:T(8,128)(2,1)S(1)} %collective-permute-done.3), channel_id=1, source_target_pairs={{4,8},{8,4},{5,9},{9,5},{6,10},{10,6},{7,11},{11,7},{20,24},{24,20... | collective-permute-start | bytes 1572872 | tf_op jit(solution)/shard_map/ppermute | solution.py:250
  43.2 15.1 %collective-permute-start.12 = (bf16[112,8,256]{2,1,0:T(8,128)(2,1)S(1)}, bf16[112,8,256]{2,1,0:T(8,128)(2,1)S(1)}, u32[]{:S(2)}, u32[]{:S(2)}) collective-permute-start(bf16[112,8,256]{2,1,0:T(8,128)(2,1)S(1)} %slice.40), channel_id=1, source_target_pairs={{4,0},{8,12},{5,1},{9,13},{6,2},{10,14},{7,3},{11,15},{20,16},{24,... | collective-permute-start | bytes 1376264 | tf_op jit(solution)/shard_map/ppermute | solution.py:251
  44.5 16.4 %collective-permute-start.14 = (bf16[16,64,256]{2,1,0:T(8,128)(2,1)S(1)}, bf16[16,64,256]{2,1,0:T(8,128)(2,1)S(1)}, u32[]{:S(2)}, u32[]{:S(2)}) collective-permute-start(bf16[16,64,256]{2,1,0:T(8,128)(2,1)S(1)} %constant_dynamic-slice_fusion), channel_id=1, source_target_pairs={{0,4},{12,8},{1,5},{13,9},{2,6},{14,10},{3,7},{15,11},{16,20},{28,... | collective-permute-start | bytes 1572872 | tf_op jit(solution)/shard_map/ppermute | solution.py:255
  53.2 13.8 %slice-start = ((s8[8388608]{0:T(1024)(128)(4,1)}), s8[4194304]{0:T(1024)(128)(4,1)S(1)}, s32[]{:S(2)}) async-start(s8[8388608]{0:T(1024)(128)(4,1)} %bitcast.8), calls=%async_computation | async-start | bytes 8388608
  53.2 13.8 %copy-start.2 = (s32[4]{0:T(128)S(1)}, s32[4]{0:T(128)}, u32[]{:S(2)}) copy-start(s32[4]{0:T(128)} %order_ref.5) | copy-start | bytes 52
  54.5 11.2 %collective-permute-start.11 = (bf16[8,128,256]{2,1,0:T(8,128)(2,1)S(1)}, bf16[8,128,256]{2,1,0:T(8,128)(2,1)S(1)}, u32[]{:S(2)}, u32[]{:S(2)}) collective-permute-start(bf16[8,128,256]{2,1,0:T(8,128)(2,1)S(1)} %pad_maximum_fusion.1.own_ref), channel_id=1, source_target_pairs={{0,2},{2,0},{1,3},{3,1},{4,6},{6,4},{5,7},{7,5},{8,10},{10,8},{9,1... | collective-permute-start | bytes 1572872 | tf_op jit(solution)/shard_map/ppermute | solution.py:258
  60.9 3.0 %collective-permute-start.15 = (bf16[16,64,256]{2,1,0:T(8,128)(2,1)S(1)}, bf16[16,64,256]{2,1,0:T(8,128)(2,1)S(1)}, u32[]{:S(2)}, u32[]{:S(2)}) collective-permute-start(bf16[16,64,256]{2,1,0:T(8,128)(2,1)S(1)} %collective-permute-done.14.mine_ref), channel_id=1, source_target_pairs={{0,1},{1,0},{2,3},{3,2},{4,5},{5,4},{6,7},{7,6},{8,9},{9,8},{10,11... | collective-permute-start | bytes 1572872 | tf_op jit(solution)/shard_map/ppermute | solution.py:256
  60.9 10.4 %collective-permute-start.13 = (bf16[56,8,256]{2,1,0:T(8,128)(2,1)S(1)}, bf16[56,8,256]{2,1,0:T(8,128)(2,1)S(1)}, u32[]{:S(2)}, u32[]{:S(2)}) collective-permute-start(bf16[56,8,256]{2,1,0:T(8,128)(2,1)S(1)} %get-tuple-element.50), channel_id=1, source_target_pairs={{4,0},{8,12},{5,1},{9,13},{6,2},{10,14},{7,3},{11,15},{20,16},{24,... | collective-permute-start | bytes 688136 | tf_op jit(solution)/shard_map/ppermute | solution.py:260
  62.2 4.8 %slice-start.1 = ((s8[8388608]{0:T(1024)(128)(4,1)}), s8[4194304]{0:T(1024)(128)(4,1)S(1)}, s32[]{:S(2)}) async-start(s8[8388608]{0:T(1024)(128)(4,1)} %bitcast.8), calls=%async_computation.1 | async-start | bytes 8388608
  62.2 13.8 %collective-permute-start.17 = (bf16[56,8,256]{2,1,0:T(8,128)(2,1)S(1)}, bf16[56,8,256]{2,1,0:T(8,128)(2,1)S(1)}, u32[]{:S(2)}, u32[]{:S(2)}) collective-permute-start(bf16[56,8,256]{2,1,0:T(8,128)(2,1)S(1)} %get-tuple-element.49), channel_id=1, source_target_pairs={{4,0},{8,12},{5,1},{9,13},{6,2},{10,14},{7,3},{11,15},{20,16},{24,... | collective-permute-start | bytes 688136 | tf_op jit(solution)/shard_map/ppermute | solution.py:261
  64.4 11.7 %collective-permute-start.16 = (f32[24,128]{1,0:T(8,128)S(1)}, f32[24,128]{1,0:T(8,128)S(1)}, u32[]{:S(2)}, u32[]{:S(2)}) collective-permute-start(f32[24,128]{1,0:T(8,128)S(1)} %shard_map.62), channel_id=1, source_target_pairs={{4,0},{8,12},{5,1},{9,13},{6,2},{10,14},{7,3},{11,15},{20,16},{24,... | collective-permute-start | bytes 36872 | tf_op jit(solution)/shard_map/ppermute | solution.py:264
  77.9 3.8 %collective-permute-start.18 = (f32[24,128]{1,0:T(8,128)S(1)}, f32[24,128]{1,0:T(8,128)S(1)}, u32[]{:S(2)}, u32[]{:S(2)}) collective-permute-start(f32[24,128]{1,0:T(8,128)S(1)} %get-tuple-element.48), channel_id=1, source_target_pairs={{0,2},{2,0},{1,3},{3,1},{4,6},{6,4},{5,7},{7,5},{8,10},{10,8},{9,1... | collective-permute-start | bytes 36872 | tf_op jit(solution)/shard_map/ppermute | solution.py:280

commit v9 on v7

--- a/solution.py
+++ b/solution.py
@@ -109,8 +109,8 @@
         in_specs=[pl.BlockSpec(memory_space=pltpu.HBM)],
         out_specs=VMEM,
         scratch_shapes=[pltpu.VMEM((n, rows, width), BF16), pltpu.SemaphoreType.DMA((n // EXAMPLES,))],
-        compiler_params=pltpu.CompilerParams(vmem_limit_bytes=48 << 20),
-        cost_estimate=pl.CostEstimate(flops=6_000_000_000, bytes_accessed=16_000_000, transcendentals=0),
+        compiler_params=pltpu.CompilerParams(vmem_limit_bytes=44 << 20),
+        cost_estimate=pl.CostEstimate(flops=1000, bytes_accessed=1000, transcendentals=0),
     )(grads)
 
 
@@ -208,18 +208,18 @@
     terms = factor_terms(left_factor, after(right_factor, raw), train_grads.shape[1])
     raw_near = lax.ppermute(raw, "ex", PAIRS)
     raw_mid = lax.ppermute(raw, "ex", MIDDLE)
-    raw_mid_out = lax.ppermute(after(raw_mid, *terms), "ex", OUTWARD)
-    early_0 = jnp.concatenate([raw, after(raw_near, raw_mid)], axis=0)
+    grads = regroup(after(train_grads, *terms))
+    raw_mid_out = lax.ppermute(after(raw_mid, grads), "ex", OUTWARD)
+    early_0 = jnp.concatenate([raw, after(raw_near, raw_mid, grads)], axis=0)
     raw_far_mid = lax.ppermute(after(raw_near, early_0), "ex", MIDDLE)
 
-    late = condition(after(late_raw, raw_near, raw_mid), late_other, *terms)
+    late = condition(after(late_raw, raw_near, raw_mid, grads), late_other, *terms)
     near = lax.ppermute(late, "ex", PAIRS)
     mid = lax.ppermute(late, "ex", MIDDLE)
-    grads = regroup(after(train_grads, late))
-    early_0_other = lax.ppermute(after(early_0, late), "feat", swap)
-    raw_far_out = lax.ppermute(after(raw_far_mid, grads), "ex", OUTWARD)
-    far_mid = lax.ppermute(after(near, grads), "ex", MIDDLE)
-    mid_out = lax.ppermute(after(mid, near, grads), "ex", OUTWARD)
+    early_0_other = lax.ppermute(after(early_0, late, raw_far_mid, raw_mid_out), "feat", swap)
+    raw_far_out = lax.ppermute(after(raw_far_mid, near), "ex", OUTWARD)
+    far_mid = lax.ppermute(near, "ex", MIDDLE)
+    mid_out = lax.ppermute(mid, "ex", OUTWARD)
     cond_0 = condition(after(early_0, near, mid), early_0_other, *terms)
     early_1 = jnp.concatenate([raw_mid + raw_mid_out, after(raw_far_mid, near, mid) + raw_far_out], axis=0)
     early_1_other = lax.ppermute(after(early_1, cond_0), "feat", swap)

time: 71.9 us -> 76.4 us (1.063)
  waiting for transfers between devices: 23.9 us -> 33 us
  Pallas kernels: 19.9 us -> 16.7 us
  starting transfers between devices: 22.5 us -> 21.1 us
    ppermute x5, waiting for transfers between devices: 10.6 us -> 20.2 us  [the longest x1 7.86 us: per_device_line(): mid_out = lax.ppermute(mid, 'ex', OUTWARD)]
    ppermute x1, waiting for transfers between devices: 3.75 us -> 0.01 us  [per_device_line(): raw_near = lax.ppermute(raw, 'ex', PAIRS)]
    ppermute x1, waiting for transfers between devices: 5.08 us -> 8.64 us  [per_device_line(): near = lax.ppermute(late, 'ex', PAIRS)]
    pallas_call x1, Pallas kernels: 8.4 us -> 5.17 us  [regroup(): pl.pallas_call(regroup_kernel, out_shape=jax.ShapeDtypeStruct((rows, n, w...]
    ppermute x1, starting transfers between devices: 3.5 us -> 2.73 us  [per_device_line(): near = lax.ppermute(late, 'ex', PAIRS)]
    unnamed x8 -> x6, local copies, waits for them, and re-layouts: 1.91 us -> 1.91 us
  transfers between devices with their start and end apart: 15 -> 15, of which waited for: 7 -> 6; matrix products, arithmetic and copies ran while one was open for 2% -> 2% of each run, Pallas kernels for 25% -> 20%
where the time goes in v9:
time: 76.4 us; the launch traced here: 76 us
  waiting for transfers between devices  33 us (43%)
  starting transfers between devices  21.1 us (28%)
  Pallas kernels  16.7 us (22%)
  local copies, waits for them, and re-layouts  3.98 us (5%)
  other arithmetic  0.98 us (1%)
    ppermute x1, waiting for transfers between devices, per_device_line(): near = lax.ppermute(late, 'ex', PAIRS)  8.64 us
    ppermute x1, waiting for transfers between devices, per_device_line(): mid_out = lax.ppermute(mid, 'ex', OUTWARD)  7.86 us
    pallas_call x3, Pallas kernels, score_call(): pl.pallas_call(functools.partial(kernel, ex), out_shape=out_shape, in_spe...  7.68 us
    ppermute x1, waiting for transfers between devices, per_device_line(): raw_far_out = lax.ppermute(after(raw_far_mid, near), 'ex', OUTWARD)  7.17 us
    pallas_call x1, Pallas kernels, regroup(): pl.pallas_call(regroup_kernel, out_shape=jax.ShapeDtypeStruct((rows, n, w...  5.17 us
    ppermute x1, waiting for transfers between devices, per_device_line(): raw_mid_out = lax.ppermute(after(raw_mid, grads), 'ex', OUTWARD)  5.14 us
    ppermute x1, starting transfers between devices, per_device_line(): raw_near = lax.ppermute(raw, 'ex', PAIRS)  4.45 us
    pallas_call x3, Pallas kernels, condition(): pl.pallas_call(condition_kernel, out_shape=jax.ShapeDtypeStruct((rows, co...  3.79 us
  transfers between devices with their start and end apart: 15, of which 6 were waited for; matrix products, arithmetic and copies ran while one was open for 2% of the time, Pallas kernels for 20%

profile of v9, /device:TPU:0, one launch (start us, length us, event | category | flops | bytes accessed | tf_op | source)
XLA Modules:
  0.0 76.0 jit_solution(9723852841011451442)
XLA Ops:
  0.0 1.1 %slice_bitcast_fusion.own_ref = bf16[8,128,256]{2,1,0:T(8,128)(2,1)S(1)} fusion(bf16[1,12,128,256]{3,2,1,0:T(8,128)(2,1)} %param.6), kind=kLoop, calls=%fused_computation.2 | loop fusion | bytes 1048576 | tf_op jit(solution)/shard_map/squeeze | solution.py:205
  1.1 3.0 %collective-permute-start.2 = (bf16[8,128,256]{2,1,0:T(8,128)(2,1)S(1)}, bf16[8,128,256]{2,1,0:T(8,128)(2,1)S(1)}, u32[]{:S(2)}, u32[]{:S(2)}) collective-permute-start(bf16[8,128,256]{2,1,0:T(8,128)(2,1)S(1)} %slice_bitcast_fusion.own_ref), channel_id=1, source_target_pairs={{0,2},{2,0},{1,3},{3,1},{4,6},{6,4},{5,7},{7,5},{8,10},{10,8},{9,1... | collective-permute-start | bytes 1572872 | tf_op jit(solution)/shard_map/ppermute | solution.py:206
  4.1 1.0 %slice_bitcast_fusion.1 = bf16[4,128,256]{2,1,0:T(8,128)(2,1)S(1)} fusion(bf16[1,12,128,256]{3,2,1,0:T(8,128)(2,1)} %param.6), kind=kLoop, calls=%fused_computation.3 | loop fusion | bytes 524288 | tf_op jit(solution)/shard_map/squeeze | solution.py:207
  5.1 0.7 collective-permute-start.1
  5.7 4.4 %collective-permute-start = (bf16[4,128,256]{2,1,0:T(8,128)(2,1)S(1)}, bf16[4,128,256]{2,1,0:T(8,128)(2,1)S(1)}, u32[]{:S(2)}, u32[]{:S(2)}) collective-permute-start(bf16[4,128,256]{2,1,0:T(8,128)(2,1)S(1)} %slice_bitcast_fusion.1), channel_id=1, source_target_pairs={{0,4},{4,0},{8,12},{12,8},{1,5},{5,1},{9,13},{13,9},{2,6},{6,2},{1... | collective-permute-start | bytes 786440 | tf_op jit(solution)/shard_map/ppermute | solution.py:209
  10.2 0.9 %copy-done = f32[256,256]{1,0:T(8,128)S(1)} copy-done((f32[256,256]{1,0:T(8,128)S(1)}, f32[256,256]{1,0:T(8,128)}, u32[]{:S(2)}) %copy-start) | copy-done | bytes 262168
  11.1 0.9 %copy-done.1 = f32[256,256]{1,0:T(8,128)S(1)} copy-done((f32[256,256]{1,0:T(8,128)S(1)}, f32[256,256]{1,0:T(8,128)}, u32[]{:S(2)}) %copy-start.1) | copy-done | bytes 262168
  12.2 5.2 %shard_map.56.grad_ref = bf16[128,128,256]{2,1,0:T(8,128)(2,1)S(1)} custom-call(bf16[128,128,256]{2,1,0:T(8,128)(2,1)} %grads_ref), custom_call_target="tpu_custom_call" | custom-call | flops 1000 | bytes 1000 | tf_op jit(solution)/shard_map/pallas_call | solution.py:106
  17.4 0.7 collective-permute-start.5
  18.1 1.3 %collective-permute-start.6 = (bf16[4,128,256]{2,1,0:T(8,128)(2,1)S(1)}, bf16[4,128,256]{2,1,0:T(8,128)(2,1)S(1)}, u32[]{:S(2)}, u32[]{:S(2)}) collective-permute-start(bf16[4,128,256]{2,1,0:T(8,128)(2,1)S(1)} %collective-permute-done.1), channel_id=1, source_target_pairs={{4,0},{8,12},{5,1},{9,13},{6,2},{10,14},{7,3},{11,15},{20,16},{24,... | collective-permute-start | bytes 786440 | tf_op jit(solution)/shard_map/ppermute | solution.py:212
  19.4 1.3 %shard_map.57.own_ref = bf16[128,8,256]{2,1,0:T(8,128)(2,1)S(1)} custom-call(bf16[8,128,256]{2,1,0:T(8,128)(2,1)S(1)} %slice_bitcast_fusion.own_ref, bf16[8,128,256]{2,1,0:T(8,128)(2,1)S(1)} %collective-permute-done.2.far_ref, bf16[384,256]{1,0:T(8,128)(2,1)S(1)} %get-tuple-element.25.left_ref, bf16[512,256]{1,0:T(8,128)(2,1)S(1)} %get-tuple-element.26.right_ref), custom_call_target="tpu_custom_call" | custom-call | flops 960000000 | bytes 2097152 | tf_op jit(solution)/shard_map/pallas_call | solution.py:70
  20.7 2.7 %collective-permute-start.3 = (bf16[128,8,256]{2,1,0:T(8,128)(2,1)S(1)}, bf16[128,8,256]{2,1,0:T(8,128)(2,1)S(1)}, u32[]{:S(2)}, u32[]{:S(2)}) collective-permute-start(bf16[128,8,256]{2,1,0:T(8,128)(2,1)S(1)} %shard_map.57.own_ref), channel_id=1, source_target_pairs={{0,4},{4,0},{8,12},{12,8},{1,5},{5,1},{9,13},{13,9},{2,6},{6,2},{1... | collective-permute-start | bytes 1572872 | tf_op jit(solution)/shard_map/ppermute | solution.py:217
  23.4 0.7 collective-permute-start.4
  24.1 5.1 %collective-permute-done.6 = bf16[4,128,256]{2,1,0:T(8,128)(2,1)S(1)} collective-permute-done((bf16[4,128,256]{2,1,0:T(8,128)(2,1)S(1)}, bf16[4,128,256]{2,1,0:T(8,128)(2,1)S(1)}, u32[]{:S(2)}, u32[]{:S(2)}) %collective-permute-start.6) | collective-permute-done | bytes 262176 | tf_op jit(solution)/shard_map/ppermute | solution.py:212
  29.8 8.6 %collective-permute-done.3.near = bf16[128,8,256]{2,1,0:T(8,128)(2,1)S(1)} collective-permute-done((bf16[128,8,256]{2,1,0:T(8,128)(2,1)S(1)}, bf16[128,8,256]{2,1,0:T(8,128)(2,1)S(1)}, u32[]{:S(2)}, u32[]{:S(2)}) %collective-permute-start.3) | collective-permute-done | bytes 524320 | tf_op jit(solution)/shard_map/ppermute | solution.py:217
  38.4 0.7 collective-permute-start.9
  39.1 1.3 %collective-permute-start.8 = (bf16[4,128,256]{2,1,0:T(8,128)(2,1)S(1)}, bf16[4,128,256]{2,1,0:T(8,128)(2,1)S(1)}, u32[]{:S(2)}, u32[]{:S(2)}) collective-permute-start(bf16[4,128,256]{2,1,0:T(8,128)(2,1)S(1)} %collective-permute-done.5), channel_id=1, source_target_pairs={{4,0},{8,12},{5,1},{9,13},{6,2},{10,14},{7,3},{11,15},{20,16},{24,... | collective-permute-start | bytes 786440 | tf_op jit(solution)/shard_map/ppermute | solution.py:220
  40.5 1.3 %collective-permute-start.11 = (bf16[128,8,256]{2,1,0:T(8,128)(2,1)S(1)}, bf16[128,8,256]{2,1,0:T(8,128)(2,1)S(1)}, u32[]{:S(2)}, u32[]{:S(2)}) collective-permute-start(bf16[128,8,256]{2,1,0:T(8,128)(2,1)S(1)} %collective-permute-done.4), channel_id=1, source_target_pairs={{4,0},{8,12},{5,1},{9,13},{6,2},{10,14},{7,3},{11,15},{20,16},{24,... | collective-permute-start | bytes 1572872 | tf_op jit(solution)/shard_map/ppermute | solution.py:222
  41.8 1.3 %shard_map.58.early_0 = bf16[128,8,256]{2,1,0:T(8,128)(2,1)S(1)} custom-call(bf16[8,128,256]{2,1,0:T(8,128)(2,1)S(1)} %pad_maximum_fusion.own_ref, bf16[8,128,256]{2,1,0:T(8,128)(2,1)S(1)} %collective-permute-done.7.far_ref, bf16[384,256]{1,0:T(8,128)(2,1)S(1)} %get-tuple-element.25.left_ref, bf16[512,256]{1,0:T(8,128)(2,1)S(1)} %get-tuple-element.26.right_ref), custom_call_target="tpu_custom_call" | custom-call | flops 960000000 | bytes 2097152 | tf_op jit(solution)/shard_map/pallas_call | solution.py:70
  43.1 7.2 %collective-permute-done.8 = bf16[4,128,256]{2,1,0:T(8,128)(2,1)S(1)} collective-permute-done((bf16[4,128,256]{2,1,0:T(8,128)(2,1)S(1)}, bf16[4,128,256]{2,1,0:T(8,128)(2,1)S(1)}, u32[]{:S(2)}, u32[]{:S(2)}) %collective-permute-start.8) | collective-permute-done | bytes 262176 | tf_op jit(solution)/shard_map/ppermute | solution.py:220
  50.4 0.6 collective-permute-start.10
  51.1 1.3 %collective-permute-start.12 = (bf16[64,8,256]{2,1,0:T(8,128)(2,1)S(1)}, bf16[64,8,256]{2,1,0:T(8,128)(2,1)S(1)}, u32[]{:S(2)}, u32[]{:S(2)}) collective-permute-start(bf16[64,8,256]{2,1,0:T(8,128)(2,1)S(1)} %get-tuple-element.42), channel_id=1, source_target_pairs={{4,0},{8,12},{5,1},{9,13},{6,2},{10,14},{7,3},{11,15},{20,16},{24,... | collective-permute-start | bytes 786440 | tf_op jit(solution)/shard_map/ppermute | solution.py:227
  52.4 1.3 %collective-permute-start.13 = (bf16[64,8,256]{2,1,0:T(8,128)(2,1)S(1)}, bf16[64,8,256]{2,1,0:T(8,128)(2,1)S(1)}, u32[]{:S(2)}, u32[]{:S(2)}) collective-permute-start(bf16[64,8,256]{2,1,0:T(8,128)(2,1)S(1)} %get-tuple-element.41), channel_id=1, source_target_pairs={{4,0},{8,12},{5,1},{9,13},{6,2},{10,14},{7,3},{11,15},{20,16},{24,... | collective-permute-start | bytes 786440 | tf_op jit(solution)/shard_map/ppermute | solution.py:228
  53.7 7.9 %collective-permute-done.11 = bf16[128,8,256]{2,1,0:T(8,128)(2,1)S(1)} collective-permute-done((bf16[128,8,256]{2,1,0:T(8,128)(2,1)S(1)}, bf16[128,8,256]{2,1,0:T(8,128)(2,1)S(1)}, u32[]{:S(2)}, u32[]{:S(2)}) %collective-permute-start.11) | collective-permute-done | bytes 524320 | tf_op jit(solution)/shard_map/ppermute | solution.py:222
  61.7 1.3 %shard_map.59.early_1 = bf16[128,8,256]{2,1,0:T(8,128)(2,1)S(1)} custom-call(bf16[8,128,256]{2,1,0:T(8,128)(2,1)S(1)} %pad_maximum_fusion.1.own_ref, bf16[8,128,256]{2,1,0:T(8,128)(2,1)S(1)} %collective-permute-done.10.far_ref, bf16[384,256]{1,0:T(8,128)(2,1)S(1)} %get-tuple-element.25.left_ref, bf16[512,256]{1,0:T(8,128)(2,1)S(1)} %get-tuple-element.26.right_ref), custom_call_target="tpu_custom_call" | custom-call | flops 960000000 | bytes 2097152 | tf_op jit(solution)/shard_map/pallas_call | solution.py:70
  63.0 4.0 %shard_map.60.base_ref = f32[48,128]{1,0:T(8,128)S(1)} custom-call(bf16[128,8,256]{2,1,0:T(8,128)(2,1)S(1)} %shard_map.58.early_0, bf16[128,8,256]{2,1,0:T(8,128)(2,1)S(1)} %shard_map.59.early_1, bf16[128,8,256]{2,1,0:T(8,128)(2,1)S(1)} %shard_map.57.own_ref, bf16[128,8,256]{2,1,0:T(8,128)(2,1)S(1)} %collective-permute-done.3.near, ...), custom_call_target="tpu_custom_call" | custom-call | flops 1000 | bytes 1000 | tf_op jit(solution)/shard_map/pallas_call | solution.py:180
  67.0 1.8 %shard_map.61.far_ref = f32[8,128]{1,0:T(8,128)S(1)} custom-call(bf16[64,8,256]{2,1,0:T(8,128)(2,1)S(1)} %collective-permute-done.12.far_out, bf16[128,128,256]{2,1,0:T(8,128)(2,1)S(1)} %shard_map.56.grad_ref, s32[4]{0:T(128)S(1)} %copy-done.2), custom_call_target="tpu_custom_call" | custom-call | flops 1000 | bytes 1000 | tf_op jit(solution)/shard_map/pallas_call | solution.py:180
  68.8 1.0 %collective-permute-done.13.far_out = bf16[64,8,256]{2,1,0:T(8,128)(2,1)S(1)} collective-permute-done((bf16[64,8,256]{2,1,0:T(8,128)(2,1)S(1)}, bf16[64,8,256]{2,1,0:T(8,128)(2,1)S(1)}, u32[]{:S(2)}, u32[]{:S(2)}) %collective-permute-start.13) | collective-permute-done | bytes 262176 | tf_op jit(solution)/shard_map/ppermute | solution.py:228
  69.8 1.9 %shard_map.62 = (f32[24,128]{1,0:T(8,128)S(1)}, f32[24,128]{1,0:T(8,128)S(1)}) custom-call(f32[48,128]{1,0:T(8,128)S(1)} %shard_map.60.base_ref, f32[8,128]{1,0:T(8,128)S(1)} %shard_map.61.far_ref, bf16[64,8,256]{2,1,0:T(8,128)(2,1)S(1)} %collective-permute-done.13.far_out, bf16[128,128,256]{2,1,0:T(8,128)(2,1)S(1)} %shard_map.56.grad_ref, s32[4]{0:T(128)S(1)} %copy-done.2), custom_call_target="tpu_custom_call" | custom-call | flops 1000 | bytes 1000 | tf_op jit(solution)/shard_map/pallas_call | solution.py:180
  71.6 0.6 collective-permute-start.14
  72.3 3.1 %collective-permute-done.14 = f32[24,128]{1,0:T(8,128)S(1)} collective-permute-done((f32[24,128]{1,0:T(8,128)S(1)}, f32[24,128]{1,0:T(8,128)S(1)}, u32[]{:S(2)}, u32[]{:S(2)}) %collective-permute-start.14) | collective-permute-done | bytes 12320 | tf_op jit(solution)/shard_map/ppermute | solution.py:244
  75.4 0.6 add_bitcast_fusion
  (21 shorter events, 1.1 us)
Async XLA Ops:
  1.1 18.3 %collective-permute-start.2 = (bf16[8,128,256]{2,1,0:T(8,128)(2,1)S(1)}, bf16[8,128,256]{2,1,0:T(8,128)(2,1)S(1)}, u32[]{:S(2)}, u32[]{:S(2)}) collective-permute-start(bf16[8,128,256]{2,1,0:T(8,128)(2,1)S(1)} %slice_bitcast_fusion.own_ref), channel_id=1, source_target_pairs={{0,2},{2,0},{1,3},{3,1},{4,6},{6,4},{5,7},{7,5},{8,10},{10,8},{9,1... | collective-permute-start | bytes 1572872 | tf_op jit(solution)/shard_map/ppermute | solution.py:206
  5.1 12.3 %collective-permute-start.1 = (bf16[4,128,256]{2,1,0:T(8,128)(2,1)S(1)}, bf16[4,128,256]{2,1,0:T(8,128)(2,1)S(1)}, u32[]{:S(2)}, u32[]{:S(2)}) collective-permute-start(bf16[4,128,256]{2,1,0:T(8,128)(2,1)S(1)} %slice_bitcast_fusion.1), channel_id=1, source_target_pairs={{4,8},{8,4},{5,9},{9,5},{6,10},{10,6},{7,11},{11,7},{20,24},{24,20... | collective-permute-start | bytes 786440 | tf_op jit(solution)/shard_map/ppermute | solution.py:210
  5.7 11.6 %collective-permute-start = (bf16[4,128,256]{2,1,0:T(8,128)(2,1)S(1)}, bf16[4,128,256]{2,1,0:T(8,128)(2,1)S(1)}, u32[]{:S(2)}, u32[]{:S(2)}) collective-permute-start(bf16[4,128,256]{2,1,0:T(8,128)(2,1)S(1)} %slice_bitcast_fusion.1), channel_id=1, source_target_pairs={{0,4},{4,0},{8,12},{12,8},{1,5},{5,1},{9,13},{13,9},{2,6},{6,2},{1... | collective-permute-start | bytes 786440 | tf_op jit(solution)/shard_map/ppermute | solution.py:209
  10.2 0.9 %copy-start = (f32[256,256]{1,0:T(8,128)S(1)}, f32[256,256]{1,0:T(8,128)}, u32[]{:S(2)}) copy-start(f32[256,256]{1,0:T(8,128)} %left_ref.1) | copy-start | bytes 786436
  11.1 0.9 %copy-start.1 = (f32[256,256]{1,0:T(8,128)S(1)}, f32[256,256]{1,0:T(8,128)}, u32[]{:S(2)}) copy-start(f32[256,256]{1,0:T(8,128)} %right_ref) | copy-start | bytes 786436
  17.4 45.6 %copy-start.2 = (s32[4]{0:T(128)S(1)}, s32[4]{0:T(128)}, u32[]{:S(2)}) copy-start(s32[4]{0:T(128)} %order_ref.5) | copy-start | bytes 52
  17.4 6.7 %collective-permute-start.5 = (bf16[4,128,256]{2,1,0:T(8,128)(2,1)S(1)}, bf16[4,128,256]{2,1,0:T(8,128)(2,1)S(1)}, u32[]{:S(2)}, u32[]{:S(2)}) collective-permute-start(bf16[4,128,256]{2,1,0:T(8,128)(2,1)S(1)} %collective-permute-done), channel_id=1, source_target_pairs={{4,8},{8,4},{5,9},{9,5},{6,10},{10,6},{7,11},{11,7},{20,24},{24,20... | collective-permute-start | bytes 786440 | tf_op jit(solution)/shard_map/ppermute | solution.py:214
  18.1 11.1 %collective-permute-start.6 = (bf16[4,128,256]{2,1,0:T(8,128)(2,1)S(1)}, bf16[4,128,256]{2,1,0:T(8,128)(2,1)S(1)}, u32[]{:S(2)}, u32[]{:S(2)}) collective-permute-start(bf16[4,128,256]{2,1,0:T(8,128)(2,1)S(1)} %collective-permute-done.1), channel_id=1, source_target_pairs={{4,0},{8,12},{5,1},{9,13},{6,2},{10,14},{7,3},{11,15},{20,16},{24,... | collective-permute-start | bytes 786440 | tf_op jit(solution)/shard_map/ppermute | solution.py:212
  20.7 17.7 %collective-permute-start.3 = (bf16[128,8,256]{2,1,0:T(8,128)(2,1)S(1)}, bf16[128,8,256]{2,1,0:T(8,128)(2,1)S(1)}, u32[]{:S(2)}, u32[]{:S(2)}) collective-permute-start(bf16[128,8,256]{2,1,0:T(8,128)(2,1)S(1)} %shard_map.57.own_ref), channel_id=1, source_target_pairs={{0,4},{4,0},{8,12},{12,8},{1,5},{5,1},{9,13},{13,9},{2,6},{6,2},{1... | collective-permute-start | bytes 1572872 | tf_op jit(solution)/shard_map/ppermute | solution.py:217
  23.4 17.1 %collective-permute-start.4 = (bf16[128,8,256]{2,1,0:T(8,128)(2,1)S(1)}, bf16[128,8,256]{2,1,0:T(8,128)(2,1)S(1)}, u32[]{:S(2)}, u32[]{:S(2)}) collective-permute-start(bf16[128,8,256]{2,1,0:T(8,128)(2,1)S(1)} %shard_map.57.own_ref), channel_id=1, source_target_pairs={{4,8},{8,4},{5,9},{9,5},{6,10},{10,6},{7,11},{11,7},{20,24},{24,20... | collective-permute-start | bytes 1572872 | tf_op jit(solution)/shard_map/ppermute | solution.py:218
  29.3 12.5 %collective-permute-start.7 = (bf16[8,128,256]{2,1,0:T(8,128)(2,1)S(1)}, bf16[8,128,256]{2,1,0:T(8,128)(2,1)S(1)}, u32[]{:S(2)}, u32[]{:S(2)}) collective-permute-start(bf16[8,128,256]{2,1,0:T(8,128)(2,1)S(1)} %pad_maximum_fusion.own_ref), channel_id=1, source_target_pairs={{0,2},{2,0},{1,3},{3,1},{4,6},{6,4},{5,7},{7,5},{8,10},{10,8},{9,1... | collective-permute-start | bytes 1572872 | tf_op jit(solution)/shard_map/ppermute | solution.py:219
  38.4 12.6 %collective-permute-start.9 = (bf16[128,8,256]{2,1,0:T(8,128)(2,1)S(1)}, bf16[128,8,256]{2,1,0:T(8,128)(2,1)S(1)}, u32[]{:S(2)}, u32[]{:S(2)}) collective-permute-start(bf16[128,8,256]{2,1,0:T(8,128)(2,1)S(1)} %collective-permute-done.3.near), channel_id=1, source_target_pairs={{4,8},{8,4},{5,9},{9,5},{6,10},{10,6},{7,11},{11,7},{20,24},{24,20... | collective-permute-start | bytes 1572872 | tf_op jit(solution)/shard_map/ppermute | solution.py:221
  39.1 11.1 %collective-permute-start.8 = (bf16[4,128,256]{2,1,0:T(8,128)(2,1)S(1)}, bf16[4,128,256]{2,1,0:T(8,128)(2,1)S(1)}, u32[]{:S(2)}, u32[]{:S(2)}) collective-permute-start(bf16[4,128,256]{2,1,0:T(8,128)(2,1)S(1)} %collective-permute-done.5), channel_id=1, source_target_pairs={{4,0},{8,12},{5,1},{9,13},{6,2},{10,14},{7,3},{11,15},{20,16},{24,... | collective-permute-start | bytes 786440 | tf_op jit(solution)/shard_map/ppermute | solution.py:220
  40.5 21.0 %collective-permute-start.11 = (bf16[128,8,256]{2,1,0:T(8,128)(2,1)S(1)}, bf16[128,8,256]{2,1,0:T(8,128)(2,1)S(1)}, u32[]{:S(2)}, u32[]{:S(2)}) collective-permute-start(bf16[128,8,256]{2,1,0:T(8,128)(2,1)S(1)} %collective-permute-done.4), channel_id=1, source_target_pairs={{4,0},{8,12},{5,1},{9,13},{6,2},{10,14},{7,3},{11,15},{20,16},{24,... | collective-permute-start | bytes 1572872 | tf_op jit(solution)/shard_map/ppermute | solution.py:222
  50.4 11.3 %collective-permute-start.10 = (bf16[8,128,256]{2,1,0:T(8,128)(2,1)S(1)}, bf16[8,128,256]{2,1,0:T(8,128)(2,1)S(1)}, u32[]{:S(2)}, u32[]{:S(2)}) collective-permute-start(bf16[8,128,256]{2,1,0:T(8,128)(2,1)S(1)} %pad_maximum_fusion.1.own_ref), channel_id=1, source_target_pairs={{0,2},{2,0},{1,3},{3,1},{4,6},{6,4},{5,7},{7,5},{8,10},{10,8},{9,1... | collective-permute-start | bytes 1572872 | tf_op jit(solution)/shard_map/ppermute | solution.py:225
  51.1 15.9 %collective-permute-start.12 = (bf16[64,8,256]{2,1,0:T(8,128)(2,1)S(1)}, bf16[64,8,256]{2,1,0:T(8,128)(2,1)S(1)}, u32[]{:S(2)}, u32[]{:S(2)}) collective-permute-start(bf16[64,8,256]{2,1,0:T(8,128)(2,1)S(1)} %get-tuple-element.42), channel_id=1, source_target_pairs={{4,0},{8,12},{5,1},{9,13},{6,2},{10,14},{7,3},{11,15},{20,16},{24,... | collective-permute-start | bytes 786440 | tf_op jit(solution)/shard_map/ppermute | solution.py:227
  52.4 17.4 %collective-permute-start.13 = (bf16[64,8,256]{2,1,0:T(8,128)(2,1)S(1)}, bf16[64,8,256]{2,1,0:T(8,128)(2,1)S(1)}, u32[]{:S(2)}, u32[]{:S(2)}) collective-permute-start(bf16[64,8,256]{2,1,0:T(8,128)(2,1)S(1)} %get-tuple-element.41), channel_id=1, source_target_pairs={{4,0},{8,12},{5,1},{9,13},{6,2},{10,14},{7,3},{11,15},{20,16},{24,... | collective-permute-start | bytes 786440 | tf_op jit(solution)/shard_map/ppermute | solution.py:228
  71.6 3.8 %collective-permute-start.14 = (f32[24,128]{1,0:T(8,128)S(1)}, f32[24,128]{1,0:T(8,128)S(1)}, u32[]{:S(2)}, u32[]{:S(2)}) collective-permute-start(f32[24,128]{1,0:T(8,128)S(1)} %get-tuple-element.40), channel_id=1, source_target_pairs={{0,2},{2,0},{1,3},{3,1},{4,6},{6,4},{5,7},{7,5},{8,10},{10,8},{9,1... | collective-permute-start | bytes 36872 | tf_op jit(solution)/shard_map/ppermute | solution.py:244

commit v10 on v9

--- a/solution.py
+++ b/solution.py
@@ -62,17 +62,20 @@
         both = jnp.dot(jnp.concatenate([mixed_0, mixed_1], axis=0), right_0, preferred_element_type=F32)
         cross = jnp.dot(mixed_0, right_1, preferred_element_type=F32)
         wide_ref[:, q, :] = both[:rows] + (both[rows:] + cross)
+    for q in range(count, out_ref.shape[1]):
+        wide_ref[:, q, :] = jnp.zeros((rows, width), F32)
     out_ref[...] = wide_ref[...].astype(BF16)
 
 
 def condition(own, far, left_terms, right_terms):
     count, rows, width = own.shape
+    padded = -(-count // 8) * 8
     return pl.pallas_call(
         condition_kernel,
-        out_shape=jax.ShapeDtypeStruct((rows, count, width), BF16),
+        out_shape=jax.ShapeDtypeStruct((rows, padded, width), BF16),
         in_specs=[VMEM] * 4,
         out_specs=VMEM,
-        scratch_shapes=[pltpu.VMEM((rows, count, width), F32)],
+        scratch_shapes=[pltpu.VMEM((rows, padded, width), F32)],
         compiler_params=pltpu.CompilerParams(vmem_limit_bytes=24 << 20),
         cost_estimate=pl.CostEstimate(flops=count * 3_000_000 * 40, bytes_accessed=8 * count * rows * width, transcendentals=0),
     )(own, far, left_terms, right_terms)
@@ -114,12 +117,16 @@
     )(grads)
 
 
-def inner_products(query_refs, grad_ref, first=0):
+def inner_products(query_refs, grad_ref, first=0, rows=None):
     total = sum(ref.shape[1] for ref in query_refs)
+    rows = rows or grad_ref.shape[0]
+    starts = [0 if ref.shape[0] == rows else first for ref in query_refs]
 
     def body(i, acc):
         at = [i * DEEP + j for j in range(DEEP)]
-        queries = [jnp.concatenate([ref[r] for ref in query_refs], axis=0) for r in at]
+        queries = [
+            jnp.concatenate([ref[start + r] for ref, start in zip(query_refs, starts)], axis=0) for r in at
+        ]
         return acc + lax.dot_general(
             jnp.concatenate(queries, axis=1),
             jnp.concatenate([grad_ref[first + r] for r in at], axis=1),
@@ -128,25 +135,24 @@
         )
 
     start = jnp.zeros((total, grad_ref.shape[1]), F32)
-    return lax.fori_loop(0, query_refs[0].shape[0] // DEEP, body, start)
-
-
-def first_pass_kernel(ex, early_0, early_1, own_ref, near, mid, far_in, grad_ref, order_ref, out_ref):
+    return lax.fori_loop(0, rows // DEEP, body, start)
+
+
+def first_pass_kernel(ex, early_ref, own_ref, near, mid, far_in, grad_ref, order_ref, out_ref):
     late = own_ref.shape[1]
-    acc = inner_products((early_0, early_1, own_ref, near, mid, far_in), grad_ref)
-    me = lax.axis_index("ex")
-    sources = slot_sources(me)
-    early = [acc[EARLY * s : EARLY * (s + 1)] for s in range(ex)]
-    base = EARLY * ex
-    slots = [acc[base + late * s : base + late * (s + 1)] for s in range(4)]
+    acc = inner_products((early_ref, own_ref, near, mid, far_in), grad_ref)
+    sources = slot_sources(lax.axis_index("ex"))
+    early = [acc[EARLY * s : EARLY * (s + 1)] for s in range(ex - 1)]
+    base = early_ref.shape[1]
+    slots = [acc[base + late * s : base + late * (s + 1)] for s in range(ex)]
     for b in range(ex):
         block = order_ref[b]
         low = jnp.zeros_like(early[0])
+        for source, slot in zip(sources, early):
+            low = low + jnp.where(source == block, slot, 0.0)
         high = jnp.zeros_like(slots[0])
-        for s in range(ex):
-            hit = sources[s] == block
-            low = low + jnp.where(hit, early[s], 0.0)
-            high = high + jnp.where(hit, slots[s], 0.0)
+        for source, slot in zip(sources, slots):
+            high = high + jnp.where(source == block, slot, 0.0)
         at = b * (EARLY + late)
         out_ref[at : at + EARLY, :] = low
         out_ref[at + EARLY : at + EARLY + late, :] = high
@@ -158,18 +164,21 @@
     return [me, near, jnp.where(low_pair, 2, 1), jnp.where(low_pair, 3, 0)]
 
 
-def far_pass_kernel(ex, far_out, grad_ref, order_ref, out_ref):
-    out_ref[...] = inner_products((far_out,), grad_ref)
-
-
-def last_pass_kernel(ex, base_ref, far_ref, far_out, grad_ref, order_ref, mine_ref, send_ref, full_ref):
+def far_pass_kernel(ex, early_ref, far_out, grad_ref, order_ref, out_ref):
+    out_ref[...] = inner_products((early_ref, far_out), grad_ref, 0, far_out.shape[0])
+
+
+def last_pass_kernel(ex, base_ref, far_ref, early_ref, far_out, grad_ref, order_ref, mine_ref, send_ref, full_ref):
     late = far_out.shape[1]
-    acc = far_ref[...] + inner_products((far_out,), grad_ref, far_out.shape[0])
+    acc = far_ref[...] + inner_products((early_ref, far_out), grad_ref, far_out.shape[0], far_out.shape[0])
     far = slot_sources(lax.axis_index("ex"))[3]
     full_ref[...] = base_ref[...]
     for b in range(ex):
-        at = b * (EARLY + late) + EARLY
-        full_ref[at : at + late, :] = full_ref[at : at + late, :] + jnp.where(order_ref[b] == far, acc, 0.0)
+        hit = order_ref[b] == far
+        at = b * (EARLY + late)
+        full_ref[at : at + EARLY, :] = full_ref[at : at + EARLY, :] + jnp.where(hit, acc[:EARLY], 0.0)
+        at = at + EARLY
+        full_ref[at : at + late, :] = full_ref[at : at + late, :] + jnp.where(hit, acc[early_ref.shape[1] :], 0.0)
     half = mine_ref.shape[0]
     side = lax.axis_index("feat")
     mine_ref[...] = full_ref[pl.ds(pl.multiple_of(side * half, half), half), :]
@@ -210,18 +219,18 @@
     raw_mid = lax.ppermute(raw, "ex", MIDDLE)
     grads = regroup(after(train_grads, *terms))
     raw_mid_out = lax.ppermute(after(raw_mid, grads), "ex", OUTWARD)
-    early_0 = jnp.concatenate([raw, after(raw_near, raw_mid, grads)], axis=0)
-    raw_far_mid = lax.ppermute(after(raw_near, early_0), "ex", MIDDLE)
+    raw_far_mid = lax.ppermute(after(raw_near, late_other), "ex", MIDDLE)
 
     late = condition(after(late_raw, raw_near, raw_mid, grads), late_other, *terms)
+    mid = lax.ppermute(late, "ex", MIDDLE)
     near = lax.ppermute(late, "ex", PAIRS)
-    mid = lax.ppermute(late, "ex", MIDDLE)
-    early_0_other = lax.ppermute(after(early_0, late, raw_far_mid, raw_mid_out), "feat", swap)
-    raw_far_out = lax.ppermute(after(raw_far_mid, near), "ex", OUTWARD)
+    early_0 = jnp.concatenate([raw, raw_near, raw_mid + raw_mid_out], axis=0)
+    early_0_other = lax.ppermute(after(early_0, late, raw_far_mid), "feat", swap)
+    raw_far_out = lax.ppermute(after(raw_far_mid, mid), "ex", OUTWARD)
+    mid_out = lax.ppermute(mid, "ex", OUTWARD)
     far_mid = lax.ppermute(near, "ex", MIDDLE)
-    mid_out = lax.ppermute(mid, "ex", OUTWARD)
+    early_1 = raw_far_mid + raw_far_out
     cond_0 = condition(after(early_0, near, mid), early_0_other, *terms)
-    early_1 = jnp.concatenate([raw_mid + raw_mid_out, after(raw_far_mid, near, mid) + raw_far_out], axis=0)
     early_1_other = lax.ppermute(after(early_1, cond_0), "feat", swap)
     part = far_mid.shape[0] // 2
     far_out_0 = lax.ppermute(far_mid[:part], "ex", OUTWARD)
@@ -229,16 +238,16 @@
     cond_1 = condition(after(early_1, far_mid), early_1_other, *terms)
 
     base = score_call(
-        first_pass_kernel, ex, (cond_0, cond_1, late, near, mid + mid_out, far_mid, grads), block_order,
+        first_pass_kernel, ex, (cond_0, late, near, mid + mid_out, far_mid, grads), block_order,
         jax.ShapeDtypeStruct((ex * count, n), F32),
     )
     far_0 = score_call(
-        far_pass_kernel, ex, (far_out_0, after(grads, base)), block_order,
-        jax.ShapeDtypeStruct((count - EARLY, n), F32),
+        far_pass_kernel, ex, (cond_1, far_out_0, after(grads, base)), block_order,
+        jax.ShapeDtypeStruct((cond_1.shape[1] + count - EARLY, n), F32),
     )
     half = jax.ShapeDtypeStruct((ex * count // 2, n), F32)
     mine, send = score_call(
-        last_pass_kernel, ex, (base, far_0, far_out_1, grads), block_order, (half, half),
+        last_pass_kernel, ex, (base, far_0, cond_1, far_out_1, grads), block_order, (half, half),
         [pltpu.VMEM((ex * count, n), F32)],
     )
     scores = mine + lax.ppermute(send, "feat", swap)

time: 76.4 us -> 76.2 us (level)
  waiting for transfers between devices: 33 us -> 30.3 us
  starting transfers between devices: 21.1 us -> 22.8 us
    ppermute x3, waiting for transfers between devices: 7.18 us -> 10.4 us  [the longest x1 10.4 us: per_device_line(): raw_far_out = lax.ppermute(after(raw_far_mid, mid), 'ex', OUTWARD)]
    ppermute x1, waiting for transfers between devices: 5.14 us -> 2.77 us  [per_device_line(): raw_mid_out = lax.ppermute(after(raw_mid, grads), 'ex', OUTWARD)]
    ppermute x1, waiting for transfers between devices: 7.86 us -> 5.54 us  [per_device_line(): mid_out = lax.ppermute(mid, 'ex', OUTWARD)]
    ppermute x1, starting transfers between devices: 2.73 us -> 4.4 us  [per_device_line(): near = lax.ppermute(late, 'ex', PAIRS)]
    ppermute x1, waiting for transfers between devices: 0.96 us -> 0.01 us  [per_device_line(): far_out_1 = lax.ppermute(far_mid[part:], 'ex', OUTWARD)]
  transfers between devices with their start and end apart: 15 -> 15, of which waited for: 6 -> 5; matrix products, arithmetic and copies ran while one was open for 2% -> 2% of each run, Pallas kernels for 20% -> 21%
where the time goes in v10:
time: 76.2 us; the launch traced here: 75.8 us
  waiting for transfers between devices  30.3 us (40%)
  starting transfers between devices  22.8 us (30%)
  Pallas kernels  17.4 us (23%)
  local copies, waits for them, and re-layouts  3.98 us (5%)
  other arithmetic  0.98 us (1%)
    ppermute x1, waiting for transfers between devices, per_device_line(): raw_far_out = lax.ppermute(after(raw_far_mid, mid), 'ex', OUTWARD)  10.4 us
    ppermute x1, waiting for transfers between devices, per_device_line(): near = lax.ppermute(late, 'ex', PAIRS)  8.4 us
    pallas_call x3, Pallas kernels, score_call(): pl.pallas_call(functools.partial(kernel, ex), out_shape=out_shape, in_spe...  7.68 us
    ppermute x1, waiting for transfers between devices, per_device_line(): mid_out = lax.ppermute(mid, 'ex', OUTWARD)  5.54 us
    pallas_call x1, Pallas kernels, regroup(): pl.pallas_call(regroup_kernel, out_shape=jax.ShapeDtypeStruct((rows, n, w...  5.17 us
    pallas_call x3, Pallas kernels, condition(): pl.pallas_call(condition_kernel, out_shape=jax.ShapeDtypeStruct((rows, pa...  4.52 us
    ppermute x1, starting transfers between devices, per_device_line(): raw_near = lax.ppermute(raw, 'ex', PAIRS)  4.45 us
    ppermute x1, starting transfers between devices, per_device_line(): near = lax.ppermute(late, 'ex', PAIRS)  4.4 us
  transfers between devices with their start and end apart: 15, of which 5 were waited for; matrix products, arithmetic and copies ran while one was open for 2% of the time, Pallas kernels for 21%

profile of v10, /device:TPU:0, one launch (start us, length us, event | category | flops | bytes accessed | tf_op | source)
XLA Modules:
  0.0 75.8 jit_solution(16428121312556507979)
XLA Ops:
  0.0 1.1 %slice_bitcast_fusion.own_ref = bf16[8,128,256]{2,1,0:T(8,128)(2,1)S(1)} fusion(bf16[1,12,128,256]{3,2,1,0:T(8,128)(2,1)} %param.6), kind=kLoop, calls=%fused_computation.1 | loop fusion | bytes 1048576 | tf_op jit(solution)/shard_map/squeeze | solution.py:214
  1.1 3.0 %collective-permute-start.3 = (bf16[8,128,256]{2,1,0:T(8,128)(2,1)S(1)}, bf16[8,128,256]{2,1,0:T(8,128)(2,1)S(1)}, u32[]{:S(2)}, u32[]{:S(2)}) collective-permute-start(bf16[8,128,256]{2,1,0:T(8,128)(2,1)S(1)} %slice_bitcast_fusion.own_ref), channel_id=1, source_target_pairs={{0,2},{2,0},{1,3},{3,1},{4,6},{6,4},{5,7},{7,5},{8,10},{10,8},{9,1... | collective-permute-start | bytes 1572872 | tf_op jit(solution)/shard_map/ppermute | solution.py:215
  4.1 1.0 %slice_bitcast_fusion.1 = bf16[4,128,256]{2,1,0:T(8,128)(2,1)S(1)} fusion(bf16[1,12,128,256]{3,2,1,0:T(8,128)(2,1)} %param.6), kind=kLoop, calls=%fused_computation.2 | loop fusion | bytes 524288 | tf_op jit(solution)/shard_map/squeeze | solution.py:216
  5.1 0.7 collective-permute-start.1
  5.7 4.4 %collective-permute-start = (bf16[4,128,256]{2,1,0:T(8,128)(2,1)S(1)}, bf16[4,128,256]{2,1,0:T(8,128)(2,1)S(1)}, u32[]{:S(2)}, u32[]{:S(2)}) collective-permute-start(bf16[4,128,256]{2,1,0:T(8,128)(2,1)S(1)} %slice_bitcast_fusion.1), channel_id=1, source_target_pairs={{0,4},{4,0},{8,12},{12,8},{1,5},{5,1},{9,13},{13,9},{2,6},{6,2},{1... | collective-permute-start | bytes 786440 | tf_op jit(solution)/shard_map/ppermute | solution.py:218
  10.2 0.9 %copy-done = f32[256,256]{1,0:T(8,128)S(1)} copy-done((f32[256,256]{1,0:T(8,128)S(1)}, f32[256,256]{1,0:T(8,128)}, u32[]{:S(2)}) %copy-start) | copy-done | bytes 262168
  11.1 0.9 %copy-done.1 = f32[256,256]{1,0:T(8,128)S(1)} copy-done((f32[256,256]{1,0:T(8,128)S(1)}, f32[256,256]{1,0:T(8,128)}, u32[]{:S(2)}) %copy-start.1) | copy-done | bytes 262168
  12.2 5.2 %shard_map.56.grad_ref = bf16[128,128,256]{2,1,0:T(8,128)(2,1)S(1)} custom-call(bf16[128,128,256]{2,1,0:T(8,128)(2,1)} %grads_ref), custom_call_target="tpu_custom_call" | custom-call | flops 1000 | bytes 1000 | tf_op jit(solution)/shard_map/pallas_call | solution.py:109
  17.4 1.3 %collective-permute-start.2 = (bf16[4,128,256]{2,1,0:T(8,128)(2,1)S(1)}, bf16[4,128,256]{2,1,0:T(8,128)(2,1)S(1)}, u32[]{:S(2)}, u32[]{:S(2)}) collective-permute-start(bf16[4,128,256]{2,1,0:T(8,128)(2,1)S(1)} %collective-permute-done.1), channel_id=1, source_target_pairs={{4,0},{8,12},{5,1},{9,13},{6,2},{10,14},{7,3},{11,15},{20,16},{24,... | collective-permute-start | bytes 786440 | tf_op jit(solution)/shard_map/ppermute | solution.py:221
  18.7 0.7 collective-permute-start.6
  19.4 1.3 %shard_map.57.own_ref = bf16[128,8,256]{2,1,0:T(8,128)(2,1)S(1)} custom-call(bf16[8,128,256]{2,1,0:T(8,128)(2,1)S(1)} %slice_bitcast_fusion.own_ref, bf16[8,128,256]{2,1,0:T(8,128)(2,1)S(1)} %collective-permute-done.3.far_ref, bf16[384,256]{1,0:T(8,128)(2,1)S(1)} %get-tuple-element.23.left_ref, bf16[512,256]{1,0:T(8,128)(2,1)S(1)} %get-tuple-element.24.right_ref), custom_call_target="tpu_custom_call" | custom-call | flops 960000000 | bytes 2097152 | tf_op jit(solution)/shard_map/pallas_call | solution.py:73
  20.7 4.4 %collective-permute-start.4 = (bf16[128,8,256]{2,1,0:T(8,128)(2,1)S(1)}, bf16[128,8,256]{2,1,0:T(8,128)(2,1)S(1)}, u32[]{:S(2)}, u32[]{:S(2)}) collective-permute-start(bf16[128,8,256]{2,1,0:T(8,128)(2,1)S(1)} %shard_map.57.own_ref), channel_id=1, source_target_pairs={{0,4},{4,0},{8,12},{12,8},{1,5},{5,1},{9,13},{13,9},{2,6},{6,2},{1... | collective-permute-start | bytes 1572872 | tf_op jit(solution)/shard_map/ppermute | solution.py:226
  25.1 0.7 collective-permute-start.5
  25.7 2.8 %collective-permute-done.2 = bf16[4,128,256]{2,1,0:T(8,128)(2,1)S(1)} collective-permute-done((bf16[4,128,256]{2,1,0:T(8,128)(2,1)S(1)}, bf16[4,128,256]{2,1,0:T(8,128)(2,1)S(1)}, u32[]{:S(2)}, u32[]{:S(2)}) %collective-permute-start.2) | collective-permute-done | bytes 262176 | tf_op jit(solution)/shard_map/ppermute | solution.py:221
  28.7 0.6 collective-permute-start.7
  29.3 8.4 %collective-permute-done.4.near = bf16[128,8,256]{2,1,0:T(8,128)(2,1)S(1)} collective-permute-done((bf16[128,8,256]{2,1,0:T(8,128)(2,1)S(1)}, bf16[128,8,256]{2,1,0:T(8,128)(2,1)S(1)}, u32[]{:S(2)}, u32[]{:S(2)}) %collective-permute-start.4) | collective-permute-done | bytes 524320 | tf_op jit(solution)/shard_map/ppermute | solution.py:226
  37.7 0.7 collective-permute-start.9
  38.4 1.3 %collective-permute-start.10 = (bf16[4,128,256]{2,1,0:T(8,128)(2,1)S(1)}, bf16[4,128,256]{2,1,0:T(8,128)(2,1)S(1)}, u32[]{:S(2)}, u32[]{:S(2)}) collective-permute-start(bf16[4,128,256]{2,1,0:T(8,128)(2,1)S(1)} %collective-permute-done.6), channel_id=1, source_target_pairs={{4,0},{8,12},{5,1},{9,13},{6,2},{10,14},{7,3},{11,15},{20,16},{24,... | collective-permute-start | bytes 786440 | tf_op jit(solution)/shard_map/ppermute | solution.py:229
  39.7 1.3 %collective-permute-start.8 = (bf16[128,8,256]{2,1,0:T(8,128)(2,1)S(1)}, bf16[128,8,256]{2,1,0:T(8,128)(2,1)S(1)}, u32[]{:S(2)}, u32[]{:S(2)}) collective-permute-start(bf16[128,8,256]{2,1,0:T(8,128)(2,1)S(1)} %collective-permute-done.5), channel_id=1, source_target_pairs={{4,0},{8,12},{5,1},{9,13},{6,2},{10,14},{7,3},{11,15},{20,16},{24,... | collective-permute-start | bytes 1572872 | tf_op jit(solution)/shard_map/ppermute | solution.py:230
  41.0 10.4 %collective-permute-done.10 = bf16[4,128,256]{2,1,0:T(8,128)(2,1)S(1)} collective-permute-done((bf16[4,128,256]{2,1,0:T(8,128)(2,1)S(1)}, bf16[4,128,256]{2,1,0:T(8,128)(2,1)S(1)}, u32[]{:S(2)}, u32[]{:S(2)}) %collective-permute-start.10) | collective-permute-done | bytes 262176 | tf_op jit(solution)/shard_map/ppermute | solution.py:229
  51.5 2.4 %shard_map.58.early_ref = bf16[128,16,256]{2,1,0:T(8,128)(2,1)S(1)} custom-call(bf16[12,128,256]{2,1,0:T(8,128)(2,1)S(1)} %pad_maximum_fusion.own_ref, bf16[12,128,256]{2,1,0:T(8,128)(2,1)S(1)} %collective-permute-done.7.far_ref, bf16[384,256]{1,0:T(8,128)(2,1)S(1)} %get-tuple-element.23.left_ref, bf16[512,256]{1,0:T(8,128)(2,1)S(1)} %get-tuple-element.24.right_ref), custom_call_target="tpu_custom_call" | custom-call | flops 1440000000 | bytes 3145728 | tf_op jit(solution)/shard_map/pallas_call | solution.py:73
  53.9 0.6 collective-permute-start.11
  54.5 1.3 %collective-permute-start.12 = (bf16[64,8,256]{2,1,0:T(8,128)(2,1)S(1)}, bf16[64,8,256]{2,1,0:T(8,128)(2,1)S(1)}, u32[]{:S(2)}, u32[]{:S(2)}) collective-permute-start(bf16[64,8,256]{2,1,0:T(8,128)(2,1)S(1)} %get-tuple-element.38), channel_id=1, source_target_pairs={{4,0},{8,12},{5,1},{9,13},{6,2},{10,14},{7,3},{11,15},{20,16},{24,... | collective-permute-start | bytes 786440 | tf_op jit(solution)/shard_map/ppermute | solution.py:236
  55.8 1.3 %collective-permute-start.13 = (bf16[64,8,256]{2,1,0:T(8,128)(2,1)S(1)}, bf16[64,8,256]{2,1,0:T(8,128)(2,1)S(1)}, u32[]{:S(2)}, u32[]{:S(2)}) collective-permute-start(bf16[64,8,256]{2,1,0:T(8,128)(2,1)S(1)} %get-tuple-element.37), channel_id=1, source_target_pairs={{4,0},{8,12},{5,1},{9,13},{6,2},{10,14},{7,3},{11,15},{20,16},{24,... | collective-permute-start | bytes 786440 | tf_op jit(solution)/shard_map/ppermute | solution.py:237
  57.1 5.5 %collective-permute-done.8 = bf16[128,8,256]{2,1,0:T(8,128)(2,1)S(1)} collective-permute-done((bf16[128,8,256]{2,1,0:T(8,128)(2,1)S(1)}, bf16[128,8,256]{2,1,0:T(8,128)(2,1)S(1)}, u32[]{:S(2)}, u32[]{:S(2)}) %collective-permute-start.8) | collective-permute-done | bytes 524320 | tf_op jit(solution)/shard_map/ppermute | solution.py:230
  62.8 3.9 %shard_map.59.base_ref = f32[48,128]{1,0:T(8,128)S(1)} custom-call(bf16[128,16,256]{2,1,0:T(8,128)(2,1)S(1)} %shard_map.58.early_ref, bf16[128,8,256]{2,1,0:T(8,128)(2,1)S(1)} %shard_map.57.own_ref, bf16[128,8,256]{2,1,0:T(8,128)(2,1)S(1)} %collective-permute-done.4.near, bf16[128,8,256]{2,1,0:T(8,128)(2,1)S(1)} %add.13.mid, ...), custom_call_target="tpu_custom_call" | custom-call | flops 1000 | bytes 1000 | tf_op jit(solution)/shard_map/pallas_call | solution.py:189
  66.8 0.9 %shard_map.60.early_ref = bf16[128,8,256]{2,1,0:T(8,128)(2,1)S(1)} custom-call(bf16[4,128,256]{2,1,0:T(8,128)(2,1)S(1)} %add.14.own_ref, bf16[4,128,256]{2,1,0:T(8,128)(2,1)S(1)} %collective-permute-done.11.far_ref, bf16[384,256]{1,0:T(8,128)(2,1)S(1)} %get-tuple-element.23.left_ref, bf16[512,256]{1,0:T(8,128)(2,1)S(1)} %get-tuple-element.24.right_ref), custom_call_target="tpu_custom_call" | custom-call | flops 480000000 | bytes 1048576 | tf_op jit(solution)/shard_map/pallas_call | solution.py:73
  67.7 1.9 %shard_map.61.far_ref = f32[16,128]{1,0:T(8,128)S(1)} custom-call(bf16[128,8,256]{2,1,0:T(8,128)(2,1)S(1)} %shard_map.60.early_ref, bf16[64,8,256]{2,1,0:T(8,128)(2,1)S(1)} %collective-permute-done.12.far_out, bf16[128,128,256]{2,1,0:T(8,128)(2,1)S(1)} %shard_map.56.grad_ref, s32[4]{0:T(128)S(1)} %copy-done.2), custom_call_target="tpu_custom_call" | custom-call | flops 1000 | bytes 1000 | tf_op jit(solution)/shard_map/pallas_call | solution.py:189
  69.5 1.9 %shard_map.62 = (f32[24,128]{1,0:T(8,128)S(1)}, f32[24,128]{1,0:T(8,128)S(1)}) custom-call(f32[48,128]{1,0:T(8,128)S(1)} %shard_map.59.base_ref, f32[16,128]{1,0:T(8,128)S(1)} %shard_map.61.far_ref, bf16[128,8,256]{2,1,0:T(8,128)(2,1)S(1)} %shard_map.60.early_ref, bf16[64,8,256]{2,1,0:T(8,128)(2,1)S(1)} %collective-permute-done.13.far_out, ...), custom_call_target="tpu_custom_call" | custom-call | flops 1000 | bytes 1000 | tf_op jit(solution)/shard_map/pallas_call | solution.py:189
  71.4 0.6 collective-permute-start.14
  72.0 3.2 %collective-permute-done.14 = f32[24,128]{1,0:T(8,128)S(1)} collective-permute-done((f32[24,128]{1,0:T(8,128)S(1)}, f32[24,128]{1,0:T(8,128)S(1)}, u32[]{:S(2)}, u32[]{:S(2)}) %collective-permute-start.14) | collective-permute-done | bytes 12320 | tf_op jit(solution)/shard_map/ppermute | solution.py:253
  75.2 0.6 add_bitcast_fusion
  (20 shorter events, 0.5 us)
Async XLA Ops:
  1.1 17.6 %collective-permute-start.3 = (bf16[8,128,256]{2,1,0:T(8,128)(2,1)S(1)}, bf16[8,128,256]{2,1,0:T(8,128)(2,1)S(1)}, u32[]{:S(2)}, u32[]{:S(2)}) collective-permute-start(bf16[8,128,256]{2,1,0:T(8,128)(2,1)S(1)} %slice_bitcast_fusion.own_ref), channel_id=1, source_target_pairs={{0,2},{2,0},{1,3},{3,1},{4,6},{6,4},{5,7},{7,5},{8,10},{10,8},{9,1... | collective-permute-start | bytes 1572872 | tf_op jit(solution)/shard_map/ppermute | solution.py:215
  5.1 12.3 %collective-permute-start.1 = (bf16[4,128,256]{2,1,0:T(8,128)(2,1)S(1)}, bf16[4,128,256]{2,1,0:T(8,128)(2,1)S(1)}, u32[]{:S(2)}, u32[]{:S(2)}) collective-permute-start(bf16[4,128,256]{2,1,0:T(8,128)(2,1)S(1)} %slice_bitcast_fusion.1), channel_id=1, source_target_pairs={{4,8},{8,4},{5,9},{9,5},{6,10},{10,6},{7,11},{11,7},{20,24},{24,20... | collective-permute-start | bytes 786440 | tf_op jit(solution)/shard_map/ppermute | solution.py:219
  5.7 12.9 %collective-permute-start = (bf16[4,128,256]{2,1,0:T(8,128)(2,1)S(1)}, bf16[4,128,256]{2,1,0:T(8,128)(2,1)S(1)}, u32[]{:S(2)}, u32[]{:S(2)}) collective-permute-start(bf16[4,128,256]{2,1,0:T(8,128)(2,1)S(1)} %slice_bitcast_fusion.1), channel_id=1, source_target_pairs={{0,4},{4,0},{8,12},{12,8},{1,5},{5,1},{9,13},{13,9},{2,6},{6,2},{1... | collective-permute-start | bytes 786440 | tf_op jit(solution)/shard_map/ppermute | solution.py:218
  10.2 0.9 %copy-start = (f32[256,256]{1,0:T(8,128)S(1)}, f32[256,256]{1,0:T(8,128)}, u32[]{:S(2)}) copy-start(f32[256,256]{1,0:T(8,128)} %left_ref.1) | copy-start | bytes 786436
  11.1 0.9 %copy-start.1 = (f32[256,256]{1,0:T(8,128)S(1)}, f32[256,256]{1,0:T(8,128)}, u32[]{:S(2)}) copy-start(f32[256,256]{1,0:T(8,128)} %right_ref) | copy-start | bytes 786436
  17.4 45.5 %copy-start.2 = (s32[4]{0:T(128)S(1)}, s32[4]{0:T(128)}, u32[]{:S(2)}) copy-start(s32[4]{0:T(128)} %order_ref.5) | copy-start | bytes 52
  17.4 11.1 %collective-permute-start.2 = (bf16[4,128,256]{2,1,0:T(8,128)(2,1)S(1)}, bf16[4,128,256]{2,1,0:T(8,128)(2,1)S(1)}, u32[]{:S(2)}, u32[]{:S(2)}) collective-permute-start(bf16[4,128,256]{2,1,0:T(8,128)(2,1)S(1)} %collective-permute-done.1), channel_id=1, source_target_pairs={{4,0},{8,12},{5,1},{9,13},{6,2},{10,14},{7,3},{11,15},{20,16},{24,... | collective-permute-start | bytes 786440 | tf_op jit(solution)/shard_map/ppermute | solution.py:221
  18.7 10.0 %collective-permute-start.6 = (bf16[4,128,256]{2,1,0:T(8,128)(2,1)S(1)}, bf16[4,128,256]{2,1,0:T(8,128)(2,1)S(1)}, u32[]{:S(2)}, u32[]{:S(2)}) collective-permute-start(bf16[4,128,256]{2,1,0:T(8,128)(2,1)S(1)} %collective-permute-done), channel_id=1, source_target_pairs={{4,8},{8,4},{5,9},{9,5},{6,10},{10,6},{7,11},{11,7},{20,24},{24,20... | collective-permute-start | bytes 786440 | tf_op jit(solution)/shard_map/ppermute | solution.py:222
  20.7 17.0 %collective-permute-start.4 = (bf16[128,8,256]{2,1,0:T(8,128)(2,1)S(1)}, bf16[128,8,256]{2,1,0:T(8,128)(2,1)S(1)}, u32[]{:S(2)}, u32[]{:S(2)}) collective-permute-start(bf16[128,8,256]{2,1,0:T(8,128)(2,1)S(1)} %shard_map.57.own_ref), channel_id=1, source_target_pairs={{0,4},{4,0},{8,12},{12,8},{1,5},{5,1},{9,13},{13,9},{2,6},{6,2},{1... | collective-permute-start | bytes 1572872 | tf_op jit(solution)/shard_map/ppermute | solution.py:226
  25.1 13.3 %collective-permute-start.5 = (bf16[128,8,256]{2,1,0:T(8,128)(2,1)S(1)}, bf16[128,8,256]{2,1,0:T(8,128)(2,1)S(1)}, u32[]{:S(2)}, u32[]{:S(2)}) collective-permute-start(bf16[128,8,256]{2,1,0:T(8,128)(2,1)S(1)} %shard_map.57.own_ref), channel_id=1, source_target_pairs={{4,8},{8,4},{5,9},{9,5},{6,10},{10,6},{7,11},{11,7},{20,24},{24,20... | collective-permute-start | bytes 1572872 | tf_op jit(solution)/shard_map/ppermute | solution.py:225
  28.7 22.8 %collective-permute-start.7 = (bf16[12,128,256]{2,1,0:T(8,128)(2,1)S(1)}, bf16[12,128,256]{2,1,0:T(8,128)(2,1)S(1)}, u32[]{:S(2)}, u32[]{:S(2)}) collective-permute-start(bf16[12,128,256]{2,1,0:T(8,128)(2,1)S(1)} %pad_maximum_fusion.own_ref), channel_id=1, source_target_pairs={{0,2},{2,0},{1,3},{3,1},{4,6},{6,4},{5,7},{7,5},{8,10},{10,8},{9,1... | collective-permute-start | bytes 2359304 | tf_op jit(solution)/shard_map/ppermute | solution.py:228
  37.7 16.8 %collective-permute-start.9 = (bf16[128,8,256]{2,1,0:T(8,128)(2,1)S(1)}, bf16[128,8,256]{2,1,0:T(8,128)(2,1)S(1)}, u32[]{:S(2)}, u32[]{:S(2)}) collective-permute-start(bf16[128,8,256]{2,1,0:T(8,128)(2,1)S(1)} %collective-permute-done.4.near), channel_id=1, source_target_pairs={{4,8},{8,4},{5,9},{9,5},{6,10},{10,6},{7,11},{11,7},{20,24},{24,20... | collective-permute-start | bytes 1572872 | tf_op jit(solution)/shard_map/ppermute | solution.py:231
  38.4 13.0 %collective-permute-start.10 = (bf16[4,128,256]{2,1,0:T(8,128)(2,1)S(1)}, bf16[4,128,256]{2,1,0:T(8,128)(2,1)S(1)}, u32[]{:S(2)}, u32[]{:S(2)}) collective-permute-start(bf16[4,128,256]{2,1,0:T(8,128)(2,1)S(1)} %collective-permute-done.6), channel_id=1, source_target_pairs={{4,0},{8,12},{5,1},{9,13},{6,2},{10,14},{7,3},{11,15},{20,16},{24,... | collective-permute-start | bytes 786440 | tf_op jit(solution)/shard_map/ppermute | solution.py:229
  39.7 23.0 %collective-permute-start.8 = (bf16[128,8,256]{2,1,0:T(8,128)(2,1)S(1)}, bf16[128,8,256]{2,1,0:T(8,128)(2,1)S(1)}, u32[]{:S(2)}, u32[]{:S(2)}) collective-permute-start(bf16[128,8,256]{2,1,0:T(8,128)(2,1)S(1)} %collective-permute-done.5), channel_id=1, source_target_pairs={{4,0},{8,12},{5,1},{9,13},{6,2},{10,14},{7,3},{11,15},{20,16},{24,... | collective-permute-start | bytes 1572872 | tf_op jit(solution)/shard_map/ppermute | solution.py:230
  53.9 12.9 %collective-permute-start.11 = (bf16[4,128,256]{2,1,0:T(8,128)(2,1)S(1)}, bf16[4,128,256]{2,1,0:T(8,128)(2,1)S(1)}, u32[]{:S(2)}, u32[]{:S(2)}) collective-permute-start(bf16[4,128,256]{2,1,0:T(8,128)(2,1)S(1)} %add.14.own_ref), channel_id=1, source_target_pairs={{0,2},{2,0},{1,3},{3,1},{4,6},{6,4},{5,7},{7,5},{8,10},{10,8},{9,1... | collective-permute-start | bytes 786440 | tf_op jit(solution)/shard_map/ppermute | solution.py:234
  54.5 13.2 %collective-permute-start.12 = (bf16[64,8,256]{2,1,0:T(8,128)(2,1)S(1)}, bf16[64,8,256]{2,1,0:T(8,128)(2,1)S(1)}, u32[]{:S(2)}, u32[]{:S(2)}) collective-permute-start(bf16[64,8,256]{2,1,0:T(8,128)(2,1)S(1)} %get-tuple-element.38), channel_id=1, source_target_pairs={{4,0},{8,12},{5,1},{9,13},{6,2},{10,14},{7,3},{11,15},{20,16},{24,... | collective-permute-start | bytes 786440 | tf_op jit(solution)/shard_map/ppermute | solution.py:236
  55.8 13.7 %collective-permute-start.13 = (bf16[64,8,256]{2,1,0:T(8,128)(2,1)S(1)}, bf16[64,8,256]{2,1,0:T(8,128)(2,1)S(1)}, u32[]{:S(2)}, u32[]{:S(2)}) collective-permute-start(bf16[64,8,256]{2,1,0:T(8,128)(2,1)S(1)} %get-tuple-element.37), channel_id=1, source_target_pairs={{4,0},{8,12},{5,1},{9,13},{6,2},{10,14},{7,3},{11,15},{20,16},{24,... | collective-permute-start | bytes 786440 | tf_op jit(solution)/shard_map/ppermute | solution.py:237
  71.4 3.8 %collective-permute-start.14 = (f32[24,128]{1,0:T(8,128)S(1)}, f32[24,128]{1,0:T(8,128)S(1)}, u32[]{:S(2)}, u32[]{:S(2)}) collective-permute-start(f32[24,128]{1,0:T(8,128)S(1)} %get-tuple-element.36), channel_id=1, source_target_pairs={{0,2},{2,0},{1,3},{3,1},{4,6},{6,4},{5,7},{7,5},{8,10},{10,8},{9,1... | collective-permute-start | bytes 36872 | tf_op jit(solution)/shard_map/ppermute | solution.py:253

commit v11 on v7

--- a/solution.py
+++ b/solution.py
@@ -109,7 +109,7 @@
         in_specs=[pl.BlockSpec(memory_space=pltpu.HBM)],
         out_specs=VMEM,
         scratch_shapes=[pltpu.VMEM((n, rows, width), BF16), pltpu.SemaphoreType.DMA((n // EXAMPLES,))],
-        compiler_params=pltpu.CompilerParams(vmem_limit_bytes=48 << 20),
+        compiler_params=pltpu.CompilerParams(vmem_limit_bytes=44 << 20),
         cost_estimate=pl.CostEstimate(flops=6_000_000_000, bytes_accessed=16_000_000, transcendentals=0),
     )(grads)
 

time: 71.9 us -> 71.9 us (level)
  waiting for transfers between devices: 23.9 us -> 27.7 us
  Pallas kernels: 19.9 us -> 16.7 us
    ppermute x1, waiting for transfers between devices: 5.08 us -> 9.29 us  [per_device_line(): near = lax.ppermute(late, 'ex', PAIRS)]
    pallas_call x1, Pallas kernels: 8.4 us -> 5.16 us  [regroup(): pl.pallas_call(regroup_kernel, out_shape=jax.ShapeDtypeStruct((rows, n, w...]
    unnamed x8 -> x6, local copies, waits for them, and re-layouts: 1.91 us -> 1.91 us
  transfers between devices with their start and end apart: 15 -> 15, of which waited for: 7 -> 6; matrix products, arithmetic and copies ran while one was open for 2% -> 2% of each run, Pallas kernels for 25% -> 21%
where the time goes in v11:
time: 71.9 us; the launch traced here: 71.5 us
  waiting for transfers between devices  27.7 us (39%)
  starting transfers between devices  21.9 us (30%)
  Pallas kernels  16.7 us (23%)
  local copies, waits for them, and re-layouts  3.98 us (6%)
  other arithmetic  0.98 us (1%)
    ppermute x1, waiting for transfers between devices, per_device_line(): near = lax.ppermute(late, 'ex', PAIRS)  9.29 us
    pallas_call x3, Pallas kernels, score_call(): pl.pallas_call(functools.partial(kernel, ex), out_shape=out_shape, in_spe...  7.68 us
    ppermute x1, waiting for transfers between devices, per_device_line(): mid_out = lax.ppermute(after(mid, near, grads), 'ex', OUTWARD)  7.27 us
    pallas_call x1, Pallas kernels, regroup(): pl.pallas_call(regroup_kernel, out_shape=jax.ShapeDtypeStruct((rows, n, w...  5.16 us
    ppermute x1, starting transfers between devices, per_device_line(): raw_near = lax.ppermute(raw, 'ex', PAIRS)  4.45 us
    pallas_call x3, Pallas kernels, condition(): pl.pallas_call(condition_kernel, out_shape=jax.ShapeDtypeStruct((rows, co...  3.79 us
    ppermute x1, waiting for transfers between devices, per_device_line(): raw_near = lax.ppermute(raw, 'ex', PAIRS)  3.75 us
    ppermute x1, waiting for transfers between devices, per_device_line(): raw_far_out = lax.ppermute(after(raw_far_mid, grads), 'ex', OUTWARD)  3.53 us
  transfers between devices with their start and end apart: 15, of which 6 were waited for; matrix products, arithmetic and copies ran while one was open for 2% of the time, Pallas kernels for 21%

profile of v11, /device:TPU:0, one launch (start us, length us, event | category | flops | bytes accessed | tf_op | source)
XLA Modules:
  0.0 71.5 jit_solution(18013951617650294990)
XLA Ops:
  0.0 1.1 %slice_bitcast_fusion.own_ref = bf16[8,128,256]{2,1,0:T(8,128)(2,1)S(1)} fusion(bf16[1,12,128,256]{3,2,1,0:T(8,128)(2,1)} %param.6), kind=kLoop, calls=%fused_computation.2 | loop fusion | bytes 1048576 | tf_op jit(solution)/shard_map/squeeze | solution.py:205
  1.1 3.0 %collective-permute-start.2 = (bf16[8,128,256]{2,1,0:T(8,128)(2,1)S(1)}, bf16[8,128,256]{2,1,0:T(8,128)(2,1)S(1)}, u32[]{:S(2)}, u32[]{:S(2)}) collective-permute-start(bf16[8,128,256]{2,1,0:T(8,128)(2,1)S(1)} %slice_bitcast_fusion.own_ref), channel_id=1, source_target_pairs={{0,2},{2,0},{1,3},{3,1},{4,6},{6,4},{5,7},{7,5},{8,10},{10,8},{9,1... | collective-permute-start | bytes 1572872 | tf_op jit(solution)/shard_map/ppermute | solution.py:206
  4.1 1.0 %slice_bitcast_fusion.1 = bf16[4,128,256]{2,1,0:T(8,128)(2,1)S(1)} fusion(bf16[1,12,128,256]{3,2,1,0:T(8,128)(2,1)} %param.6), kind=kLoop, calls=%fused_computation.3 | loop fusion | bytes 524288 | tf_op jit(solution)/shard_map/squeeze | solution.py:207
  5.1 0.7 collective-permute-start.1
  5.7 4.4 %collective-permute-start = (bf16[4,128,256]{2,1,0:T(8,128)(2,1)S(1)}, bf16[4,128,256]{2,1,0:T(8,128)(2,1)S(1)}, u32[]{:S(2)}, u32[]{:S(2)}) collective-permute-start(bf16[4,128,256]{2,1,0:T(8,128)(2,1)S(1)} %slice_bitcast_fusion.1), channel_id=1, source_target_pairs={{0,4},{4,0},{8,12},{12,8},{1,5},{5,1},{9,13},{13,9},{2,6},{6,2},{1... | collective-permute-start | bytes 786440 | tf_op jit(solution)/shard_map/ppermute | solution.py:209
  10.2 0.9 %copy-done = f32[256,256]{1,0:T(8,128)S(1)} copy-done((f32[256,256]{1,0:T(8,128)S(1)}, f32[256,256]{1,0:T(8,128)}, u32[]{:S(2)}) %copy-start) | copy-done | bytes 262168
  11.1 0.9 %copy-done.1 = f32[256,256]{1,0:T(8,128)S(1)} copy-done((f32[256,256]{1,0:T(8,128)S(1)}, f32[256,256]{1,0:T(8,128)}, u32[]{:S(2)}) %copy-start.1) | copy-done | bytes 262168
  12.2 3.8 %collective-permute-done = bf16[4,128,256]{2,1,0:T(8,128)(2,1)S(1)} collective-permute-done((bf16[4,128,256]{2,1,0:T(8,128)(2,1)S(1)}, bf16[4,128,256]{2,1,0:T(8,128)(2,1)S(1)}, u32[]{:S(2)}, u32[]{:S(2)}) %collective-permute-start) | collective-permute-done | bytes 262176 | tf_op jit(solution)/shard_map/ppermute | solution.py:209
  16.0 0.7 collective-permute-start.7
  16.7 1.3 %collective-permute-start.6 = (bf16[4,128,256]{2,1,0:T(8,128)(2,1)S(1)}, bf16[4,128,256]{2,1,0:T(8,128)(2,1)S(1)}, u32[]{:S(2)}, u32[]{:S(2)}) collective-permute-start(bf16[4,128,256]{2,1,0:T(8,128)(2,1)S(1)} %collective-permute-done.1), channel_id=1, source_target_pairs={{4,0},{8,12},{5,1},{9,13},{6,2},{10,14},{7,3},{11,15},{20,16},{24,... | collective-permute-start | bytes 786440 | tf_op jit(solution)/shard_map/ppermute | solution.py:211
  18.0 1.3 %shard_map.56.own_ref = bf16[128,8,256]{2,1,0:T(8,128)(2,1)S(1)} custom-call(bf16[8,128,256]{2,1,0:T(8,128)(2,1)S(1)} %slice_bitcast_fusion.own_ref, bf16[8,128,256]{2,1,0:T(8,128)(2,1)S(1)} %collective-permute-done.2.far_ref, bf16[384,256]{1,0:T(8,128)(2,1)S(1)} %get-tuple-element.29.left_ref, bf16[512,256]{1,0:T(8,128)(2,1)S(1)} %get-tuple-element.30.right_ref), custom_call_target="tpu_custom_call" | custom-call | flops 960000000 | bytes 2097152 | tf_op jit(solution)/shard_map/pallas_call | solution.py:70
  19.2 3.5 %collective-permute-start.3 = (bf16[128,8,256]{2,1,0:T(8,128)(2,1)S(1)}, bf16[128,8,256]{2,1,0:T(8,128)(2,1)S(1)}, u32[]{:S(2)}, u32[]{:S(2)}) collective-permute-start(bf16[128,8,256]{2,1,0:T(8,128)(2,1)S(1)} %shard_map.56.own_ref), channel_id=1, source_target_pairs={{0,4},{4,0},{8,12},{12,8},{1,5},{5,1},{9,13},{13,9},{2,6},{6,2},{1... | collective-permute-start | bytes 1572872 | tf_op jit(solution)/shard_map/ppermute | solution.py:216
  22.7 0.7 collective-permute-start.4
  23.4 0.6 collective-permute-start.5
  24.0 5.2 %shard_map.58.grad_ref = bf16[128,128,256]{2,1,0:T(8,128)(2,1)S(1)} custom-call(bf16[128,128,256]{2,1,0:T(8,128)(2,1)} %grads_ref), custom_call_target="tpu_custom_call" | custom-call | flops 6000000000 | bytes 16000000 | tf_op jit(solution)/shard_map/pallas_call | solution.py:106
  29.2 1.3 %collective-permute-start.8 = (bf16[4,128,256]{2,1,0:T(8,128)(2,1)S(1)}, bf16[4,128,256]{2,1,0:T(8,128)(2,1)S(1)}, u32[]{:S(2)}, u32[]{:S(2)}) collective-permute-start(bf16[4,128,256]{2,1,0:T(8,128)(2,1)S(1)} %collective-permute-done.7), channel_id=1, source_target_pairs={{4,0},{8,12},{5,1},{9,13},{6,2},{10,14},{7,3},{11,15},{20,16},{24,... | collective-permute-start | bytes 786440 | tf_op jit(solution)/shard_map/ppermute | solution.py:220
  30.5 9.3 %collective-permute-done.3.near = bf16[128,8,256]{2,1,0:T(8,128)(2,1)S(1)} collective-permute-done((bf16[128,8,256]{2,1,0:T(8,128)(2,1)S(1)}, bf16[128,8,256]{2,1,0:T(8,128)(2,1)S(1)}, u32[]{:S(2)}, u32[]{:S(2)}) %collective-permute-start.3) | collective-permute-done | bytes 524320 | tf_op jit(solution)/shard_map/ppermute | solution.py:216
  39.8 0.7 collective-permute-start.9
  40.6 1.3 %collective-permute-start.11 = (bf16[128,8,256]{2,1,0:T(8,128)(2,1)S(1)}, bf16[128,8,256]{2,1,0:T(8,128)(2,1)S(1)}, u32[]{:S(2)}, u32[]{:S(2)}) collective-permute-start(bf16[128,8,256]{2,1,0:T(8,128)(2,1)S(1)} %collective-permute-done.4), channel_id=1, source_target_pairs={{4,0},{8,12},{5,1},{9,13},{6,2},{10,14},{7,3},{11,15},{20,16},{24,... | collective-permute-start | bytes 1572872 | tf_op jit(solution)/shard_map/ppermute | solution.py:222
  41.9 3.5 %collective-permute-done.8 = bf16[4,128,256]{2,1,0:T(8,128)(2,1)S(1)} collective-permute-done((bf16[4,128,256]{2,1,0:T(8,128)(2,1)S(1)}, bf16[4,128,256]{2,1,0:T(8,128)(2,1)S(1)}, u32[]{:S(2)}, u32[]{:S(2)}) %collective-permute-start.8) | collective-permute-done | bytes 262176 | tf_op jit(solution)/shard_map/ppermute | solution.py:220
  45.5 1.3 %shard_map.57.early_0 = bf16[128,8,256]{2,1,0:T(8,128)(2,1)S(1)} custom-call(bf16[8,128,256]{2,1,0:T(8,128)(2,1)S(1)} %pad_maximum_fusion.own_ref, bf16[8,128,256]{2,1,0:T(8,128)(2,1)S(1)} %collective-permute-done.5.far_ref, bf16[384,256]{1,0:T(8,128)(2,1)S(1)} %get-tuple-element.29.left_ref, bf16[512,256]{1,0:T(8,128)(2,1)S(1)} %get-tuple-element.30.right_ref), custom_call_target="tpu_custom_call" | custom-call | flops 960000000 | bytes 2097152 | tf_op jit(solution)/shard_map/pallas_call | solution.py:70
  46.8 0.6 collective-permute-start.10
  47.5 1.3 %collective-permute-start.12 = (bf16[64,8,256]{2,1,0:T(8,128)(2,1)S(1)}, bf16[64,8,256]{2,1,0:T(8,128)(2,1)S(1)}, u32[]{:S(2)}, u32[]{:S(2)}) collective-permute-start(bf16[64,8,256]{2,1,0:T(8,128)(2,1)S(1)} %get-tuple-element.46), channel_id=1, source_target_pairs={{4,0},{8,12},{5,1},{9,13},{6,2},{10,14},{7,3},{11,15},{20,16},{24,... | collective-permute-start | bytes 786440 | tf_op jit(solution)/shard_map/ppermute | solution.py:227
  48.8 1.3 %collective-permute-start.13 = (bf16[64,8,256]{2,1,0:T(8,128)(2,1)S(1)}, bf16[64,8,256]{2,1,0:T(8,128)(2,1)S(1)}, u32[]{:S(2)}, u32[]{:S(2)}) collective-permute-start(bf16[64,8,256]{2,1,0:T(8,128)(2,1)S(1)} %get-tuple-element.45), channel_id=1, source_target_pairs={{4,0},{8,12},{5,1},{9,13},{6,2},{10,14},{7,3},{11,15},{20,16},{24,... | collective-permute-start | bytes 786440 | tf_op jit(solution)/shard_map/ppermute | solution.py:228
  50.1 7.3 %collective-permute-done.11 = bf16[128,8,256]{2,1,0:T(8,128)(2,1)S(1)} collective-permute-done((bf16[128,8,256]{2,1,0:T(8,128)(2,1)S(1)}, bf16[128,8,256]{2,1,0:T(8,128)(2,1)S(1)}, u32[]{:S(2)}, u32[]{:S(2)}) %collective-permute-start.11) | collective-permute-done | bytes 524320 | tf_op jit(solution)/shard_map/ppermute | solution.py:222
  57.5 1.3 %shard_map.59.early_1 = bf16[128,8,256]{2,1,0:T(8,128)(2,1)S(1)} custom-call(bf16[8,128,256]{2,1,0:T(8,128)(2,1)S(1)} %pad_maximum_fusion.1.own_ref, bf16[8,128,256]{2,1,0:T(8,128)(2,1)S(1)} %collective-permute-done.10.far_ref, bf16[384,256]{1,0:T(8,128)(2,1)S(1)} %get-tuple-element.29.left_ref, bf16[512,256]{1,0:T(8,128)(2,1)S(1)} %get-tuple-element.30.right_ref), custom_call_target="tpu_custom_call" | custom-call | flops 960000000 | bytes 2097152 | tf_op jit(solution)/shard_map/pallas_call | solution.py:70
  58.8 4.0 %shard_map.60.base_ref = f32[48,128]{1,0:T(8,128)S(1)} custom-call(bf16[128,8,256]{2,1,0:T(8,128)(2,1)S(1)} %shard_map.57.early_0, bf16[128,8,256]{2,1,0:T(8,128)(2,1)S(1)} %shard_map.59.early_1, bf16[128,8,256]{2,1,0:T(8,128)(2,1)S(1)} %shard_map.56.own_ref, bf16[128,8,256]{2,1,0:T(8,128)(2,1)S(1)} %collective-permute-done.3.near, ...), custom_call_target="tpu_custom_call" | custom-call | flops 1000 | bytes 1000 | tf_op jit(solution)/shard_map/pallas_call | solution.py:180
  62.8 1.8 %shard_map.61.far_ref = f32[8,128]{1,0:T(8,128)S(1)} custom-call(bf16[64,8,256]{2,1,0:T(8,128)(2,1)S(1)} %collective-permute-done.12.far_out, bf16[128,128,256]{2,1,0:T(8,128)(2,1)S(1)} %shard_map.58.grad_ref, s32[4]{0:T(128)S(1)} %copy-done.2), custom_call_target="tpu_custom_call" | custom-call | flops 1000 | bytes 1000 | tf_op jit(solution)/shard_map/pallas_call | solution.py:180
  64.6 0.6 collective-permute-done.13.far_out
  65.3 1.9 %shard_map.62 = (f32[24,128]{1,0:T(8,128)S(1)}, f32[24,128]{1,0:T(8,128)S(1)}) custom-call(f32[48,128]{1,0:T(8,128)S(1)} %shard_map.60.base_ref, f32[8,128]{1,0:T(8,128)S(1)} %shard_map.61.far_ref, bf16[64,8,256]{2,1,0:T(8,128)(2,1)S(1)} %collective-permute-done.13.far_out, bf16[128,128,256]{2,1,0:T(8,128)(2,1)S(1)} %shard_map.58.grad_ref, s32[4]{0:T(128)S(1)} %copy-done.2), custom_call_target="tpu_custom_call" | custom-call | flops 1000 | bytes 1000 | tf_op jit(solution)/shard_map/pallas_call | solution.py:180
  67.8 3.2 %collective-permute-done.14 = f32[24,128]{1,0:T(8,128)S(1)} collective-permute-done((f32[24,128]{1,0:T(8,128)S(1)}, f32[24,128]{1,0:T(8,128)S(1)}, u32[]{:S(2)}, u32[]{:S(2)}) %collective-permute-start.14) | collective-permute-done | bytes 12320 | tf_op jit(solution)/shard_map/ppermute | solution.py:244
  70.9 0.6 add_bitcast_fusion
  (21 shorter events, 1.1 us)
Async XLA Ops:
  1.1 16.9 %collective-permute-start.2 = (bf16[8,128,256]{2,1,0:T(8,128)(2,1)S(1)}, bf16[8,128,256]{2,1,0:T(8,128)(2,1)S(1)}, u32[]{:S(2)}, u32[]{:S(2)}) collective-permute-start(bf16[8,128,256]{2,1,0:T(8,128)(2,1)S(1)} %slice_bitcast_fusion.own_ref), channel_id=1, source_target_pairs={{0,2},{2,0},{1,3},{3,1},{4,6},{6,4},{5,7},{7,5},{8,10},{10,8},{9,1... | collective-permute-start | bytes 1572872 | tf_op jit(solution)/shard_map/ppermute | solution.py:206
  5.1 7.1 %collective-permute-start.1 = (bf16[4,128,256]{2,1,0:T(8,128)(2,1)S(1)}, bf16[4,128,256]{2,1,0:T(8,128)(2,1)S(1)}, u32[]{:S(2)}, u32[]{:S(2)}) collective-permute-start(bf16[4,128,256]{2,1,0:T(8,128)(2,1)S(1)} %slice_bitcast_fusion.1), channel_id=1, source_target_pairs={{4,8},{8,4},{5,9},{9,5},{6,10},{10,6},{7,11},{11,7},{20,24},{24,20... | collective-permute-start | bytes 786440 | tf_op jit(solution)/shard_map/ppermute | solution.py:210
  5.7 10.2 %collective-permute-start = (bf16[4,128,256]{2,1,0:T(8,128)(2,1)S(1)}, bf16[4,128,256]{2,1,0:T(8,128)(2,1)S(1)}, u32[]{:S(2)}, u32[]{:S(2)}) collective-permute-start(bf16[4,128,256]{2,1,0:T(8,128)(2,1)S(1)} %slice_bitcast_fusion.1), channel_id=1, source_target_pairs={{0,4},{4,0},{8,12},{12,8},{1,5},{5,1},{9,13},{13,9},{2,6},{6,2},{1... | collective-permute-start | bytes 786440 | tf_op jit(solution)/shard_map/ppermute | solution.py:209
  10.2 0.9 %copy-start = (f32[256,256]{1,0:T(8,128)S(1)}, f32[256,256]{1,0:T(8,128)}, u32[]{:S(2)}) copy-start(f32[256,256]{1,0:T(8,128)} %left_ref.1) | copy-start | bytes 786436
  11.1 0.9 %copy-start.1 = (f32[256,256]{1,0:T(8,128)S(1)}, f32[256,256]{1,0:T(8,128)}, u32[]{:S(2)}) copy-start(f32[256,256]{1,0:T(8,128)} %right_ref) | copy-start | bytes 786436
  16.0 13.2 %collective-permute-start.7 = (bf16[4,128,256]{2,1,0:T(8,128)(2,1)S(1)}, bf16[4,128,256]{2,1,0:T(8,128)(2,1)S(1)}, u32[]{:S(2)}, u32[]{:S(2)}) collective-permute-start(bf16[4,128,256]{2,1,0:T(8,128)(2,1)S(1)} %collective-permute-done), channel_id=1, source_target_pairs={{4,8},{8,4},{5,9},{9,5},{6,10},{10,6},{7,11},{11,7},{20,24},{24,20... | collective-permute-start | bytes 786440 | tf_op jit(solution)/shard_map/ppermute | solution.py:213
  16.7 23.8 %collective-permute-start.6 = (bf16[4,128,256]{2,1,0:T(8,128)(2,1)S(1)}, bf16[4,128,256]{2,1,0:T(8,128)(2,1)S(1)}, u32[]{:S(2)}, u32[]{:S(2)}) collective-permute-start(bf16[4,128,256]{2,1,0:T(8,128)(2,1)S(1)} %collective-permute-done.1), channel_id=1, source_target_pairs={{4,0},{8,12},{5,1},{9,13},{6,2},{10,14},{7,3},{11,15},{20,16},{24,... | collective-permute-start | bytes 786440 | tf_op jit(solution)/shard_map/ppermute | solution.py:211
  19.2 20.6 %collective-permute-start.3 = (bf16[128,8,256]{2,1,0:T(8,128)(2,1)S(1)}, bf16[128,8,256]{2,1,0:T(8,128)(2,1)S(1)}, u32[]{:S(2)}, u32[]{:S(2)}) collective-permute-start(bf16[128,8,256]{2,1,0:T(8,128)(2,1)S(1)} %shard_map.56.own_ref), channel_id=1, source_target_pairs={{0,4},{4,0},{8,12},{12,8},{1,5},{5,1},{9,13},{13,9},{2,6},{6,2},{1... | collective-permute-start | bytes 1572872 | tf_op jit(solution)/shard_map/ppermute | solution.py:216
  22.7 17.9 %collective-permute-start.4 = (bf16[128,8,256]{2,1,0:T(8,128)(2,1)S(1)}, bf16[128,8,256]{2,1,0:T(8,128)(2,1)S(1)}, u32[]{:S(2)}, u32[]{:S(2)}) collective-permute-start(bf16[128,8,256]{2,1,0:T(8,128)(2,1)S(1)} %shard_map.56.own_ref), channel_id=1, source_target_pairs={{4,8},{8,4},{5,9},{9,5},{6,10},{10,6},{7,11},{11,7},{20,24},{24,20... | collective-permute-start | bytes 1572872 | tf_op jit(solution)/shard_map/ppermute | solution.py:217
  23.4 22.1 %collective-permute-start.5 = (bf16[8,128,256]{2,1,0:T(8,128)(2,1)S(1)}, bf16[8,128,256]{2,1,0:T(8,128)(2,1)S(1)}, u32[]{:S(2)}, u32[]{:S(2)}) collective-permute-start(bf16[8,128,256]{2,1,0:T(8,128)(2,1)S(1)} %pad_maximum_fusion.own_ref), channel_id=1, source_target_pairs={{0,2},{2,0},{1,3},{3,1},{4,6},{6,4},{5,7},{7,5},{8,10},{10,8},{9,1... | collective-permute-start | bytes 1572872 | tf_op jit(solution)/shard_map/ppermute | solution.py:219
  29.2 29.6 %copy-start.2 = (s32[4]{0:T(128)S(1)}, s32[4]{0:T(128)}, u32[]{:S(2)}) copy-start(s32[4]{0:T(128)} %order_ref.5) | copy-start | bytes 52
  29.2 16.2 %collective-permute-start.8 = (bf16[4,128,256]{2,1,0:T(8,128)(2,1)S(1)}, bf16[4,128,256]{2,1,0:T(8,128)(2,1)S(1)}, u32[]{:S(2)}, u32[]{:S(2)}) collective-permute-start(bf16[4,128,256]{2,1,0:T(8,128)(2,1)S(1)} %collective-permute-done.7), channel_id=1, source_target_pairs={{4,0},{8,12},{5,1},{9,13},{6,2},{10,14},{7,3},{11,15},{20,16},{24,... | collective-permute-start | bytes 786440 | tf_op jit(solution)/shard_map/ppermute | solution.py:220
  39.8 7.6 %collective-permute-start.9 = (bf16[128,8,256]{2,1,0:T(8,128)(2,1)S(1)}, bf16[128,8,256]{2,1,0:T(8,128)(2,1)S(1)}, u32[]{:S(2)}, u32[]{:S(2)}) collective-permute-start(bf16[128,8,256]{2,1,0:T(8,128)(2,1)S(1)} %collective-permute-done.3.near), channel_id=1, source_target_pairs={{4,8},{8,4},{5,9},{9,5},{6,10},{10,6},{7,11},{11,7},{20,24},{24,20... | collective-permute-start | bytes 1572872 | tf_op jit(solution)/shard_map/ppermute | solution.py:221
  40.6 16.8 %collective-permute-start.11 = (bf16[128,8,256]{2,1,0:T(8,128)(2,1)S(1)}, bf16[128,8,256]{2,1,0:T(8,128)(2,1)S(1)}, u32[]{:S(2)}, u32[]{:S(2)}) collective-permute-start(bf16[128,8,256]{2,1,0:T(8,128)(2,1)S(1)} %collective-permute-done.4), channel_id=1, source_target_pairs={{4,0},{8,12},{5,1},{9,13},{6,2},{10,14},{7,3},{11,15},{20,16},{24,... | collective-permute-start | bytes 1572872 | tf_op jit(solution)/shard_map/ppermute | solution.py:222
  46.8 10.7 %collective-permute-start.10 = (bf16[8,128,256]{2,1,0:T(8,128)(2,1)S(1)}, bf16[8,128,256]{2,1,0:T(8,128)(2,1)S(1)}, u32[]{:S(2)}, u32[]{:S(2)}) collective-permute-start(bf16[8,128,256]{2,1,0:T(8,128)(2,1)S(1)} %pad_maximum_fusion.1.own_ref), channel_id=1, source_target_pairs={{0,2},{2,0},{1,3},{3,1},{4,6},{6,4},{5,7},{7,5},{8,10},{10,8},{9,1... | collective-permute-start | bytes 1572872 | tf_op jit(solution)/shard_map/ppermute | solution.py:225
  47.5 15.3 %collective-permute-start.12 = (bf16[64,8,256]{2,1,0:T(8,128)(2,1)S(1)}, bf16[64,8,256]{2,1,0:T(8,128)(2,1)S(1)}, u32[]{:S(2)}, u32[]{:S(2)}) collective-permute-start(bf16[64,8,256]{2,1,0:T(8,128)(2,1)S(1)} %get-tuple-element.46), channel_id=1, source_target_pairs={{4,0},{8,12},{5,1},{9,13},{6,2},{10,14},{7,3},{11,15},{20,16},{24,... | collective-permute-start | bytes 786440 | tf_op jit(solution)/shard_map/ppermute | solution.py:227
  48.8 16.5 %collective-permute-start.13 = (bf16[64,8,256]{2,1,0:T(8,128)(2,1)S(1)}, bf16[64,8,256]{2,1,0:T(8,128)(2,1)S(1)}, u32[]{:S(2)}, u32[]{:S(2)}) collective-permute-start(bf16[64,8,256]{2,1,0:T(8,128)(2,1)S(1)} %get-tuple-element.45), channel_id=1, source_target_pairs={{4,0},{8,12},{5,1},{9,13},{6,2},{10,14},{7,3},{11,15},{20,16},{24,... | collective-permute-start | bytes 786440 | tf_op jit(solution)/shard_map/ppermute | solution.py:228
  67.2 3.8 %collective-permute-start.14 = (f32[24,128]{1,0:T(8,128)S(1)}, f32[24,128]{1,0:T(8,128)S(1)}, u32[]{:S(2)}, u32[]{:S(2)}) collective-permute-start(f32[24,128]{1,0:T(8,128)S(1)} %get-tuple-element.44), channel_id=1, source_target_pairs={{0,2},{2,0},{1,3},{3,1},{4,6},{6,4},{5,7},{7,5},{8,10},{10,8},{9,1... | collective-permute-start | bytes 36872 | tf_op jit(solution)/shard_map/ppermute | solution.py:244

commit v12 on v10

--- a/solution.py
+++ b/solution.py
@@ -62,20 +62,17 @@
         both = jnp.dot(jnp.concatenate([mixed_0, mixed_1], axis=0), right_0, preferred_element_type=F32)
         cross = jnp.dot(mixed_0, right_1, preferred_element_type=F32)
         wide_ref[:, q, :] = both[:rows] + (both[rows:] + cross)
-    for q in range(count, out_ref.shape[1]):
-        wide_ref[:, q, :] = jnp.zeros((rows, width), F32)
     out_ref[...] = wide_ref[...].astype(BF16)
 
 
 def condition(own, far, left_terms, right_terms):
     count, rows, width = own.shape
-    padded = -(-count // 8) * 8
     return pl.pallas_call(
         condition_kernel,
-        out_shape=jax.ShapeDtypeStruct((rows, padded, width), BF16),
+        out_shape=jax.ShapeDtypeStruct((rows, count, width), BF16),
         in_specs=[VMEM] * 4,
         out_specs=VMEM,
-        scratch_shapes=[pltpu.VMEM((rows, padded, width), F32)],
+        scratch_shapes=[pltpu.VMEM((rows, count, width), F32)],
         compiler_params=pltpu.CompilerParams(vmem_limit_bytes=24 << 20),
         cost_estimate=pl.CostEstimate(flops=count * 3_000_000 * 40, bytes_accessed=8 * count * rows * width, transcendentals=0),
     )(own, far, left_terms, right_terms)
@@ -113,7 +110,7 @@
         out_specs=VMEM,
         scratch_shapes=[pltpu.VMEM((n, rows, width), BF16), pltpu.SemaphoreType.DMA((n // EXAMPLES,))],
         compiler_params=pltpu.CompilerParams(vmem_limit_bytes=44 << 20),
-        cost_estimate=pl.CostEstimate(flops=1000, bytes_accessed=1000, transcendentals=0),
+        cost_estimate=pl.CostEstimate(flops=6_000_000_000, bytes_accessed=16_000_000, transcendentals=0),
     )(grads)
 
 
@@ -142,7 +139,7 @@
     late = own_ref.shape[1]
     acc = inner_products((early_ref, own_ref, near, mid, far_in), grad_ref)
     sources = slot_sources(lax.axis_index("ex"))
-    early = [acc[EARLY * s : EARLY * (s + 1)] for s in range(ex - 1)]
+    early = [acc[EARLY * s : EARLY * (s + 1)] for s in range(2)]
     base = early_ref.shape[1]
     slots = [acc[base + late * s : base + late * (s + 1)] for s in range(ex)]
     for b in range(ex):
@@ -171,14 +168,15 @@
 def last_pass_kernel(ex, base_ref, far_ref, early_ref, far_out, grad_ref, order_ref, mine_ref, send_ref, full_ref):
     late = far_out.shape[1]
     acc = far_ref[...] + inner_products((early_ref, far_out), grad_ref, far_out.shape[0], far_out.shape[0])
-    far = slot_sources(lax.axis_index("ex"))[3]
+    mid, far = slot_sources(lax.axis_index("ex"))[2:]
     full_ref[...] = base_ref[...]
     for b in range(ex):
-        hit = order_ref[b] == far
+        near_hit, hit = order_ref[b] == mid, order_ref[b] == far
+        low = jnp.where(near_hit, acc[:EARLY], 0.0) + jnp.where(hit, acc[EARLY : 2 * EARLY], 0.0)
         at = b * (EARLY + late)
-        full_ref[at : at + EARLY, :] = full_ref[at : at + EARLY, :] + jnp.where(hit, acc[:EARLY], 0.0)
+        full_ref[at : at + EARLY, :] = full_ref[at : at + EARLY, :] + low
         at = at + EARLY
-        full_ref[at : at + late, :] = full_ref[at : at + late, :] + jnp.where(hit, acc[early_ref.shape[1] :], 0.0)
+        full_ref[at : at + late, :] = full_ref[at : at + late, :] + jnp.where(hit, acc[2 * EARLY :], 0.0)
     half = mine_ref.shape[0]
     side = lax.axis_index("feat")
     mine_ref[...] = full_ref[pl.ds(pl.multiple_of(side * half, half), half), :]
@@ -217,20 +215,20 @@
     terms = factor_terms(left_factor, after(right_factor, raw), train_grads.shape[1])
     raw_near = lax.ppermute(raw, "ex", PAIRS)
     raw_mid = lax.ppermute(raw, "ex", MIDDLE)
-    grads = regroup(after(train_grads, *terms))
-    raw_mid_out = lax.ppermute(after(raw_mid, grads), "ex", OUTWARD)
-    raw_far_mid = lax.ppermute(after(raw_near, late_other), "ex", MIDDLE)
-
-    late = condition(after(late_raw, raw_near, raw_mid, grads), late_other, *terms)
+    raw_mid_out = lax.ppermute(after(raw_mid, *terms), "ex", OUTWARD)
+    early_0 = jnp.concatenate([raw, after(raw_near, raw_mid)], axis=0)
+    raw_far_mid = lax.ppermute(after(raw_near, early_0, late_other), "ex", MIDDLE)
+
+    late = condition(after(late_raw, raw_near, raw_mid), late_other, *terms)
+    near = lax.ppermute(late, "ex", PAIRS)
     mid = lax.ppermute(late, "ex", MIDDLE)
-    near = lax.ppermute(late, "ex", PAIRS)
-    early_0 = jnp.concatenate([raw, raw_near, raw_mid + raw_mid_out], axis=0)
-    early_0_other = lax.ppermute(after(early_0, late, raw_far_mid), "feat", swap)
-    raw_far_out = lax.ppermute(after(raw_far_mid, mid), "ex", OUTWARD)
-    mid_out = lax.ppermute(mid, "ex", OUTWARD)
-    far_mid = lax.ppermute(near, "ex", MIDDLE)
-    early_1 = raw_far_mid + raw_far_out
+    grads = regroup(after(train_grads, late, raw_mid_out))
+    early_0_other = lax.ppermute(after(early_0, late, raw_far_mid, raw_mid_out), "feat", swap)
+    raw_far_out = lax.ppermute(after(raw_far_mid, grads), "ex", OUTWARD)
+    far_mid = lax.ppermute(after(near, grads), "ex", MIDDLE)
+    mid_out = lax.ppermute(after(mid, near, grads), "ex", OUTWARD)
     cond_0 = condition(after(early_0, near, mid), early_0_other, *terms)
+    early_1 = jnp.concatenate([raw_mid + raw_mid_out, after(raw_far_mid, near, mid) + raw_far_out], axis=0)
     early_1_other = lax.ppermute(after(early_1, cond_0), "feat", swap)
     part = far_mid.shape[0] // 2
     far_out_0 = lax.ppermute(far_mid[:part], "ex", OUTWARD)
@@ -243,7 +241,7 @@
     )
     far_0 = score_call(
         far_pass_kernel, ex, (cond_1, far_out_0, after(grads, base)), block_order,
-        jax.ShapeDtypeStruct((cond_1.shape[1] + count - EARLY, n), F32),
+        jax.ShapeDtypeStruct((2 * EARLY + count - EARLY, n), F32),
     )
     half = jax.ShapeDtypeStruct((ex * count // 2, n), F32)
     mine, send = score_call(

time: 76.2 us -> 69.8 us (0.916)
  waiting for transfers between devices: 30.3 us -> 26 us
  starting transfers between devices: 22.8 us -> 21.6 us
    ppermute x6, waiting for transfers between devices: 18.7 us -> 11.6 us  [the longest x1 7.89 us: per_device_line(): mid_out = lax.ppermute(after(mid, near, grads), 'ex', OUTWARD)]
    ppermute x1, waiting for transfers between devices: 0.01 us -> 3.53 us  [per_device_line(): raw_near = lax.ppermute(raw, 'ex', PAIRS)]
    ppermute x1, waiting for transfers between devices: 8.4 us -> 5.05 us  [per_device_line(): near = lax.ppermute(late, 'ex', PAIRS)]
    ppermute x1, starting transfers between devices: 4.45 us -> 1.64 us  [per_device_line(): raw_near = lax.ppermute(raw, 'ex', PAIRS)]
    ppermute x1, waiting for transfers between devices: 0.01 us -> 1.77 us  [per_device_line(): late_other = lax.ppermute(late_raw, 'feat', swap)]
    ppermute x1, starting transfers between devices: 4.4 us -> 5.89 us  [per_device_line(): near = lax.ppermute(late, 'ex', PAIRS)]
    ppermute x1, waiting for transfers between devices: 0.01 us -> 0.98 us  [per_device_line(): far_out_1 = lax.ppermute(far_mid[part:], 'ex', OUTWARD)]
  transfers between devices with their start and end apart: 15 -> 15, of which waited for: 5 -> 9; matrix products, arithmetic and copies ran while one was open for 2% -> 2% of each run, Pallas kernels for 21% -> 21%
where the time goes in v12:
time: 69.8 us; the launch traced here: 69.4 us
  waiting for transfers between devices  26 us (37%)
  starting transfers between devices  21.6 us (31%)
  Pallas kernels  16.7 us (24%)
  local copies, waits for them, and re-layouts  3.98 us (6%)
  other arithmetic  0.98 us (1%)
    ppermute x1, waiting for transfers between devices, per_device_line(): mid_out = lax.ppermute(after(mid, near, grads), 'ex', OUTWARD)  7.89 us
    pallas_call x3, Pallas kernels, score_call(): pl.pallas_call(functools.partial(kernel, ex), out_shape=out_shape, in_spe...  7.66 us
    ppermute x1, starting transfers between devices, per_device_line(): near = lax.ppermute(late, 'ex', PAIRS)  5.89 us
    pallas_call x1, Pallas kernels, regroup(): pl.pallas_call(regroup_kernel, out_shape=jax.ShapeDtypeStruct((rows, n, w...  5.16 us
    ppermute x1, waiting for transfers between devices, per_device_line(): near = lax.ppermute(late, 'ex', PAIRS)  5.05 us
    pallas_call x3, Pallas kernels, condition(): pl.pallas_call(condition_kernel, out_shape=jax.ShapeDtypeStruct((rows, co...  3.79 us
    ppermute x1, waiting for transfers between devices, per_device_line(): raw_near = lax.ppermute(raw, 'ex', PAIRS)  3.53 us
    ppermute x1, waiting for transfers between devices, per_device_line(): raw_far_out = lax.ppermute(after(raw_far_mid, grads), 'ex', OUTWARD)  3.31 us
  transfers between devices with their start and end apart: 15, of which 9 were waited for; matrix products, arithmetic and copies ran while one was open for 2% of the time, Pallas kernels for 21%

profile of v12, /device:TPU:0, one launch (start us, length us, event | category | flops | bytes accessed | tf_op | source)
XLA Modules:
  0.0 69.4 jit_solution(1702425802352805968)
XLA Ops:
  0.0 1.1 %slice_bitcast_fusion.own_ref = bf16[8,128,256]{2,1,0:T(8,128)(2,1)S(1)} fusion(bf16[1,12,128,256]{3,2,1,0:T(8,128)(2,1)} %param.6), kind=kLoop, calls=%fused_computation.2 | loop fusion | bytes 1048576 | tf_op jit(solution)/shard_map/squeeze | solution.py:212
  1.1 3.0 %collective-permute-start.2 = (bf16[8,128,256]{2,1,0:T(8,128)(2,1)S(1)}, bf16[8,128,256]{2,1,0:T(8,128)(2,1)S(1)}, u32[]{:S(2)}, u32[]{:S(2)}) collective-permute-start(bf16[8,128,256]{2,1,0:T(8,128)(2,1)S(1)} %slice_bitcast_fusion.own_ref), channel_id=1, source_target_pairs={{0,2},{2,0},{1,3},{3,1},{4,6},{6,4},{5,7},{7,5},{8,10},{10,8},{9,1... | collective-permute-start | bytes 1572872 | tf_op jit(solution)/shard_map/ppermute | solution.py:213
  4.1 1.0 %slice_bitcast_fusion.1 = bf16[4,128,256]{2,1,0:T(8,128)(2,1)S(1)} fusion(bf16[1,12,128,256]{3,2,1,0:T(8,128)(2,1)} %param.6), kind=kLoop, calls=%fused_computation.3 | loop fusion | bytes 524288 | tf_op jit(solution)/shard_map/squeeze | solution.py:214
  5.1 1.6 %collective-permute-start = (bf16[4,128,256]{2,1,0:T(8,128)(2,1)S(1)}, bf16[4,128,256]{2,1,0:T(8,128)(2,1)S(1)}, u32[]{:S(2)}, u32[]{:S(2)}) collective-permute-start(bf16[4,128,256]{2,1,0:T(8,128)(2,1)S(1)} %slice_bitcast_fusion.1), channel_id=1, source_target_pairs={{0,4},{4,0},{8,12},{12,8},{1,5},{5,1},{9,13},{13,9},{2,6},{6,2},{1... | collective-permute-start | bytes 786440 | tf_op jit(solution)/shard_map/ppermute | solution.py:216
  6.7 0.7 collective-permute-start.1
  7.4 0.9 %copy-done = f32[256,256]{1,0:T(8,128)S(1)} copy-done((f32[256,256]{1,0:T(8,128)S(1)}, f32[256,256]{1,0:T(8,128)}, u32[]{:S(2)}) %copy-start) | copy-done | bytes 262168
  8.3 0.9 %copy-done.1 = f32[256,256]{1,0:T(8,128)S(1)} copy-done((f32[256,256]{1,0:T(8,128)S(1)}, f32[256,256]{1,0:T(8,128)}, u32[]{:S(2)}) %copy-start.1) | copy-done | bytes 262168
  9.4 3.5 %collective-permute-done = bf16[4,128,256]{2,1,0:T(8,128)(2,1)S(1)} collective-permute-done((bf16[4,128,256]{2,1,0:T(8,128)(2,1)S(1)}, bf16[4,128,256]{2,1,0:T(8,128)(2,1)S(1)}, u32[]{:S(2)}, u32[]{:S(2)}) %collective-permute-start) | collective-permute-done | bytes 262176 | tf_op jit(solution)/shard_map/ppermute | solution.py:216
  12.9 1.3 %collective-permute-start.6 = (bf16[4,128,256]{2,1,0:T(8,128)(2,1)S(1)}, bf16[4,128,256]{2,1,0:T(8,128)(2,1)S(1)}, u32[]{:S(2)}, u32[]{:S(2)}) collective-permute-start(bf16[4,128,256]{2,1,0:T(8,128)(2,1)S(1)} %collective-permute-done.1), channel_id=1, source_target_pairs={{4,0},{8,12},{5,1},{9,13},{6,2},{10,14},{7,3},{11,15},{20,16},{24,... | collective-permute-start | bytes 786440 | tf_op jit(solution)/shard_map/ppermute | solution.py:218
  14.2 1.8 %collective-permute-done.2.far_ref = bf16[8,128,256]{2,1,0:T(8,128)(2,1)S(1)} collective-permute-done((bf16[8,128,256]{2,1,0:T(8,128)(2,1)S(1)}, bf16[8,128,256]{2,1,0:T(8,128)(2,1)S(1)}, u32[]{:S(2)}, u32[]{:S(2)}) %collective-permute-start.2) | collective-permute-done | bytes 524320 | tf_op jit(solution)/shard_map/ppermute | solution.py:213
  16.0 0.7 collective-permute-start.5
  16.7 1.3 %shard_map.56.own_ref = bf16[128,8,256]{2,1,0:T(8,128)(2,1)S(1)} custom-call(bf16[8,128,256]{2,1,0:T(8,128)(2,1)S(1)} %slice_bitcast_fusion.own_ref, bf16[8,128,256]{2,1,0:T(8,128)(2,1)S(1)} %collective-permute-done.2.far_ref, bf16[384,256]{1,0:T(8,128)(2,1)S(1)} %get-tuple-element.29.left_ref, bf16[512,256]{1,0:T(8,128)(2,1)S(1)} %get-tuple-element.30.right_ref), custom_call_target="tpu_custom_call" | custom-call | flops 960000000 | bytes 2097152 | tf_op jit(solution)/shard_map/pallas_call | solution.py:70
  18.0 5.9 %collective-permute-start.3 = (bf16[128,8,256]{2,1,0:T(8,128)(2,1)S(1)}, bf16[128,8,256]{2,1,0:T(8,128)(2,1)S(1)}, u32[]{:S(2)}, u32[]{:S(2)}) collective-permute-start(bf16[128,8,256]{2,1,0:T(8,128)(2,1)S(1)} %shard_map.56.own_ref), channel_id=1, source_target_pairs={{0,4},{4,0},{8,12},{12,8},{1,5},{5,1},{9,13},{13,9},{2,6},{6,2},{1... | collective-permute-start | bytes 1572872 | tf_op jit(solution)/shard_map/ppermute | solution.py:223
  23.8 0.7 collective-permute-start.4
  25.1 5.2 %shard_map.58.grad_ref = bf16[128,128,256]{2,1,0:T(8,128)(2,1)S(1)} custom-call(bf16[128,128,256]{2,1,0:T(8,128)(2,1)} %grads_ref), custom_call_target="tpu_custom_call" | custom-call | flops 6000000000 | bytes 16000000 | tf_op jit(solution)/shard_map/pallas_call | solution.py:106
  30.3 1.3 %collective-permute-start.10 = (bf16[4,128,256]{2,1,0:T(8,128)(2,1)S(1)}, bf16[4,128,256]{2,1,0:T(8,128)(2,1)S(1)}, u32[]{:S(2)}, u32[]{:S(2)}) collective-permute-start(bf16[4,128,256]{2,1,0:T(8,128)(2,1)S(1)} %collective-permute-done.5), channel_id=1, source_target_pairs={{4,0},{8,12},{5,1},{9,13},{6,2},{10,14},{7,3},{11,15},{20,16},{24,... | collective-permute-start | bytes 786440 | tf_op jit(solution)/shard_map/ppermute | solution.py:227
  31.6 5.1 %collective-permute-done.3.near = bf16[128,8,256]{2,1,0:T(8,128)(2,1)S(1)} collective-permute-done((bf16[128,8,256]{2,1,0:T(8,128)(2,1)S(1)}, bf16[128,8,256]{2,1,0:T(8,128)(2,1)S(1)}, u32[]{:S(2)}, u32[]{:S(2)}) %collective-permute-start.3) | collective-permute-done | bytes 524320 | tf_op jit(solution)/shard_map/ppermute | solution.py:223
  36.7 0.7 collective-permute-start.9
  37.5 1.3 %collective-permute-start.8 = (bf16[128,8,256]{2,1,0:T(8,128)(2,1)S(1)}, bf16[128,8,256]{2,1,0:T(8,128)(2,1)S(1)}, u32[]{:S(2)}, u32[]{:S(2)}) collective-permute-start(bf16[128,8,256]{2,1,0:T(8,128)(2,1)S(1)} %collective-permute-done.4), channel_id=1, source_target_pairs={{4,0},{8,12},{5,1},{9,13},{6,2},{10,14},{7,3},{11,15},{20,16},{24,... | collective-permute-start | bytes 1572872 | tf_op jit(solution)/shard_map/ppermute | solution.py:229
  38.8 3.3 %collective-permute-done.10 = bf16[4,128,256]{2,1,0:T(8,128)(2,1)S(1)} collective-permute-done((bf16[4,128,256]{2,1,0:T(8,128)(2,1)S(1)}, bf16[4,128,256]{2,1,0:T(8,128)(2,1)S(1)}, u32[]{:S(2)}, u32[]{:S(2)}) %collective-permute-start.10) | collective-permute-done | bytes 262176 | tf_op jit(solution)/shard_map/ppermute | solution.py:227
  42.2 1.3 %shard_map.57.early_ref = bf16[128,8,256]{2,1,0:T(8,128)(2,1)S(1)} custom-call(bf16[8,128,256]{2,1,0:T(8,128)(2,1)S(1)} %pad_maximum_fusion.own_ref, bf16[8,128,256]{2,1,0:T(8,128)(2,1)S(1)} %collective-permute-done.7.far_ref, bf16[384,256]{1,0:T(8,128)(2,1)S(1)} %get-tuple-element.29.left_ref, bf16[512,256]{1,0:T(8,128)(2,1)S(1)} %get-tuple-element.30.right_ref), custom_call_target="tpu_custom_call" | custom-call | flops 960000000 | bytes 2097152 | tf_op jit(solution)/shard_map/pallas_call | solution.py:70
  43.5 0.7 %collective-permute-start.11 = (bf16[8,128,256]{2,1,0:T(8,128)(2,1)S(1)}, bf16[8,128,256]{2,1,0:T(8,128)(2,1)S(1)}, u32[]{:S(2)}, u32[]{:S(2)}) collective-permute-start(bf16[8,128,256]{2,1,0:T(8,128)(2,1)S(1)} %pad_maximum_fusion.1.own_ref), channel_id=1, source_target_pairs={{0,2},{2,0},{1,3},{3,1},{4,6},{6,4},{5,7},{7,5},{8,10},{10,8},{9,1... | collective-permute-start | bytes 1572872 | tf_op jit(solution)/shard_map/ppermute | solution.py:232
  44.3 1.3 %collective-permute-start.12 = (bf16[64,8,256]{2,1,0:T(8,128)(2,1)S(1)}, bf16[64,8,256]{2,1,0:T(8,128)(2,1)S(1)}, u32[]{:S(2)}, u32[]{:S(2)}) collective-permute-start(bf16[64,8,256]{2,1,0:T(8,128)(2,1)S(1)} %get-tuple-element.46), channel_id=1, source_target_pairs={{4,0},{8,12},{5,1},{9,13},{6,2},{10,14},{7,3},{11,15},{20,16},{24,... | collective-permute-start | bytes 786440 | tf_op jit(solution)/shard_map/ppermute | solution.py:234
  45.6 1.3 %collective-permute-start.13 = (bf16[64,8,256]{2,1,0:T(8,128)(2,1)S(1)}, bf16[64,8,256]{2,1,0:T(8,128)(2,1)S(1)}, u32[]{:S(2)}, u32[]{:S(2)}) collective-permute-start(bf16[64,8,256]{2,1,0:T(8,128)(2,1)S(1)} %get-tuple-element.45), channel_id=1, source_target_pairs={{4,0},{8,12},{5,1},{9,13},{6,2},{10,14},{7,3},{11,15},{20,16},{24,... | collective-permute-start | bytes 786440 | tf_op jit(solution)/shard_map/ppermute | solution.py:235
  46.9 7.9 %collective-permute-done.8 = bf16[128,8,256]{2,1,0:T(8,128)(2,1)S(1)} collective-permute-done((bf16[128,8,256]{2,1,0:T(8,128)(2,1)S(1)}, bf16[128,8,256]{2,1,0:T(8,128)(2,1)S(1)}, u32[]{:S(2)}, u32[]{:S(2)}) %collective-permute-start.8) | collective-permute-done | bytes 524320 | tf_op jit(solution)/shard_map/ppermute | solution.py:229
  54.9 3.9 %shard_map.59.base_ref = f32[48,128]{1,0:T(8,128)S(1)} custom-call(bf16[128,8,256]{2,1,0:T(8,128)(2,1)S(1)} %shard_map.57.early_ref, bf16[128,8,256]{2,1,0:T(8,128)(2,1)S(1)} %shard_map.56.own_ref, bf16[128,8,256]{2,1,0:T(8,128)(2,1)S(1)} %collective-permute-done.3.near, bf16[128,8,256]{2,1,0:T(8,128)(2,1)S(1)} %add.12.mid, ...), custom_call_target="tpu_custom_call" | custom-call | flops 1000 | bytes 1000 | tf_op jit(solution)/shard_map/pallas_call | solution.py:187
  58.8 1.3 %shard_map.60.early_ref = bf16[128,8,256]{2,1,0:T(8,128)(2,1)S(1)} custom-call(bf16[8,128,256]{2,1,0:T(8,128)(2,1)S(1)} %pad_maximum_fusion.1.own_ref, bf16[8,128,256]{2,1,0:T(8,128)(2,1)S(1)} %collective-permute-done.11.far_ref, bf16[384,256]{1,0:T(8,128)(2,1)S(1)} %get-tuple-element.29.left_ref, bf16[512,256]{1,0:T(8,128)(2,1)S(1)} %get-tuple-element.30.right_ref), custom_call_target="tpu_custom_call" | custom-call | flops 960000000 | bytes 2097152 | tf_op jit(solution)/shard_map/pallas_call | solution.py:70
  60.4 1.8 %shard_map.61.far_ref = f32[16,128]{1,0:T(8,128)S(1)} custom-call(bf16[128,8,256]{2,1,0:T(8,128)(2,1)S(1)} %shard_map.60.early_ref, bf16[64,8,256]{2,1,0:T(8,128)(2,1)S(1)} %collective-permute-done.12.far_out, bf16[128,128,256]{2,1,0:T(8,128)(2,1)S(1)} %shard_map.58.grad_ref, s32[4]{0:T(128)S(1)} %copy-done.2), custom_call_target="tpu_custom_call" | custom-call | flops 1000 | bytes 1000 | tf_op jit(solution)/shard_map/pallas_call | solution.py:187
  62.2 1.0 %collective-permute-done.13.far_out = bf16[64,8,256]{2,1,0:T(8,128)(2,1)S(1)} collective-permute-done((bf16[64,8,256]{2,1,0:T(8,128)(2,1)S(1)}, bf16[64,8,256]{2,1,0:T(8,128)(2,1)S(1)}, u32[]{:S(2)}, u32[]{:S(2)}) %collective-permute-start.13) | collective-permute-done | bytes 262176 | tf_op jit(solution)/shard_map/ppermute | solution.py:235
  63.2 1.9 %shard_map.62 = (f32[24,128]{1,0:T(8,128)S(1)}, f32[24,128]{1,0:T(8,128)S(1)}) custom-call(f32[48,128]{1,0:T(8,128)S(1)} %shard_map.59.base_ref, f32[16,128]{1,0:T(8,128)S(1)} %shard_map.61.far_ref, bf16[128,8,256]{2,1,0:T(8,128)(2,1)S(1)} %shard_map.60.early_ref, bf16[64,8,256]{2,1,0:T(8,128)(2,1)S(1)} %collective-permute-done.13.far_out, ...), custom_call_target="tpu_custom_call" | custom-call | flops 1000 | bytes 1000 | tf_op jit(solution)/shard_map/pallas_call | solution.py:187
  65.1 0.9 %collective-permute-start.14 = (f32[24,128]{1,0:T(8,128)S(1)}, f32[24,128]{1,0:T(8,128)S(1)}, u32[]{:S(2)}, u32[]{:S(2)}) collective-permute-start(f32[24,128]{1,0:T(8,128)S(1)} %get-tuple-element.44), channel_id=1, source_target_pairs={{0,2},{2,0},{1,3},{3,1},{4,6},{6,4},{5,7},{7,5},{8,10},{10,8},{9,1... | collective-permute-start | bytes 36872 | tf_op jit(solution)/shard_map/ppermute | solution.py:251
  66.0 2.8 %collective-permute-done.14 = f32[24,128]{1,0:T(8,128)S(1)} collective-permute-done((f32[24,128]{1,0:T(8,128)S(1)}, f32[24,128]{1,0:T(8,128)S(1)}, u32[]{:S(2)}, u32[]{:S(2)}) %collective-permute-start.14) | collective-permute-done | bytes 12320 | tf_op jit(solution)/shard_map/ppermute | solution.py:251
  (21 shorter events, 2.0 us)
Async XLA Ops:
  1.1 14.9 %collective-permute-start.2 = (bf16[8,128,256]{2,1,0:T(8,128)(2,1)S(1)}, bf16[8,128,256]{2,1,0:T(8,128)(2,1)S(1)}, u32[]{:S(2)}, u32[]{:S(2)}) collective-permute-start(bf16[8,128,256]{2,1,0:T(8,128)(2,1)S(1)} %slice_bitcast_fusion.own_ref), channel_id=1, source_target_pairs={{0,2},{2,0},{1,3},{3,1},{4,6},{6,4},{5,7},{7,5},{8,10},{10,8},{9,1... | collective-permute-start | bytes 1572872 | tf_op jit(solution)/shard_map/ppermute | solution.py:213
  5.1 7.8 %collective-permute-start = (bf16[4,128,256]{2,1,0:T(8,128)(2,1)S(1)}, bf16[4,128,256]{2,1,0:T(8,128)(2,1)S(1)}, u32[]{:S(2)}, u32[]{:S(2)}) collective-permute-start(bf16[4,128,256]{2,1,0:T(8,128)(2,1)S(1)} %slice_bitcast_fusion.1), channel_id=1, source_target_pairs={{0,4},{4,0},{8,12},{12,8},{1,5},{5,1},{9,13},{13,9},{2,6},{6,2},{1... | collective-permute-start | bytes 786440 | tf_op jit(solution)/shard_map/ppermute | solution.py:216
  6.7 6.2 %collective-permute-start.1 = (bf16[4,128,256]{2,1,0:T(8,128)(2,1)S(1)}, bf16[4,128,256]{2,1,0:T(8,128)(2,1)S(1)}, u32[]{:S(2)}, u32[]{:S(2)}) collective-permute-start(bf16[4,128,256]{2,1,0:T(8,128)(2,1)S(1)} %slice_bitcast_fusion.1), channel_id=1, source_target_pairs={{4,8},{8,4},{5,9},{9,5},{6,10},{10,6},{7,11},{11,7},{20,24},{24,20... | collective-permute-start | bytes 786440 | tf_op jit(solution)/shard_map/ppermute | solution.py:217
  7.4 1.0 %copy-start = (f32[256,256]{1,0:T(8,128)S(1)}, f32[256,256]{1,0:T(8,128)}, u32[]{:S(2)}) copy-start(f32[256,256]{1,0:T(8,128)} %left_ref.1) | copy-start | bytes 786436
  8.3 0.9 %copy-start.1 = (f32[256,256]{1,0:T(8,128)S(1)}, f32[256,256]{1,0:T(8,128)}, u32[]{:S(2)}) copy-start(f32[256,256]{1,0:T(8,128)} %right_ref) | copy-start | bytes 786436
  12.9 12.0 %collective-permute-start.6 = (bf16[4,128,256]{2,1,0:T(8,128)(2,1)S(1)}, bf16[4,128,256]{2,1,0:T(8,128)(2,1)S(1)}, u32[]{:S(2)}, u32[]{:S(2)}) collective-permute-start(bf16[4,128,256]{2,1,0:T(8,128)(2,1)S(1)} %collective-permute-done.1), channel_id=1, source_target_pairs={{4,0},{8,12},{5,1},{9,13},{6,2},{10,14},{7,3},{11,15},{20,16},{24,... | collective-permute-start | bytes 786440 | tf_op jit(solution)/shard_map/ppermute | solution.py:218
  16.0 8.9 %collective-permute-start.5 = (bf16[4,128,256]{2,1,0:T(8,128)(2,1)S(1)}, bf16[4,128,256]{2,1,0:T(8,128)(2,1)S(1)}, u32[]{:S(2)}, u32[]{:S(2)}) collective-permute-start(bf16[4,128,256]{2,1,0:T(8,128)(2,1)S(1)} %collective-permute-done), channel_id=1, source_target_pairs={{4,8},{8,4},{5,9},{9,5},{6,10},{10,6},{7,11},{11,7},{20,24},{24,20... | collective-permute-start | bytes 786440 | tf_op jit(solution)/shard_map/ppermute | solution.py:220
  18.0 18.7 %collective-permute-start.3 = (bf16[128,8,256]{2,1,0:T(8,128)(2,1)S(1)}, bf16[128,8,256]{2,1,0:T(8,128)(2,1)S(1)}, u32[]{:S(2)}, u32[]{:S(2)}) collective-permute-start(bf16[128,8,256]{2,1,0:T(8,128)(2,1)S(1)} %shard_map.56.own_ref), channel_id=1, source_target_pairs={{0,4},{4,0},{8,12},{12,8},{1,5},{5,1},{9,13},{13,9},{2,6},{6,2},{1... | collective-permute-start | bytes 1572872 | tf_op jit(solution)/shard_map/ppermute | solution.py:223
  23.8 13.6 %collective-permute-start.4 = (bf16[128,8,256]{2,1,0:T(8,128)(2,1)S(1)}, bf16[128,8,256]{2,1,0:T(8,128)(2,1)S(1)}, u32[]{:S(2)}, u32[]{:S(2)}) collective-permute-start(bf16[128,8,256]{2,1,0:T(8,128)(2,1)S(1)} %shard_map.56.own_ref), channel_id=1, source_target_pairs={{4,8},{8,4},{5,9},{9,5},{6,10},{10,6},{7,11},{11,7},{20,24},{24,20... | collective-permute-start | bytes 1572872 | tf_op jit(solution)/shard_map/ppermute | solution.py:224
  24.9 17.3 %collective-permute-start.7 = (bf16[8,128,256]{2,1,0:T(8,128)(2,1)S(1)}, bf16[8,128,256]{2,1,0:T(8,128)(2,1)S(1)}, u32[]{:S(2)}, u32[]{:S(2)}) collective-permute-start(bf16[8,128,256]{2,1,0:T(8,128)(2,1)S(1)} %pad_maximum_fusion.own_ref), channel_id=1, source_target_pairs={{0,2},{2,0},{1,3},{3,1},{4,6},{6,4},{5,7},{7,5},{8,10},{10,8},{9,1... | collective-permute-start | bytes 1572872 | tf_op jit(solution)/shard_map/ppermute | solution.py:226
  30.3 24.6 %copy-start.2 = (s32[4]{0:T(128)S(1)}, s32[4]{0:T(128)}, u32[]{:S(2)}) copy-start(s32[4]{0:T(128)} %order_ref.5) | copy-start | bytes 52
  30.3 11.7 %collective-permute-start.10 = (bf16[4,128,256]{2,1,0:T(8,128)(2,1)S(1)}, bf16[4,128,256]{2,1,0:T(8,128)(2,1)S(1)}, u32[]{:S(2)}, u32[]{:S(2)}) collective-permute-start(bf16[4,128,256]{2,1,0:T(8,128)(2,1)S(1)} %collective-permute-done.5), channel_id=1, source_target_pairs={{4,0},{8,12},{5,1},{9,13},{6,2},{10,14},{7,3},{11,15},{20,16},{24,... | collective-permute-start | bytes 786440 | tf_op jit(solution)/shard_map/ppermute | solution.py:227
  36.7 7.5 %collective-permute-start.9 = (bf16[128,8,256]{2,1,0:T(8,128)(2,1)S(1)}, bf16[128,8,256]{2,1,0:T(8,128)(2,1)S(1)}, u32[]{:S(2)}, u32[]{:S(2)}) collective-permute-start(bf16[128,8,256]{2,1,0:T(8,128)(2,1)S(1)} %collective-permute-done.3.near), channel_id=1, source_target_pairs={{4,8},{8,4},{5,9},{9,5},{6,10},{10,6},{7,11},{11,7},{20,24},{24,20... | collective-permute-start | bytes 1572872 | tf_op jit(solution)/shard_map/ppermute | solution.py:228
  37.5 17.3 %collective-permute-start.8 = (bf16[128,8,256]{2,1,0:T(8,128)(2,1)S(1)}, bf16[128,8,256]{2,1,0:T(8,128)(2,1)S(1)}, u32[]{:S(2)}, u32[]{:S(2)}) collective-permute-start(bf16[128,8,256]{2,1,0:T(8,128)(2,1)S(1)} %collective-permute-done.4), channel_id=1, source_target_pairs={{4,0},{8,12},{5,1},{9,13},{6,2},{10,14},{7,3},{11,15},{20,16},{24,... | collective-permute-start | bytes 1572872 | tf_op jit(solution)/shard_map/ppermute | solution.py:229
  43.5 15.4 %collective-permute-start.11 = (bf16[8,128,256]{2,1,0:T(8,128)(2,1)S(1)}, bf16[8,128,256]{2,1,0:T(8,128)(2,1)S(1)}, u32[]{:S(2)}, u32[]{:S(2)}) collective-permute-start(bf16[8,128,256]{2,1,0:T(8,128)(2,1)S(1)} %pad_maximum_fusion.1.own_ref), channel_id=1, source_target_pairs={{0,2},{2,0},{1,3},{3,1},{4,6},{6,4},{5,7},{7,5},{8,10},{10,8},{9,1... | collective-permute-start | bytes 1572872 | tf_op jit(solution)/shard_map/ppermute | solution.py:232
  44.3 16.1 %collective-permute-start.12 = (bf16[64,8,256]{2,1,0:T(8,128)(2,1)S(1)}, bf16[64,8,256]{2,1,0:T(8,128)(2,1)S(1)}, u32[]{:S(2)}, u32[]{:S(2)}) collective-permute-start(bf16[64,8,256]{2,1,0:T(8,128)(2,1)S(1)} %get-tuple-element.46), channel_id=1, source_target_pairs={{4,0},{8,12},{5,1},{9,13},{6,2},{10,14},{7,3},{11,15},{20,16},{24,... | collective-permute-start | bytes 786440 | tf_op jit(solution)/shard_map/ppermute | solution.py:234
  45.6 17.6 %collective-permute-start.13 = (bf16[64,8,256]{2,1,0:T(8,128)(2,1)S(1)}, bf16[64,8,256]{2,1,0:T(8,128)(2,1)S(1)}, u32[]{:S(2)}, u32[]{:S(2)}) collective-permute-start(bf16[64,8,256]{2,1,0:T(8,128)(2,1)S(1)} %get-tuple-element.45), channel_id=1, source_target_pairs={{4,0},{8,12},{5,1},{9,13},{6,2},{10,14},{7,3},{11,15},{20,16},{24,... | collective-permute-start | bytes 786440 | tf_op jit(solution)/shard_map/ppermute | solution.py:235
  65.1 3.8 %collective-permute-start.14 = (f32[24,128]{1,0:T(8,128)S(1)}, f32[24,128]{1,0:T(8,128)S(1)}, u32[]{:S(2)}, u32[]{:S(2)}) collective-permute-start(f32[24,128]{1,0:T(8,128)S(1)} %get-tuple-element.44), channel_id=1, source_target_pairs={{0,2},{2,0},{1,3},{3,1},{4,6},{6,4},{5,7},{7,5},{8,10},{10,8},{9,1... | collective-permute-start | bytes 36872 | tf_op jit(solution)/shard_map/ppermute | solution.py:251

commit v13 on v12

--- a/solution.py
+++ b/solution.py
@@ -135,20 +135,20 @@
     return lax.fori_loop(0, rows // DEEP, body, start)
 
 
-def first_pass_kernel(ex, early_ref, own_ref, near, mid, far_in, grad_ref, order_ref, out_ref):
+def first_pass_kernel(ex, early_ref, own_ref, near, far_in, grad_ref, order_ref, out_ref):
     late = own_ref.shape[1]
-    acc = inner_products((early_ref, own_ref, near, mid, far_in), grad_ref)
+    acc = inner_products((early_ref, own_ref, near, far_in), grad_ref)
     sources = slot_sources(lax.axis_index("ex"))
     early = [acc[EARLY * s : EARLY * (s + 1)] for s in range(2)]
     base = early_ref.shape[1]
-    slots = [acc[base + late * s : base + late * (s + 1)] for s in range(ex)]
+    slots = [acc[base + late * s : base + late * (s + 1)] for s in range(3)]
     for b in range(ex):
         block = order_ref[b]
         low = jnp.zeros_like(early[0])
         for source, slot in zip(sources, early):
             low = low + jnp.where(source == block, slot, 0.0)
         high = jnp.zeros_like(slots[0])
-        for source, slot in zip(sources, slots):
+        for source, slot in zip(sources[:2] + sources[3:], slots):
             high = high + jnp.where(source == block, slot, 0.0)
         at = b * (EARLY + late)
         out_ref[at : at + EARLY, :] = low
@@ -161,22 +161,28 @@
     return [me, near, jnp.where(low_pair, 2, 1), jnp.where(low_pair, 3, 0)]
 
 
-def far_pass_kernel(ex, early_ref, far_out, grad_ref, order_ref, out_ref):
-    out_ref[...] = inner_products((early_ref, far_out), grad_ref, 0, far_out.shape[0])
-
-
-def last_pass_kernel(ex, base_ref, far_ref, early_ref, far_out, grad_ref, order_ref, mine_ref, send_ref, full_ref):
+def far_pass_kernel(ex, early_ref, mid_ref, far_out, grad_ref, order_ref, out_ref):
+    out_ref[...] = inner_products((early_ref, mid_ref, far_out), grad_ref, 0, far_out.shape[0])
+
+
+def last_pass_kernel(
+    ex, base_ref, far_ref, early_ref, mid_ref, far_out, grad_ref, order_ref, mine_ref, send_ref, full_ref
+):
     late = far_out.shape[1]
-    acc = far_ref[...] + inner_products((early_ref, far_out), grad_ref, far_out.shape[0], far_out.shape[0])
+    rows = far_out.shape[0]
+    acc = far_ref[...] + inner_products((early_ref, mid_ref, far_out), grad_ref, rows, rows)
     mid, far = slot_sources(lax.axis_index("ex"))[2:]
+    low_mid, low_far = acc[:EARLY], acc[EARLY : 2 * EARLY]
+    high_mid, high_far = acc[2 * EARLY : 2 * EARLY + late], acc[2 * EARLY + late :]
     full_ref[...] = base_ref[...]
     for b in range(ex):
-        near_hit, hit = order_ref[b] == mid, order_ref[b] == far
-        low = jnp.where(near_hit, acc[:EARLY], 0.0) + jnp.where(hit, acc[EARLY : 2 * EARLY], 0.0)
+        mid_hit, far_hit = order_ref[b] == mid, order_ref[b] == far
+        low = jnp.where(mid_hit, low_mid, 0.0) + jnp.where(far_hit, low_far, 0.0)
+        high = jnp.where(mid_hit, high_mid, 0.0) + jnp.where(far_hit, high_far, 0.0)
         at = b * (EARLY + late)
         full_ref[at : at + EARLY, :] = full_ref[at : at + EARLY, :] + low
         at = at + EARLY
-        full_ref[at : at + late, :] = full_ref[at : at + late, :] + jnp.where(hit, acc[2 * EARLY :], 0.0)
+        full_ref[at : at + late, :] = full_ref[at : at + late, :] + high
     half = mine_ref.shape[0]
     side = lax.axis_index("feat")
     mine_ref[...] = full_ref[pl.ds(pl.multiple_of(side * half, half), half), :]
@@ -236,16 +242,17 @@
     cond_1 = condition(after(early_1, far_mid), early_1_other, *terms)
 
     base = score_call(
-        first_pass_kernel, ex, (cond_0, late, near, mid + mid_out, far_mid, grads), block_order,
+        first_pass_kernel, ex, (cond_0, late, near, far_mid, grads), block_order,
         jax.ShapeDtypeStruct((ex * count, n), F32),
     )
+    mid = mid + mid_out
     far_0 = score_call(
-        far_pass_kernel, ex, (cond_1, far_out_0, after(grads, base)), block_order,
-        jax.ShapeDtypeStruct((2 * EARLY + count - EARLY, n), F32),
+        far_pass_kernel, ex, (cond_1, mid, far_out_0, after(grads, base)), block_order,
+        jax.ShapeDtypeStruct((2 * count, n), F32),
     )
     half = jax.ShapeDtypeStruct((ex * count // 2, n), F32)
     mine, send = score_call(
-        last_pass_kernel, ex, (base, far_0, cond_1, far_out_1, grads), block_order, (half, half),
+        last_pass_kernel, ex, (base, far_0, cond_1, mid, far_out_1, grads), block_order, (half, half),
         [pltpu.VMEM((ex * count, n), F32)],
     )
     scores = mine + lax.ppermute(send, "feat", swap)

time: 69.8 us -> 70.2 us (level)
    ppermute x1, waiting for transfers between devices: 0.25 us -> 4.21 us  [per_device_line(): far_out_0 = lax.ppermute(far_mid[:part], 'ex', OUTWARD)]
    ppermute x1, waiting for transfers between devices: 7.89 us -> 4.04 us  [per_device_line(): mid_out = lax.ppermute(after(mid, near, grads), 'ex', OUTWARD)]
  transfers between devices with their start and end apart: 15 -> 15, of which waited for: 9 -> 9; matrix products, arithmetic and copies ran while one was open for 2% -> 2% of each run, Pallas kernels for 21% -> 22%
where the time goes in v13:
time: 70.2 us; the launch traced here: 69.8 us
  waiting for transfers between devices  25.8 us (37%)
  starting transfers between devices  21.5 us (31%)
  Pallas kernels  17.2 us (25%)
  local copies, waits for them, and re-layouts  3.98 us (6%)
  other arithmetic  0.96 us (1%)
    pallas_call x3, Pallas kernels, score_call(): pl.pallas_call(functools.partial(kernel, ex), out_shape=out_shape, in_spe...  8.23 us
    ppermute x1, starting transfers between devices, per_device_line(): near = lax.ppermute(late, 'ex', PAIRS)  5.89 us
    pallas_call x1, Pallas kernels, regroup(): pl.pallas_call(regroup_kernel, out_shape=jax.ShapeDtypeStruct((rows, n, w...  5.16 us
    ppermute x1, waiting for transfers between devices, per_device_line(): near = lax.ppermute(late, 'ex', PAIRS)  5.06 us
    ppermute x1, waiting for transfers between devices, per_device_line(): far_out_0 = lax.ppermute(far_mid[:part], 'ex', OUTWARD)  4.21 us
    ppermute x1, waiting for transfers between devices, per_device_line(): mid_out = lax.ppermute(after(mid, near, grads), 'ex', OUTWARD)  4.04 us
    pallas_call x3, Pallas kernels, condition(): pl.pallas_call(condition_kernel, out_shape=jax.ShapeDtypeStruct((rows, co...  3.77 us
    ppermute x1, waiting for transfers between devices, per_device_line(): raw_near = lax.ppermute(raw, 'ex', PAIRS)  3.53 us
  transfers between devices with their start and end apart: 15, of which 9 were waited for; matrix products, arithmetic and copies ran while one was open for 2% of the time, Pallas kernels for 22%

profile of v13, /device:TPU:0, one launch (start us, length us, event | category | flops | bytes accessed | tf_op | source)
XLA Modules:
  0.0 69.8 jit_solution(218528315326998525)
XLA Ops:
  0.0 1.1 %slice_bitcast_fusion.own_ref = bf16[8,128,256]{2,1,0:T(8,128)(2,1)S(1)} fusion(bf16[1,12,128,256]{3,2,1,0:T(8,128)(2,1)} %param.6), kind=kLoop, calls=%fused_computation.2 | loop fusion | bytes 1048576 | tf_op jit(solution)/shard_map/squeeze | solution.py:218
  1.1 3.0 %collective-permute-start.2 = (bf16[8,128,256]{2,1,0:T(8,128)(2,1)S(1)}, bf16[8,128,256]{2,1,0:T(8,128)(2,1)S(1)}, u32[]{:S(2)}, u32[]{:S(2)}) collective-permute-start(bf16[8,128,256]{2,1,0:T(8,128)(2,1)S(1)} %slice_bitcast_fusion.own_ref), channel_id=1, source_target_pairs={{0,2},{2,0},{1,3},{3,1},{4,6},{6,4},{5,7},{7,5},{8,10},{10,8},{9,1... | collective-permute-start | bytes 1572872 | tf_op jit(solution)/shard_map/ppermute | solution.py:219
  4.1 1.0 %slice_bitcast_fusion.1 = bf16[4,128,256]{2,1,0:T(8,128)(2,1)S(1)} fusion(bf16[1,12,128,256]{3,2,1,0:T(8,128)(2,1)} %param.6), kind=kLoop, calls=%fused_computation.3 | loop fusion | bytes 524288 | tf_op jit(solution)/shard_map/squeeze | solution.py:220
  5.1 1.6 %collective-permute-start = (bf16[4,128,256]{2,1,0:T(8,128)(2,1)S(1)}, bf16[4,128,256]{2,1,0:T(8,128)(2,1)S(1)}, u32[]{:S(2)}, u32[]{:S(2)}) collective-permute-start(bf16[4,128,256]{2,1,0:T(8,128)(2,1)S(1)} %slice_bitcast_fusion.1), channel_id=1, source_target_pairs={{0,4},{4,0},{8,12},{12,8},{1,5},{5,1},{9,13},{13,9},{2,6},{6,2},{1... | collective-permute-start | bytes 786440 | tf_op jit(solution)/shard_map/ppermute | solution.py:222
  6.7 0.7 collective-permute-start.1
  7.4 0.9 %copy-done = f32[256,256]{1,0:T(8,128)S(1)} copy-done((f32[256,256]{1,0:T(8,128)S(1)}, f32[256,256]{1,0:T(8,128)}, u32[]{:S(2)}) %copy-start) | copy-done | bytes 262168
  8.3 0.9 %copy-done.1 = f32[256,256]{1,0:T(8,128)S(1)} copy-done((f32[256,256]{1,0:T(8,128)S(1)}, f32[256,256]{1,0:T(8,128)}, u32[]{:S(2)}) %copy-start.1) | copy-done | bytes 262168
  9.4 3.5 %collective-permute-done = bf16[4,128,256]{2,1,0:T(8,128)(2,1)S(1)} collective-permute-done((bf16[4,128,256]{2,1,0:T(8,128)(2,1)S(1)}, bf16[4,128,256]{2,1,0:T(8,128)(2,1)S(1)}, u32[]{:S(2)}, u32[]{:S(2)}) %collective-permute-start) | collective-permute-done | bytes 262176 | tf_op jit(solution)/shard_map/ppermute | solution.py:222
  12.9 1.3 %collective-permute-start.6 = (bf16[4,128,256]{2,1,0:T(8,128)(2,1)S(1)}, bf16[4,128,256]{2,1,0:T(8,128)(2,1)S(1)}, u32[]{:S(2)}, u32[]{:S(2)}) collective-permute-start(bf16[4,128,256]{2,1,0:T(8,128)(2,1)S(1)} %collective-permute-done.1), channel_id=1, source_target_pairs={{4,0},{8,12},{5,1},{9,13},{6,2},{10,14},{7,3},{11,15},{20,16},{24,... | collective-permute-start | bytes 786440 | tf_op jit(solution)/shard_map/ppermute | solution.py:224
  14.2 1.8 %collective-permute-done.2.far_ref = bf16[8,128,256]{2,1,0:T(8,128)(2,1)S(1)} collective-permute-done((bf16[8,128,256]{2,1,0:T(8,128)(2,1)S(1)}, bf16[8,128,256]{2,1,0:T(8,128)(2,1)S(1)}, u32[]{:S(2)}, u32[]{:S(2)}) %collective-permute-start.2) | collective-permute-done | bytes 524320 | tf_op jit(solution)/shard_map/ppermute | solution.py:219
  16.0 0.7 collective-permute-start.5
  16.7 1.3 %shard_map.56.own_ref = bf16[128,8,256]{2,1,0:T(8,128)(2,1)S(1)} custom-call(bf16[8,128,256]{2,1,0:T(8,128)(2,1)S(1)} %slice_bitcast_fusion.own_ref, bf16[8,128,256]{2,1,0:T(8,128)(2,1)S(1)} %collective-permute-done.2.far_ref, bf16[384,256]{1,0:T(8,128)(2,1)S(1)} %get-tuple-element.29.left_ref, bf16[512,256]{1,0:T(8,128)(2,1)S(1)} %get-tuple-element.30.right_ref), custom_call_target="tpu_custom_call" | custom-call | flops 960000000 | bytes 2097152 | tf_op jit(solution)/shard_map/pallas_call | solution.py:70
  18.0 5.9 %collective-permute-start.3 = (bf16[128,8,256]{2,1,0:T(8,128)(2,1)S(1)}, bf16[128,8,256]{2,1,0:T(8,128)(2,1)S(1)}, u32[]{:S(2)}, u32[]{:S(2)}) collective-permute-start(bf16[128,8,256]{2,1,0:T(8,128)(2,1)S(1)} %shard_map.56.own_ref), channel_id=1, source_target_pairs={{0,4},{4,0},{8,12},{12,8},{1,5},{5,1},{9,13},{13,9},{2,6},{6,2},{1... | collective-permute-start | bytes 1572872 | tf_op jit(solution)/shard_map/ppermute | solution.py:229
  23.8 0.7 collective-permute-start.4
  25.2 5.2 %shard_map.58.grad_ref = bf16[128,128,256]{2,1,0:T(8,128)(2,1)S(1)} custom-call(bf16[128,128,256]{2,1,0:T(8,128)(2,1)} %grads_ref), custom_call_target="tpu_custom_call" | custom-call | flops 6000000000 | bytes 16000000 | tf_op jit(solution)/shard_map/pallas_call | solution.py:106
  30.3 1.3 %collective-permute-start.9 = (bf16[4,128,256]{2,1,0:T(8,128)(2,1)S(1)}, bf16[4,128,256]{2,1,0:T(8,128)(2,1)S(1)}, u32[]{:S(2)}, u32[]{:S(2)}) collective-permute-start(bf16[4,128,256]{2,1,0:T(8,128)(2,1)S(1)} %collective-permute-done.5), channel_id=1, source_target_pairs={{4,0},{8,12},{5,1},{9,13},{6,2},{10,14},{7,3},{11,15},{20,16},{24,... | collective-permute-start | bytes 786440 | tf_op jit(solution)/shard_map/ppermute | solution.py:233
  31.6 5.1 %collective-permute-done.3.near = bf16[128,8,256]{2,1,0:T(8,128)(2,1)S(1)} collective-permute-done((bf16[128,8,256]{2,1,0:T(8,128)(2,1)S(1)}, bf16[128,8,256]{2,1,0:T(8,128)(2,1)S(1)}, u32[]{:S(2)}, u32[]{:S(2)}) %collective-permute-start.3) | collective-permute-done | bytes 524320 | tf_op jit(solution)/shard_map/ppermute | solution.py:229
  36.7 0.7 collective-permute-start.8
  37.5 1.3 %collective-permute-start.11 = (bf16[128,8,256]{2,1,0:T(8,128)(2,1)S(1)}, bf16[128,8,256]{2,1,0:T(8,128)(2,1)S(1)}, u32[]{:S(2)}, u32[]{:S(2)}) collective-permute-start(bf16[128,8,256]{2,1,0:T(8,128)(2,1)S(1)} %collective-permute-done.4), channel_id=1, source_target_pairs={{4,0},{8,12},{5,1},{9,13},{6,2},{10,14},{7,3},{11,15},{20,16},{24,... | collective-permute-start | bytes 1572872 | tf_op jit(solution)/shard_map/ppermute | solution.py:235
  38.8 3.3 %collective-permute-done.9 = bf16[4,128,256]{2,1,0:T(8,128)(2,1)S(1)} collective-permute-done((bf16[4,128,256]{2,1,0:T(8,128)(2,1)S(1)}, bf16[4,128,256]{2,1,0:T(8,128)(2,1)S(1)}, u32[]{:S(2)}, u32[]{:S(2)}) %collective-permute-start.9) | collective-permute-done | bytes 262176 | tf_op jit(solution)/shard_map/ppermute | solution.py:233
  42.2 1.3 %shard_map.57.early_ref = bf16[128,8,256]{2,1,0:T(8,128)(2,1)S(1)} custom-call(bf16[8,128,256]{2,1,0:T(8,128)(2,1)S(1)} %pad_maximum_fusion.own_ref, bf16[8,128,256]{2,1,0:T(8,128)(2,1)S(1)} %collective-permute-done.7.far_ref, bf16[384,256]{1,0:T(8,128)(2,1)S(1)} %get-tuple-element.29.left_ref, bf16[512,256]{1,0:T(8,128)(2,1)S(1)} %get-tuple-element.30.right_ref), custom_call_target="tpu_custom_call" | custom-call | flops 960000000 | bytes 2097152 | tf_op jit(solution)/shard_map/pallas_call | solution.py:70
  43.5 0.7 %collective-permute-start.10 = (bf16[8,128,256]{2,1,0:T(8,128)(2,1)S(1)}, bf16[8,128,256]{2,1,0:T(8,128)(2,1)S(1)}, u32[]{:S(2)}, u32[]{:S(2)}) collective-permute-start(bf16[8,128,256]{2,1,0:T(8,128)(2,1)S(1)} %pad_maximum_fusion.1.own_ref), channel_id=1, source_target_pairs={{0,2},{2,0},{1,3},{3,1},{4,6},{6,4},{5,7},{7,5},{8,10},{10,8},{9,1... | collective-permute-start | bytes 1572872 | tf_op jit(solution)/shard_map/ppermute | solution.py:238
  44.2 1.3 %collective-permute-start.12 = (bf16[64,8,256]{2,1,0:T(8,128)(2,1)S(1)}, bf16[64,8,256]{2,1,0:T(8,128)(2,1)S(1)}, u32[]{:S(2)}, u32[]{:S(2)}) collective-permute-start(bf16[64,8,256]{2,1,0:T(8,128)(2,1)S(1)} %get-tuple-element.46), channel_id=1, source_target_pairs={{4,0},{8,12},{5,1},{9,13},{6,2},{10,14},{7,3},{11,15},{20,16},{24,... | collective-permute-start | bytes 786440 | tf_op jit(solution)/shard_map/ppermute | solution.py:240
  45.5 1.3 %collective-permute-start.13 = (bf16[64,8,256]{2,1,0:T(8,128)(2,1)S(1)}, bf16[64,8,256]{2,1,0:T(8,128)(2,1)S(1)}, u32[]{:S(2)}, u32[]{:S(2)}) collective-permute-start(bf16[64,8,256]{2,1,0:T(8,128)(2,1)S(1)} %get-tuple-element.45), channel_id=1, source_target_pairs={{4,0},{8,12},{5,1},{9,13},{6,2},{10,14},{7,3},{11,15},{20,16},{24,... | collective-permute-start | bytes 786440 | tf_op jit(solution)/shard_map/ppermute | solution.py:241
  46.8 3.8 %shard_map.59.base_ref = f32[48,128]{1,0:T(8,128)S(1)} custom-call(bf16[128,8,256]{2,1,0:T(8,128)(2,1)S(1)} %shard_map.57.early_ref, bf16[128,8,256]{2,1,0:T(8,128)(2,1)S(1)} %shard_map.56.own_ref, bf16[128,8,256]{2,1,0:T(8,128)(2,1)S(1)} %collective-permute-done.3.near, bf16[128,8,256]{2,1,0:T(8,128)(2,1)S(1)} %collective-permute-done.8.far_in, ...), custom_call_target="tpu_custom_call" | custom-call | flops 1000 | bytes 1000 | tf_op jit(solution)/shard_map/pallas_call | solution.py:193
  50.7 4.0 %collective-permute-done.11 = bf16[128,8,256]{2,1,0:T(8,128)(2,1)S(1)} collective-permute-done((bf16[128,8,256]{2,1,0:T(8,128)(2,1)S(1)}, bf16[128,8,256]{2,1,0:T(8,128)(2,1)S(1)}, u32[]{:S(2)}, u32[]{:S(2)}) %collective-permute-start.11) | collective-permute-done | bytes 524320 | tf_op jit(solution)/shard_map/ppermute | solution.py:235
  54.9 1.3 %shard_map.60.early_ref = bf16[128,8,256]{2,1,0:T(8,128)(2,1)S(1)} custom-call(bf16[8,128,256]{2,1,0:T(8,128)(2,1)S(1)} %pad_maximum_fusion.1.own_ref, bf16[8,128,256]{2,1,0:T(8,128)(2,1)S(1)} %collective-permute-done.10.far_ref, bf16[384,256]{1,0:T(8,128)(2,1)S(1)} %get-tuple-element.29.left_ref, bf16[512,256]{1,0:T(8,128)(2,1)S(1)} %get-tuple-element.30.right_ref), custom_call_target="tpu_custom_call" | custom-call | flops 960000000 | bytes 2097152 | tf_op jit(solution)/shard_map/pallas_call | solution.py:70
  56.1 4.2 %collective-permute-done.12.far_out = bf16[64,8,256]{2,1,0:T(8,128)(2,1)S(1)} collective-permute-done((bf16[64,8,256]{2,1,0:T(8,128)(2,1)S(1)}, bf16[64,8,256]{2,1,0:T(8,128)(2,1)S(1)}, u32[]{:S(2)}, u32[]{:S(2)}) %collective-permute-start.12) | collective-permute-done | bytes 262176 | tf_op jit(solution)/shard_map/ppermute | solution.py:240
  60.3 2.2 %shard_map.61.far_ref = f32[24,128]{1,0:T(8,128)S(1)} custom-call(bf16[128,8,256]{2,1,0:T(8,128)(2,1)S(1)} %shard_map.60.early_ref, bf16[128,8,256]{2,1,0:T(8,128)(2,1)S(1)} %add.14.mid_ref, bf16[64,8,256]{2,1,0:T(8,128)(2,1)S(1)} %collective-permute-done.12.far_out, bf16[128,128,256]{2,1,0:T(8,128)(2,1)S(1)} %shard_map.58.grad_ref, s32[4]{0:T(128)S(1)} %copy-done.2), custom_call_target="tpu_custom_call" | custom-call | flops 1000 | bytes 1000 | tf_op jit(solution)/shard_map/pallas_call | solution.py:193
  63.2 2.2 %shard_map.62 = (f32[24,128]{1,0:T(8,128)S(1)}, f32[24,128]{1,0:T(8,128)S(1)}) custom-call(f32[48,128]{1,0:T(8,128)S(1)} %shard_map.59.base_ref, f32[24,128]{1,0:T(8,128)S(1)} %shard_map.61.far_ref, bf16[128,8,256]{2,1,0:T(8,128)(2,1)S(1)} %shard_map.60.early_ref, bf16[128,8,256]{2,1,0:T(8,128)(2,1)S(1)} %add.14.mid_ref, ...), custom_call_target="tpu_custom_call" | custom-call | flops 1000 | bytes 1000 | tf_op jit(solution)/shard_map/pallas_call | solution.py:193
  65.4 0.9 %collective-permute-start.14 = (f32[24,128]{1,0:T(8,128)S(1)}, f32[24,128]{1,0:T(8,128)S(1)}, u32[]{:S(2)}, u32[]{:S(2)}) collective-permute-start(f32[24,128]{1,0:T(8,128)S(1)} %get-tuple-element.44), channel_id=1, source_target_pairs={{0,2},{2,0},{1,3},{3,1},{4,6},{6,4},{5,7},{7,5},{8,10},{10,8},{9,1... | collective-permute-start | bytes 36872 | tf_op jit(solution)/shard_map/ppermute | solution.py:258
  66.3 2.9 %collective-permute-done.14 = f32[24,128]{1,0:T(8,128)S(1)} collective-permute-done((f32[24,128]{1,0:T(8,128)S(1)}, f32[24,128]{1,0:T(8,128)S(1)}, u32[]{:S(2)}, u32[]{:S(2)}) %collective-permute-start.14) | collective-permute-done | bytes 12320 | tf_op jit(solution)/shard_map/ppermute | solution.py:258
  (21 shorter events, 2.4 us)
Async XLA Ops:
  1.1 14.9 %collective-permute-start.2 = (bf16[8,128,256]{2,1,0:T(8,128)(2,1)S(1)}, bf16[8,128,256]{2,1,0:T(8,128)(2,1)S(1)}, u32[]{:S(2)}, u32[]{:S(2)}) collective-permute-start(bf16[8,128,256]{2,1,0:T(8,128)(2,1)S(1)} %slice_bitcast_fusion.own_ref), channel_id=1, source_target_pairs={{0,2},{2,0},{1,3},{3,1},{4,6},{6,4},{5,7},{7,5},{8,10},{10,8},{9,1... | collective-permute-start | bytes 1572872 | tf_op jit(solution)/shard_map/ppermute | solution.py:219
  5.1 7.8 %collective-permute-start = (bf16[4,128,256]{2,1,0:T(8,128)(2,1)S(1)}, bf16[4,128,256]{2,1,0:T(8,128)(2,1)S(1)}, u32[]{:S(2)}, u32[]{:S(2)}) collective-permute-start(bf16[4,128,256]{2,1,0:T(8,128)(2,1)S(1)} %slice_bitcast_fusion.1), channel_id=1, source_target_pairs={{0,4},{4,0},{8,12},{12,8},{1,5},{5,1},{9,13},{13,9},{2,6},{6,2},{1... | collective-permute-start | bytes 786440 | tf_op jit(solution)/shard_map/ppermute | solution.py:222
  6.7 6.2 %collective-permute-start.1 = (bf16[4,128,256]{2,1,0:T(8,128)(2,1)S(1)}, bf16[4,128,256]{2,1,0:T(8,128)(2,1)S(1)}, u32[]{:S(2)}, u32[]{:S(2)}) collective-permute-start(bf16[4,128,256]{2,1,0:T(8,128)(2,1)S(1)} %slice_bitcast_fusion.1), channel_id=1, source_target_pairs={{4,8},{8,4},{5,9},{9,5},{6,10},{10,6},{7,11},{11,7},{20,24},{24,20... | collective-permute-start | bytes 786440 | tf_op jit(solution)/shard_map/ppermute | solution.py:223
  7.4 1.0 %copy-start = (f32[256,256]{1,0:T(8,128)S(1)}, f32[256,256]{1,0:T(8,128)}, u32[]{:S(2)}) copy-start(f32[256,256]{1,0:T(8,128)} %left_ref.1) | copy-start | bytes 786436
  8.3 0.9 %copy-start.1 = (f32[256,256]{1,0:T(8,128)S(1)}, f32[256,256]{1,0:T(8,128)}, u32[]{:S(2)}) copy-start(f32[256,256]{1,0:T(8,128)} %right_ref) | copy-start | bytes 786436
  12.9 12.0 %collective-permute-start.6 = (bf16[4,128,256]{2,1,0:T(8,128)(2,1)S(1)}, bf16[4,128,256]{2,1,0:T(8,128)(2,1)S(1)}, u32[]{:S(2)}, u32[]{:S(2)}) collective-permute-start(bf16[4,128,256]{2,1,0:T(8,128)(2,1)S(1)} %collective-permute-done.1), channel_id=1, source_target_pairs={{4,0},{8,12},{5,1},{9,13},{6,2},{10,14},{7,3},{11,15},{20,16},{24,... | collective-permute-start | bytes 786440 | tf_op jit(solution)/shard_map/ppermute | solution.py:224
  16.0 8.9 %collective-permute-start.5 = (bf16[4,128,256]{2,1,0:T(8,128)(2,1)S(1)}, bf16[4,128,256]{2,1,0:T(8,128)(2,1)S(1)}, u32[]{:S(2)}, u32[]{:S(2)}) collective-permute-start(bf16[4,128,256]{2,1,0:T(8,128)(2,1)S(1)} %collective-permute-done), channel_id=1, source_target_pairs={{4,8},{8,4},{5,9},{9,5},{6,10},{10,6},{7,11},{11,7},{20,24},{24,20... | collective-permute-start | bytes 786440 | tf_op jit(solution)/shard_map/ppermute | solution.py:226
  17.9 28.9 %copy-start.2 = (s32[4]{0:T(128)S(1)}, s32[4]{0:T(128)}, u32[]{:S(2)}) copy-start(s32[4]{0:T(128)} %order_ref.5) | copy-start | bytes 52
  18.0 18.7 %collective-permute-start.3 = (bf16[128,8,256]{2,1,0:T(8,128)(2,1)S(1)}, bf16[128,8,256]{2,1,0:T(8,128)(2,1)S(1)}, u32[]{:S(2)}, u32[]{:S(2)}) collective-permute-start(bf16[128,8,256]{2,1,0:T(8,128)(2,1)S(1)} %shard_map.56.own_ref), channel_id=1, source_target_pairs={{0,4},{4,0},{8,12},{12,8},{1,5},{5,1},{9,13},{13,9},{2,6},{6,2},{1... | collective-permute-start | bytes 1572872 | tf_op jit(solution)/shard_map/ppermute | solution.py:229
  23.8 13.6 %collective-permute-start.4 = (bf16[128,8,256]{2,1,0:T(8,128)(2,1)S(1)}, bf16[128,8,256]{2,1,0:T(8,128)(2,1)S(1)}, u32[]{:S(2)}, u32[]{:S(2)}) collective-permute-start(bf16[128,8,256]{2,1,0:T(8,128)(2,1)S(1)} %shard_map.56.own_ref), channel_id=1, source_target_pairs={{4,8},{8,4},{5,9},{9,5},{6,10},{10,6},{7,11},{11,7},{20,24},{24,20... | collective-permute-start | bytes 1572872 | tf_op jit(solution)/shard_map/ppermute | solution.py:230
  24.9 17.3 %collective-permute-start.7 = (bf16[8,128,256]{2,1,0:T(8,128)(2,1)S(1)}, bf16[8,128,256]{2,1,0:T(8,128)(2,1)S(1)}, u32[]{:S(2)}, u32[]{:S(2)}) collective-permute-start(bf16[8,128,256]{2,1,0:T(8,128)(2,1)S(1)} %pad_maximum_fusion.own_ref), channel_id=1, source_target_pairs={{0,2},{2,0},{1,3},{3,1},{4,6},{6,4},{5,7},{7,5},{8,10},{10,8},{9,1... | collective-permute-start | bytes 1572872 | tf_op jit(solution)/shard_map/ppermute | solution.py:232
  30.3 11.8 %collective-permute-start.9 = (bf16[4,128,256]{2,1,0:T(8,128)(2,1)S(1)}, bf16[4,128,256]{2,1,0:T(8,128)(2,1)S(1)}, u32[]{:S(2)}, u32[]{:S(2)}) collective-permute-start(bf16[4,128,256]{2,1,0:T(8,128)(2,1)S(1)} %collective-permute-done.5), channel_id=1, source_target_pairs={{4,0},{8,12},{5,1},{9,13},{6,2},{10,14},{7,3},{11,15},{20,16},{24,... | collective-permute-start | bytes 786440 | tf_op jit(solution)/shard_map/ppermute | solution.py:233
  36.7 7.5 %collective-permute-start.8 = (bf16[128,8,256]{2,1,0:T(8,128)(2,1)S(1)}, bf16[128,8,256]{2,1,0:T(8,128)(2,1)S(1)}, u32[]{:S(2)}, u32[]{:S(2)}) collective-permute-start(bf16[128,8,256]{2,1,0:T(8,128)(2,1)S(1)} %collective-permute-done.3.near), channel_id=1, source_target_pairs={{4,8},{8,4},{5,9},{9,5},{6,10},{10,6},{7,11},{11,7},{20,24},{24,20... | collective-permute-start | bytes 1572872 | tf_op jit(solution)/shard_map/ppermute | solution.py:234
  37.5 17.3 %collective-permute-start.11 = (bf16[128,8,256]{2,1,0:T(8,128)(2,1)S(1)}, bf16[128,8,256]{2,1,0:T(8,128)(2,1)S(1)}, u32[]{:S(2)}, u32[]{:S(2)}) collective-permute-start(bf16[128,8,256]{2,1,0:T(8,128)(2,1)S(1)} %collective-permute-done.4), channel_id=1, source_target_pairs={{4,0},{8,12},{5,1},{9,13},{6,2},{10,14},{7,3},{11,15},{20,16},{24,... | collective-permute-start | bytes 1572872 | tf_op jit(solution)/shard_map/ppermute | solution.py:235
  43.5 11.4 %collective-permute-start.10 = (bf16[8,128,256]{2,1,0:T(8,128)(2,1)S(1)}, bf16[8,128,256]{2,1,0:T(8,128)(2,1)S(1)}, u32[]{:S(2)}, u32[]{:S(2)}) collective-permute-start(bf16[8,128,256]{2,1,0:T(8,128)(2,1)S(1)} %pad_maximum_fusion.1.own_ref), channel_id=1, source_target_pairs={{0,2},{2,0},{1,3},{3,1},{4,6},{6,4},{5,7},{7,5},{8,10},{10,8},{9,1... | collective-permute-start | bytes 1572872 | tf_op jit(solution)/shard_map/ppermute | solution.py:238
  44.2 16.1 %collective-permute-start.12 = (bf16[64,8,256]{2,1,0:T(8,128)(2,1)S(1)}, bf16[64,8,256]{2,1,0:T(8,128)(2,1)S(1)}, u32[]{:S(2)}, u32[]{:S(2)}) collective-permute-start(bf16[64,8,256]{2,1,0:T(8,128)(2,1)S(1)} %get-tuple-element.46), channel_id=1, source_target_pairs={{4,0},{8,12},{5,1},{9,13},{6,2},{10,14},{7,3},{11,15},{20,16},{24,... | collective-permute-start | bytes 786440 | tf_op jit(solution)/shard_map/ppermute | solution.py:240
  45.5 17.7 %collective-permute-start.13 = (bf16[64,8,256]{2,1,0:T(8,128)(2,1)S(1)}, bf16[64,8,256]{2,1,0:T(8,128)(2,1)S(1)}, u32[]{:S(2)}, u32[]{:S(2)}) collective-permute-start(bf16[64,8,256]{2,1,0:T(8,128)(2,1)S(1)} %get-tuple-element.45), channel_id=1, source_target_pairs={{4,0},{8,12},{5,1},{9,13},{6,2},{10,14},{7,3},{11,15},{20,16},{24,... | collective-permute-start | bytes 786440 | tf_op jit(solution)/shard_map/ppermute | solution.py:241
  65.4 3.8 %collective-permute-start.14 = (f32[24,128]{1,0:T(8,128)S(1)}, f32[24,128]{1,0:T(8,128)S(1)}, u32[]{:S(2)}, u32[]{:S(2)}) collective-permute-start(f32[24,128]{1,0:T(8,128)S(1)} %get-tuple-element.44), channel_id=1, source_target_pairs={{0,2},{2,0},{1,3},{3,1},{4,6},{6,4},{5,7},{7,5},{8,10},{10,8},{9,1... | collective-permute-start | bytes 36872 | tf_op jit(solution)/shard_map/ppermute | solution.py:258

commit v14 on v13

--- a/solution.py
+++ b/solution.py
@@ -76,6 +76,30 @@
         compiler_params=pltpu.CompilerParams(vmem_limit_bytes=24 << 20),
         cost_estimate=pl.CostEstimate(flops=count * 3_000_000 * 40, bytes_accessed=8 * count * rows * width, transcendentals=0),
     )(own, far, left_terms, right_terms)
+
+
+def split_kernel(queries_ref, early_ref, late_ref, sems):
+    early = pltpu.make_async_copy(queries_ref.at[0, pl.ds(0, EARLY)], early_ref, sems.at[0])
+    late = pltpu.make_async_copy(queries_ref.at[0, pl.ds(EARLY, late_ref.shape[0])], late_ref, sems.at[1])
+    early.start()
+    late.start()
+    early.wait()
+    late.wait()
+
+
+def split(queries):
+    _, count, rows, width = queries.shape
+    return pl.pallas_call(
+        split_kernel,
+        out_shape=(
+            jax.ShapeDtypeStruct((EARLY, rows, width), BF16),
+            jax.ShapeDtypeStruct((count - EARLY, rows, width), BF16),
+        ),
+        in_specs=[pl.BlockSpec(memory_space=pltpu.HBM)],
+        out_specs=(VMEM, VMEM),
+        scratch_shapes=[pltpu.SemaphoreType.DMA((2,))],
+        compiler_params=pltpu.CompilerParams(vmem_limit_bytes=62_300_000),
+    )(queries)
 
 
 def regroup_kernel(grads_ref, out_ref, held_ref, sems):
@@ -215,9 +239,8 @@
     swap = [(0, 1), (1, 0)]
     count = queries.shape[1]
     n = train_grads.shape[0]
-    late_raw = queries[0, EARLY:]
+    raw, late_raw = split(queries)
     late_other = lax.ppermute(late_raw, "feat", swap)
-    raw = after(queries, late_raw)[0, :EARLY]
     terms = factor_terms(left_factor, after(right_factor, raw), train_grads.shape[1])
     raw_near = lax.ppermute(raw, "ex", PAIRS)
     raw_mid = lax.ppermute(raw, "ex", MIDDLE)

time: 70.2 us -> 70.7 us (level)
  waiting for transfers between devices: 25.8 us -> 23 us
  Pallas kernels: 17.2 us -> 19.3 us
  starting transfers between devices: 21.5 us -> 22.9 us
    ppermute x1, waiting for transfers between devices: 5.06 us -> 2.68 us  [per_device_line(): near = lax.ppermute(late, 'ex', PAIRS)]
    squeeze x2 -> x0, local copies, waits for them, and re-layouts: 2.04 us -> none  [the longest x1 1.08 us: per_device_line(): late_raw = queries[0, EARLY:]]
    pallas_call x0 -> x1, Pallas kernels: none -> 2.03 us  [split(): pl.pallas_call(split_kernel, out_shape=(jax.ShapeDtypeStruct((EARLY, rows...]
    unnamed x6 -> x9, local copies, waits for them, and re-layouts: 1.9 us -> 3.9 us
    ppermute x1, waiting for transfers between devices: 4.04 us -> 2.51 us  [per_device_line(): mid_out = lax.ppermute(after(mid, near, grads), 'ex', OUTWARD)]
    ppermute x1, waiting for transfers between devices: 3.31 us -> 4.65 us  [per_device_line(): raw_far_out = lax.ppermute(after(raw_far_mid, grads), 'ex', OUTWARD)]
    ppermute x1, starting transfers between devices: 0.25 us -> 1.43 us  [per_device_line(): lax.ppermute(after(early_0, late, raw_far_mid, raw_mid_out), 'feat', swap)]
    ppermute x1, starting transfers between devices: 5.89 us -> 4.82 us  [per_device_line(): near = lax.ppermute(late, 'ex', PAIRS)]
  transfers between devices with their start and end apart: 15 -> 15, of which waited for: 9 -> 8; matrix products, arithmetic and copies ran while one was open for 2% -> 2% of each run, Pallas kernels for 22% -> 21%
where the time goes in v14:
time: 70.7 us; the launch traced here: 70.3 us
  waiting for transfers between devices  23 us (33%)
  starting transfers between devices  22.9 us (32%)
  Pallas kernels  19.3 us (27%)
  local copies, waits for them, and re-layouts  3.96 us (6%)
  other arithmetic  0.91 us (1%)
    pallas_call x3, Pallas kernels, score_call(): pl.pallas_call(functools.partial(kernel, ex), out_shape=out_shape, in_spe...  8.23 us
    pallas_call x1, Pallas kernels, regroup(): pl.pallas_call(regroup_kernel, out_shape=jax.ShapeDtypeStruct((rows, n, w...  5.17 us
    ppermute x1, starting transfers between devices, per_device_line(): near = lax.ppermute(late, 'ex', PAIRS)  4.82 us
    ppermute x1, waiting for transfers between devices, per_device_line(): raw_far_out = lax.ppermute(after(raw_far_mid, grads), 'ex', OUTWARD)  4.65 us
    ppermute x1, waiting for transfers between devices, per_device_line(): far_out_0 = lax.ppermute(far_mid[:part], 'ex', OUTWARD)  4.21 us
    unnamed x9, local copies, waits for them, and re-layouts  3.9 us
    pallas_call x3, Pallas kernels, condition(): pl.pallas_call(condition_kernel, out_shape=jax.ShapeDtypeStruct((rows, co...  3.76 us
    ppermute x1, starting transfers between devices, per_device_line(): late_other = lax.ppermute(late_raw, 'feat', swap)  3 us
  transfers between devices with their start and end apart: 15, of which 8 were waited for; matrix products, arithmetic and copies ran while one was open for 2% of the time, Pallas kernels for 21%

profile of v14, /device:TPU:0, one launch (start us, length us, event | category | flops | bytes accessed | tf_op | source)
XLA Modules:
  0.0 70.3 jit_solution(5293205279424111485)
XLA Ops:
  0.0 2.0 %shard_map.55 = (bf16[4,128,256]{2,1,0:T(8,128)(2,1)}, bf16[8,128,256]{2,1,0:T(8,128)(2,1)}) custom-call(bf16[1,12,128,256]{3,2,1,0:T(8,128)(2,1)} %queries_ref.1), custom_call_target="tpu_custom_call" | custom-call | tf_op jit(solution)/shard_map/pallas_call | solution.py:92
  2.0 3.0 %collective-permute-start.2 = (bf16[8,128,256]{2,1,0:T(8,128)(2,1)}, bf16[8,128,256]{2,1,0:T(8,128)(2,1)S(1)}, u32[]{:S(2)}, u32[]{:S(2)}) collective-permute-start(bf16[8,128,256]{2,1,0:T(8,128)(2,1)} %get-tuple-element.29.own_ref), channel_id=1, source_target_pairs={{0,2},{2,0},{1,3},{3,1},{4,6},{6,4},{5,7},{7,5},{8,10},{10,8},{9,1... | collective-permute-start | bytes 1572872 | tf_op jit(solution)/shard_map/ppermute | solution.py:243
  5.0 1.6 %collective-permute-start = (bf16[4,128,256]{2,1,0:T(8,128)(2,1)}, bf16[4,128,256]{2,1,0:T(8,128)(2,1)S(1)}, u32[]{:S(2)}, u32[]{:S(2)}) collective-permute-start(bf16[4,128,256]{2,1,0:T(8,128)(2,1)} %get-tuple-element.26), channel_id=1, source_target_pairs={{0,4},{4,0},{8,12},{12,8},{1,5},{5,1},{9,13},{13,9},{2,6},{6,2},{1... | collective-permute-start | bytes 786440 | tf_op jit(solution)/shard_map/ppermute | solution.py:245
  7.3 0.9 %copy-done = f32[256,256]{1,0:T(8,128)S(1)} copy-done((f32[256,256]{1,0:T(8,128)S(1)}, f32[256,256]{1,0:T(8,128)}, u32[]{:S(2)}) %copy-start) | copy-done | bytes 262168
  8.2 0.9 %copy-done.1 = f32[256,256]{1,0:T(8,128)S(1)} copy-done((f32[256,256]{1,0:T(8,128)S(1)}, f32[256,256]{1,0:T(8,128)}, u32[]{:S(2)}) %copy-start.1) | copy-done | bytes 262168
  9.3 1.0 %constant_dynamic-update-slice_fusion.1 = bf16[8,128,256]{2,1,0:T(8,128)(2,1)S(1)} fusion(bf16[4,128,256]{2,1,0:T(8,128)(2,1)} %get-tuple-element.26), kind=kLoop, calls=%fused_computation.3 | loop fusion | bytes 524288
  10.2 2.8 %collective-permute-done = bf16[4,128,256]{2,1,0:T(8,128)(2,1)S(1)} collective-permute-done((bf16[4,128,256]{2,1,0:T(8,128)(2,1)}, bf16[4,128,256]{2,1,0:T(8,128)(2,1)S(1)}, u32[]{:S(2)}, u32[]{:S(2)}) %collective-permute-start) | collective-permute-done | bytes 262176 | tf_op jit(solution)/shard_map/ppermute | solution.py:245
  13.0 1.3 %collective-permute-start.6 = (bf16[4,128,256]{2,1,0:T(8,128)(2,1)S(1)}, bf16[4,128,256]{2,1,0:T(8,128)(2,1)S(1)}, u32[]{:S(2)}, u32[]{:S(2)}) collective-permute-start(bf16[4,128,256]{2,1,0:T(8,128)(2,1)S(1)} %collective-permute-done.1), channel_id=1, source_target_pairs={{4,0},{8,12},{5,1},{9,13},{6,2},{10,14},{7,3},{11,15},{20,16},{24,... | collective-permute-start | bytes 786440 | tf_op jit(solution)/shard_map/ppermute | solution.py:247
  14.3 2.8 %collective-permute-done.2.far_ref = bf16[8,128,256]{2,1,0:T(8,128)(2,1)S(1)} collective-permute-done((bf16[8,128,256]{2,1,0:T(8,128)(2,1)}, bf16[8,128,256]{2,1,0:T(8,128)(2,1)S(1)}, u32[]{:S(2)}, u32[]{:S(2)}) %collective-permute-start.2) | collective-permute-done | bytes 524320 | tf_op jit(solution)/shard_map/ppermute | solution.py:243
  17.9 1.0 %copy-done.3 = bf16[8,128,256]{2,1,0:T(8,128)(2,1)S(1)} copy-done((bf16[8,128,256]{2,1,0:T(8,128)(2,1)S(1)}, bf16[8,128,256]{2,1,0:T(8,128)(2,1)}, u32[]{:S(2)}) %copy-start.3) | copy-done | bytes 524312
  18.9 1.3 %shard_map.57.own_ref = bf16[128,8,256]{2,1,0:T(8,128)(2,1)S(1)} custom-call(bf16[8,128,256]{2,1,0:T(8,128)(2,1)S(1)} %copy-done.3, bf16[8,128,256]{2,1,0:T(8,128)(2,1)S(1)} %collective-permute-done.2.far_ref, bf16[384,256]{1,0:T(8,128)(2,1)S(1)} %get-tuple-element.31.left_ref, bf16[512,256]{1,0:T(8,128)(2,1)S(1)} %get-tuple-element.32.right_ref), custom_call_target="tpu_custom_call" | custom-call | flops 960000000 | bytes 2097152 | tf_op jit(solution)/shard_map/pallas_call | solution.py:70
  20.2 4.8 %collective-permute-start.3 = (bf16[128,8,256]{2,1,0:T(8,128)(2,1)S(1)}, bf16[128,8,256]{2,1,0:T(8,128)(2,1)S(1)}, u32[]{:S(2)}, u32[]{:S(2)}) collective-permute-start(bf16[128,8,256]{2,1,0:T(8,128)(2,1)S(1)} %shard_map.57.own_ref), channel_id=1, source_target_pairs={{0,4},{4,0},{8,12},{12,8},{1,5},{5,1},{9,13},{13,9},{2,6},{6,2},{1... | collective-permute-start | bytes 1572872 | tf_op jit(solution)/shard_map/ppermute | solution.py:252
  25.7 1.4 %collective-permute-start.7 = (bf16[8,128,256]{2,1,0:T(8,128)(2,1)S(1)}, bf16[8,128,256]{2,1,0:T(8,128)(2,1)S(1)}, u32[]{:S(2)}, u32[]{:S(2)}) collective-permute-start(bf16[8,128,256]{2,1,0:T(8,128)(2,1)S(1)} %constant_dynamic-update-slice_fusion.own_ref), channel_id=1, source_target_pairs={{0,2},{2,0},{1,3},{3,1},{4,6},{6,4},{5,7},{7,5},{8,10},{10,8},{9,1... | collective-permute-start | bytes 1572872 | tf_op jit(solution)/shard_map/ppermute | solution.py:255
  27.1 5.2 %shard_map.59.grad_ref = bf16[128,128,256]{2,1,0:T(8,128)(2,1)S(1)} custom-call(bf16[128,128,256]{2,1,0:T(8,128)(2,1)} %grads_ref), custom_call_target="tpu_custom_call" | custom-call | flops 6000000000 | bytes 16000000 | tf_op jit(solution)/shard_map/pallas_call | solution.py:130
  32.3 1.3 %collective-permute-start.9 = (bf16[4,128,256]{2,1,0:T(8,128)(2,1)S(1)}, bf16[4,128,256]{2,1,0:T(8,128)(2,1)S(1)}, u32[]{:S(2)}, u32[]{:S(2)}) collective-permute-start(bf16[4,128,256]{2,1,0:T(8,128)(2,1)S(1)} %collective-permute-done.5), channel_id=1, source_target_pairs={{4,0},{8,12},{5,1},{9,13},{6,2},{10,14},{7,3},{11,15},{20,16},{24,... | collective-permute-start | bytes 786440 | tf_op jit(solution)/shard_map/ppermute | solution.py:256
  33.6 2.7 %collective-permute-done.3.near = bf16[128,8,256]{2,1,0:T(8,128)(2,1)S(1)} collective-permute-done((bf16[128,8,256]{2,1,0:T(8,128)(2,1)S(1)}, bf16[128,8,256]{2,1,0:T(8,128)(2,1)S(1)}, u32[]{:S(2)}, u32[]{:S(2)}) %collective-permute-start.3) | collective-permute-done | bytes 524320 | tf_op jit(solution)/shard_map/ppermute | solution.py:252
  36.3 0.7 collective-permute-start.8
  37.1 1.3 %collective-permute-start.11 = (bf16[128,8,256]{2,1,0:T(8,128)(2,1)S(1)}, bf16[128,8,256]{2,1,0:T(8,128)(2,1)S(1)}, u32[]{:S(2)}, u32[]{:S(2)}) collective-permute-start(bf16[128,8,256]{2,1,0:T(8,128)(2,1)S(1)} %collective-permute-done.4), channel_id=1, source_target_pairs={{4,0},{8,12},{5,1},{9,13},{6,2},{10,14},{7,3},{11,15},{20,16},{24,... | collective-permute-start | bytes 1572872 | tf_op jit(solution)/shard_map/ppermute | solution.py:258
  38.4 4.7 %collective-permute-done.9 = bf16[4,128,256]{2,1,0:T(8,128)(2,1)S(1)} collective-permute-done((bf16[4,128,256]{2,1,0:T(8,128)(2,1)S(1)}, bf16[4,128,256]{2,1,0:T(8,128)(2,1)S(1)}, u32[]{:S(2)}, u32[]{:S(2)}) %collective-permute-start.9) | collective-permute-done | bytes 262176 | tf_op jit(solution)/shard_map/ppermute | solution.py:256
  43.1 1.3 %shard_map.58.early_ref = bf16[128,8,256]{2,1,0:T(8,128)(2,1)S(1)} custom-call(bf16[8,128,256]{2,1,0:T(8,128)(2,1)S(1)} %constant_dynamic-update-slice_fusion.own_ref, bf16[8,128,256]{2,1,0:T(8,128)(2,1)S(1)} %collective-permute-done.7.far_ref, bf16[384,256]{1,0:T(8,128)(2,1)S(1)} %get-tuple-element.31.left_ref, bf16[512,256]{1,0:T(8,128)(2,1)S(1)} %get-tuple-element.32.right_ref), custom_call_target="tpu_custom_call" | custom-call | flops 960000000 | bytes 2097152 | tf_op jit(solution)/shard_map/pallas_call | solution.py:70
  44.4 1.4 %collective-permute-start.10 = (bf16[8,128,256]{2,1,0:T(8,128)(2,1)S(1)}, bf16[8,128,256]{2,1,0:T(8,128)(2,1)S(1)}, u32[]{:S(2)}, u32[]{:S(2)}) collective-permute-start(bf16[8,128,256]{2,1,0:T(8,128)(2,1)S(1)} %pad_maximum_fusion.own_ref), channel_id=1, source_target_pairs={{0,2},{2,0},{1,3},{3,1},{4,6},{6,4},{5,7},{7,5},{8,10},{10,8},{9,1... | collective-permute-start | bytes 1572872 | tf_op jit(solution)/shard_map/ppermute | solution.py:261
  45.9 1.3 %collective-permute-start.12 = (bf16[64,8,256]{2,1,0:T(8,128)(2,1)S(1)}, bf16[64,8,256]{2,1,0:T(8,128)(2,1)S(1)}, u32[]{:S(2)}, u32[]{:S(2)}) collective-permute-start(bf16[64,8,256]{2,1,0:T(8,128)(2,1)S(1)} %get-tuple-element.48), channel_id=1, source_target_pairs={{4,0},{8,12},{5,1},{9,13},{6,2},{10,14},{7,3},{11,15},{20,16},{24,... | collective-permute-start | bytes 786440 | tf_op jit(solution)/shard_map/ppermute | solution.py:263
  47.2 1.3 %collective-permute-start.13 = (bf16[64,8,256]{2,1,0:T(8,128)(2,1)S(1)}, bf16[64,8,256]{2,1,0:T(8,128)(2,1)S(1)}, u32[]{:S(2)}, u32[]{:S(2)}) collective-permute-start(bf16[64,8,256]{2,1,0:T(8,128)(2,1)S(1)} %get-tuple-element.47), channel_id=1, source_target_pairs={{4,0},{8,12},{5,1},{9,13},{6,2},{10,14},{7,3},{11,15},{20,16},{24,... | collective-permute-start | bytes 786440 | tf_op jit(solution)/shard_map/ppermute | solution.py:264
  48.5 3.8 %shard_map.60.base_ref = f32[48,128]{1,0:T(8,128)S(1)} custom-call(bf16[128,8,256]{2,1,0:T(8,128)(2,1)S(1)} %shard_map.58.early_ref, bf16[128,8,256]{2,1,0:T(8,128)(2,1)S(1)} %shard_map.57.own_ref, bf16[128,8,256]{2,1,0:T(8,128)(2,1)S(1)} %collective-permute-done.3.near, bf16[128,8,256]{2,1,0:T(8,128)(2,1)S(1)} %collective-permute-done.8.far_in, ...), custom_call_target="tpu_custom_call" | custom-call | flops 1000 | bytes 1000 | tf_op jit(solution)/shard_map/pallas_call | solution.py:217
  52.3 2.5 %collective-permute-done.11 = bf16[128,8,256]{2,1,0:T(8,128)(2,1)S(1)} collective-permute-done((bf16[128,8,256]{2,1,0:T(8,128)(2,1)S(1)}, bf16[128,8,256]{2,1,0:T(8,128)(2,1)S(1)}, u32[]{:S(2)}, u32[]{:S(2)}) %collective-permute-start.11) | collective-permute-done | bytes 524320 | tf_op jit(solution)/shard_map/ppermute | solution.py:258
  55.0 1.3 %shard_map.61.early_ref = bf16[128,8,256]{2,1,0:T(8,128)(2,1)S(1)} custom-call(bf16[8,128,256]{2,1,0:T(8,128)(2,1)S(1)} %pad_maximum_fusion.own_ref, bf16[8,128,256]{2,1,0:T(8,128)(2,1)S(1)} %collective-permute-done.10.far_ref, bf16[384,256]{1,0:T(8,128)(2,1)S(1)} %get-tuple-element.31.left_ref, bf16[512,256]{1,0:T(8,128)(2,1)S(1)} %get-tuple-element.32.right_ref), custom_call_target="tpu_custom_call" | custom-call | flops 960000000 | bytes 2097152 | tf_op jit(solution)/shard_map/pallas_call | solution.py:70
  56.2 4.2 %collective-permute-done.12.far_out = bf16[64,8,256]{2,1,0:T(8,128)(2,1)S(1)} collective-permute-done((bf16[64,8,256]{2,1,0:T(8,128)(2,1)S(1)}, bf16[64,8,256]{2,1,0:T(8,128)(2,1)S(1)}, u32[]{:S(2)}, u32[]{:S(2)}) %collective-permute-start.12) | collective-permute-done | bytes 262176 | tf_op jit(solution)/shard_map/ppermute | solution.py:263
  60.4 2.2 %shard_map.62.far_ref = f32[24,128]{1,0:T(8,128)S(1)} custom-call(bf16[128,8,256]{2,1,0:T(8,128)(2,1)S(1)} %shard_map.61.early_ref, bf16[128,8,256]{2,1,0:T(8,128)(2,1)S(1)} %add.14.mid_ref, bf16[64,8,256]{2,1,0:T(8,128)(2,1)S(1)} %collective-permute-done.12.far_out, bf16[128,128,256]{2,1,0:T(8,128)(2,1)S(1)} %shard_map.59.grad_ref, s32[4]{0:T(128)S(1)} %copy-done.2), custom_call_target="tpu_custom_call" | custom-call | flops 1000 | bytes 1000 | tf_op jit(solution)/shard_map/pallas_call | solution.py:217
  62.6 1.1 %collective-permute-done.13.far_out = bf16[64,8,256]{2,1,0:T(8,128)(2,1)S(1)} collective-permute-done((bf16[64,8,256]{2,1,0:T(8,128)(2,1)S(1)}, bf16[64,8,256]{2,1,0:T(8,128)(2,1)S(1)}, u32[]{:S(2)}, u32[]{:S(2)}) %collective-permute-start.13) | collective-permute-done | bytes 262176 | tf_op jit(solution)/shard_map/ppermute | solution.py:264
  63.7 2.2 %shard_map.63 = (f32[24,128]{1,0:T(8,128)S(1)}, f32[24,128]{1,0:T(8,128)S(1)}) custom-call(f32[48,128]{1,0:T(8,128)S(1)} %shard_map.60.base_ref, f32[24,128]{1,0:T(8,128)S(1)} %shard_map.62.far_ref, bf16[128,8,256]{2,1,0:T(8,128)(2,1)S(1)} %shard_map.61.early_ref, bf16[128,8,256]{2,1,0:T(8,128)(2,1)S(1)} %add.14.mid_ref, ...), custom_call_target="tpu_custom_call" | custom-call | flops 1000 | bytes 1000 | tf_op jit(solution)/shard_map/pallas_call | solution.py:217
  65.9 1.6 %collective-permute-start.14 = (f32[24,128]{1,0:T(8,128)S(1)}, f32[24,128]{1,0:T(8,128)S(1)}, u32[]{:S(2)}, u32[]{:S(2)}) collective-permute-start(f32[24,128]{1,0:T(8,128)S(1)} %get-tuple-element.46), channel_id=1, source_target_pairs={{0,2},{2,0},{1,3},{3,1},{4,6},{6,4},{5,7},{7,5},{8,10},{10,8},{9,1... | collective-permute-start | bytes 36872 | tf_op jit(solution)/shard_map/ppermute | solution.py:281
  67.5 2.2 %collective-permute-done.14 = f32[24,128]{1,0:T(8,128)S(1)} collective-permute-done((f32[24,128]{1,0:T(8,128)S(1)}, f32[24,128]{1,0:T(8,128)S(1)}, u32[]{:S(2)}, u32[]{:S(2)}) %collective-permute-start.14) | collective-permute-done | bytes 12320 | tf_op jit(solution)/shard_map/ppermute | solution.py:281
  (23 shorter events, 3.1 us)
Async XLA Ops:
  2.0 15.1 %collective-permute-start.2 = (bf16[8,128,256]{2,1,0:T(8,128)(2,1)}, bf16[8,128,256]{2,1,0:T(8,128)(2,1)S(1)}, u32[]{:S(2)}, u32[]{:S(2)}) collective-permute-start(bf16[8,128,256]{2,1,0:T(8,128)(2,1)} %get-tuple-element.29.own_ref), channel_id=1, source_target_pairs={{0,2},{2,0},{1,3},{3,1},{4,6},{6,4},{5,7},{7,5},{8,10},{10,8},{9,1... | collective-permute-start | bytes 1572872 | tf_op jit(solution)/shard_map/ppermute | solution.py:243
  5.0 8.0 %collective-permute-start = (bf16[4,128,256]{2,1,0:T(8,128)(2,1)}, bf16[4,128,256]{2,1,0:T(8,128)(2,1)S(1)}, u32[]{:S(2)}, u32[]{:S(2)}) collective-permute-start(bf16[4,128,256]{2,1,0:T(8,128)(2,1)} %get-tuple-element.26), channel_id=1, source_target_pairs={{0,4},{4,0},{8,12},{12,8},{1,5},{5,1},{9,13},{13,9},{2,6},{6,2},{1... | collective-permute-start | bytes 786440 | tf_op jit(solution)/shard_map/ppermute | solution.py:245
  6.6 6.4 %collective-permute-start.1 = (bf16[4,128,256]{2,1,0:T(8,128)(2,1)}, bf16[4,128,256]{2,1,0:T(8,128)(2,1)S(1)}, u32[]{:S(2)}, u32[]{:S(2)}) collective-permute-start(bf16[4,128,256]{2,1,0:T(8,128)(2,1)} %get-tuple-element.26), channel_id=1, source_target_pairs={{4,8},{8,4},{5,9},{9,5},{6,10},{10,6},{7,11},{11,7},{20,24},{24,20... | collective-permute-start | bytes 786440 | tf_op jit(solution)/shard_map/ppermute | solution.py:246
  7.3 1.0 %copy-start = (f32[256,256]{1,0:T(8,128)S(1)}, f32[256,256]{1,0:T(8,128)}, u32[]{:S(2)}) copy-start(f32[256,256]{1,0:T(8,128)} %left_ref.1) | copy-start | bytes 786436
  8.2 0.9 %copy-start.1 = (f32[256,256]{1,0:T(8,128)S(1)}, f32[256,256]{1,0:T(8,128)}, u32[]{:S(2)}) copy-start(f32[256,256]{1,0:T(8,128)} %right_ref) | copy-start | bytes 786436
  13.0 12.7 %collective-permute-start.6 = (bf16[4,128,256]{2,1,0:T(8,128)(2,1)S(1)}, bf16[4,128,256]{2,1,0:T(8,128)(2,1)S(1)}, u32[]{:S(2)}, u32[]{:S(2)}) collective-permute-start(bf16[4,128,256]{2,1,0:T(8,128)(2,1)S(1)} %collective-permute-done.1), channel_id=1, source_target_pairs={{4,0},{8,12},{5,1},{9,13},{6,2},{10,14},{7,3},{11,15},{20,16},{24,... | collective-permute-start | bytes 786440 | tf_op jit(solution)/shard_map/ppermute | solution.py:247
  17.2 8.5 %collective-permute-start.5 = (bf16[4,128,256]{2,1,0:T(8,128)(2,1)S(1)}, bf16[4,128,256]{2,1,0:T(8,128)(2,1)S(1)}, u32[]{:S(2)}, u32[]{:S(2)}) collective-permute-start(bf16[4,128,256]{2,1,0:T(8,128)(2,1)S(1)} %collective-permute-done), channel_id=1, source_target_pairs={{4,8},{8,4},{5,9},{9,5},{6,10},{10,6},{7,11},{11,7},{20,24},{24,20... | collective-permute-start | bytes 786440 | tf_op jit(solution)/shard_map/ppermute | solution.py:249
  17.8 1.0 %copy-start.3 = (bf16[8,128,256]{2,1,0:T(8,128)(2,1)S(1)}, bf16[8,128,256]{2,1,0:T(8,128)(2,1)}, u32[]{:S(2)}) copy-start(bf16[8,128,256]{2,1,0:T(8,128)(2,1)} %get-tuple-element.29.own_ref) | copy-start | bytes 1572868
  20.1 28.3 %copy-start.2 = (s32[4]{0:T(128)S(1)}, s32[4]{0:T(128)}, u32[]{:S(2)}) copy-start(s32[4]{0:T(128)} %order_ref.5) | copy-start | bytes 52
  20.2 16.1 %collective-permute-start.3 = (bf16[128,8,256]{2,1,0:T(8,128)(2,1)S(1)}, bf16[128,8,256]{2,1,0:T(8,128)(2,1)S(1)}, u32[]{:S(2)}, u32[]{:S(2)}) collective-permute-start(bf16[128,8,256]{2,1,0:T(8,128)(2,1)S(1)} %shard_map.57.own_ref), channel_id=1, source_target_pairs={{0,4},{4,0},{8,12},{12,8},{1,5},{5,1},{9,13},{13,9},{2,6},{6,2},{1... | collective-permute-start | bytes 1572872 | tf_op jit(solution)/shard_map/ppermute | solution.py:252
  25.0 12.1 %collective-permute-start.4 = (bf16[128,8,256]{2,1,0:T(8,128)(2,1)S(1)}, bf16[128,8,256]{2,1,0:T(8,128)(2,1)S(1)}, u32[]{:S(2)}, u32[]{:S(2)}) collective-permute-start(bf16[128,8,256]{2,1,0:T(8,128)(2,1)S(1)} %shard_map.57.own_ref), channel_id=1, source_target_pairs={{4,8},{8,4},{5,9},{9,5},{6,10},{10,6},{7,11},{11,7},{20,24},{24,20... | collective-permute-start | bytes 1572872 | tf_op jit(solution)/shard_map/ppermute | solution.py:253
  25.7 17.4 %collective-permute-start.7 = (bf16[8,128,256]{2,1,0:T(8,128)(2,1)S(1)}, bf16[8,128,256]{2,1,0:T(8,128)(2,1)S(1)}, u32[]{:S(2)}, u32[]{:S(2)}) collective-permute-start(bf16[8,128,256]{2,1,0:T(8,128)(2,1)S(1)} %constant_dynamic-update-slice_fusion.own_ref), channel_id=1, source_target_pairs={{0,2},{2,0},{1,3},{3,1},{4,6},{6,4},{5,7},{7,5},{8,10},{10,8},{9,1... | collective-permute-start | bytes 1572872 | tf_op jit(solution)/shard_map/ppermute | solution.py:255
  32.3 10.7 %collective-permute-start.9 = (bf16[4,128,256]{2,1,0:T(8,128)(2,1)S(1)}, bf16[4,128,256]{2,1,0:T(8,128)(2,1)S(1)}, u32[]{:S(2)}, u32[]{:S(2)}) collective-permute-start(bf16[4,128,256]{2,1,0:T(8,128)(2,1)S(1)} %collective-permute-done.5), channel_id=1, source_target_pairs={{4,0},{8,12},{5,1},{9,13},{6,2},{10,14},{7,3},{11,15},{20,16},{24,... | collective-permute-start | bytes 786440 | tf_op jit(solution)/shard_map/ppermute | solution.py:256
  36.3 9.5 %collective-permute-start.8 = (bf16[128,8,256]{2,1,0:T(8,128)(2,1)S(1)}, bf16[128,8,256]{2,1,0:T(8,128)(2,1)S(1)}, u32[]{:S(2)}, u32[]{:S(2)}) collective-permute-start(bf16[128,8,256]{2,1,0:T(8,128)(2,1)S(1)} %collective-permute-done.3.near), channel_id=1, source_target_pairs={{4,8},{8,4},{5,9},{9,5},{6,10},{10,6},{7,11},{11,7},{20,24},{24,20... | collective-permute-start | bytes 1572872 | tf_op jit(solution)/shard_map/ppermute | solution.py:257
  37.1 17.8 %collective-permute-start.11 = (bf16[128,8,256]{2,1,0:T(8,128)(2,1)S(1)}, bf16[128,8,256]{2,1,0:T(8,128)(2,1)S(1)}, u32[]{:S(2)}, u32[]{:S(2)}) collective-permute-start(bf16[128,8,256]{2,1,0:T(8,128)(2,1)S(1)} %collective-permute-done.4), channel_id=1, source_target_pairs={{4,0},{8,12},{5,1},{9,13},{6,2},{10,14},{7,3},{11,15},{20,16},{24,... | collective-permute-start | bytes 1572872 | tf_op jit(solution)/shard_map/ppermute | solution.py:258
  44.4 10.6 %collective-permute-start.10 = (bf16[8,128,256]{2,1,0:T(8,128)(2,1)S(1)}, bf16[8,128,256]{2,1,0:T(8,128)(2,1)S(1)}, u32[]{:S(2)}, u32[]{:S(2)}) collective-permute-start(bf16[8,128,256]{2,1,0:T(8,128)(2,1)S(1)} %pad_maximum_fusion.own_ref), channel_id=1, source_target_pairs={{0,2},{2,0},{1,3},{3,1},{4,6},{6,4},{5,7},{7,5},{8,10},{10,8},{9,1... | collective-permute-start | bytes 1572872 | tf_op jit(solution)/shard_map/ppermute | solution.py:261
  45.9 14.6 %collective-permute-start.12 = (bf16[64,8,256]{2,1,0:T(8,128)(2,1)S(1)}, bf16[64,8,256]{2,1,0:T(8,128)(2,1)S(1)}, u32[]{:S(2)}, u32[]{:S(2)}) collective-permute-start(bf16[64,8,256]{2,1,0:T(8,128)(2,1)S(1)} %get-tuple-element.48), channel_id=1, source_target_pairs={{4,0},{8,12},{5,1},{9,13},{6,2},{10,14},{7,3},{11,15},{20,16},{24,... | collective-permute-start | bytes 786440 | tf_op jit(solution)/shard_map/ppermute | solution.py:263
  47.2 16.6 %collective-permute-start.13 = (bf16[64,8,256]{2,1,0:T(8,128)(2,1)S(1)}, bf16[64,8,256]{2,1,0:T(8,128)(2,1)S(1)}, u32[]{:S(2)}, u32[]{:S(2)}) collective-permute-start(bf16[64,8,256]{2,1,0:T(8,128)(2,1)S(1)} %get-tuple-element.47), channel_id=1, source_target_pairs={{4,0},{8,12},{5,1},{9,13},{6,2},{10,14},{7,3},{11,15},{20,16},{24,... | collective-permute-start | bytes 786440 | tf_op jit(solution)/shard_map/ppermute | solution.py:264
  65.9 3.8 %collective-permute-start.14 = (f32[24,128]{1,0:T(8,128)S(1)}, f32[24,128]{1,0:T(8,128)S(1)}, u32[]{:S(2)}, u32[]{:S(2)}) collective-permute-start(f32[24,128]{1,0:T(8,128)S(1)} %get-tuple-element.46), channel_id=1, source_target_pairs={{0,2},{2,0},{1,3},{3,1},{4,6},{6,4},{5,7},{7,5},{8,10},{10,8},{9,1... | collective-permute-start | bytes 36872 | tf_op jit(solution)/shard_map/ppermute | solution.py:281

commit v15 on v13

--- a/solution.py
+++ b/solution.py
@@ -222,10 +222,10 @@
     raw_near = lax.ppermute(raw, "ex", PAIRS)
     raw_mid = lax.ppermute(raw, "ex", MIDDLE)
     raw_mid_out = lax.ppermute(after(raw_mid, *terms), "ex", OUTWARD)
-    early_0 = jnp.concatenate([raw, after(raw_near, raw_mid)], axis=0)
+    early_0 = jnp.concatenate([raw, raw_near], axis=0)
     raw_far_mid = lax.ppermute(after(raw_near, early_0, late_other), "ex", MIDDLE)
 
-    late = condition(after(late_raw, raw_near, raw_mid), late_other, *terms)
+    late = condition(after(late_raw, raw_near, raw_mid, early_0), late_other, *terms)
     near = lax.ppermute(late, "ex", PAIRS)
     mid = lax.ppermute(late, "ex", MIDDLE)
     grads = regroup(after(train_grads, late, raw_mid_out))

time: 70.2 us -> 69.8 us (level)
  waiting for transfers between devices: 25.8 us -> 23.4 us
  starting transfers between devices: 21.5 us -> 23.5 us
    ppermute x1, starting transfers between devices: 1.64 us -> 4.45 us  [per_device_line(): raw_near = lax.ppermute(raw, 'ex', PAIRS)]
    ppermute x1, waiting for transfers between devices: 5.06 us -> 2.9 us  [per_device_line(): near = lax.ppermute(late, 'ex', PAIRS)]
    ppermute x1, waiting for transfers between devices: 3.31 us -> 5.19 us  [per_device_line(): raw_far_out = lax.ppermute(after(raw_far_mid, grads), 'ex', OUTWARD)]
    ppermute x1, waiting for transfers between devices: 1.77 us -> 0.02 us  [per_device_line(): late_other = lax.ppermute(late_raw, 'feat', swap)]
    ppermute x1, starting transfers between devices: 0.25 us -> 1.56 us  [per_device_line(): lax.ppermute(after(early_0, late, raw_far_mid, raw_mid_out), 'feat', swap)]
    ppermute x1, starting transfers between devices: 5.89 us -> 4.7 us  [per_device_line(): near = lax.ppermute(late, 'ex', PAIRS)]
    ppermute x1, waiting for transfers between devices: 3.53 us -> 2.45 us  [per_device_line(): raw_near = lax.ppermute(raw, 'ex', PAIRS)]
    ppermute x1, waiting for transfers between devices: 4.04 us -> 5.07 us  [per_device_line(): mid_out = lax.ppermute(after(mid, near, grads), 'ex', OUTWARD)]
  transfers between devices with their start and end apart: 15 -> 15, of which waited for: 9 -> 7; matrix products, arithmetic and copies ran while one was open for 2% -> 2% of each run, Pallas kernels for 22% -> 22%
where the time goes in v15:
time: 69.8 us; the launch traced here: 69.4 us
  starting transfers between devices  23.5 us (34%)
  waiting for transfers between devices  23.4 us (34%)
  Pallas kernels  17.2 us (25%)
  local copies, waits for them, and re-layouts  3.98 us (6%)
  other arithmetic  0.96 us (1%)
    pallas_call x3, Pallas kernels, score_call(): pl.pallas_call(functools.partial(kernel, ex), out_shape=out_shape, in_spe...  8.23 us
    ppermute x1, waiting for transfers between devices, per_device_line(): raw_far_out = lax.ppermute(after(raw_far_mid, grads), 'ex', OUTWARD)  5.19 us
    pallas_call x1, Pallas kernels, regroup(): pl.pallas_call(regroup_kernel, out_shape=jax.ShapeDtypeStruct((rows, n, w...  5.17 us
    ppermute x1, waiting for transfers between devices, per_device_line(): mid_out = lax.ppermute(after(mid, near, grads), 'ex', OUTWARD)  5.07 us
    ppermute x1, starting transfers between devices, per_device_line(): near = lax.ppermute(late, 'ex', PAIRS)  4.7 us
    ppermute x1, starting transfers between devices, per_device_line(): raw_near = lax.ppermute(raw, 'ex', PAIRS)  4.45 us
    ppermute x1, waiting for transfers between devices, per_device_line(): far_out_0 = lax.ppermute(far_mid[:part], 'ex', OUTWARD)  3.97 us
    pallas_call x3, Pallas kernels, condition(): pl.pallas_call(condition_kernel, out_shape=jax.ShapeDtypeStruct((rows, co...  3.77 us
  transfers between devices with their start and end apart: 15, of which 7 were waited for; matrix products, arithmetic and copies ran while one was open for 2% of the time, Pallas kernels for 22%

profile of v15, /device:TPU:0, one launch (start us, length us, event | category | flops | bytes accessed | tf_op | source)
XLA Modules:
  0.0 69.4 jit_solution(3262819759772175079)
XLA Ops:
  0.0 1.1 %slice_bitcast_fusion.own_ref = bf16[8,128,256]{2,1,0:T(8,128)(2,1)S(1)} fusion(bf16[1,12,128,256]{3,2,1,0:T(8,128)(2,1)} %param.6), kind=kLoop, calls=%fused_computation.2 | loop fusion | bytes 1048576 | tf_op jit(solution)/shard_map/squeeze | solution.py:218
  1.1 3.0 %collective-permute-start.2 = (bf16[8,128,256]{2,1,0:T(8,128)(2,1)S(1)}, bf16[8,128,256]{2,1,0:T(8,128)(2,1)S(1)}, u32[]{:S(2)}, u32[]{:S(2)}) collective-permute-start(bf16[8,128,256]{2,1,0:T(8,128)(2,1)S(1)} %slice_bitcast_fusion.own_ref), channel_id=1, source_target_pairs={{0,2},{2,0},{1,3},{3,1},{4,6},{6,4},{5,7},{7,5},{8,10},{10,8},{9,1... | collective-permute-start | bytes 1572872 | tf_op jit(solution)/shard_map/ppermute | solution.py:219
  4.1 1.0 %slice_bitcast_fusion.1 = bf16[4,128,256]{2,1,0:T(8,128)(2,1)S(1)} fusion(bf16[1,12,128,256]{3,2,1,0:T(8,128)(2,1)} %param.6), kind=kLoop, calls=%fused_computation.3 | loop fusion | bytes 524288 | tf_op jit(solution)/shard_map/squeeze | solution.py:220
  5.1 0.7 collective-permute-start.1
  5.7 4.4 %collective-permute-start = (bf16[4,128,256]{2,1,0:T(8,128)(2,1)S(1)}, bf16[4,128,256]{2,1,0:T(8,128)(2,1)S(1)}, u32[]{:S(2)}, u32[]{:S(2)}) collective-permute-start(bf16[4,128,256]{2,1,0:T(8,128)(2,1)S(1)} %slice_bitcast_fusion.1), channel_id=1, source_target_pairs={{0,4},{4,0},{8,12},{12,8},{1,5},{5,1},{9,13},{13,9},{2,6},{6,2},{1... | collective-permute-start | bytes 786440 | tf_op jit(solution)/shard_map/ppermute | solution.py:222
  10.2 0.9 %copy-done = f32[256,256]{1,0:T(8,128)S(1)} copy-done((f32[256,256]{1,0:T(8,128)S(1)}, f32[256,256]{1,0:T(8,128)}, u32[]{:S(2)}) %copy-start) | copy-done | bytes 262168
  11.1 0.9 %copy-done.1 = f32[256,256]{1,0:T(8,128)S(1)} copy-done((f32[256,256]{1,0:T(8,128)S(1)}, f32[256,256]{1,0:T(8,128)}, u32[]{:S(2)}) %copy-start.1) | copy-done | bytes 262168
  12.2 1.3 %collective-permute-start.6 = (bf16[4,128,256]{2,1,0:T(8,128)(2,1)S(1)}, bf16[4,128,256]{2,1,0:T(8,128)(2,1)S(1)}, u32[]{:S(2)}, u32[]{:S(2)}) collective-permute-start(bf16[4,128,256]{2,1,0:T(8,128)(2,1)S(1)} %collective-permute-done.1), channel_id=1, source_target_pairs={{4,0},{8,12},{5,1},{9,13},{6,2},{10,14},{7,3},{11,15},{20,16},{24,... | collective-permute-start | bytes 786440 | tf_op jit(solution)/shard_map/ppermute | solution.py:224
  13.5 2.5 %collective-permute-done = bf16[4,128,256]{2,1,0:T(8,128)(2,1)S(1)} collective-permute-done((bf16[4,128,256]{2,1,0:T(8,128)(2,1)S(1)}, bf16[4,128,256]{2,1,0:T(8,128)(2,1)S(1)}, u32[]{:S(2)}, u32[]{:S(2)}) %collective-permute-start) | collective-permute-done | bytes 262176 | tf_op jit(solution)/shard_map/ppermute | solution.py:222
  16.0 0.7 collective-permute-start.5
  16.7 1.3 %shard_map.56.own_ref = bf16[128,8,256]{2,1,0:T(8,128)(2,1)S(1)} custom-call(bf16[8,128,256]{2,1,0:T(8,128)(2,1)S(1)} %slice_bitcast_fusion.own_ref, bf16[8,128,256]{2,1,0:T(8,128)(2,1)S(1)} %collective-permute-done.2.far_ref, bf16[384,256]{1,0:T(8,128)(2,1)S(1)} %get-tuple-element.27.left_ref, bf16[512,256]{1,0:T(8,128)(2,1)S(1)} %get-tuple-element.28.right_ref), custom_call_target="tpu_custom_call" | custom-call | flops 960000000 | bytes 2097152 | tf_op jit(solution)/shard_map/pallas_call | solution.py:70
  18.0 4.7 %collective-permute-start.3 = (bf16[128,8,256]{2,1,0:T(8,128)(2,1)S(1)}, bf16[128,8,256]{2,1,0:T(8,128)(2,1)S(1)}, u32[]{:S(2)}, u32[]{:S(2)}) collective-permute-start(bf16[128,8,256]{2,1,0:T(8,128)(2,1)S(1)} %shard_map.56.own_ref), channel_id=1, source_target_pairs={{0,4},{4,0},{8,12},{12,8},{1,5},{5,1},{9,13},{13,9},{2,6},{6,2},{1... | collective-permute-start | bytes 1572872 | tf_op jit(solution)/shard_map/ppermute | solution.py:229
  22.7 0.7 collective-permute-start.4
  23.4 1.6 %collective-permute-start.7 = (bf16[8,128,256]{2,1,0:T(8,128)(2,1)S(1)}, bf16[8,128,256]{2,1,0:T(8,128)(2,1)S(1)}, u32[]{:S(2)}, u32[]{:S(2)}) collective-permute-start(bf16[8,128,256]{2,1,0:T(8,128)(2,1)S(1)} %pad_maximum_fusion.own_ref), channel_id=1, source_target_pairs={{0,2},{2,0},{1,3},{3,1},{4,6},{6,4},{5,7},{7,5},{8,10},{10,8},{9,1... | collective-permute-start | bytes 1572872 | tf_op jit(solution)/shard_map/ppermute | solution.py:232
  24.9 5.2 %shard_map.58.grad_ref = bf16[128,128,256]{2,1,0:T(8,128)(2,1)S(1)} custom-call(bf16[128,128,256]{2,1,0:T(8,128)(2,1)} %grads_ref), custom_call_target="tpu_custom_call" | custom-call | flops 6000000000 | bytes 16000000 | tf_op jit(solution)/shard_map/pallas_call | solution.py:106
  30.1 1.3 %collective-permute-start.9 = (bf16[4,128,256]{2,1,0:T(8,128)(2,1)S(1)}, bf16[4,128,256]{2,1,0:T(8,128)(2,1)S(1)}, u32[]{:S(2)}, u32[]{:S(2)}) collective-permute-start(bf16[4,128,256]{2,1,0:T(8,128)(2,1)S(1)} %collective-permute-done.5), channel_id=1, source_target_pairs={{4,0},{8,12},{5,1},{9,13},{6,2},{10,14},{7,3},{11,15},{20,16},{24,... | collective-permute-start | bytes 786440 | tf_op jit(solution)/shard_map/ppermute | solution.py:233
  31.4 2.9 %collective-permute-done.3.near = bf16[128,8,256]{2,1,0:T(8,128)(2,1)S(1)} collective-permute-done((bf16[128,8,256]{2,1,0:T(8,128)(2,1)S(1)}, bf16[128,8,256]{2,1,0:T(8,128)(2,1)S(1)}, u32[]{:S(2)}, u32[]{:S(2)}) %collective-permute-start.3) | collective-permute-done | bytes 524320 | tf_op jit(solution)/shard_map/ppermute | solution.py:229
  34.3 0.7 collective-permute-start.8
  35.1 1.3 %collective-permute-start.11 = (bf16[128,8,256]{2,1,0:T(8,128)(2,1)S(1)}, bf16[128,8,256]{2,1,0:T(8,128)(2,1)S(1)}, u32[]{:S(2)}, u32[]{:S(2)}) collective-permute-start(bf16[128,8,256]{2,1,0:T(8,128)(2,1)S(1)} %collective-permute-done.4), channel_id=1, source_target_pairs={{4,0},{8,12},{5,1},{9,13},{6,2},{10,14},{7,3},{11,15},{20,16},{24,... | collective-permute-start | bytes 1572872 | tf_op jit(solution)/shard_map/ppermute | solution.py:235
  36.4 5.2 %collective-permute-done.9 = bf16[4,128,256]{2,1,0:T(8,128)(2,1)S(1)} collective-permute-done((bf16[4,128,256]{2,1,0:T(8,128)(2,1)S(1)}, bf16[4,128,256]{2,1,0:T(8,128)(2,1)S(1)}, u32[]{:S(2)}, u32[]{:S(2)}) %collective-permute-start.9) | collective-permute-done | bytes 262176 | tf_op jit(solution)/shard_map/ppermute | solution.py:233
  41.7 1.3 %shard_map.57.early_ref = bf16[128,8,256]{2,1,0:T(8,128)(2,1)S(1)} custom-call(bf16[8,128,256]{2,1,0:T(8,128)(2,1)S(1)} %pad_maximum_fusion.own_ref, bf16[8,128,256]{2,1,0:T(8,128)(2,1)S(1)} %collective-permute-done.7.far_ref, bf16[384,256]{1,0:T(8,128)(2,1)S(1)} %get-tuple-element.27.left_ref, bf16[512,256]{1,0:T(8,128)(2,1)S(1)} %get-tuple-element.28.right_ref), custom_call_target="tpu_custom_call" | custom-call | flops 960000000 | bytes 2097152 | tf_op jit(solution)/shard_map/pallas_call | solution.py:70
  43.1 1.3 %collective-permute-start.12 = (bf16[64,8,256]{2,1,0:T(8,128)(2,1)S(1)}, bf16[64,8,256]{2,1,0:T(8,128)(2,1)S(1)}, u32[]{:S(2)}, u32[]{:S(2)}) collective-permute-start(bf16[64,8,256]{2,1,0:T(8,128)(2,1)S(1)} %get-tuple-element.44), channel_id=1, source_target_pairs={{4,0},{8,12},{5,1},{9,13},{6,2},{10,14},{7,3},{11,15},{20,16},{24,... | collective-permute-start | bytes 786440 | tf_op jit(solution)/shard_map/ppermute | solution.py:240
  44.4 1.3 %collective-permute-start.13 = (bf16[64,8,256]{2,1,0:T(8,128)(2,1)S(1)}, bf16[64,8,256]{2,1,0:T(8,128)(2,1)S(1)}, u32[]{:S(2)}, u32[]{:S(2)}) collective-permute-start(bf16[64,8,256]{2,1,0:T(8,128)(2,1)S(1)} %get-tuple-element.43), channel_id=1, source_target_pairs={{4,0},{8,12},{5,1},{9,13},{6,2},{10,14},{7,3},{11,15},{20,16},{24,... | collective-permute-start | bytes 786440 | tf_op jit(solution)/shard_map/ppermute | solution.py:241
  45.7 3.8 %shard_map.59.base_ref = f32[48,128]{1,0:T(8,128)S(1)} custom-call(bf16[128,8,256]{2,1,0:T(8,128)(2,1)S(1)} %shard_map.57.early_ref, bf16[128,8,256]{2,1,0:T(8,128)(2,1)S(1)} %shard_map.56.own_ref, bf16[128,8,256]{2,1,0:T(8,128)(2,1)S(1)} %collective-permute-done.3.near, bf16[128,8,256]{2,1,0:T(8,128)(2,1)S(1)} %collective-permute-done.8.far_in, ...), custom_call_target="tpu_custom_call" | custom-call | flops 1000 | bytes 1000 | tf_op jit(solution)/shard_map/pallas_call | solution.py:193
  49.6 5.1 %collective-permute-done.11 = bf16[128,8,256]{2,1,0:T(8,128)(2,1)S(1)} collective-permute-done((bf16[128,8,256]{2,1,0:T(8,128)(2,1)S(1)}, bf16[128,8,256]{2,1,0:T(8,128)(2,1)S(1)}, u32[]{:S(2)}, u32[]{:S(2)}) %collective-permute-start.11) | collective-permute-done | bytes 524320 | tf_op jit(solution)/shard_map/ppermute | solution.py:235
  54.8 1.3 %shard_map.60.early_ref = bf16[128,8,256]{2,1,0:T(8,128)(2,1)S(1)} custom-call(bf16[8,128,256]{2,1,0:T(8,128)(2,1)S(1)} %pad_maximum_fusion.1.own_ref, bf16[8,128,256]{2,1,0:T(8,128)(2,1)S(1)} %collective-permute-done.10.far_ref, bf16[384,256]{1,0:T(8,128)(2,1)S(1)} %get-tuple-element.27.left_ref, bf16[512,256]{1,0:T(8,128)(2,1)S(1)} %get-tuple-element.28.right_ref), custom_call_target="tpu_custom_call" | custom-call | flops 960000000 | bytes 2097152 | tf_op jit(solution)/shard_map/pallas_call | solution.py:70
  56.0 4.0 %collective-permute-done.12.far_out = bf16[64,8,256]{2,1,0:T(8,128)(2,1)S(1)} collective-permute-done((bf16[64,8,256]{2,1,0:T(8,128)(2,1)S(1)}, bf16[64,8,256]{2,1,0:T(8,128)(2,1)S(1)}, u32[]{:S(2)}, u32[]{:S(2)}) %collective-permute-start.12) | collective-permute-done | bytes 262176 | tf_op jit(solution)/shard_map/ppermute | solution.py:240
  60.0 2.2 %shard_map.61.far_ref = f32[24,128]{1,0:T(8,128)S(1)} custom-call(bf16[128,8,256]{2,1,0:T(8,128)(2,1)S(1)} %shard_map.60.early_ref, bf16[128,8,256]{2,1,0:T(8,128)(2,1)S(1)} %add.14.mid_ref, bf16[64,8,256]{2,1,0:T(8,128)(2,1)S(1)} %collective-permute-done.12.far_out, bf16[128,128,256]{2,1,0:T(8,128)(2,1)S(1)} %shard_map.58.grad_ref, s32[4]{0:T(128)S(1)} %copy-done.2), custom_call_target="tpu_custom_call" | custom-call | flops 1000 | bytes 1000 | tf_op jit(solution)/shard_map/pallas_call | solution.py:193
  62.2 0.6 collective-permute-done.13.far_out
  62.8 2.2 %shard_map.62 = (f32[24,128]{1,0:T(8,128)S(1)}, f32[24,128]{1,0:T(8,128)S(1)}) custom-call(f32[48,128]{1,0:T(8,128)S(1)} %shard_map.59.base_ref, f32[24,128]{1,0:T(8,128)S(1)} %shard_map.61.far_ref, bf16[128,8,256]{2,1,0:T(8,128)(2,1)S(1)} %shard_map.60.early_ref, bf16[128,8,256]{2,1,0:T(8,128)(2,1)S(1)} %add.14.mid_ref, ...), custom_call_target="tpu_custom_call" | custom-call | flops 1000 | bytes 1000 | tf_op jit(solution)/shard_map/pallas_call | solution.py:193
  65.6 3.2 %collective-permute-done.14 = f32[24,128]{1,0:T(8,128)S(1)} collective-permute-done((f32[24,128]{1,0:T(8,128)S(1)}, f32[24,128]{1,0:T(8,128)S(1)}, u32[]{:S(2)}, u32[]{:S(2)}) %collective-permute-start.14) | collective-permute-done | bytes 12320 | tf_op jit(solution)/shard_map/ppermute | solution.py:258
  68.8 0.6 add_bitcast_fusion
  (21 shorter events, 1.2 us)
Async XLA Ops:
  1.1 14.9 %collective-permute-start.2 = (bf16[8,128,256]{2,1,0:T(8,128)(2,1)S(1)}, bf16[8,128,256]{2,1,0:T(8,128)(2,1)S(1)}, u32[]{:S(2)}, u32[]{:S(2)}) collective-permute-start(bf16[8,128,256]{2,1,0:T(8,128)(2,1)S(1)} %slice_bitcast_fusion.own_ref), channel_id=1, source_target_pairs={{0,2},{2,0},{1,3},{3,1},{4,6},{6,4},{5,7},{7,5},{8,10},{10,8},{9,1... | collective-permute-start | bytes 1572872 | tf_op jit(solution)/shard_map/ppermute | solution.py:219
  5.1 7.1 %collective-permute-start.1 = (bf16[4,128,256]{2,1,0:T(8,128)(2,1)S(1)}, bf16[4,128,256]{2,1,0:T(8,128)(2,1)S(1)}, u32[]{:S(2)}, u32[]{:S(2)}) collective-permute-start(bf16[4,128,256]{2,1,0:T(8,128)(2,1)S(1)} %slice_bitcast_fusion.1), channel_id=1, source_target_pairs={{4,8},{8,4},{5,9},{9,5},{6,10},{10,6},{7,11},{11,7},{20,24},{24,20... | collective-permute-start | bytes 786440 | tf_op jit(solution)/shard_map/ppermute | solution.py:223
  5.7 10.2 %collective-permute-start = (bf16[4,128,256]{2,1,0:T(8,128)(2,1)S(1)}, bf16[4,128,256]{2,1,0:T(8,128)(2,1)S(1)}, u32[]{:S(2)}, u32[]{:S(2)}) collective-permute-start(bf16[4,128,256]{2,1,0:T(8,128)(2,1)S(1)} %slice_bitcast_fusion.1), channel_id=1, source_target_pairs={{0,4},{4,0},{8,12},{12,8},{1,5},{5,1},{9,13},{13,9},{2,6},{6,2},{1... | collective-permute-start | bytes 786440 | tf_op jit(solution)/shard_map/ppermute | solution.py:222
  10.2 0.9 %copy-start = (f32[256,256]{1,0:T(8,128)S(1)}, f32[256,256]{1,0:T(8,128)}, u32[]{:S(2)}) copy-start(f32[256,256]{1,0:T(8,128)} %left_ref.1) | copy-start | bytes 786436
  11.1 0.9 %copy-start.1 = (f32[256,256]{1,0:T(8,128)S(1)}, f32[256,256]{1,0:T(8,128)}, u32[]{:S(2)}) copy-start(f32[256,256]{1,0:T(8,128)} %right_ref) | copy-start | bytes 786436
  12.2 11.2 %collective-permute-start.6 = (bf16[4,128,256]{2,1,0:T(8,128)(2,1)S(1)}, bf16[4,128,256]{2,1,0:T(8,128)(2,1)S(1)}, u32[]{:S(2)}, u32[]{:S(2)}) collective-permute-start(bf16[4,128,256]{2,1,0:T(8,128)(2,1)S(1)} %collective-permute-done.1), channel_id=1, source_target_pairs={{4,0},{8,12},{5,1},{9,13},{6,2},{10,14},{7,3},{11,15},{20,16},{24,... | collective-permute-start | bytes 786440 | tf_op jit(solution)/shard_map/ppermute | solution.py:224
  16.0 7.3 %collective-permute-start.5 = (bf16[4,128,256]{2,1,0:T(8,128)(2,1)S(1)}, bf16[4,128,256]{2,1,0:T(8,128)(2,1)S(1)}, u32[]{:S(2)}, u32[]{:S(2)}) collective-permute-start(bf16[4,128,256]{2,1,0:T(8,128)(2,1)S(1)} %collective-permute-done), channel_id=1, source_target_pairs={{4,8},{8,4},{5,9},{9,5},{6,10},{10,6},{7,11},{11,7},{20,24},{24,20... | collective-permute-start | bytes 786440 | tf_op jit(solution)/shard_map/ppermute | solution.py:226
  17.9 27.8 %copy-start.2 = (s32[4]{0:T(128)S(1)}, s32[4]{0:T(128)}, u32[]{:S(2)}) copy-start(s32[4]{0:T(128)} %order_ref.5) | copy-start | bytes 52
  18.0 16.4 %collective-permute-start.3 = (bf16[128,8,256]{2,1,0:T(8,128)(2,1)S(1)}, bf16[128,8,256]{2,1,0:T(8,128)(2,1)S(1)}, u32[]{:S(2)}, u32[]{:S(2)}) collective-permute-start(bf16[128,8,256]{2,1,0:T(8,128)(2,1)S(1)} %shard_map.56.own_ref), channel_id=1, source_target_pairs={{0,4},{4,0},{8,12},{12,8},{1,5},{5,1},{9,13},{13,9},{2,6},{6,2},{1... | collective-permute-start | bytes 1572872 | tf_op jit(solution)/shard_map/ppermute | solution.py:229
  22.7 12.4 %collective-permute-start.4 = (bf16[128,8,256]{2,1,0:T(8,128)(2,1)S(1)}, bf16[128,8,256]{2,1,0:T(8,128)(2,1)S(1)}, u32[]{:S(2)}, u32[]{:S(2)}) collective-permute-start(bf16[128,8,256]{2,1,0:T(8,128)(2,1)S(1)} %shard_map.56.own_ref), channel_id=1, source_target_pairs={{4,8},{8,4},{5,9},{9,5},{6,10},{10,6},{7,11},{11,7},{20,24},{24,20... | collective-permute-start | bytes 1572872 | tf_op jit(solution)/shard_map/ppermute | solution.py:230
  23.4 18.3 %collective-permute-start.7 = (bf16[8,128,256]{2,1,0:T(8,128)(2,1)S(1)}, bf16[8,128,256]{2,1,0:T(8,128)(2,1)S(1)}, u32[]{:S(2)}, u32[]{:S(2)}) collective-permute-start(bf16[8,128,256]{2,1,0:T(8,128)(2,1)S(1)} %pad_maximum_fusion.own_ref), channel_id=1, source_target_pairs={{0,2},{2,0},{1,3},{3,1},{4,6},{6,4},{5,7},{7,5},{8,10},{10,8},{9,1... | collective-permute-start | bytes 1572872 | tf_op jit(solution)/shard_map/ppermute | solution.py:232
  30.1 11.5 %collective-permute-start.9 = (bf16[4,128,256]{2,1,0:T(8,128)(2,1)S(1)}, bf16[4,128,256]{2,1,0:T(8,128)(2,1)S(1)}, u32[]{:S(2)}, u32[]{:S(2)}) collective-permute-start(bf16[4,128,256]{2,1,0:T(8,128)(2,1)S(1)} %collective-permute-done.5), channel_id=1, source_target_pairs={{4,0},{8,12},{5,1},{9,13},{6,2},{10,14},{7,3},{11,15},{20,16},{24,... | collective-permute-start | bytes 786440 | tf_op jit(solution)/shard_map/ppermute | solution.py:233
  34.3 8.7 %collective-permute-start.8 = (bf16[128,8,256]{2,1,0:T(8,128)(2,1)S(1)}, bf16[128,8,256]{2,1,0:T(8,128)(2,1)S(1)}, u32[]{:S(2)}, u32[]{:S(2)}) collective-permute-start(bf16[128,8,256]{2,1,0:T(8,128)(2,1)S(1)} %collective-permute-done.3.near), channel_id=1, source_target_pairs={{4,8},{8,4},{5,9},{9,5},{6,10},{10,6},{7,11},{11,7},{20,24},{24,20... | collective-permute-start | bytes 1572872 | tf_op jit(solution)/shard_map/ppermute | solution.py:234
  35.1 19.6 %collective-permute-start.11 = (bf16[128,8,256]{2,1,0:T(8,128)(2,1)S(1)}, bf16[128,8,256]{2,1,0:T(8,128)(2,1)S(1)}, u32[]{:S(2)}, u32[]{:S(2)}) collective-permute-start(bf16[128,8,256]{2,1,0:T(8,128)(2,1)S(1)} %collective-permute-done.4), channel_id=1, source_target_pairs={{4,0},{8,12},{5,1},{9,13},{6,2},{10,14},{7,3},{11,15},{20,16},{24,... | collective-permute-start | bytes 1572872 | tf_op jit(solution)/shard_map/ppermute | solution.py:235
  43.0 11.8 %collective-permute-start.10 = (bf16[8,128,256]{2,1,0:T(8,128)(2,1)S(1)}, bf16[8,128,256]{2,1,0:T(8,128)(2,1)S(1)}, u32[]{:S(2)}, u32[]{:S(2)}) collective-permute-start(bf16[8,128,256]{2,1,0:T(8,128)(2,1)S(1)} %pad_maximum_fusion.1.own_ref), channel_id=1, source_target_pairs={{0,2},{2,0},{1,3},{3,1},{4,6},{6,4},{5,7},{7,5},{8,10},{10,8},{9,1... | collective-permute-start | bytes 1572872 | tf_op jit(solution)/shard_map/ppermute | solution.py:238
  43.1 16.9 %collective-permute-start.12 = (bf16[64,8,256]{2,1,0:T(8,128)(2,1)S(1)}, bf16[64,8,256]{2,1,0:T(8,128)(2,1)S(1)}, u32[]{:S(2)}, u32[]{:S(2)}) collective-permute-start(bf16[64,8,256]{2,1,0:T(8,128)(2,1)S(1)} %get-tuple-element.44), channel_id=1, source_target_pairs={{4,0},{8,12},{5,1},{9,13},{6,2},{10,14},{7,3},{11,15},{20,16},{24,... | collective-permute-start | bytes 786440 | tf_op jit(solution)/shard_map/ppermute | solution.py:240
  44.4 18.4 %collective-permute-start.13 = (bf16[64,8,256]{2,1,0:T(8,128)(2,1)S(1)}, bf16[64,8,256]{2,1,0:T(8,128)(2,1)S(1)}, u32[]{:S(2)}, u32[]{:S(2)}) collective-permute-start(bf16[64,8,256]{2,1,0:T(8,128)(2,1)S(1)} %get-tuple-element.43), channel_id=1, source_target_pairs={{4,0},{8,12},{5,1},{9,13},{6,2},{10,14},{7,3},{11,15},{20,16},{24,... | collective-permute-start | bytes 786440 | tf_op jit(solution)/shard_map/ppermute | solution.py:241
  65.0 3.8 %collective-permute-start.14 = (f32[24,128]{1,0:T(8,128)S(1)}, f32[24,128]{1,0:T(8,128)S(1)}, u32[]{:S(2)}, u32[]{:S(2)}) collective-permute-start(f32[24,128]{1,0:T(8,128)S(1)} %get-tuple-element.42), channel_id=1, source_target_pairs={{0,2},{2,0},{1,3},{3,1},{4,6},{6,4},{5,7},{7,5},{8,10},{10,8},{9,1... | collective-permute-start | bytes 36872 | tf_op jit(solution)/shard_map/ppermute | solution.py:258

commit v16 on v15

--- a/solution.py
+++ b/solution.py
@@ -228,8 +228,8 @@
     late = condition(after(late_raw, raw_near, raw_mid, early_0), late_other, *terms)
     near = lax.ppermute(late, "ex", PAIRS)
     mid = lax.ppermute(late, "ex", MIDDLE)
-    grads = regroup(after(train_grads, late, raw_mid_out))
-    early_0_other = lax.ppermute(after(early_0, late, raw_far_mid, raw_mid_out), "feat", swap)
+    grads = regroup(after(train_grads, late, raw_mid_out, raw_far_mid))
+    early_0_other = lax.ppermute(after(early_0, late, raw_mid_out), "feat", swap)
     raw_far_out = lax.ppermute(after(raw_far_mid, grads), "ex", OUTWARD)
     far_mid = lax.ppermute(after(near, grads), "ex", MIDDLE)
     mid_out = lax.ppermute(after(mid, near, grads), "ex", OUTWARD)
@@ -239,7 +239,7 @@
     part = far_mid.shape[0] // 2
     far_out_0 = lax.ppermute(far_mid[:part], "ex", OUTWARD)
     far_out_1 = lax.ppermute(far_mid[part:], "ex", OUTWARD)
-    cond_1 = condition(after(early_1, far_mid), early_1_other, *terms)
+    cond_1 = condition(after(early_1, far_mid, mid_out), early_1_other, *terms)
 
     base = score_call(
         first_pass_kernel, ex, (cond_0, late, near, far_mid, grads), block_order,

time: 69.8 us -> 69 us (0.989)
  waiting for transfers between devices: 23.4 us -> 21.5 us
  starting transfers between devices: 23.5 us -> 24.6 us
    ppermute x1, waiting for transfers between devices: 5.19 us -> 2.81 us  [per_device_line(): raw_far_out = lax.ppermute(after(raw_far_mid, grads), 'ex', OUTWARD)]
    ppermute x1, waiting for transfers between devices: 0.63 us -> 1.83 us  [per_device_line(): far_out_1 = lax.ppermute(far_mid[part:], 'ex', OUTWARD)]
    ppermute x1, waiting for transfers between devices: 5.07 us -> 3.86 us  [per_device_line(): mid_out = lax.ppermute(after(mid, near, grads), 'ex', OUTWARD)]
    ppermute x1, waiting for transfers between devices: 2.9 us -> 3.65 us  [per_device_line(): near = lax.ppermute(late, 'ex', PAIRS)]
  transfers between devices with their start and end apart: 15 -> 15, of which waited for: 7 -> 8; matrix products, arithmetic and copies ran while one was open for 2% -> 2% of each run, Pallas kernels for 22% -> 22%
where the time goes in v16:
time: 69 us; the launch traced here: 68.6 us
  starting transfers between devices  24.6 us (36%)
  waiting for transfers between devices  21.5 us (31%)
  Pallas kernels  17.2 us (25%)
  local copies, waits for them, and re-layouts  3.98 us (6%)
  other arithmetic  0.96 us (1%)
    pallas_call x3, Pallas kernels, score_call(): pl.pallas_call(functools.partial(kernel, ex), out_shape=out_shape, in_spe...  8.23 us
    pallas_call x1, Pallas kernels, regroup(): pl.pallas_call(regroup_kernel, out_shape=jax.ShapeDtypeStruct((rows, n, w...  5.16 us
    ppermute x1, starting transfers between devices, per_device_line(): near = lax.ppermute(late, 'ex', PAIRS)  4.7 us
    ppermute x1, starting transfers between devices, per_device_line(): raw_near = lax.ppermute(raw, 'ex', PAIRS)  4.45 us
    ppermute x1, waiting for transfers between devices, per_device_line(): far_out_0 = lax.ppermute(far_mid[:part], 'ex', OUTWARD)  4 us
    ppermute x1, waiting for transfers between devices, per_device_line(): mid_out = lax.ppermute(after(mid, near, grads), 'ex', OUTWARD)  3.86 us
    pallas_call x3, Pallas kernels, condition(): pl.pallas_call(condition_kernel, out_shape=jax.ShapeDtypeStruct((rows, co...  3.77 us
    ppermute x1, waiting for transfers between devices, per_device_line(): near = lax.ppermute(late, 'ex', PAIRS)  3.65 us
  transfers between devices with their start and end apart: 15, of which 8 were waited for; matrix products, arithmetic and copies ran while one was open for 2% of the time, Pallas kernels for 22%

profile of v16, /device:TPU:0, one launch (start us, length us, event | category | flops | bytes accessed | tf_op | source)
XLA Modules:
  0.0 68.6 jit_solution(14199986818631565178)
XLA Ops:
  0.0 1.1 %slice_bitcast_fusion.own_ref = bf16[8,128,256]{2,1,0:T(8,128)(2,1)S(1)} fusion(bf16[1,12,128,256]{3,2,1,0:T(8,128)(2,1)} %param.6), kind=kLoop, calls=%fused_computation.2 | loop fusion | bytes 1048576 | tf_op jit(solution)/shard_map/squeeze | solution.py:218
  1.1 3.0 %collective-permute-start.2 = (bf16[8,128,256]{2,1,0:T(8,128)(2,1)S(1)}, bf16[8,128,256]{2,1,0:T(8,128)(2,1)S(1)}, u32[]{:S(2)}, u32[]{:S(2)}) collective-permute-start(bf16[8,128,256]{2,1,0:T(8,128)(2,1)S(1)} %slice_bitcast_fusion.own_ref), channel_id=1, source_target_pairs={{0,2},{2,0},{1,3},{3,1},{4,6},{6,4},{5,7},{7,5},{8,10},{10,8},{9,1... | collective-permute-start | bytes 1572872 | tf_op jit(solution)/shard_map/ppermute | solution.py:219
  4.1 1.0 %slice_bitcast_fusion.1 = bf16[4,128,256]{2,1,0:T(8,128)(2,1)S(1)} fusion(bf16[1,12,128,256]{3,2,1,0:T(8,128)(2,1)} %param.6), kind=kLoop, calls=%fused_computation.3 | loop fusion | bytes 524288 | tf_op jit(solution)/shard_map/squeeze | solution.py:220
  5.1 0.7 collective-permute-start.1
  5.7 4.4 %collective-permute-start = (bf16[4,128,256]{2,1,0:T(8,128)(2,1)S(1)}, bf16[4,128,256]{2,1,0:T(8,128)(2,1)S(1)}, u32[]{:S(2)}, u32[]{:S(2)}) collective-permute-start(bf16[4,128,256]{2,1,0:T(8,128)(2,1)S(1)} %slice_bitcast_fusion.1), channel_id=1, source_target_pairs={{0,4},{4,0},{8,12},{12,8},{1,5},{5,1},{9,13},{13,9},{2,6},{6,2},{1... | collective-permute-start | bytes 786440 | tf_op jit(solution)/shard_map/ppermute | solution.py:222
  10.2 0.9 %copy-done = f32[256,256]{1,0:T(8,128)S(1)} copy-done((f32[256,256]{1,0:T(8,128)S(1)}, f32[256,256]{1,0:T(8,128)}, u32[]{:S(2)}) %copy-start) | copy-done | bytes 262168
  11.1 0.9 %copy-done.1 = f32[256,256]{1,0:T(8,128)S(1)} copy-done((f32[256,256]{1,0:T(8,128)S(1)}, f32[256,256]{1,0:T(8,128)}, u32[]{:S(2)}) %copy-start.1) | copy-done | bytes 262168
  12.2 1.3 %collective-permute-start.5 = (bf16[4,128,256]{2,1,0:T(8,128)(2,1)S(1)}, bf16[4,128,256]{2,1,0:T(8,128)(2,1)S(1)}, u32[]{:S(2)}, u32[]{:S(2)}) collective-permute-start(bf16[4,128,256]{2,1,0:T(8,128)(2,1)S(1)} %collective-permute-done.1), channel_id=1, source_target_pairs={{4,0},{8,12},{5,1},{9,13},{6,2},{10,14},{7,3},{11,15},{20,16},{24,... | collective-permute-start | bytes 786440 | tf_op jit(solution)/shard_map/ppermute | solution.py:224
  13.5 2.5 %collective-permute-done = bf16[4,128,256]{2,1,0:T(8,128)(2,1)S(1)} collective-permute-done((bf16[4,128,256]{2,1,0:T(8,128)(2,1)S(1)}, bf16[4,128,256]{2,1,0:T(8,128)(2,1)S(1)}, u32[]{:S(2)}, u32[]{:S(2)}) %collective-permute-start) | collective-permute-done | bytes 262176 | tf_op jit(solution)/shard_map/ppermute | solution.py:222
  16.7 1.3 %shard_map.56.own_ref = bf16[128,8,256]{2,1,0:T(8,128)(2,1)S(1)} custom-call(bf16[8,128,256]{2,1,0:T(8,128)(2,1)S(1)} %slice_bitcast_fusion.own_ref, bf16[8,128,256]{2,1,0:T(8,128)(2,1)S(1)} %collective-permute-done.2.far_ref, bf16[384,256]{1,0:T(8,128)(2,1)S(1)} %get-tuple-element.27.left_ref, bf16[512,256]{1,0:T(8,128)(2,1)S(1)} %get-tuple-element.28.right_ref), custom_call_target="tpu_custom_call" | custom-call | flops 960000000 | bytes 2097152 | tf_op jit(solution)/shard_map/pallas_call | solution.py:70
  18.0 4.7 %collective-permute-start.3 = (bf16[128,8,256]{2,1,0:T(8,128)(2,1)S(1)}, bf16[128,8,256]{2,1,0:T(8,128)(2,1)S(1)}, u32[]{:S(2)}, u32[]{:S(2)}) collective-permute-start(bf16[128,8,256]{2,1,0:T(8,128)(2,1)S(1)} %shard_map.56.own_ref), channel_id=1, source_target_pairs={{0,4},{4,0},{8,12},{12,8},{1,5},{5,1},{9,13},{13,9},{2,6},{6,2},{1... | collective-permute-start | bytes 1572872 | tf_op jit(solution)/shard_map/ppermute | solution.py:229
  22.7 0.7 collective-permute-start.4
  23.4 1.6 %collective-permute-start.6 = (bf16[8,128,256]{2,1,0:T(8,128)(2,1)S(1)}, bf16[8,128,256]{2,1,0:T(8,128)(2,1)S(1)}, u32[]{:S(2)}, u32[]{:S(2)}) collective-permute-start(bf16[8,128,256]{2,1,0:T(8,128)(2,1)S(1)} %pad_maximum_fusion.own_ref), channel_id=1, source_target_pairs={{0,2},{2,0},{1,3},{3,1},{4,6},{6,4},{5,7},{7,5},{8,10},{10,8},{9,1... | collective-permute-start | bytes 1572872 | tf_op jit(solution)/shard_map/ppermute | solution.py:232
  24.9 5.2 %shard_map.58.grad_ref = bf16[128,128,256]{2,1,0:T(8,128)(2,1)S(1)} custom-call(bf16[128,128,256]{2,1,0:T(8,128)(2,1)} %grads_ref), custom_call_target="tpu_custom_call" | custom-call | flops 6000000000 | bytes 16000000 | tf_op jit(solution)/shard_map/pallas_call | solution.py:106
  30.1 1.3 %collective-permute-start.9 = (bf16[4,128,256]{2,1,0:T(8,128)(2,1)S(1)}, bf16[4,128,256]{2,1,0:T(8,128)(2,1)S(1)}, u32[]{:S(2)}, u32[]{:S(2)}) collective-permute-start(bf16[4,128,256]{2,1,0:T(8,128)(2,1)S(1)} %collective-permute-done.7), channel_id=1, source_target_pairs={{4,0},{8,12},{5,1},{9,13},{6,2},{10,14},{7,3},{11,15},{20,16},{24,... | collective-permute-start | bytes 786440 | tf_op jit(solution)/shard_map/ppermute | solution.py:233
  31.4 3.7 %collective-permute-done.3.near = bf16[128,8,256]{2,1,0:T(8,128)(2,1)S(1)} collective-permute-done((bf16[128,8,256]{2,1,0:T(8,128)(2,1)S(1)}, bf16[128,8,256]{2,1,0:T(8,128)(2,1)S(1)}, u32[]{:S(2)}, u32[]{:S(2)}) %collective-permute-start.3) | collective-permute-done | bytes 524320 | tf_op jit(solution)/shard_map/ppermute | solution.py:229
  35.0 0.7 collective-permute-start.8
  35.8 1.3 %collective-permute-start.10 = (bf16[128,8,256]{2,1,0:T(8,128)(2,1)S(1)}, bf16[128,8,256]{2,1,0:T(8,128)(2,1)S(1)}, u32[]{:S(2)}, u32[]{:S(2)}) collective-permute-start(bf16[128,8,256]{2,1,0:T(8,128)(2,1)S(1)} %collective-permute-done.4), channel_id=1, source_target_pairs={{4,0},{8,12},{5,1},{9,13},{6,2},{10,14},{7,3},{11,15},{20,16},{24,... | collective-permute-start | bytes 1572872 | tf_op jit(solution)/shard_map/ppermute | solution.py:235
  37.1 2.8 %collective-permute-done.9 = bf16[4,128,256]{2,1,0:T(8,128)(2,1)S(1)} collective-permute-done((bf16[4,128,256]{2,1,0:T(8,128)(2,1)S(1)}, bf16[4,128,256]{2,1,0:T(8,128)(2,1)S(1)}, u32[]{:S(2)}, u32[]{:S(2)}) %collective-permute-start.9) | collective-permute-done | bytes 262176 | tf_op jit(solution)/shard_map/ppermute | solution.py:233
  40.1 1.3 %shard_map.57.early_ref = bf16[128,8,256]{2,1,0:T(8,128)(2,1)S(1)} custom-call(bf16[8,128,256]{2,1,0:T(8,128)(2,1)S(1)} %pad_maximum_fusion.own_ref, bf16[8,128,256]{2,1,0:T(8,128)(2,1)S(1)} %collective-permute-done.6.far_ref, bf16[384,256]{1,0:T(8,128)(2,1)S(1)} %get-tuple-element.27.left_ref, bf16[512,256]{1,0:T(8,128)(2,1)S(1)} %get-tuple-element.28.right_ref), custom_call_target="tpu_custom_call" | custom-call | flops 960000000 | bytes 2097152 | tf_op jit(solution)/shard_map/pallas_call | solution.py:70
  41.3 0.7 collective-permute-start.11
  42.0 1.3 %collective-permute-start.12 = (bf16[64,8,256]{2,1,0:T(8,128)(2,1)S(1)}, bf16[64,8,256]{2,1,0:T(8,128)(2,1)S(1)}, u32[]{:S(2)}, u32[]{:S(2)}) collective-permute-start(bf16[64,8,256]{2,1,0:T(8,128)(2,1)S(1)} %get-tuple-element.44), channel_id=1, source_target_pairs={{4,0},{8,12},{5,1},{9,13},{6,2},{10,14},{7,3},{11,15},{20,16},{24,... | collective-permute-start | bytes 786440 | tf_op jit(solution)/shard_map/ppermute | solution.py:240
  43.3 1.3 %collective-permute-start.13 = (bf16[64,8,256]{2,1,0:T(8,128)(2,1)S(1)}, bf16[64,8,256]{2,1,0:T(8,128)(2,1)S(1)}, u32[]{:S(2)}, u32[]{:S(2)}) collective-permute-start(bf16[64,8,256]{2,1,0:T(8,128)(2,1)S(1)} %get-tuple-element.43), channel_id=1, source_target_pairs={{4,0},{8,12},{5,1},{9,13},{6,2},{10,14},{7,3},{11,15},{20,16},{24,... | collective-permute-start | bytes 786440 | tf_op jit(solution)/shard_map/ppermute | solution.py:241
  44.6 3.8 %shard_map.59.base_ref = f32[48,128]{1,0:T(8,128)S(1)} custom-call(bf16[128,8,256]{2,1,0:T(8,128)(2,1)S(1)} %shard_map.57.early_ref, bf16[128,8,256]{2,1,0:T(8,128)(2,1)S(1)} %shard_map.56.own_ref, bf16[128,8,256]{2,1,0:T(8,128)(2,1)S(1)} %collective-permute-done.3.near, bf16[128,8,256]{2,1,0:T(8,128)(2,1)S(1)} %collective-permute-done.8.far_in, ...), custom_call_target="tpu_custom_call" | custom-call | flops 1000 | bytes 1000 | tf_op jit(solution)/shard_map/pallas_call | solution.py:193
  48.5 3.9 %collective-permute-done.10 = bf16[128,8,256]{2,1,0:T(8,128)(2,1)S(1)} collective-permute-done((bf16[128,8,256]{2,1,0:T(8,128)(2,1)S(1)}, bf16[128,8,256]{2,1,0:T(8,128)(2,1)S(1)}, u32[]{:S(2)}, u32[]{:S(2)}) %collective-permute-start.10) | collective-permute-done | bytes 524320 | tf_op jit(solution)/shard_map/ppermute | solution.py:235
  52.7 1.3 %shard_map.60.early_ref = bf16[128,8,256]{2,1,0:T(8,128)(2,1)S(1)} custom-call(bf16[8,128,256]{2,1,0:T(8,128)(2,1)S(1)} %pad_maximum_fusion.1.own_ref, bf16[8,128,256]{2,1,0:T(8,128)(2,1)S(1)} %collective-permute-done.11.far_ref, bf16[384,256]{1,0:T(8,128)(2,1)S(1)} %get-tuple-element.27.left_ref, bf16[512,256]{1,0:T(8,128)(2,1)S(1)} %get-tuple-element.28.right_ref), custom_call_target="tpu_custom_call" | custom-call | flops 960000000 | bytes 2097152 | tf_op jit(solution)/shard_map/pallas_call | solution.py:70
  54.0 4.0 %collective-permute-done.12.far_out = bf16[64,8,256]{2,1,0:T(8,128)(2,1)S(1)} collective-permute-done((bf16[64,8,256]{2,1,0:T(8,128)(2,1)S(1)}, bf16[64,8,256]{2,1,0:T(8,128)(2,1)S(1)}, u32[]{:S(2)}, u32[]{:S(2)}) %collective-permute-start.12) | collective-permute-done | bytes 262176 | tf_op jit(solution)/shard_map/ppermute | solution.py:240
  58.0 2.2 %shard_map.61.far_ref = f32[24,128]{1,0:T(8,128)S(1)} custom-call(bf16[128,8,256]{2,1,0:T(8,128)(2,1)S(1)} %shard_map.60.early_ref, bf16[128,8,256]{2,1,0:T(8,128)(2,1)S(1)} %add.14.mid_ref, bf16[64,8,256]{2,1,0:T(8,128)(2,1)S(1)} %collective-permute-done.12.far_out, bf16[128,128,256]{2,1,0:T(8,128)(2,1)S(1)} %shard_map.58.grad_ref, s32[4]{0:T(128)S(1)} %copy-done.2), custom_call_target="tpu_custom_call" | custom-call | flops 1000 | bytes 1000 | tf_op jit(solution)/shard_map/pallas_call | solution.py:193
  60.2 1.8 %collective-permute-done.13.far_out = bf16[64,8,256]{2,1,0:T(8,128)(2,1)S(1)} collective-permute-done((bf16[64,8,256]{2,1,0:T(8,128)(2,1)S(1)}, bf16[64,8,256]{2,1,0:T(8,128)(2,1)S(1)}, u32[]{:S(2)}, u32[]{:S(2)}) %collective-permute-start.13) | collective-permute-done | bytes 262176 | tf_op jit(solution)/shard_map/ppermute | solution.py:241
  62.0 2.2 %shard_map.62 = (f32[24,128]{1,0:T(8,128)S(1)}, f32[24,128]{1,0:T(8,128)S(1)}) custom-call(f32[48,128]{1,0:T(8,128)S(1)} %shard_map.59.base_ref, f32[24,128]{1,0:T(8,128)S(1)} %shard_map.61.far_ref, bf16[128,8,256]{2,1,0:T(8,128)(2,1)S(1)} %shard_map.60.early_ref, bf16[128,8,256]{2,1,0:T(8,128)(2,1)S(1)} %add.14.mid_ref, ...), custom_call_target="tpu_custom_call" | custom-call | flops 1000 | bytes 1000 | tf_op jit(solution)/shard_map/pallas_call | solution.py:193
  64.2 1.1 %collective-permute-start.14 = (f32[24,128]{1,0:T(8,128)S(1)}, f32[24,128]{1,0:T(8,128)S(1)}, u32[]{:S(2)}, u32[]{:S(2)}) collective-permute-start(f32[24,128]{1,0:T(8,128)S(1)} %get-tuple-element.42), channel_id=1, source_target_pairs={{0,2},{2,0},{1,3},{3,1},{4,6},{6,4},{5,7},{7,5},{8,10},{10,8},{9,1... | collective-permute-start | bytes 36872 | tf_op jit(solution)/shard_map/ppermute | solution.py:258
  65.3 2.7 %collective-permute-done.14 = f32[24,128]{1,0:T(8,128)S(1)} collective-permute-done((f32[24,128]{1,0:T(8,128)S(1)}, f32[24,128]{1,0:T(8,128)S(1)}, u32[]{:S(2)}, u32[]{:S(2)}) %collective-permute-start.14) | collective-permute-done | bytes 12320 | tf_op jit(solution)/shard_map/ppermute | solution.py:258
  (21 shorter events, 2.0 us)
Async XLA Ops:
  1.1 14.9 %collective-permute-start.2 = (bf16[8,128,256]{2,1,0:T(8,128)(2,1)S(1)}, bf16[8,128,256]{2,1,0:T(8,128)(2,1)S(1)}, u32[]{:S(2)}, u32[]{:S(2)}) collective-permute-start(bf16[8,128,256]{2,1,0:T(8,128)(2,1)S(1)} %slice_bitcast_fusion.own_ref), channel_id=1, source_target_pairs={{0,2},{2,0},{1,3},{3,1},{4,6},{6,4},{5,7},{7,5},{8,10},{10,8},{9,1... | collective-permute-start | bytes 1572872 | tf_op jit(solution)/shard_map/ppermute | solution.py:219
  5.1 7.1 %collective-permute-start.1 = (bf16[4,128,256]{2,1,0:T(8,128)(2,1)S(1)}, bf16[4,128,256]{2,1,0:T(8,128)(2,1)S(1)}, u32[]{:S(2)}, u32[]{:S(2)}) collective-permute-start(bf16[4,128,256]{2,1,0:T(8,128)(2,1)S(1)} %slice_bitcast_fusion.1), channel_id=1, source_target_pairs={{4,8},{8,4},{5,9},{9,5},{6,10},{10,6},{7,11},{11,7},{20,24},{24,20... | collective-permute-start | bytes 786440 | tf_op jit(solution)/shard_map/ppermute | solution.py:223
  5.7 10.2 %collective-permute-start = (bf16[4,128,256]{2,1,0:T(8,128)(2,1)S(1)}, bf16[4,128,256]{2,1,0:T(8,128)(2,1)S(1)}, u32[]{:S(2)}, u32[]{:S(2)}) collective-permute-start(bf16[4,128,256]{2,1,0:T(8,128)(2,1)S(1)} %slice_bitcast_fusion.1), channel_id=1, source_target_pairs={{0,4},{4,0},{8,12},{12,8},{1,5},{5,1},{9,13},{13,9},{2,6},{6,2},{1... | collective-permute-start | bytes 786440 | tf_op jit(solution)/shard_map/ppermute | solution.py:222
  10.2 0.9 %copy-start = (f32[256,256]{1,0:T(8,128)S(1)}, f32[256,256]{1,0:T(8,128)}, u32[]{:S(2)}) copy-start(f32[256,256]{1,0:T(8,128)} %left_ref.1) | copy-start | bytes 786436
  11.1 0.9 %copy-start.1 = (f32[256,256]{1,0:T(8,128)S(1)}, f32[256,256]{1,0:T(8,128)}, u32[]{:S(2)}) copy-start(f32[256,256]{1,0:T(8,128)} %right_ref) | copy-start | bytes 786436
  12.2 11.2 %collective-permute-start.5 = (bf16[4,128,256]{2,1,0:T(8,128)(2,1)S(1)}, bf16[4,128,256]{2,1,0:T(8,128)(2,1)S(1)}, u32[]{:S(2)}, u32[]{:S(2)}) collective-permute-start(bf16[4,128,256]{2,1,0:T(8,128)(2,1)S(1)} %collective-permute-done.1), channel_id=1, source_target_pairs={{4,0},{8,12},{5,1},{9,13},{6,2},{10,14},{7,3},{11,15},{20,16},{24,... | collective-permute-start | bytes 786440 | tf_op jit(solution)/shard_map/ppermute | solution.py:224
  16.0 8.9 %collective-permute-start.7 = (bf16[4,128,256]{2,1,0:T(8,128)(2,1)S(1)}, bf16[4,128,256]{2,1,0:T(8,128)(2,1)S(1)}, u32[]{:S(2)}, u32[]{:S(2)}) collective-permute-start(bf16[4,128,256]{2,1,0:T(8,128)(2,1)S(1)} %collective-permute-done), channel_id=1, source_target_pairs={{4,8},{8,4},{5,9},{9,5},{6,10},{10,6},{7,11},{11,7},{20,24},{24,20... | collective-permute-start | bytes 786440 | tf_op jit(solution)/shard_map/ppermute | solution.py:226
  17.9 26.7 %copy-start.2 = (s32[4]{0:T(128)S(1)}, s32[4]{0:T(128)}, u32[]{:S(2)}) copy-start(s32[4]{0:T(128)} %order_ref.5) | copy-start | bytes 52
  18.0 17.1 %collective-permute-start.3 = (bf16[128,8,256]{2,1,0:T(8,128)(2,1)S(1)}, bf16[128,8,256]{2,1,0:T(8,128)(2,1)S(1)}, u32[]{:S(2)}, u32[]{:S(2)}) collective-permute-start(bf16[128,8,256]{2,1,0:T(8,128)(2,1)S(1)} %shard_map.56.own_ref), channel_id=1, source_target_pairs={{0,4},{4,0},{8,12},{12,8},{1,5},{5,1},{9,13},{13,9},{2,6},{6,2},{1... | collective-permute-start | bytes 1572872 | tf_op jit(solution)/shard_map/ppermute | solution.py:229
  22.7 13.1 %collective-permute-start.4 = (bf16[128,8,256]{2,1,0:T(8,128)(2,1)S(1)}, bf16[128,8,256]{2,1,0:T(8,128)(2,1)S(1)}, u32[]{:S(2)}, u32[]{:S(2)}) collective-permute-start(bf16[128,8,256]{2,1,0:T(8,128)(2,1)S(1)} %shard_map.56.own_ref), channel_id=1, source_target_pairs={{4,8},{8,4},{5,9},{9,5},{6,10},{10,6},{7,11},{11,7},{20,24},{24,20... | collective-permute-start | bytes 1572872 | tf_op jit(solution)/shard_map/ppermute | solution.py:230
  23.4 16.7 %collective-permute-start.6 = (bf16[8,128,256]{2,1,0:T(8,128)(2,1)S(1)}, bf16[8,128,256]{2,1,0:T(8,128)(2,1)S(1)}, u32[]{:S(2)}, u32[]{:S(2)}) collective-permute-start(bf16[8,128,256]{2,1,0:T(8,128)(2,1)S(1)} %pad_maximum_fusion.own_ref), channel_id=1, source_target_pairs={{0,2},{2,0},{1,3},{3,1},{4,6},{6,4},{5,7},{7,5},{8,10},{10,8},{9,1... | collective-permute-start | bytes 1572872 | tf_op jit(solution)/shard_map/ppermute | solution.py:232
  30.1 9.8 %collective-permute-start.9 = (bf16[4,128,256]{2,1,0:T(8,128)(2,1)S(1)}, bf16[4,128,256]{2,1,0:T(8,128)(2,1)S(1)}, u32[]{:S(2)}, u32[]{:S(2)}) collective-permute-start(bf16[4,128,256]{2,1,0:T(8,128)(2,1)S(1)} %collective-permute-done.7), channel_id=1, source_target_pairs={{4,0},{8,12},{5,1},{9,13},{6,2},{10,14},{7,3},{11,15},{20,16},{24,... | collective-permute-start | bytes 786440 | tf_op jit(solution)/shard_map/ppermute | solution.py:233
  35.0 7.0 %collective-permute-start.8 = (bf16[128,8,256]{2,1,0:T(8,128)(2,1)S(1)}, bf16[128,8,256]{2,1,0:T(8,128)(2,1)S(1)}, u32[]{:S(2)}, u32[]{:S(2)}) collective-permute-start(bf16[128,8,256]{2,1,0:T(8,128)(2,1)S(1)} %collective-permute-done.3.near), channel_id=1, source_target_pairs={{4,8},{8,4},{5,9},{9,5},{6,10},{10,6},{7,11},{11,7},{20,24},{24,20... | collective-permute-start | bytes 1572872 | tf_op jit(solution)/shard_map/ppermute | solution.py:234
  35.8 16.6 %collective-permute-start.10 = (bf16[128,8,256]{2,1,0:T(8,128)(2,1)S(1)}, bf16[128,8,256]{2,1,0:T(8,128)(2,1)S(1)}, u32[]{:S(2)}, u32[]{:S(2)}) collective-permute-start(bf16[128,8,256]{2,1,0:T(8,128)(2,1)S(1)} %collective-permute-done.4), channel_id=1, source_target_pairs={{4,0},{8,12},{5,1},{9,13},{6,2},{10,14},{7,3},{11,15},{20,16},{24,... | collective-permute-start | bytes 1572872 | tf_op jit(solution)/shard_map/ppermute | solution.py:235
  41.3 11.4 %collective-permute-start.11 = (bf16[8,128,256]{2,1,0:T(8,128)(2,1)S(1)}, bf16[8,128,256]{2,1,0:T(8,128)(2,1)S(1)}, u32[]{:S(2)}, u32[]{:S(2)}) collective-permute-start(bf16[8,128,256]{2,1,0:T(8,128)(2,1)S(1)} %pad_maximum_fusion.1.own_ref), channel_id=1, source_target_pairs={{0,2},{2,0},{1,3},{3,1},{4,6},{6,4},{5,7},{7,5},{8,10},{10,8},{9,1... | collective-permute-start | bytes 1572872 | tf_op jit(solution)/shard_map/ppermute | solution.py:238
  42.0 15.9 %collective-permute-start.12 = (bf16[64,8,256]{2,1,0:T(8,128)(2,1)S(1)}, bf16[64,8,256]{2,1,0:T(8,128)(2,1)S(1)}, u32[]{:S(2)}, u32[]{:S(2)}) collective-permute-start(bf16[64,8,256]{2,1,0:T(8,128)(2,1)S(1)} %get-tuple-element.44), channel_id=1, source_target_pairs={{4,0},{8,12},{5,1},{9,13},{6,2},{10,14},{7,3},{11,15},{20,16},{24,... | collective-permute-start | bytes 786440 | tf_op jit(solution)/shard_map/ppermute | solution.py:240
  43.3 18.7 %collective-permute-start.13 = (bf16[64,8,256]{2,1,0:T(8,128)(2,1)S(1)}, bf16[64,8,256]{2,1,0:T(8,128)(2,1)S(1)}, u32[]{:S(2)}, u32[]{:S(2)}) collective-permute-start(bf16[64,8,256]{2,1,0:T(8,128)(2,1)S(1)} %get-tuple-element.43), channel_id=1, source_target_pairs={{4,0},{8,12},{5,1},{9,13},{6,2},{10,14},{7,3},{11,15},{20,16},{24,... | collective-permute-start | bytes 786440 | tf_op jit(solution)/shard_map/ppermute | solution.py:241
  64.2 3.8 %collective-permute-start.14 = (f32[24,128]{1,0:T(8,128)S(1)}, f32[24,128]{1,0:T(8,128)S(1)}, u32[]{:S(2)}, u32[]{:S(2)}) collective-permute-start(f32[24,128]{1,0:T(8,128)S(1)} %get-tuple-element.42), channel_id=1, source_target_pairs={{0,2},{2,0},{1,3},{3,1},{4,6},{6,4},{5,7},{7,5},{8,10},{10,8},{9,1... | collective-permute-start | bytes 36872 | tf_op jit(solution)/shard_map/ppermute | solution.py:258

commit v17 on v16

--- a/solution.py
+++ b/solution.py
@@ -161,16 +161,17 @@
     return [me, near, jnp.where(low_pair, 2, 1), jnp.where(low_pair, 3, 0)]
 
 
-def far_pass_kernel(ex, early_ref, mid_ref, far_out, grad_ref, order_ref, out_ref):
-    out_ref[...] = inner_products((early_ref, mid_ref, far_out), grad_ref, 0, far_out.shape[0])
+def far_pass_kernel(first, ex, early_ref, mid_ref, far_out, grad_ref, order_ref, out_ref):
+    out_ref[...] = inner_products((early_ref, mid_ref, far_out), grad_ref, first, far_out.shape[0])
 
 
 def last_pass_kernel(
-    ex, base_ref, far_ref, early_ref, mid_ref, far_out, grad_ref, order_ref, mine_ref, send_ref, full_ref
+    ex, base_ref, far_0, far_1, early_ref, mid_ref, far_out, grad_ref, order_ref, mine_ref, send_ref, full_ref
 ):
     late = far_out.shape[1]
     rows = far_out.shape[0]
-    acc = far_ref[...] + inner_products((early_ref, mid_ref, far_out), grad_ref, rows, rows)
+    first = grad_ref.shape[0] - rows
+    acc = far_0[...] + far_1[...] + inner_products((early_ref, mid_ref, far_out), grad_ref, first, rows)
     mid, far = slot_sources(lax.axis_index("ex"))[2:]
     low_mid, low_far = acc[:EARLY], acc[EARLY : 2 * EARLY]
     high_mid, high_far = acc[2 * EARLY : 2 * EARLY + late], acc[2 * EARLY + late :]
@@ -236,9 +237,9 @@
     cond_0 = condition(after(early_0, near, mid), early_0_other, *terms)
     early_1 = jnp.concatenate([raw_mid + raw_mid_out, after(raw_far_mid, near, mid) + raw_far_out], axis=0)
     early_1_other = lax.ppermute(after(early_1, cond_0), "feat", swap)
-    part = far_mid.shape[0] // 2
-    far_out_0 = lax.ppermute(far_mid[:part], "ex", OUTWARD)
-    far_out_1 = lax.ppermute(far_mid[part:], "ex", OUTWARD)
+    rows = far_mid.shape[0]
+    cuts = [0, rows // 2, 3 * rows // 4, rows]
+    far_out = [lax.ppermute(far_mid[a:b], "ex", OUTWARD) for a, b in zip(cuts, cuts[1:])]
     cond_1 = condition(after(early_1, far_mid, mid_out), early_1_other, *terms)
 
     base = score_call(
@@ -246,13 +247,16 @@
         jax.ShapeDtypeStruct((ex * count, n), F32),
     )
     mid = mid + mid_out
-    far_0 = score_call(
-        far_pass_kernel, ex, (cond_1, mid, far_out_0, after(grads, base)), block_order,
-        jax.ShapeDtypeStruct((2 * count, n), F32),
-    )
+    far_sums, earlier = [], base
+    for first, arrived in zip(cuts, far_out[:-1]):
+        earlier = score_call(
+            functools.partial(far_pass_kernel, first), ex, (cond_1, mid, arrived, after(grads, earlier)), block_order,
+            jax.ShapeDtypeStruct((2 * count, n), F32),
+        )
+        far_sums.append(earlier)
     half = jax.ShapeDtypeStruct((ex * count // 2, n), F32)
     mine, send = score_call(
-        last_pass_kernel, ex, (base, far_0, cond_1, mid, far_out_1, grads), block_order, (half, half),
+        last_pass_kernel, ex, (base, *far_sums, cond_1, mid, far_out[-1], grads), block_order, (half, half),
         [pltpu.VMEM((ex * count, n), F32)],
     )
     scores = mine + lax.ppermute(send, "feat", swap)

time: 69 us -> 68.2 us (0.988)
  waiting for transfers between devices: 21.5 us -> 18.9 us
  starting transfers between devices: 24.6 us -> 25.9 us
    ppermute x2 -> x3, waiting for transfers between devices: 5.84 us -> 4.54 us  [per_device_line(): lax.ppermute(far_mid[a:b], 'ex', OUTWARD)]
    ppermute x1, waiting for transfers between devices: 3.86 us -> 2.57 us  [per_device_line(): mid_out = lax.ppermute(after(mid, near, grads), 'ex', OUTWARD)]
    ppermute x2 -> x3, starting transfers between devices: 2.58 us -> 3.88 us  [per_device_line(): lax.ppermute(far_mid[a:b], 'ex', OUTWARD)]
    pallas_call x3 -> x4, Pallas kernels: 8.23 us -> 8.7 us  [score_call(): pl.pallas_call(functools.partial(kernel, ex), out_shape=out_shape, in_spe...]
  transfers between devices with their start and end apart: 15 -> 16, of which waited for: 8 -> 9; matrix products, arithmetic and copies ran while one was open for 2% -> 2% of each run, Pallas kernels for 22% -> 24%
where the time goes in v17:
time: 68.2 us; the launch traced here: 67.7 us
  starting transfers between devices  25.9 us (38%)
  waiting for transfers between devices  18.9 us (28%)
  Pallas kernels  17.7 us (26%)
  local copies, waits for them, and re-layouts  3.98 us (6%)
  other arithmetic  0.96 us (1%)
    pallas_call x4, Pallas kernels, score_call(): pl.pallas_call(functools.partial(kernel, ex), out_shape=out_shape, in_spe...  8.7 us
    pallas_call x1, Pallas kernels, regroup(): pl.pallas_call(regroup_kernel, out_shape=jax.ShapeDtypeStruct((rows, n, w...  5.16 us
    ppermute x1, starting transfers between devices, per_device_line(): near = lax.ppermute(late, 'ex', PAIRS)  4.7 us
    ppermute x3, waiting for transfers between devices, per_device_line(): lax.ppermute(far_mid[a:b], 'ex', OUTWARD)  4.54 us
    ppermute x1, starting transfers between devices, per_device_line(): raw_near = lax.ppermute(raw, 'ex', PAIRS)  4.45 us
    ppermute x3, starting transfers between devices, per_device_line(): lax.ppermute(far_mid[a:b], 'ex', OUTWARD)  3.88 us
    pallas_call x3, Pallas kernels, condition(): pl.pallas_call(condition_kernel, out_shape=jax.ShapeDtypeStruct((rows, co...  3.77 us
    ppermute x1, waiting for transfers between devices, per_device_line(): near = lax.ppermute(late, 'ex', PAIRS)  3.65 us
  transfers between devices with their start and end apart: 16, of which 9 were waited for; matrix products, arithmetic and copies ran while one was open for 2% of the time, Pallas kernels for 24%

profile of v17, /device:TPU:0, one launch (start us, length us, event | category | flops | bytes accessed | tf_op | source)
XLA Modules:
  0.0 67.7 jit_solution(2603196583942014681)
XLA Ops:
  0.0 1.1 %slice_bitcast_fusion.own_ref = bf16[8,128,256]{2,1,0:T(8,128)(2,1)S(1)} fusion(bf16[1,12,128,256]{3,2,1,0:T(8,128)(2,1)} %param.6), kind=kLoop, calls=%fused_computation.2 | loop fusion | bytes 1048576 | tf_op jit(solution)/shard_map/squeeze | solution.py:219
  1.1 3.0 %collective-permute-start.2 = (bf16[8,128,256]{2,1,0:T(8,128)(2,1)S(1)}, bf16[8,128,256]{2,1,0:T(8,128)(2,1)S(1)}, u32[]{:S(2)}, u32[]{:S(2)}) collective-permute-start(bf16[8,128,256]{2,1,0:T(8,128)(2,1)S(1)} %slice_bitcast_fusion.own_ref), channel_id=1, source_target_pairs={{0,2},{2,0},{1,3},{3,1},{4,6},{6,4},{5,7},{7,5},{8,10},{10,8},{9,1... | collective-permute-start | bytes 1572872 | tf_op jit(solution)/shard_map/ppermute | solution.py:220
  4.1 1.0 %slice_bitcast_fusion.1 = bf16[4,128,256]{2,1,0:T(8,128)(2,1)S(1)} fusion(bf16[1,12,128,256]{3,2,1,0:T(8,128)(2,1)} %param.6), kind=kLoop, calls=%fused_computation.3 | loop fusion | bytes 524288 | tf_op jit(solution)/shard_map/squeeze | solution.py:221
  5.7 4.4 %collective-permute-start = (bf16[4,128,256]{2,1,0:T(8,128)(2,1)S(1)}, bf16[4,128,256]{2,1,0:T(8,128)(2,1)S(1)}, u32[]{:S(2)}, u32[]{:S(2)}) collective-permute-start(bf16[4,128,256]{2,1,0:T(8,128)(2,1)S(1)} %slice_bitcast_fusion.1), channel_id=1, source_target_pairs={{0,4},{4,0},{8,12},{12,8},{1,5},{5,1},{9,13},{13,9},{2,6},{6,2},{1... | collective-permute-start | bytes 786440 | tf_op jit(solution)/shard_map/ppermute | solution.py:223
  10.2 0.9 %copy-done = f32[256,256]{1,0:T(8,128)S(1)} copy-done((f32[256,256]{1,0:T(8,128)S(1)}, f32[256,256]{1,0:T(8,128)}, u32[]{:S(2)}) %copy-start) | copy-done | bytes 262168
  11.1 0.9 %copy-done.1 = f32[256,256]{1,0:T(8,128)S(1)} copy-done((f32[256,256]{1,0:T(8,128)S(1)}, f32[256,256]{1,0:T(8,128)}, u32[]{:S(2)}) %copy-start.1) | copy-done | bytes 262168
  12.2 1.3 %collective-permute-start.5 = (bf16[4,128,256]{2,1,0:T(8,128)(2,1)S(1)}, bf16[4,128,256]{2,1,0:T(8,128)(2,1)S(1)}, u32[]{:S(2)}, u32[]{:S(2)}) collective-permute-start(bf16[4,128,256]{2,1,0:T(8,128)(2,1)S(1)} %collective-permute-done.1), channel_id=1, source_target_pairs={{4,0},{8,12},{5,1},{9,13},{6,2},{10,14},{7,3},{11,15},{20,16},{24,... | collective-permute-start | bytes 786440 | tf_op jit(solution)/shard_map/ppermute | solution.py:225
  13.5 2.5 %collective-permute-done = bf16[4,128,256]{2,1,0:T(8,128)(2,1)S(1)} collective-permute-done((bf16[4,128,256]{2,1,0:T(8,128)(2,1)S(1)}, bf16[4,128,256]{2,1,0:T(8,128)(2,1)S(1)}, u32[]{:S(2)}, u32[]{:S(2)}) %collective-permute-start) | collective-permute-done | bytes 262176 | tf_op jit(solution)/shard_map/ppermute | solution.py:223
  16.7 1.3 %shard_map.56.own_ref = bf16[128,8,256]{2,1,0:T(8,128)(2,1)S(1)} custom-call(bf16[8,128,256]{2,1,0:T(8,128)(2,1)S(1)} %slice_bitcast_fusion.own_ref, bf16[8,128,256]{2,1,0:T(8,128)(2,1)S(1)} %collective-permute-done.2.far_ref, bf16[384,256]{1,0:T(8,128)(2,1)S(1)} %get-tuple-element.28.left_ref, bf16[512,256]{1,0:T(8,128)(2,1)S(1)} %get-tuple-element.29.right_ref), custom_call_target="tpu_custom_call" | custom-call | flops 960000000 | bytes 2097152 | tf_op jit(solution)/shard_map/pallas_call | solution.py:70
  18.0 4.7 %collective-permute-start.3 = (bf16[128,8,256]{2,1,0:T(8,128)(2,1)S(1)}, bf16[128,8,256]{2,1,0:T(8,128)(2,1)S(1)}, u32[]{:S(2)}, u32[]{:S(2)}) collective-permute-start(bf16[128,8,256]{2,1,0:T(8,128)(2,1)S(1)} %shard_map.56.own_ref), channel_id=1, source_target_pairs={{0,4},{4,0},{8,12},{12,8},{1,5},{5,1},{9,13},{13,9},{2,6},{6,2},{1... | collective-permute-start | bytes 1572872 | tf_op jit(solution)/shard_map/ppermute | solution.py:230
  22.7 0.7 %collective-permute-start.4 = (bf16[128,8,256]{2,1,0:T(8,128)(2,1)S(1)}, bf16[128,8,256]{2,1,0:T(8,128)(2,1)S(1)}, u32[]{:S(2)}, u32[]{:S(2)}) collective-permute-start(bf16[128,8,256]{2,1,0:T(8,128)(2,1)S(1)} %shard_map.56.own_ref), channel_id=1, source_target_pairs={{4,8},{8,4},{5,9},{9,5},{6,10},{10,6},{7,11},{11,7},{20,24},{24,20... | collective-permute-start | bytes 1572872 | tf_op jit(solution)/shard_map/ppermute | solution.py:231
  23.4 1.6 %collective-permute-start.6 = (bf16[8,128,256]{2,1,0:T(8,128)(2,1)S(1)}, bf16[8,128,256]{2,1,0:T(8,128)(2,1)S(1)}, u32[]{:S(2)}, u32[]{:S(2)}) collective-permute-start(bf16[8,128,256]{2,1,0:T(8,128)(2,1)S(1)} %pad_maximum_fusion.own_ref), channel_id=1, source_target_pairs={{0,2},{2,0},{1,3},{3,1},{4,6},{6,4},{5,7},{7,5},{8,10},{10,8},{9,1... | collective-permute-start | bytes 1572872 | tf_op jit(solution)/shard_map/ppermute | solution.py:233
  24.9 5.2 %shard_map.58.grad_ref = bf16[128,128,256]{2,1,0:T(8,128)(2,1)S(1)} custom-call(bf16[128,128,256]{2,1,0:T(8,128)(2,1)} %grads_ref), custom_call_target="tpu_custom_call" | custom-call | flops 6000000000 | bytes 16000000 | tf_op jit(solution)/shard_map/pallas_call | solution.py:106
  30.1 1.3 %collective-permute-start.9 = (bf16[4,128,256]{2,1,0:T(8,128)(2,1)S(1)}, bf16[4,128,256]{2,1,0:T(8,128)(2,1)S(1)}, u32[]{:S(2)}, u32[]{:S(2)}) collective-permute-start(bf16[4,128,256]{2,1,0:T(8,128)(2,1)S(1)} %collective-permute-done.7), channel_id=1, source_target_pairs={{4,0},{8,12},{5,1},{9,13},{6,2},{10,14},{7,3},{11,15},{20,16},{24,... | collective-permute-start | bytes 786440 | tf_op jit(solution)/shard_map/ppermute | solution.py:234
  31.4 3.7 %collective-permute-done.3.near = bf16[128,8,256]{2,1,0:T(8,128)(2,1)S(1)} collective-permute-done((bf16[128,8,256]{2,1,0:T(8,128)(2,1)S(1)}, bf16[128,8,256]{2,1,0:T(8,128)(2,1)S(1)}, u32[]{:S(2)}, u32[]{:S(2)}) %collective-permute-start.3) | collective-permute-done | bytes 524320 | tf_op jit(solution)/shard_map/ppermute | solution.py:230
  35.0 0.7 %collective-permute-start.8 = (bf16[128,8,256]{2,1,0:T(8,128)(2,1)S(1)}, bf16[128,8,256]{2,1,0:T(8,128)(2,1)S(1)}, u32[]{:S(2)}, u32[]{:S(2)}) collective-permute-start(bf16[128,8,256]{2,1,0:T(8,128)(2,1)S(1)} %collective-permute-done.3.near), channel_id=1, source_target_pairs={{4,8},{8,4},{5,9},{9,5},{6,10},{10,6},{7,11},{11,7},{20,24},{24,20... | collective-permute-start | bytes 1572872 | tf_op jit(solution)/shard_map/ppermute | solution.py:235
  35.8 1.3 %collective-permute-start.10 = (bf16[128,8,256]{2,1,0:T(8,128)(2,1)S(1)}, bf16[128,8,256]{2,1,0:T(8,128)(2,1)S(1)}, u32[]{:S(2)}, u32[]{:S(2)}) collective-permute-start(bf16[128,8,256]{2,1,0:T(8,128)(2,1)S(1)} %collective-permute-done.4), channel_id=1, source_target_pairs={{4,0},{8,12},{5,1},{9,13},{6,2},{10,14},{7,3},{11,15},{20,16},{24,... | collective-permute-start | bytes 1572872 | tf_op jit(solution)/shard_map/ppermute | solution.py:236
  37.1 2.8 %collective-permute-done.9 = bf16[4,128,256]{2,1,0:T(8,128)(2,1)S(1)} collective-permute-done((bf16[4,128,256]{2,1,0:T(8,128)(2,1)S(1)}, bf16[4,128,256]{2,1,0:T(8,128)(2,1)S(1)}, u32[]{:S(2)}, u32[]{:S(2)}) %collective-permute-start.9) | collective-permute-done | bytes 262176 | tf_op jit(solution)/shard_map/ppermute | solution.py:234
  40.1 1.3 %shard_map.57.early_ref = bf16[128,8,256]{2,1,0:T(8,128)(2,1)S(1)} custom-call(bf16[8,128,256]{2,1,0:T(8,128)(2,1)S(1)} %pad_maximum_fusion.own_ref, bf16[8,128,256]{2,1,0:T(8,128)(2,1)S(1)} %collective-permute-done.6.far_ref, bf16[384,256]{1,0:T(8,128)(2,1)S(1)} %get-tuple-element.28.left_ref, bf16[512,256]{1,0:T(8,128)(2,1)S(1)} %get-tuple-element.29.right_ref), custom_call_target="tpu_custom_call" | custom-call | flops 960000000 | bytes 2097152 | tf_op jit(solution)/shard_map/pallas_call | solution.py:70
  41.3 0.7 %collective-permute-start.11 = (bf16[8,128,256]{2,1,0:T(8,128)(2,1)S(1)}, bf16[8,128,256]{2,1,0:T(8,128)(2,1)S(1)}, u32[]{:S(2)}, u32[]{:S(2)}) collective-permute-start(bf16[8,128,256]{2,1,0:T(8,128)(2,1)S(1)} %pad_maximum_fusion.1.own_ref), channel_id=1, source_target_pairs={{0,2},{2,0},{1,3},{3,1},{4,6},{6,4},{5,7},{7,5},{8,10},{10,8},{9,1... | collective-permute-start | bytes 1572872 | tf_op jit(solution)/shard_map/ppermute | solution.py:239
  42.0 1.3 %collective-permute-start.12 = (bf16[64,8,256]{2,1,0:T(8,128)(2,1)S(1)}, bf16[64,8,256]{2,1,0:T(8,128)(2,1)S(1)}, u32[]{:S(2)}, u32[]{:S(2)}) collective-permute-start(bf16[64,8,256]{2,1,0:T(8,128)(2,1)S(1)} %slice.20), channel_id=1, source_target_pairs={{4,0},{8,12},{5,1},{9,13},{6,2},{10,14},{7,3},{11,15},{20,16},{24,... | collective-permute-start | bytes 786440 | tf_op jit(solution)/shard_map/ppermute | solution.py:242
  43.3 1.3 %collective-permute-start.13 = (bf16[32,8,256]{2,1,0:T(8,128)(2,1)S(1)}, bf16[32,8,256]{2,1,0:T(8,128)(2,1)S(1)}, u32[]{:S(2)}, u32[]{:S(2)}) collective-permute-start(bf16[32,8,256]{2,1,0:T(8,128)(2,1)S(1)} %get-tuple-element.46), channel_id=1, source_target_pairs={{4,0},{8,12},{5,1},{9,13},{6,2},{10,14},{7,3},{11,15},{20,16},{24,... | collective-permute-start | bytes 393224 | tf_op jit(solution)/shard_map/ppermute | solution.py:242
  44.6 1.3 %collective-permute-start.14 = (bf16[32,8,256]{2,1,0:T(8,128)(2,1)S(1)}, bf16[32,8,256]{2,1,0:T(8,128)(2,1)S(1)}, u32[]{:S(2)}, u32[]{:S(2)}) collective-permute-start(bf16[32,8,256]{2,1,0:T(8,128)(2,1)S(1)} %get-tuple-element.45), channel_id=1, source_target_pairs={{4,0},{8,12},{5,1},{9,13},{6,2},{10,14},{7,3},{11,15},{20,16},{24,... | collective-permute-start | bytes 393224 | tf_op jit(solution)/shard_map/ppermute | solution.py:242
  46.0 3.8 %shard_map.59.base_ref = f32[48,128]{1,0:T(8,128)S(1)} custom-call(bf16[128,8,256]{2,1,0:T(8,128)(2,1)S(1)} %shard_map.57.early_ref, bf16[128,8,256]{2,1,0:T(8,128)(2,1)S(1)} %shard_map.56.own_ref, bf16[128,8,256]{2,1,0:T(8,128)(2,1)S(1)} %collective-permute-done.3.near, bf16[128,8,256]{2,1,0:T(8,128)(2,1)S(1)} %collective-permute-done.8.far_in, ...), custom_call_target="tpu_custom_call" | custom-call | flops 1000 | bytes 1000 | tf_op jit(solution)/shard_map/pallas_call | solution.py:194
  49.8 2.6 %collective-permute-done.10 = bf16[128,8,256]{2,1,0:T(8,128)(2,1)S(1)} collective-permute-done((bf16[128,8,256]{2,1,0:T(8,128)(2,1)S(1)}, bf16[128,8,256]{2,1,0:T(8,128)(2,1)S(1)}, u32[]{:S(2)}, u32[]{:S(2)}) %collective-permute-start.10) | collective-permute-done | bytes 524320 | tf_op jit(solution)/shard_map/ppermute | solution.py:236
  52.7 1.3 %shard_map.60.early_ref = bf16[128,8,256]{2,1,0:T(8,128)(2,1)S(1)} custom-call(bf16[8,128,256]{2,1,0:T(8,128)(2,1)S(1)} %pad_maximum_fusion.1.own_ref, bf16[8,128,256]{2,1,0:T(8,128)(2,1)S(1)} %collective-permute-done.11.far_ref, bf16[384,256]{1,0:T(8,128)(2,1)S(1)} %get-tuple-element.28.left_ref, bf16[512,256]{1,0:T(8,128)(2,1)S(1)} %get-tuple-element.29.right_ref), custom_call_target="tpu_custom_call" | custom-call | flops 960000000 | bytes 2097152 | tf_op jit(solution)/shard_map/pallas_call | solution.py:70
  54.0 4.0 %collective-permute-done.12.far_out = bf16[64,8,256]{2,1,0:T(8,128)(2,1)S(1)} collective-permute-done((bf16[64,8,256]{2,1,0:T(8,128)(2,1)S(1)}, bf16[64,8,256]{2,1,0:T(8,128)(2,1)S(1)}, u32[]{:S(2)}, u32[]{:S(2)}) %collective-permute-start.12) | collective-permute-done | bytes 262176 | tf_op jit(solution)/shard_map/ppermute | solution.py:242
  58.0 2.2 %shard_map.61.far_0 = f32[24,128]{1,0:T(8,128)S(1)} custom-call(bf16[128,8,256]{2,1,0:T(8,128)(2,1)S(1)} %shard_map.60.early_ref, bf16[128,8,256]{2,1,0:T(8,128)(2,1)S(1)} %add.14.mid_ref, bf16[64,8,256]{2,1,0:T(8,128)(2,1)S(1)} %collective-permute-done.12.far_out, bf16[128,128,256]{2,1,0:T(8,128)(2,1)S(1)} %shard_map.58.grad_ref, s32[4]{0:T(128)S(1)} %copy-done.2), custom_call_target="tpu_custom_call" | custom-call | flops 1000 | bytes 1000 | tf_op jit(solution)/shard_map/pallas_call | solution.py:194
  60.6 1.3 %shard_map.62.far_1 = f32[24,128]{1,0:T(8,128)S(1)} custom-call(bf16[128,8,256]{2,1,0:T(8,128)(2,1)S(1)} %shard_map.60.early_ref, bf16[128,8,256]{2,1,0:T(8,128)(2,1)S(1)} %add.14.mid_ref, bf16[32,8,256]{2,1,0:T(8,128)(2,1)S(1)} %collective-permute-done.13.far_out, bf16[128,128,256]{2,1,0:T(8,128)(2,1)S(1)} %shard_map.58.grad_ref, s32[4]{0:T(128)S(1)} %copy-done.2), custom_call_target="tpu_custom_call" | custom-call | flops 1000 | bytes 1000 | tf_op jit(solution)/shard_map/pallas_call | solution.py:194
  62.0 1.4 %shard_map.63 = (f32[24,128]{1,0:T(8,128)S(1)}, f32[24,128]{1,0:T(8,128)S(1)}) custom-call(f32[48,128]{1,0:T(8,128)S(1)} %shard_map.59.base_ref, f32[24,128]{1,0:T(8,128)S(1)} %shard_map.61.far_0, f32[24,128]{1,0:T(8,128)S(1)} %shard_map.62.far_1, bf16[128,8,256]{2,1,0:T(8,128)(2,1)S(1)} %shard_map.60.early_ref, bf16[128,8,256]{2,1,0:T(8,128)(2,1)S(1)} %add.14.mid_ref, ...), custom_call_target="tpu_custom_call" | custom-call | flops 1000 | bytes 1000 | tf_op jit(solution)/shard_map/pallas_call | solution.py:194
  63.4 1.1 %collective-permute-start.15 = (f32[24,128]{1,0:T(8,128)S(1)}, f32[24,128]{1,0:T(8,128)S(1)}, u32[]{:S(2)}, u32[]{:S(2)}) collective-permute-start(f32[24,128]{1,0:T(8,128)S(1)} %get-tuple-element.44), channel_id=1, source_target_pairs={{0,2},{2,0},{1,3},{3,1},{4,6},{6,4},{5,7},{7,5},{8,10},{10,8},{9,1... | collective-permute-start | bytes 36872 | tf_op jit(solution)/shard_map/ppermute | solution.py:262
  64.5 2.7 %collective-permute-done.15 = f32[24,128]{1,0:T(8,128)S(1)} collective-permute-done((f32[24,128]{1,0:T(8,128)S(1)}, f32[24,128]{1,0:T(8,128)S(1)}, u32[]{:S(2)}, u32[]{:S(2)}) %collective-permute-start.15) | collective-permute-done | bytes 12320 | tf_op jit(solution)/shard_map/ppermute | solution.py:262
  (25 shorter events, 3.2 us)
Async XLA Ops:
  1.1 14.9 %collective-permute-start.2 = (bf16[8,128,256]{2,1,0:T(8,128)(2,1)S(1)}, bf16[8,128,256]{2,1,0:T(8,128)(2,1)S(1)}, u32[]{:S(2)}, u32[]{:S(2)}) collective-permute-start(bf16[8,128,256]{2,1,0:T(8,128)(2,1)S(1)} %slice_bitcast_fusion.own_ref), channel_id=1, source_target_pairs={{0,2},{2,0},{1,3},{3,1},{4,6},{6,4},{5,7},{7,5},{8,10},{10,8},{9,1... | collective-permute-start | bytes 1572872 | tf_op jit(solution)/shard_map/ppermute | solution.py:220
  5.1 7.1 %collective-permute-start.1 = (bf16[4,128,256]{2,1,0:T(8,128)(2,1)S(1)}, bf16[4,128,256]{2,1,0:T(8,128)(2,1)S(1)}, u32[]{:S(2)}, u32[]{:S(2)}) collective-permute-start(bf16[4,128,256]{2,1,0:T(8,128)(2,1)S(1)} %slice_bitcast_fusion.1), channel_id=1, source_target_pairs={{4,8},{8,4},{5,9},{9,5},{6,10},{10,6},{7,11},{11,7},{20,24},{24,20... | collective-permute-start | bytes 786440 | tf_op jit(solution)/shard_map/ppermute | solution.py:224
  5.7 10.2 %collective-permute-start = (bf16[4,128,256]{2,1,0:T(8,128)(2,1)S(1)}, bf16[4,128,256]{2,1,0:T(8,128)(2,1)S(1)}, u32[]{:S(2)}, u32[]{:S(2)}) collective-permute-start(bf16[4,128,256]{2,1,0:T(8,128)(2,1)S(1)} %slice_bitcast_fusion.1), channel_id=1, source_target_pairs={{0,4},{4,0},{8,12},{12,8},{1,5},{5,1},{9,13},{13,9},{2,6},{6,2},{1... | collective-permute-start | bytes 786440 | tf_op jit(solution)/shard_map/ppermute | solution.py:223
  10.2 0.9 %copy-start = (f32[256,256]{1,0:T(8,128)S(1)}, f32[256,256]{1,0:T(8,128)}, u32[]{:S(2)}) copy-start(f32[256,256]{1,0:T(8,128)} %left_ref.1) | copy-start | bytes 786436
  11.1 0.9 %copy-start.1 = (f32[256,256]{1,0:T(8,128)S(1)}, f32[256,256]{1,0:T(8,128)}, u32[]{:S(2)}) copy-start(f32[256,256]{1,0:T(8,128)} %right_ref) | copy-start | bytes 786436
  12.2 11.2 %collective-permute-start.5 = (bf16[4,128,256]{2,1,0:T(8,128)(2,1)S(1)}, bf16[4,128,256]{2,1,0:T(8,128)(2,1)S(1)}, u32[]{:S(2)}, u32[]{:S(2)}) collective-permute-start(bf16[4,128,256]{2,1,0:T(8,128)(2,1)S(1)} %collective-permute-done.1), channel_id=1, source_target_pairs={{4,0},{8,12},{5,1},{9,13},{6,2},{10,14},{7,3},{11,15},{20,16},{24,... | collective-permute-start | bytes 786440 | tf_op jit(solution)/shard_map/ppermute | solution.py:225
  16.0 8.9 %collective-permute-start.7 = (bf16[4,128,256]{2,1,0:T(8,128)(2,1)S(1)}, bf16[4,128,256]{2,1,0:T(8,128)(2,1)S(1)}, u32[]{:S(2)}, u32[]{:S(2)}) collective-permute-start(bf16[4,128,256]{2,1,0:T(8,128)(2,1)S(1)} %collective-permute-done), channel_id=1, source_target_pairs={{4,8},{8,4},{5,9},{9,5},{6,10},{10,6},{7,11},{11,7},{20,24},{24,20... | collective-permute-start | bytes 786440 | tf_op jit(solution)/shard_map/ppermute | solution.py:227
  17.9 28.0 %copy-start.2 = (s32[4]{0:T(128)S(1)}, s32[4]{0:T(128)}, u32[]{:S(2)}) copy-start(s32[4]{0:T(128)} %order_ref.7) | copy-start | bytes 52
  18.0 17.1 %collective-permute-start.3 = (bf16[128,8,256]{2,1,0:T(8,128)(2,1)S(1)}, bf16[128,8,256]{2,1,0:T(8,128)(2,1)S(1)}, u32[]{:S(2)}, u32[]{:S(2)}) collective-permute-start(bf16[128,8,256]{2,1,0:T(8,128)(2,1)S(1)} %shard_map.56.own_ref), channel_id=1, source_target_pairs={{0,4},{4,0},{8,12},{12,8},{1,5},{5,1},{9,13},{13,9},{2,6},{6,2},{1... | collective-permute-start | bytes 1572872 | tf_op jit(solution)/shard_map/ppermute | solution.py:230
  22.7 13.1 %collective-permute-start.4 = (bf16[128,8,256]{2,1,0:T(8,128)(2,1)S(1)}, bf16[128,8,256]{2,1,0:T(8,128)(2,1)S(1)}, u32[]{:S(2)}, u32[]{:S(2)}) collective-permute-start(bf16[128,8,256]{2,1,0:T(8,128)(2,1)S(1)} %shard_map.56.own_ref), channel_id=1, source_target_pairs={{4,8},{8,4},{5,9},{9,5},{6,10},{10,6},{7,11},{11,7},{20,24},{24,20... | collective-permute-start | bytes 1572872 | tf_op jit(solution)/shard_map/ppermute | solution.py:231
  23.4 16.7 %collective-permute-start.6 = (bf16[8,128,256]{2,1,0:T(8,128)(2,1)S(1)}, bf16[8,128,256]{2,1,0:T(8,128)(2,1)S(1)}, u32[]{:S(2)}, u32[]{:S(2)}) collective-permute-start(bf16[8,128,256]{2,1,0:T(8,128)(2,1)S(1)} %pad_maximum_fusion.own_ref), channel_id=1, source_target_pairs={{0,2},{2,0},{1,3},{3,1},{4,6},{6,4},{5,7},{7,5},{8,10},{10,8},{9,1... | collective-permute-start | bytes 1572872 | tf_op jit(solution)/shard_map/ppermute | solution.py:233
  30.1 9.8 %collective-permute-start.9 = (bf16[4,128,256]{2,1,0:T(8,128)(2,1)S(1)}, bf16[4,128,256]{2,1,0:T(8,128)(2,1)S(1)}, u32[]{:S(2)}, u32[]{:S(2)}) collective-permute-start(bf16[4,128,256]{2,1,0:T(8,128)(2,1)S(1)} %collective-permute-done.7), channel_id=1, source_target_pairs={{4,0},{8,12},{5,1},{9,13},{6,2},{10,14},{7,3},{11,15},{20,16},{24,... | collective-permute-start | bytes 786440 | tf_op jit(solution)/shard_map/ppermute | solution.py:234
  35.0 7.0 %collective-permute-start.8 = (bf16[128,8,256]{2,1,0:T(8,128)(2,1)S(1)}, bf16[128,8,256]{2,1,0:T(8,128)(2,1)S(1)}, u32[]{:S(2)}, u32[]{:S(2)}) collective-permute-start(bf16[128,8,256]{2,1,0:T(8,128)(2,1)S(1)} %collective-permute-done.3.near), channel_id=1, source_target_pairs={{4,8},{8,4},{5,9},{9,5},{6,10},{10,6},{7,11},{11,7},{20,24},{24,20... | collective-permute-start | bytes 1572872 | tf_op jit(solution)/shard_map/ppermute | solution.py:235
  35.8 16.6 %collective-permute-start.10 = (bf16[128,8,256]{2,1,0:T(8,128)(2,1)S(1)}, bf16[128,8,256]{2,1,0:T(8,128)(2,1)S(1)}, u32[]{:S(2)}, u32[]{:S(2)}) collective-permute-start(bf16[128,8,256]{2,1,0:T(8,128)(2,1)S(1)} %collective-permute-done.4), channel_id=1, source_target_pairs={{4,0},{8,12},{5,1},{9,13},{6,2},{10,14},{7,3},{11,15},{20,16},{24,... | collective-permute-start | bytes 1572872 | tf_op jit(solution)/shard_map/ppermute | solution.py:236
  41.3 11.4 %collective-permute-start.11 = (bf16[8,128,256]{2,1,0:T(8,128)(2,1)S(1)}, bf16[8,128,256]{2,1,0:T(8,128)(2,1)S(1)}, u32[]{:S(2)}, u32[]{:S(2)}) collective-permute-start(bf16[8,128,256]{2,1,0:T(8,128)(2,1)S(1)} %pad_maximum_fusion.1.own_ref), channel_id=1, source_target_pairs={{0,2},{2,0},{1,3},{3,1},{4,6},{6,4},{5,7},{7,5},{8,10},{10,8},{9,1... | collective-permute-start | bytes 1572872 | tf_op jit(solution)/shard_map/ppermute | solution.py:239
  42.0 16.0 %collective-permute-start.12 = (bf16[64,8,256]{2,1,0:T(8,128)(2,1)S(1)}, bf16[64,8,256]{2,1,0:T(8,128)(2,1)S(1)}, u32[]{:S(2)}, u32[]{:S(2)}) collective-permute-start(bf16[64,8,256]{2,1,0:T(8,128)(2,1)S(1)} %slice.20), channel_id=1, source_target_pairs={{4,0},{8,12},{5,1},{9,13},{6,2},{10,14},{7,3},{11,15},{20,16},{24,... | collective-permute-start | bytes 786440 | tf_op jit(solution)/shard_map/ppermute | solution.py:242
  43.3 17.2 %collective-permute-start.13 = (bf16[32,8,256]{2,1,0:T(8,128)(2,1)S(1)}, bf16[32,8,256]{2,1,0:T(8,128)(2,1)S(1)}, u32[]{:S(2)}, u32[]{:S(2)}) collective-permute-start(bf16[32,8,256]{2,1,0:T(8,128)(2,1)S(1)} %get-tuple-element.46), channel_id=1, source_target_pairs={{4,0},{8,12},{5,1},{9,13},{6,2},{10,14},{7,3},{11,15},{20,16},{24,... | collective-permute-start | bytes 393224 | tf_op jit(solution)/shard_map/ppermute | solution.py:242
  44.6 17.3 %collective-permute-start.14 = (bf16[32,8,256]{2,1,0:T(8,128)(2,1)S(1)}, bf16[32,8,256]{2,1,0:T(8,128)(2,1)S(1)}, u32[]{:S(2)}, u32[]{:S(2)}) collective-permute-start(bf16[32,8,256]{2,1,0:T(8,128)(2,1)S(1)} %get-tuple-element.45), channel_id=1, source_target_pairs={{4,0},{8,12},{5,1},{9,13},{6,2},{10,14},{7,3},{11,15},{20,16},{24,... | collective-permute-start | bytes 393224 | tf_op jit(solution)/shard_map/ppermute | solution.py:242
  63.4 3.8 %collective-permute-start.15 = (f32[24,128]{1,0:T(8,128)S(1)}, f32[24,128]{1,0:T(8,128)S(1)}, u32[]{:S(2)}, u32[]{:S(2)}) collective-permute-start(f32[24,128]{1,0:T(8,128)S(1)} %get-tuple-element.44), channel_id=1, source_target_pairs={{0,2},{2,0},{1,3},{3,1},{4,6},{6,4},{5,7},{7,5},{8,10},{10,8},{9,1... | collective-permute-start | bytes 36872 | tf_op jit(solution)/shard_map/ppermute | solution.py:262

commit v18 on v17

--- a/solution.py
+++ b/solution.py
@@ -135,20 +135,20 @@
     return lax.fori_loop(0, rows // DEEP, body, start)
 
 
-def first_pass_kernel(ex, early_ref, own_ref, near, far_in, grad_ref, order_ref, out_ref):
+def first_pass_kernel(ex, early_ref, own_ref, near, grad_ref, order_ref, out_ref):
     late = own_ref.shape[1]
-    acc = inner_products((early_ref, own_ref, near, far_in), grad_ref)
+    acc = inner_products((early_ref, own_ref, near), grad_ref)
     sources = slot_sources(lax.axis_index("ex"))
     early = [acc[EARLY * s : EARLY * (s + 1)] for s in range(2)]
     base = early_ref.shape[1]
-    slots = [acc[base + late * s : base + late * (s + 1)] for s in range(3)]
+    slots = [acc[base + late * s : base + late * (s + 1)] for s in range(2)]
     for b in range(ex):
         block = order_ref[b]
         low = jnp.zeros_like(early[0])
         for source, slot in zip(sources, early):
             low = low + jnp.where(source == block, slot, 0.0)
         high = jnp.zeros_like(slots[0])
-        for source, slot in zip(sources[:2] + sources[3:], slots):
+        for source, slot in zip(sources, slots):
             high = high + jnp.where(source == block, slot, 0.0)
         at = b * (EARLY + late)
         out_ref[at : at + EARLY, :] = low
@@ -161,17 +161,20 @@
     return [me, near, jnp.where(low_pair, 2, 1), jnp.where(low_pair, 3, 0)]
 
 
-def far_pass_kernel(first, ex, early_ref, mid_ref, far_out, grad_ref, order_ref, out_ref):
-    out_ref[...] = inner_products((early_ref, mid_ref, far_out), grad_ref, first, far_out.shape[0])
+def far_pass_kernel(first, ex, early_ref, mid_ref, far_in, far_out, grad_ref, order_ref, out_ref, far_ref):
+    far_ref[...] = far_in[...] + far_out[...]
+    out_ref[...] = inner_products((early_ref, mid_ref, far_ref), grad_ref, first, far_out.shape[0])
 
 
 def last_pass_kernel(
-    ex, base_ref, far_0, far_1, early_ref, mid_ref, far_out, grad_ref, order_ref, mine_ref, send_ref, full_ref
+    ex, base_ref, far_0, far_1, early_ref, mid_ref, far_in, far_out, grad_ref, order_ref,
+    mine_ref, send_ref, full_ref, far_ref,
 ):
     late = far_out.shape[1]
     rows = far_out.shape[0]
     first = grad_ref.shape[0] - rows
-    acc = far_0[...] + far_1[...] + inner_products((early_ref, mid_ref, far_out), grad_ref, first, rows)
+    far_ref[...] = far_in[...] + far_out[...]
+    acc = far_0[...] + far_1[...] + inner_products((early_ref, mid_ref, far_ref), grad_ref, first, rows)
     mid, far = slot_sources(lax.axis_index("ex"))[2:]
     low_mid, low_far = acc[:EARLY], acc[EARLY : 2 * EARLY]
     high_mid, high_far = acc[2 * EARLY : 2 * EARLY + late], acc[2 * EARLY + late :]
@@ -237,27 +240,28 @@
     cond_0 = condition(after(early_0, near, mid), early_0_other, *terms)
     early_1 = jnp.concatenate([raw_mid + raw_mid_out, after(raw_far_mid, near, mid) + raw_far_out], axis=0)
     early_1_other = lax.ppermute(after(early_1, cond_0), "feat", swap)
+    base = score_call(
+        first_pass_kernel, ex, (cond_0, late, near, grads), block_order,
+        jax.ShapeDtypeStruct((ex * count, n), F32),
+    )
     rows = far_mid.shape[0]
     cuts = [0, rows // 2, 3 * rows // 4, rows]
-    far_out = [lax.ppermute(far_mid[a:b], "ex", OUTWARD) for a, b in zip(cuts, cuts[1:])]
+    far_in = [after(far_mid, base)[a:b] for a, b in zip(cuts, cuts[1:])]
+    far_out = [lax.ppermute(x, "ex", OUTWARD) for x in far_in]
     cond_1 = condition(after(early_1, far_mid, mid_out), early_1_other, *terms)
 
-    base = score_call(
-        first_pass_kernel, ex, (cond_0, late, near, far_mid, grads), block_order,
-        jax.ShapeDtypeStruct((ex * count, n), F32),
-    )
     mid = mid + mid_out
     far_sums, earlier = [], base
-    for first, arrived in zip(cuts, far_out[:-1]):
+    for first, held, arrived in zip(cuts, far_in[:-1], far_out[:-1]):
         earlier = score_call(
-            functools.partial(far_pass_kernel, first), ex, (cond_1, mid, arrived, after(grads, earlier)), block_order,
-            jax.ShapeDtypeStruct((2 * count, n), F32),
+            functools.partial(far_pass_kernel, first), ex, (cond_1, mid, held, arrived, after(grads, earlier)),
+            block_order, jax.ShapeDtypeStruct((2 * count, n), F32), [pltpu.VMEM(arrived.shape, BF16)],
         )
         far_sums.append(earlier)
     half = jax.ShapeDtypeStruct((ex * count // 2, n), F32)
     mine, send = score_call(
-        last_pass_kernel, ex, (base, *far_sums, cond_1, mid, far_out[-1], grads), block_order, (half, half),
-        [pltpu.VMEM((ex * count, n), F32)],
+        last_pass_kernel, ex, (base, *far_sums, cond_1, mid, far_in[-1], far_out[-1], grads), block_order,
+        (half, half), [pltpu.VMEM((ex * count, n), F32), pltpu.VMEM(far_out[-1].shape, BF16)],
     )
     scores = mine + lax.ppermute(send, "feat", swap)
     return scores.T[:, None, :]

time: 68.2 us -> 68.2 us (level)
  no operation moved by 1% of the time
where the time goes in v18:
time: 68.2 us; the launch traced here: 67.7 us
  starting transfers between devices  25.9 us (38%)
  waiting for transfers between devices  18.9 us (28%)
  Pallas kernels  17.7 us (26%)
  local copies, waits for them, and re-layouts  3.99 us (6%)
  other arithmetic  0.96 us (1%)
    pallas_call x4, Pallas kernels, score_call(): pl.pallas_call(functools.partial(kernel, ex), out_shape=out_shape, in_spe...  8.73 us
    pallas_call x1, Pallas kernels, regroup(): pl.pallas_call(regroup_kernel, out_shape=jax.ShapeDtypeStruct((rows, n, w...  5.17 us
    ppermute x1, starting transfers between devices, per_device_line(): near = lax.ppermute(late, 'ex', PAIRS)  4.7 us
    ppermute x3, waiting for transfers between devices, per_device_line(): far_out = [lax.ppermute(x, 'ex', OUTWARD) for x in far_in]  4.53 us
    ppermute x1, starting transfers between devices, per_device_line(): raw_near = lax.ppermute(raw, 'ex', PAIRS)  4.45 us
    ppermute x3, starting transfers between devices, per_device_line(): far_out = [lax.ppermute(x, 'ex', OUTWARD) for x in far_in]  3.88 us
    pallas_call x3, Pallas kernels, condition(): pl.pallas_call(condition_kernel, out_shape=jax.ShapeDtypeStruct((rows, co...  3.74 us
    ppermute x1, waiting for transfers between devices, per_device_line(): near = lax.ppermute(late, 'ex', PAIRS)  3.67 us
  transfers between devices with their start and end apart: 16, of which 9 were waited for; matrix products, arithmetic and copies ran while one was open for 2% of the time, Pallas kernels for 24%

profile of v18, /device:TPU:0, one launch (start us, length us, event | category | flops | bytes accessed | tf_op | source)
XLA Modules:
  0.0 67.7 jit_solution(15577565724506542771)
XLA Ops:
  0.0 1.1 %slice_bitcast_fusion.own_ref = bf16[8,128,256]{2,1,0:T(8,128)(2,1)S(1)} fusion(bf16[1,12,128,256]{3,2,1,0:T(8,128)(2,1)} %param.6), kind=kLoop, calls=%fused_computation.2 | loop fusion | bytes 1048576 | tf_op jit(solution)/shard_map/squeeze | solution.py:222
  1.1 3.0 %collective-permute-start.2 = (bf16[8,128,256]{2,1,0:T(8,128)(2,1)S(1)}, bf16[8,128,256]{2,1,0:T(8,128)(2,1)S(1)}, u32[]{:S(2)}, u32[]{:S(2)}) collective-permute-start(bf16[8,128,256]{2,1,0:T(8,128)(2,1)S(1)} %slice_bitcast_fusion.own_ref), channel_id=1, source_target_pairs={{0,2},{2,0},{1,3},{3,1},{4,6},{6,4},{5,7},{7,5},{8,10},{10,8},{9,1... | collective-permute-start | bytes 1572872 | tf_op jit(solution)/shard_map/ppermute | solution.py:223
  4.1 1.0 %slice_bitcast_fusion.1 = bf16[4,128,256]{2,1,0:T(8,128)(2,1)S(1)} fusion(bf16[1,12,128,256]{3,2,1,0:T(8,128)(2,1)} %param.6), kind=kLoop, calls=%fused_computation.3 | loop fusion | bytes 524288 | tf_op jit(solution)/shard_map/squeeze | solution.py:224
  5.1 0.7 %collective-permute-start.1 = (bf16[4,128,256]{2,1,0:T(8,128)(2,1)S(1)}, bf16[4,128,256]{2,1,0:T(8,128)(2,1)S(1)}, u32[]{:S(2)}, u32[]{:S(2)}) collective-permute-start(bf16[4,128,256]{2,1,0:T(8,128)(2,1)S(1)} %slice_bitcast_fusion.1), channel_id=1, source_target_pairs={{4,8},{8,4},{5,9},{9,5},{6,10},{10,6},{7,11},{11,7},{20,24},{24,20... | collective-permute-start | bytes 786440 | tf_op jit(solution)/shard_map/ppermute | solution.py:227
  5.7 4.4 %collective-permute-start = (bf16[4,128,256]{2,1,0:T(8,128)(2,1)S(1)}, bf16[4,128,256]{2,1,0:T(8,128)(2,1)S(1)}, u32[]{:S(2)}, u32[]{:S(2)}) collective-permute-start(bf16[4,128,256]{2,1,0:T(8,128)(2,1)S(1)} %slice_bitcast_fusion.1), channel_id=1, source_target_pairs={{0,4},{4,0},{8,12},{12,8},{1,5},{5,1},{9,13},{13,9},{2,6},{6,2},{1... | collective-permute-start | bytes 786440 | tf_op jit(solution)/shard_map/ppermute | solution.py:226
  10.2 0.9 %copy-done = f32[256,256]{1,0:T(8,128)S(1)} copy-done((f32[256,256]{1,0:T(8,128)S(1)}, f32[256,256]{1,0:T(8,128)}, u32[]{:S(2)}) %copy-start) | copy-done | bytes 262168
  11.1 0.9 %copy-done.1 = f32[256,256]{1,0:T(8,128)S(1)} copy-done((f32[256,256]{1,0:T(8,128)S(1)}, f32[256,256]{1,0:T(8,128)}, u32[]{:S(2)}) %copy-start.1) | copy-done | bytes 262168
  12.2 1.3 %collective-permute-start.5 = (bf16[4,128,256]{2,1,0:T(8,128)(2,1)S(1)}, bf16[4,128,256]{2,1,0:T(8,128)(2,1)S(1)}, u32[]{:S(2)}, u32[]{:S(2)}) collective-permute-start(bf16[4,128,256]{2,1,0:T(8,128)(2,1)S(1)} %collective-permute-done.1), channel_id=1, source_target_pairs={{4,0},{8,12},{5,1},{9,13},{6,2},{10,14},{7,3},{11,15},{20,16},{24,... | collective-permute-start | bytes 786440 | tf_op jit(solution)/shard_map/ppermute | solution.py:228
  13.5 2.5 %collective-permute-done = bf16[4,128,256]{2,1,0:T(8,128)(2,1)S(1)} collective-permute-done((bf16[4,128,256]{2,1,0:T(8,128)(2,1)S(1)}, bf16[4,128,256]{2,1,0:T(8,128)(2,1)S(1)}, u32[]{:S(2)}, u32[]{:S(2)}) %collective-permute-start) | collective-permute-done | bytes 262176 | tf_op jit(solution)/shard_map/ppermute | solution.py:226
  16.7 1.2 %shard_map.56.own_ref = bf16[128,8,256]{2,1,0:T(8,128)(2,1)S(1)} custom-call(bf16[8,128,256]{2,1,0:T(8,128)(2,1)S(1)} %slice_bitcast_fusion.own_ref, bf16[8,128,256]{2,1,0:T(8,128)(2,1)S(1)} %collective-permute-done.2.far_ref, bf16[384,256]{1,0:T(8,128)(2,1)S(1)} %get-tuple-element.29.left_ref, bf16[512,256]{1,0:T(8,128)(2,1)S(1)} %get-tuple-element.30.right_ref), custom_call_target="tpu_custom_call" | custom-call | flops 960000000 | bytes 2097152 | tf_op jit(solution)/shard_map/pallas_call | solution.py:70
  17.9 4.7 %collective-permute-start.3 = (bf16[128,8,256]{2,1,0:T(8,128)(2,1)S(1)}, bf16[128,8,256]{2,1,0:T(8,128)(2,1)S(1)}, u32[]{:S(2)}, u32[]{:S(2)}) collective-permute-start(bf16[128,8,256]{2,1,0:T(8,128)(2,1)S(1)} %shard_map.56.own_ref), channel_id=1, source_target_pairs={{0,4},{4,0},{8,12},{12,8},{1,5},{5,1},{9,13},{13,9},{2,6},{6,2},{1... | collective-permute-start | bytes 1572872 | tf_op jit(solution)/shard_map/ppermute | solution.py:233
  22.6 0.7 %collective-permute-start.4 = (bf16[128,8,256]{2,1,0:T(8,128)(2,1)S(1)}, bf16[128,8,256]{2,1,0:T(8,128)(2,1)S(1)}, u32[]{:S(2)}, u32[]{:S(2)}) collective-permute-start(bf16[128,8,256]{2,1,0:T(8,128)(2,1)S(1)} %shard_map.56.own_ref), channel_id=1, source_target_pairs={{4,8},{8,4},{5,9},{9,5},{6,10},{10,6},{7,11},{11,7},{20,24},{24,20... | collective-permute-start | bytes 1572872 | tf_op jit(solution)/shard_map/ppermute | solution.py:234
  23.3 1.6 %collective-permute-start.6 = (bf16[8,128,256]{2,1,0:T(8,128)(2,1)S(1)}, bf16[8,128,256]{2,1,0:T(8,128)(2,1)S(1)}, u32[]{:S(2)}, u32[]{:S(2)}) collective-permute-start(bf16[8,128,256]{2,1,0:T(8,128)(2,1)S(1)} %pad_maximum_fusion.own_ref), channel_id=1, source_target_pairs={{0,2},{2,0},{1,3},{3,1},{4,6},{6,4},{5,7},{7,5},{8,10},{10,8},{9,1... | collective-permute-start | bytes 1572872 | tf_op jit(solution)/shard_map/ppermute | solution.py:236
  24.9 5.2 %shard_map.58.grad_ref = bf16[128,128,256]{2,1,0:T(8,128)(2,1)S(1)} custom-call(bf16[128,128,256]{2,1,0:T(8,128)(2,1)} %grads_ref), custom_call_target="tpu_custom_call" | custom-call | flops 6000000000 | bytes 16000000 | tf_op jit(solution)/shard_map/pallas_call | solution.py:106
  30.1 1.3 %collective-permute-start.8 = (bf16[4,128,256]{2,1,0:T(8,128)(2,1)S(1)}, bf16[4,128,256]{2,1,0:T(8,128)(2,1)S(1)}, u32[]{:S(2)}, u32[]{:S(2)}) collective-permute-start(bf16[4,128,256]{2,1,0:T(8,128)(2,1)S(1)} %collective-permute-done.7), channel_id=1, source_target_pairs={{4,0},{8,12},{5,1},{9,13},{6,2},{10,14},{7,3},{11,15},{20,16},{24,... | collective-permute-start | bytes 786440 | tf_op jit(solution)/shard_map/ppermute | solution.py:237
  31.4 3.7 %collective-permute-done.3.near = bf16[128,8,256]{2,1,0:T(8,128)(2,1)S(1)} collective-permute-done((bf16[128,8,256]{2,1,0:T(8,128)(2,1)S(1)}, bf16[128,8,256]{2,1,0:T(8,128)(2,1)S(1)}, u32[]{:S(2)}, u32[]{:S(2)}) %collective-permute-start.3) | collective-permute-done | bytes 524320 | tf_op jit(solution)/shard_map/ppermute | solution.py:233
  35.1 0.7 %collective-permute-start.9 = (bf16[128,8,256]{2,1,0:T(8,128)(2,1)S(1)}, bf16[128,8,256]{2,1,0:T(8,128)(2,1)S(1)}, u32[]{:S(2)}, u32[]{:S(2)}) collective-permute-start(bf16[128,8,256]{2,1,0:T(8,128)(2,1)S(1)} %collective-permute-done.3.near), channel_id=1, source_target_pairs={{4,8},{8,4},{5,9},{9,5},{6,10},{10,6},{7,11},{11,7},{20,24},{24,20... | collective-permute-start | bytes 1572872 | tf_op jit(solution)/shard_map/ppermute | solution.py:238
  35.8 1.3 %collective-permute-start.10 = (bf16[128,8,256]{2,1,0:T(8,128)(2,1)S(1)}, bf16[128,8,256]{2,1,0:T(8,128)(2,1)S(1)}, u32[]{:S(2)}, u32[]{:S(2)}) collective-permute-start(bf16[128,8,256]{2,1,0:T(8,128)(2,1)S(1)} %collective-permute-done.4), channel_id=1, source_target_pairs={{4,0},{8,12},{5,1},{9,13},{6,2},{10,14},{7,3},{11,15},{20,16},{24,... | collective-permute-start | bytes 1572872 | tf_op jit(solution)/shard_map/ppermute | solution.py:239
  37.1 2.8 %collective-permute-done.8 = bf16[4,128,256]{2,1,0:T(8,128)(2,1)S(1)} collective-permute-done((bf16[4,128,256]{2,1,0:T(8,128)(2,1)S(1)}, bf16[4,128,256]{2,1,0:T(8,128)(2,1)S(1)}, u32[]{:S(2)}, u32[]{:S(2)}) %collective-permute-start.8) | collective-permute-done | bytes 262176 | tf_op jit(solution)/shard_map/ppermute | solution.py:237
  40.0 1.2 %shard_map.57.early_ref = bf16[128,8,256]{2,1,0:T(8,128)(2,1)S(1)} custom-call(bf16[8,128,256]{2,1,0:T(8,128)(2,1)S(1)} %pad_maximum_fusion.own_ref, bf16[8,128,256]{2,1,0:T(8,128)(2,1)S(1)} %collective-permute-done.6.far_ref, bf16[384,256]{1,0:T(8,128)(2,1)S(1)} %get-tuple-element.29.left_ref, bf16[512,256]{1,0:T(8,128)(2,1)S(1)} %get-tuple-element.30.right_ref), custom_call_target="tpu_custom_call" | custom-call | flops 960000000 | bytes 2097152 | tf_op jit(solution)/shard_map/pallas_call | solution.py:70
  42.0 3.9 %shard_map.59.base_ref = f32[48,128]{1,0:T(8,128)S(1)} custom-call(bf16[128,8,256]{2,1,0:T(8,128)(2,1)S(1)} %shard_map.57.early_ref, bf16[128,8,256]{2,1,0:T(8,128)(2,1)S(1)} %shard_map.56.own_ref, bf16[128,8,256]{2,1,0:T(8,128)(2,1)S(1)} %collective-permute-done.3.near, bf16[128,128,256]{2,1,0:T(8,128)(2,1)S(1)} %shard_map.58.grad_ref, s32[4]{0:T(128)S(1)} %copy-done.2), custom_call_target="tpu_custom_call" | custom-call | flops 1000 | bytes 1000 | tf_op jit(solution)/shard_map/pallas_call | solution.py:197
  45.9 1.3 %collective-permute-start.12 = (bf16[64,8,256]{2,1,0:T(8,128)(2,1)S(1)}, bf16[64,8,256]{2,1,0:T(8,128)(2,1)S(1)}, u32[]{:S(2)}, u32[]{:S(2)}) collective-permute-start(bf16[64,8,256]{2,1,0:T(8,128)(2,1)S(1)} %slice.17.far_in), channel_id=1, source_target_pairs={{4,0},{8,12},{5,1},{9,13},{6,2},{10,14},{7,3},{11,15},{20,16},{24,... | collective-permute-start | bytes 786440 | tf_op jit(solution)/shard_map/ppermute | solution.py:250
  47.2 1.3 %collective-permute-start.13 = (bf16[32,8,256]{2,1,0:T(8,128)(2,1)S(1)}, bf16[32,8,256]{2,1,0:T(8,128)(2,1)S(1)}, u32[]{:S(2)}, u32[]{:S(2)}) collective-permute-start(bf16[32,8,256]{2,1,0:T(8,128)(2,1)S(1)} %get-tuple-element.48.far_in), channel_id=1, source_target_pairs={{4,0},{8,12},{5,1},{9,13},{6,2},{10,14},{7,3},{11,15},{20,16},{24,... | collective-permute-start | bytes 393224 | tf_op jit(solution)/shard_map/ppermute | solution.py:250
  48.5 1.3 %collective-permute-start.14 = (bf16[32,8,256]{2,1,0:T(8,128)(2,1)S(1)}, bf16[32,8,256]{2,1,0:T(8,128)(2,1)S(1)}, u32[]{:S(2)}, u32[]{:S(2)}) collective-permute-start(bf16[32,8,256]{2,1,0:T(8,128)(2,1)S(1)} %get-tuple-element.47.far_in), channel_id=1, source_target_pairs={{4,0},{8,12},{5,1},{9,13},{6,2},{10,14},{7,3},{11,15},{20,16},{24,... | collective-permute-start | bytes 393224 | tf_op jit(solution)/shard_map/ppermute | solution.py:250
  49.8 2.6 %collective-permute-done.10 = bf16[128,8,256]{2,1,0:T(8,128)(2,1)S(1)} collective-permute-done((bf16[128,8,256]{2,1,0:T(8,128)(2,1)S(1)}, bf16[128,8,256]{2,1,0:T(8,128)(2,1)S(1)}, u32[]{:S(2)}, u32[]{:S(2)}) %collective-permute-start.10) | collective-permute-done | bytes 524320 | tf_op jit(solution)/shard_map/ppermute | solution.py:239
  52.7 1.3 %shard_map.60.early_ref = bf16[128,8,256]{2,1,0:T(8,128)(2,1)S(1)} custom-call(bf16[8,128,256]{2,1,0:T(8,128)(2,1)S(1)} %pad_maximum_fusion.1.own_ref, bf16[8,128,256]{2,1,0:T(8,128)(2,1)S(1)} %collective-permute-done.11.far_ref, bf16[384,256]{1,0:T(8,128)(2,1)S(1)} %get-tuple-element.29.left_ref, bf16[512,256]{1,0:T(8,128)(2,1)S(1)} %get-tuple-element.30.right_ref), custom_call_target="tpu_custom_call" | custom-call | flops 960000000 | bytes 2097152 | tf_op jit(solution)/shard_map/pallas_call | solution.py:70
  54.0 4.0 %collective-permute-done.12.far_out = bf16[64,8,256]{2,1,0:T(8,128)(2,1)S(1)} collective-permute-done((bf16[64,8,256]{2,1,0:T(8,128)(2,1)S(1)}, bf16[64,8,256]{2,1,0:T(8,128)(2,1)S(1)}, u32[]{:S(2)}, u32[]{:S(2)}) %collective-permute-start.12) | collective-permute-done | bytes 262176 | tf_op jit(solution)/shard_map/ppermute | solution.py:250
  58.0 2.2 %shard_map.61.far_0 = f32[24,128]{1,0:T(8,128)S(1)} custom-call(bf16[128,8,256]{2,1,0:T(8,128)(2,1)S(1)} %shard_map.60.early_ref, bf16[128,8,256]{2,1,0:T(8,128)(2,1)S(1)} %add.14.mid_ref, bf16[64,8,256]{2,1,0:T(8,128)(2,1)S(1)} %slice.17.far_in, bf16[64,8,256]{2,1,0:T(8,128)(2,1)S(1)} %collective-permute-done.12.far_out, ...), custom_call_target="tpu_custom_call" | custom-call | flops 1000 | bytes 1000 | tf_op jit(solution)/shard_map/pallas_call | solution.py:197
  60.6 1.3 %shard_map.62.far_1 = f32[24,128]{1,0:T(8,128)S(1)} custom-call(bf16[128,8,256]{2,1,0:T(8,128)(2,1)S(1)} %shard_map.60.early_ref, bf16[128,8,256]{2,1,0:T(8,128)(2,1)S(1)} %add.14.mid_ref, bf16[32,8,256]{2,1,0:T(8,128)(2,1)S(1)} %get-tuple-element.48.far_in, bf16[32,8,256]{2,1,0:T(8,128)(2,1)S(1)} %collective-permute-done.13.far_out, ...), custom_call_target="tpu_custom_call" | custom-call | flops 1000 | bytes 1000 | tf_op jit(solution)/shard_map/pallas_call | solution.py:197
  62.0 1.4 %shard_map.63 = (f32[24,128]{1,0:T(8,128)S(1)}, f32[24,128]{1,0:T(8,128)S(1)}) custom-call(f32[48,128]{1,0:T(8,128)S(1)} %shard_map.59.base_ref, f32[24,128]{1,0:T(8,128)S(1)} %shard_map.61.far_0, f32[24,128]{1,0:T(8,128)S(1)} %shard_map.62.far_1, bf16[128,8,256]{2,1,0:T(8,128)(2,1)S(1)} %shard_map.60.early_ref, bf16[128,8,256]{2,1,0:T(8,128)(2,1)S(1)} %add.14.mid_ref, ...), custom_call_target="tpu_custom_call" | custom-call | flops 1000 | bytes 1000 | tf_op jit(solution)/shard_map/pallas_call | solution.py:197
  63.4 1.1 %collective-permute-start.15 = (f32[24,128]{1,0:T(8,128)S(1)}, f32[24,128]{1,0:T(8,128)S(1)}, u32[]{:S(2)}, u32[]{:S(2)}) collective-permute-start(f32[24,128]{1,0:T(8,128)S(1)} %get-tuple-element.46), channel_id=1, source_target_pairs={{0,2},{2,0},{1,3},{3,1},{4,6},{6,4},{5,7},{7,5},{8,10},{10,8},{9,1... | collective-permute-start | bytes 36872 | tf_op jit(solution)/shard_map/ppermute | solution.py:266
  64.5 2.7 %collective-permute-done.15 = f32[24,128]{1,0:T(8,128)S(1)} collective-permute-done((f32[24,128]{1,0:T(8,128)S(1)}, f32[24,128]{1,0:T(8,128)S(1)}, u32[]{:S(2)}, u32[]{:S(2)}) %collective-permute-start.15) | collective-permute-done | bytes 12320 | tf_op jit(solution)/shard_map/ppermute | solution.py:266
  (25 shorter events, 3.2 us)
Async XLA Ops:
  1.1 14.9 %collective-permute-start.2 = (bf16[8,128,256]{2,1,0:T(8,128)(2,1)S(1)}, bf16[8,128,256]{2,1,0:T(8,128)(2,1)S(1)}, u32[]{:S(2)}, u32[]{:S(2)}) collective-permute-start(bf16[8,128,256]{2,1,0:T(8,128)(2,1)S(1)} %slice_bitcast_fusion.own_ref), channel_id=1, source_target_pairs={{0,2},{2,0},{1,3},{3,1},{4,6},{6,4},{5,7},{7,5},{8,10},{10,8},{9,1... | collective-permute-start | bytes 1572872 | tf_op jit(solution)/shard_map/ppermute | solution.py:223
  5.1 7.1 %collective-permute-start.1 = (bf16[4,128,256]{2,1,0:T(8,128)(2,1)S(1)}, bf16[4,128,256]{2,1,0:T(8,128)(2,1)S(1)}, u32[]{:S(2)}, u32[]{:S(2)}) collective-permute-start(bf16[4,128,256]{2,1,0:T(8,128)(2,1)S(1)} %slice_bitcast_fusion.1), channel_id=1, source_target_pairs={{4,8},{8,4},{5,9},{9,5},{6,10},{10,6},{7,11},{11,7},{20,24},{24,20... | collective-permute-start | bytes 786440 | tf_op jit(solution)/shard_map/ppermute | solution.py:227
  5.7 10.2 %collective-permute-start = (bf16[4,128,256]{2,1,0:T(8,128)(2,1)S(1)}, bf16[4,128,256]{2,1,0:T(8,128)(2,1)S(1)}, u32[]{:S(2)}, u32[]{:S(2)}) collective-permute-start(bf16[4,128,256]{2,1,0:T(8,128)(2,1)S(1)} %slice_bitcast_fusion.1), channel_id=1, source_target_pairs={{0,4},{4,0},{8,12},{12,8},{1,5},{5,1},{9,13},{13,9},{2,6},{6,2},{1... | collective-permute-start | bytes 786440 | tf_op jit(solution)/shard_map/ppermute | solution.py:226
  10.2 0.9 %copy-start = (f32[256,256]{1,0:T(8,128)S(1)}, f32[256,256]{1,0:T(8,128)}, u32[]{:S(2)}) copy-start(f32[256,256]{1,0:T(8,128)} %left_ref.1) | copy-start | bytes 786436
  11.1 0.9 %copy-start.1 = (f32[256,256]{1,0:T(8,128)S(1)}, f32[256,256]{1,0:T(8,128)}, u32[]{:S(2)}) copy-start(f32[256,256]{1,0:T(8,128)} %right_ref) | copy-start | bytes 786436
  12.2 11.2 %collective-permute-start.5 = (bf16[4,128,256]{2,1,0:T(8,128)(2,1)S(1)}, bf16[4,128,256]{2,1,0:T(8,128)(2,1)S(1)}, u32[]{:S(2)}, u32[]{:S(2)}) collective-permute-start(bf16[4,128,256]{2,1,0:T(8,128)(2,1)S(1)} %collective-permute-done.1), channel_id=1, source_target_pairs={{4,0},{8,12},{5,1},{9,13},{6,2},{10,14},{7,3},{11,15},{20,16},{24,... | collective-permute-start | bytes 786440 | tf_op jit(solution)/shard_map/ppermute | solution.py:228
  16.0 8.9 %collective-permute-start.7 = (bf16[4,128,256]{2,1,0:T(8,128)(2,1)S(1)}, bf16[4,128,256]{2,1,0:T(8,128)(2,1)S(1)}, u32[]{:S(2)}, u32[]{:S(2)}) collective-permute-start(bf16[4,128,256]{2,1,0:T(8,128)(2,1)S(1)} %collective-permute-done), channel_id=1, source_target_pairs={{4,8},{8,4},{5,9},{9,5},{6,10},{10,6},{7,11},{11,7},{20,24},{24,20... | collective-permute-start | bytes 786440 | tf_op jit(solution)/shard_map/ppermute | solution.py:230
  17.9 24.0 %copy-start.2 = (s32[4]{0:T(128)S(1)}, s32[4]{0:T(128)}, u32[]{:S(2)}) copy-start(s32[4]{0:T(128)} %order_ref.7) | copy-start | bytes 52
  17.9 17.1 %collective-permute-start.3 = (bf16[128,8,256]{2,1,0:T(8,128)(2,1)S(1)}, bf16[128,8,256]{2,1,0:T(8,128)(2,1)S(1)}, u32[]{:S(2)}, u32[]{:S(2)}) collective-permute-start(bf16[128,8,256]{2,1,0:T(8,128)(2,1)S(1)} %shard_map.56.own_ref), channel_id=1, source_target_pairs={{0,4},{4,0},{8,12},{12,8},{1,5},{5,1},{9,13},{13,9},{2,6},{6,2},{1... | collective-permute-start | bytes 1572872 | tf_op jit(solution)/shard_map/ppermute | solution.py:233
  22.6 13.2 %collective-permute-start.4 = (bf16[128,8,256]{2,1,0:T(8,128)(2,1)S(1)}, bf16[128,8,256]{2,1,0:T(8,128)(2,1)S(1)}, u32[]{:S(2)}, u32[]{:S(2)}) collective-permute-start(bf16[128,8,256]{2,1,0:T(8,128)(2,1)S(1)} %shard_map.56.own_ref), channel_id=1, source_target_pairs={{4,8},{8,4},{5,9},{9,5},{6,10},{10,6},{7,11},{11,7},{20,24},{24,20... | collective-permute-start | bytes 1572872 | tf_op jit(solution)/shard_map/ppermute | solution.py:234
  23.3 16.7 %collective-permute-start.6 = (bf16[8,128,256]{2,1,0:T(8,128)(2,1)S(1)}, bf16[8,128,256]{2,1,0:T(8,128)(2,1)S(1)}, u32[]{:S(2)}, u32[]{:S(2)}) collective-permute-start(bf16[8,128,256]{2,1,0:T(8,128)(2,1)S(1)} %pad_maximum_fusion.own_ref), channel_id=1, source_target_pairs={{0,2},{2,0},{1,3},{3,1},{4,6},{6,4},{5,7},{7,5},{8,10},{10,8},{9,1... | collective-permute-start | bytes 1572872 | tf_op jit(solution)/shard_map/ppermute | solution.py:236
  30.1 9.8 %collective-permute-start.8 = (bf16[4,128,256]{2,1,0:T(8,128)(2,1)S(1)}, bf16[4,128,256]{2,1,0:T(8,128)(2,1)S(1)}, u32[]{:S(2)}, u32[]{:S(2)}) collective-permute-start(bf16[4,128,256]{2,1,0:T(8,128)(2,1)S(1)} %collective-permute-done.7), channel_id=1, source_target_pairs={{4,0},{8,12},{5,1},{9,13},{6,2},{10,14},{7,3},{11,15},{20,16},{24,... | collective-permute-start | bytes 786440 | tf_op jit(solution)/shard_map/ppermute | solution.py:237
  35.1 10.8 %collective-permute-start.9 = (bf16[128,8,256]{2,1,0:T(8,128)(2,1)S(1)}, bf16[128,8,256]{2,1,0:T(8,128)(2,1)S(1)}, u32[]{:S(2)}, u32[]{:S(2)}) collective-permute-start(bf16[128,8,256]{2,1,0:T(8,128)(2,1)S(1)} %collective-permute-done.3.near), channel_id=1, source_target_pairs={{4,8},{8,4},{5,9},{9,5},{6,10},{10,6},{7,11},{11,7},{20,24},{24,20... | collective-permute-start | bytes 1572872 | tf_op jit(solution)/shard_map/ppermute | solution.py:238
  35.8 16.5 %collective-permute-start.10 = (bf16[128,8,256]{2,1,0:T(8,128)(2,1)S(1)}, bf16[128,8,256]{2,1,0:T(8,128)(2,1)S(1)}, u32[]{:S(2)}, u32[]{:S(2)}) collective-permute-start(bf16[128,8,256]{2,1,0:T(8,128)(2,1)S(1)} %collective-permute-done.4), channel_id=1, source_target_pairs={{4,0},{8,12},{5,1},{9,13},{6,2},{10,14},{7,3},{11,15},{20,16},{24,... | collective-permute-start | bytes 1572872 | tf_op jit(solution)/shard_map/ppermute | solution.py:239
  41.3 11.4 %collective-permute-start.11 = (bf16[8,128,256]{2,1,0:T(8,128)(2,1)S(1)}, bf16[8,128,256]{2,1,0:T(8,128)(2,1)S(1)}, u32[]{:S(2)}, u32[]{:S(2)}) collective-permute-start(bf16[8,128,256]{2,1,0:T(8,128)(2,1)S(1)} %pad_maximum_fusion.1.own_ref), channel_id=1, source_target_pairs={{0,2},{2,0},{1,3},{3,1},{4,6},{6,4},{5,7},{7,5},{8,10},{10,8},{9,1... | collective-permute-start | bytes 1572872 | tf_op jit(solution)/shard_map/ppermute | solution.py:242
  45.9 12.1 %collective-permute-start.12 = (bf16[64,8,256]{2,1,0:T(8,128)(2,1)S(1)}, bf16[64,8,256]{2,1,0:T(8,128)(2,1)S(1)}, u32[]{:S(2)}, u32[]{:S(2)}) collective-permute-start(bf16[64,8,256]{2,1,0:T(8,128)(2,1)S(1)} %slice.17.far_in), channel_id=1, source_target_pairs={{4,0},{8,12},{5,1},{9,13},{6,2},{10,14},{7,3},{11,15},{20,16},{24,... | collective-permute-start | bytes 786440 | tf_op jit(solution)/shard_map/ppermute | solution.py:250
  47.2 13.4 %collective-permute-start.13 = (bf16[32,8,256]{2,1,0:T(8,128)(2,1)S(1)}, bf16[32,8,256]{2,1,0:T(8,128)(2,1)S(1)}, u32[]{:S(2)}, u32[]{:S(2)}) collective-permute-start(bf16[32,8,256]{2,1,0:T(8,128)(2,1)S(1)} %get-tuple-element.48.far_in), channel_id=1, source_target_pairs={{4,0},{8,12},{5,1},{9,13},{6,2},{10,14},{7,3},{11,15},{20,16},{24,... | collective-permute-start | bytes 393224 | tf_op jit(solution)/shard_map/ppermute | solution.py:250
  48.5 13.5 %collective-permute-start.14 = (bf16[32,8,256]{2,1,0:T(8,128)(2,1)S(1)}, bf16[32,8,256]{2,1,0:T(8,128)(2,1)S(1)}, u32[]{:S(2)}, u32[]{:S(2)}) collective-permute-start(bf16[32,8,256]{2,1,0:T(8,128)(2,1)S(1)} %get-tuple-element.47.far_in), channel_id=1, source_target_pairs={{4,0},{8,12},{5,1},{9,13},{6,2},{10,14},{7,3},{11,15},{20,16},{24,... | collective-permute-start | bytes 393224 | tf_op jit(solution)/shard_map/ppermute | solution.py:250
  63.4 3.8 %collective-permute-start.15 = (f32[24,128]{1,0:T(8,128)S(1)}, f32[24,128]{1,0:T(8,128)S(1)}, u32[]{:S(2)}, u32[]{:S(2)}) collective-permute-start(f32[24,128]{1,0:T(8,128)S(1)} %get-tuple-element.46), channel_id=1, source_target_pairs={{0,2},{2,0},{1,3},{3,1},{4,6},{6,4},{5,7},{7,5},{8,10},{10,8},{9,1... | collective-permute-start | bytes 36872 | tf_op jit(solution)/shard_map/ppermute | solution.py:266

commit v19 on v18

--- a/solution.py
+++ b/solution.py
@@ -161,32 +161,36 @@
     return [me, near, jnp.where(low_pair, 2, 1), jnp.where(low_pair, 3, 0)]
 
 
-def far_pass_kernel(first, ex, early_ref, mid_ref, far_in, far_out, grad_ref, order_ref, out_ref, far_ref):
+def middle_pass_kernel(ex, base_ref, early_ref, mid_ref, grad_ref, order_ref, out_ref):
+    late = mid_ref.shape[1]
+    acc = inner_products((early_ref, mid_ref), grad_ref)
+    mid, far = slot_sources(lax.axis_index("ex"))[2:]
+    out_ref[...] = base_ref[...]
+    for b in range(ex):
+        mid_hit, far_hit = order_ref[b] == mid, order_ref[b] == far
+        low = jnp.where(mid_hit, acc[:EARLY], 0.0) + jnp.where(far_hit, acc[EARLY : 2 * EARLY], 0.0)
+        at = b * (EARLY + late)
+        out_ref[at : at + EARLY, :] = out_ref[at : at + EARLY, :] + low
+        at = at + EARLY
+        out_ref[at : at + late, :] = out_ref[at : at + late, :] + jnp.where(mid_hit, acc[2 * EARLY :], 0.0)
+
+
+def far_pass_kernel(first, ex, far_in, far_out, grad_ref, order_ref, out_ref, far_ref):
     far_ref[...] = far_in[...] + far_out[...]
-    out_ref[...] = inner_products((early_ref, mid_ref, far_ref), grad_ref, first, far_out.shape[0])
+    out_ref[...] = inner_products((far_ref,), grad_ref, first, far_out.shape[0])
 
 
 def last_pass_kernel(
-    ex, base_ref, far_0, far_1, early_ref, mid_ref, far_in, far_out, grad_ref, order_ref,
-    mine_ref, send_ref, full_ref, far_ref,
+    ex, base_ref, far_0, far_1, far_in, far_out, grad_ref, order_ref, mine_ref, send_ref, full_ref, far_ref
 ):
-    late = far_out.shape[1]
-    rows = far_out.shape[0]
-    first = grad_ref.shape[0] - rows
+    rows, late, _ = far_out.shape
     far_ref[...] = far_in[...] + far_out[...]
-    acc = far_0[...] + far_1[...] + inner_products((early_ref, mid_ref, far_ref), grad_ref, first, rows)
-    mid, far = slot_sources(lax.axis_index("ex"))[2:]
-    low_mid, low_far = acc[:EARLY], acc[EARLY : 2 * EARLY]
-    high_mid, high_far = acc[2 * EARLY : 2 * EARLY + late], acc[2 * EARLY + late :]
+    acc = far_0[...] + far_1[...] + inner_products((far_ref,), grad_ref, grad_ref.shape[0] - rows, rows)
+    far = slot_sources(lax.axis_index("ex"))[3]
     full_ref[...] = base_ref[...]
     for b in range(ex):
-        mid_hit, far_hit = order_ref[b] == mid, order_ref[b] == far
-        low = jnp.where(mid_hit, low_mid, 0.0) + jnp.where(far_hit, low_far, 0.0)
-        high = jnp.where(mid_hit, high_mid, 0.0) + jnp.where(far_hit, high_far, 0.0)
-        at = b * (EARLY + late)
-        full_ref[at : at + EARLY, :] = full_ref[at : at + EARLY, :] + low
-        at = at + EARLY
-        full_ref[at : at + late, :] = full_ref[at : at + late, :] + high
+        at = b * (EARLY + late) + EARLY
+        full_ref[at : at + late, :] = full_ref[at : at + late, :] + jnp.where(order_ref[b] == far, acc, 0.0)
     half = mine_ref.shape[0]
     side = lax.axis_index("feat")
     mine_ref[...] = full_ref[pl.ds(pl.multiple_of(side * half, half), half), :]
@@ -251,16 +255,20 @@
     cond_1 = condition(after(early_1, far_mid, mid_out), early_1_other, *terms)
 
     mid = mid + mid_out
+    base = score_call(
+        middle_pass_kernel, ex, (base, cond_1, mid, grads), block_order,
+        jax.ShapeDtypeStruct((ex * count, n), F32),
+    )
     far_sums, earlier = [], base
     for first, held, arrived in zip(cuts, far_in[:-1], far_out[:-1]):
         earlier = score_call(
-            functools.partial(far_pass_kernel, first), ex, (cond_1, mid, held, arrived, after(grads, earlier)),
-            block_order, jax.ShapeDtypeStruct((2 * count, n), F32), [pltpu.VMEM(arrived.shape, BF16)],
+            functools.partial(far_pass_kernel, first), ex, (held, arrived, after(grads, earlier)),
+            block_order, jax.ShapeDtypeStruct((count - EARLY, n), F32), [pltpu.VMEM(arrived.shape, BF16)],
         )
         far_sums.append(earlier)
     half = jax.ShapeDtypeStruct((ex * count // 2, n), F32)
     mine, send = score_call(
-        last_pass_kernel, ex, (base, *far_sums, cond_1, mid, far_in[-1], far_out[-1], grads), block_order,
+        last_pass_kernel, ex, (base, *far_sums, far_in[-1], far_out[-1], grads), block_order,
         (half, half), [pltpu.VMEM((ex * count, n), F32), pltpu.VMEM(far_out[-1].shape, BF16)],
     )
     scores = mine + lax.ppermute(send, "feat", swap)

time: 68.2 us -> 68 us (level)
  waiting for transfers between devices: 18.9 us -> 16.1 us
  Pallas kernels: 17.7 us -> 20.3 us
    ppermute x3, waiting for transfers between devices: 4.53 us -> 1.62 us  [per_device_line(): far_out = [lax.ppermute(x, 'ex', OUTWARD) for x in far_in]]
    pallas_call x4 -> x5, Pallas kernels: 8.73 us -> 11.3 us  [score_call(): pl.pallas_call(functools.partial(kernel, ex), out_shape=out_shape, in_spe...]
  transfers between devices with their start and end apart: 16 -> 16, of which waited for: 9 -> 9; matrix products, arithmetic and copies ran while one was open for 2% -> 2% of each run, Pallas kernels for 24% -> 28%
where the time goes in v19:
time: 68 us; the launch traced here: 67.5 us
  starting transfers between devices  25.9 us (38%)
  Pallas kernels  20.3 us (30%)
  waiting for transfers between devices  16.1 us (24%)
  local copies, waits for them, and re-layouts  3.99 us (6%)
  other arithmetic  0.97 us (1%)
    pallas_call x5, Pallas kernels, score_call(): pl.pallas_call(functools.partial(kernel, ex), out_shape=out_shape, in_spe...  11.3 us
    pallas_call x1, Pallas kernels, regroup(): pl.pallas_call(regroup_kernel, out_shape=jax.ShapeDtypeStruct((rows, n, w...  5.17 us
    ppermute x1, starting transfers between devices, per_device_line(): near = lax.ppermute(late, 'ex', PAIRS)  4.7 us
    ppermute x1, starting transfers between devices, per_device_line(): raw_near = lax.ppermute(raw, 'ex', PAIRS)  4.45 us
    ppermute x3, starting transfers between devices, per_device_line(): far_out = [lax.ppermute(x, 'ex', OUTWARD) for x in far_in]  3.88 us
    pallas_call x3, Pallas kernels, condition(): pl.pallas_call(condition_kernel, out_shape=jax.ShapeDtypeStruct((rows, co...  3.74 us
    ppermute x1, waiting for transfers between devices, per_device_line(): near = lax.ppermute(late, 'ex', PAIRS)  3.67 us
    ppermute x1, starting transfers between devices, per_device_line(): late_other = lax.ppermute(late_raw, 'feat', swap)  3 us
  transfers between devices with their start and end apart: 16, of which 9 were waited for; matrix products, arithmetic and copies ran while one was open for 2% of the time, Pallas kernels for 28%

profile of v19, /device:TPU:0, one launch (start us, length us, event | category | flops | bytes accessed | tf_op | source)
XLA Modules:
  0.0 67.5 jit_solution(15966401528410155419)
XLA Ops:
  0.0 1.1 %slice_bitcast_fusion.own_ref = bf16[8,128,256]{2,1,0:T(8,128)(2,1)S(1)} fusion(bf16[1,12,128,256]{3,2,1,0:T(8,128)(2,1)} %param.6), kind=kLoop, calls=%fused_computation.2 | loop fusion | bytes 1048576 | tf_op jit(solution)/shard_map/squeeze | solution.py:226
  1.1 3.0 %collective-permute-start.2 = (bf16[8,128,256]{2,1,0:T(8,128)(2,1)S(1)}, bf16[8,128,256]{2,1,0:T(8,128)(2,1)S(1)}, u32[]{:S(2)}, u32[]{:S(2)}) collective-permute-start(bf16[8,128,256]{2,1,0:T(8,128)(2,1)S(1)} %slice_bitcast_fusion.own_ref), channel_id=1, source_target_pairs={{0,2},{2,0},{1,3},{3,1},{4,6},{6,4},{5,7},{7,5},{8,10},{10,8},{9,1... | collective-permute-start | bytes 1572872 | tf_op jit(solution)/shard_map/ppermute | solution.py:227
  4.1 1.0 %slice_bitcast_fusion.1 = bf16[4,128,256]{2,1,0:T(8,128)(2,1)S(1)} fusion(bf16[1,12,128,256]{3,2,1,0:T(8,128)(2,1)} %param.6), kind=kLoop, calls=%fused_computation.3 | loop fusion | bytes 524288 | tf_op jit(solution)/shard_map/squeeze | solution.py:228
  5.7 4.4 %collective-permute-start = (bf16[4,128,256]{2,1,0:T(8,128)(2,1)S(1)}, bf16[4,128,256]{2,1,0:T(8,128)(2,1)S(1)}, u32[]{:S(2)}, u32[]{:S(2)}) collective-permute-start(bf16[4,128,256]{2,1,0:T(8,128)(2,1)S(1)} %slice_bitcast_fusion.1), channel_id=1, source_target_pairs={{0,4},{4,0},{8,12},{12,8},{1,5},{5,1},{9,13},{13,9},{2,6},{6,2},{1... | collective-permute-start | bytes 786440 | tf_op jit(solution)/shard_map/ppermute | solution.py:230
  10.2 0.9 %copy-done = f32[256,256]{1,0:T(8,128)S(1)} copy-done((f32[256,256]{1,0:T(8,128)S(1)}, f32[256,256]{1,0:T(8,128)}, u32[]{:S(2)}) %copy-start) | copy-done | bytes 262168
  11.1 0.9 %copy-done.1 = f32[256,256]{1,0:T(8,128)S(1)} copy-done((f32[256,256]{1,0:T(8,128)S(1)}, f32[256,256]{1,0:T(8,128)}, u32[]{:S(2)}) %copy-start.1) | copy-done | bytes 262168
  12.2 1.3 %collective-permute-start.5 = (bf16[4,128,256]{2,1,0:T(8,128)(2,1)S(1)}, bf16[4,128,256]{2,1,0:T(8,128)(2,1)S(1)}, u32[]{:S(2)}, u32[]{:S(2)}) collective-permute-start(bf16[4,128,256]{2,1,0:T(8,128)(2,1)S(1)} %collective-permute-done.1), channel_id=1, source_target_pairs={{4,0},{8,12},{5,1},{9,13},{6,2},{10,14},{7,3},{11,15},{20,16},{24,... | collective-permute-start | bytes 786440 | tf_op jit(solution)/shard_map/ppermute | solution.py:232
  13.5 2.5 %collective-permute-done = bf16[4,128,256]{2,1,0:T(8,128)(2,1)S(1)} collective-permute-done((bf16[4,128,256]{2,1,0:T(8,128)(2,1)S(1)}, bf16[4,128,256]{2,1,0:T(8,128)(2,1)S(1)}, u32[]{:S(2)}, u32[]{:S(2)}) %collective-permute-start) | collective-permute-done | bytes 262176 | tf_op jit(solution)/shard_map/ppermute | solution.py:230
  16.7 1.2 %shard_map.56.own_ref = bf16[128,8,256]{2,1,0:T(8,128)(2,1)S(1)} custom-call(bf16[8,128,256]{2,1,0:T(8,128)(2,1)S(1)} %slice_bitcast_fusion.own_ref, bf16[8,128,256]{2,1,0:T(8,128)(2,1)S(1)} %collective-permute-done.2.far_ref, bf16[384,256]{1,0:T(8,128)(2,1)S(1)} %get-tuple-element.29.left_ref, bf16[512,256]{1,0:T(8,128)(2,1)S(1)} %get-tuple-element.30.right_ref), custom_call_target="tpu_custom_call" | custom-call | flops 960000000 | bytes 2097152 | tf_op jit(solution)/shard_map/pallas_call | solution.py:70
  17.9 4.7 %collective-permute-start.3 = (bf16[128,8,256]{2,1,0:T(8,128)(2,1)S(1)}, bf16[128,8,256]{2,1,0:T(8,128)(2,1)S(1)}, u32[]{:S(2)}, u32[]{:S(2)}) collective-permute-start(bf16[128,8,256]{2,1,0:T(8,128)(2,1)S(1)} %shard_map.56.own_ref), channel_id=1, source_target_pairs={{0,4},{4,0},{8,12},{12,8},{1,5},{5,1},{9,13},{13,9},{2,6},{6,2},{1... | collective-permute-start | bytes 1572872 | tf_op jit(solution)/shard_map/ppermute | solution.py:237
  22.6 0.7 %collective-permute-start.4 = (bf16[128,8,256]{2,1,0:T(8,128)(2,1)S(1)}, bf16[128,8,256]{2,1,0:T(8,128)(2,1)S(1)}, u32[]{:S(2)}, u32[]{:S(2)}) collective-permute-start(bf16[128,8,256]{2,1,0:T(8,128)(2,1)S(1)} %shard_map.56.own_ref), channel_id=1, source_target_pairs={{4,8},{8,4},{5,9},{9,5},{6,10},{10,6},{7,11},{11,7},{20,24},{24,20... | collective-permute-start | bytes 1572872 | tf_op jit(solution)/shard_map/ppermute | solution.py:238
  23.3 1.6 %collective-permute-start.6 = (bf16[8,128,256]{2,1,0:T(8,128)(2,1)S(1)}, bf16[8,128,256]{2,1,0:T(8,128)(2,1)S(1)}, u32[]{:S(2)}, u32[]{:S(2)}) collective-permute-start(bf16[8,128,256]{2,1,0:T(8,128)(2,1)S(1)} %pad_maximum_fusion.own_ref), channel_id=1, source_target_pairs={{0,2},{2,0},{1,3},{3,1},{4,6},{6,4},{5,7},{7,5},{8,10},{10,8},{9,1... | collective-permute-start | bytes 1572872 | tf_op jit(solution)/shard_map/ppermute | solution.py:240
  24.9 5.2 %shard_map.58.grad_ref = bf16[128,128,256]{2,1,0:T(8,128)(2,1)S(1)} custom-call(bf16[128,128,256]{2,1,0:T(8,128)(2,1)} %grads_ref), custom_call_target="tpu_custom_call" | custom-call | flops 6000000000 | bytes 16000000 | tf_op jit(solution)/shard_map/pallas_call | solution.py:106
  30.1 1.3 %collective-permute-start.8 = (bf16[4,128,256]{2,1,0:T(8,128)(2,1)S(1)}, bf16[4,128,256]{2,1,0:T(8,128)(2,1)S(1)}, u32[]{:S(2)}, u32[]{:S(2)}) collective-permute-start(bf16[4,128,256]{2,1,0:T(8,128)(2,1)S(1)} %collective-permute-done.7), channel_id=1, source_target_pairs={{4,0},{8,12},{5,1},{9,13},{6,2},{10,14},{7,3},{11,15},{20,16},{24,... | collective-permute-start | bytes 786440 | tf_op jit(solution)/shard_map/ppermute | solution.py:241
  31.4 3.7 %collective-permute-done.3.near = bf16[128,8,256]{2,1,0:T(8,128)(2,1)S(1)} collective-permute-done((bf16[128,8,256]{2,1,0:T(8,128)(2,1)S(1)}, bf16[128,8,256]{2,1,0:T(8,128)(2,1)S(1)}, u32[]{:S(2)}, u32[]{:S(2)}) %collective-permute-start.3) | collective-permute-done | bytes 524320 | tf_op jit(solution)/shard_map/ppermute | solution.py:237
  35.1 0.7 %collective-permute-start.9 = (bf16[128,8,256]{2,1,0:T(8,128)(2,1)S(1)}, bf16[128,8,256]{2,1,0:T(8,128)(2,1)S(1)}, u32[]{:S(2)}, u32[]{:S(2)}) collective-permute-start(bf16[128,8,256]{2,1,0:T(8,128)(2,1)S(1)} %collective-permute-done.3.near), channel_id=1, source_target_pairs={{4,8},{8,4},{5,9},{9,5},{6,10},{10,6},{7,11},{11,7},{20,24},{24,20... | collective-permute-start | bytes 1572872 | tf_op jit(solution)/shard_map/ppermute | solution.py:242
  35.8 1.3 %collective-permute-start.10 = (bf16[128,8,256]{2,1,0:T(8,128)(2,1)S(1)}, bf16[128,8,256]{2,1,0:T(8,128)(2,1)S(1)}, u32[]{:S(2)}, u32[]{:S(2)}) collective-permute-start(bf16[128,8,256]{2,1,0:T(8,128)(2,1)S(1)} %collective-permute-done.4), channel_id=1, source_target_pairs={{4,0},{8,12},{5,1},{9,13},{6,2},{10,14},{7,3},{11,15},{20,16},{24,... | collective-permute-start | bytes 1572872 | tf_op jit(solution)/shard_map/ppermute | solution.py:243
  37.1 2.8 %collective-permute-done.8 = bf16[4,128,256]{2,1,0:T(8,128)(2,1)S(1)} collective-permute-done((bf16[4,128,256]{2,1,0:T(8,128)(2,1)S(1)}, bf16[4,128,256]{2,1,0:T(8,128)(2,1)S(1)}, u32[]{:S(2)}, u32[]{:S(2)}) %collective-permute-start.8) | collective-permute-done | bytes 262176 | tf_op jit(solution)/shard_map/ppermute | solution.py:241
  40.0 1.2 %shard_map.57.early_ref = bf16[128,8,256]{2,1,0:T(8,128)(2,1)S(1)} custom-call(bf16[8,128,256]{2,1,0:T(8,128)(2,1)S(1)} %pad_maximum_fusion.own_ref, bf16[8,128,256]{2,1,0:T(8,128)(2,1)S(1)} %collective-permute-done.6.far_ref, bf16[384,256]{1,0:T(8,128)(2,1)S(1)} %get-tuple-element.29.left_ref, bf16[512,256]{1,0:T(8,128)(2,1)S(1)} %get-tuple-element.30.right_ref), custom_call_target="tpu_custom_call" | custom-call | flops 960000000 | bytes 2097152 | tf_op jit(solution)/shard_map/pallas_call | solution.py:70
  42.0 3.9 %shard_map.59.base_ref = f32[48,128]{1,0:T(8,128)S(1)} custom-call(bf16[128,8,256]{2,1,0:T(8,128)(2,1)S(1)} %shard_map.57.early_ref, bf16[128,8,256]{2,1,0:T(8,128)(2,1)S(1)} %shard_map.56.own_ref, bf16[128,8,256]{2,1,0:T(8,128)(2,1)S(1)} %collective-permute-done.3.near, bf16[128,128,256]{2,1,0:T(8,128)(2,1)S(1)} %shard_map.58.grad_ref, s32[4]{0:T(128)S(1)} %copy-done.2), custom_call_target="tpu_custom_call" | custom-call | flops 1000 | bytes 1000 | tf_op jit(solution)/shard_map/pallas_call | solution.py:201
  45.9 1.3 %collective-permute-start.12 = (bf16[64,8,256]{2,1,0:T(8,128)(2,1)S(1)}, bf16[64,8,256]{2,1,0:T(8,128)(2,1)S(1)}, u32[]{:S(2)}, u32[]{:S(2)}) collective-permute-start(bf16[64,8,256]{2,1,0:T(8,128)(2,1)S(1)} %slice.17.far_in), channel_id=1, source_target_pairs={{4,0},{8,12},{5,1},{9,13},{6,2},{10,14},{7,3},{11,15},{20,16},{24,... | collective-permute-start | bytes 786440 | tf_op jit(solution)/shard_map/ppermute | solution.py:254
  47.2 1.3 %collective-permute-start.13 = (bf16[32,8,256]{2,1,0:T(8,128)(2,1)S(1)}, bf16[32,8,256]{2,1,0:T(8,128)(2,1)S(1)}, u32[]{:S(2)}, u32[]{:S(2)}) collective-permute-start(bf16[32,8,256]{2,1,0:T(8,128)(2,1)S(1)} %get-tuple-element.48.far_in), channel_id=1, source_target_pairs={{4,0},{8,12},{5,1},{9,13},{6,2},{10,14},{7,3},{11,15},{20,16},{24,... | collective-permute-start | bytes 393224 | tf_op jit(solution)/shard_map/ppermute | solution.py:254
  48.5 1.3 %collective-permute-start.14 = (bf16[32,8,256]{2,1,0:T(8,128)(2,1)S(1)}, bf16[32,8,256]{2,1,0:T(8,128)(2,1)S(1)}, u32[]{:S(2)}, u32[]{:S(2)}) collective-permute-start(bf16[32,8,256]{2,1,0:T(8,128)(2,1)S(1)} %get-tuple-element.47.far_in), channel_id=1, source_target_pairs={{4,0},{8,12},{5,1},{9,13},{6,2},{10,14},{7,3},{11,15},{20,16},{24,... | collective-permute-start | bytes 393224 | tf_op jit(solution)/shard_map/ppermute | solution.py:254
  49.8 2.6 %collective-permute-done.10 = bf16[128,8,256]{2,1,0:T(8,128)(2,1)S(1)} collective-permute-done((bf16[128,8,256]{2,1,0:T(8,128)(2,1)S(1)}, bf16[128,8,256]{2,1,0:T(8,128)(2,1)S(1)}, u32[]{:S(2)}, u32[]{:S(2)}) %collective-permute-start.10) | collective-permute-done | bytes 524320 | tf_op jit(solution)/shard_map/ppermute | solution.py:243
  52.7 1.3 %shard_map.60.early_ref = bf16[128,8,256]{2,1,0:T(8,128)(2,1)S(1)} custom-call(bf16[8,128,256]{2,1,0:T(8,128)(2,1)S(1)} %pad_maximum_fusion.1.own_ref, bf16[8,128,256]{2,1,0:T(8,128)(2,1)S(1)} %collective-permute-done.11.far_ref, bf16[384,256]{1,0:T(8,128)(2,1)S(1)} %get-tuple-element.29.left_ref, bf16[512,256]{1,0:T(8,128)(2,1)S(1)} %get-tuple-element.30.right_ref), custom_call_target="tpu_custom_call" | custom-call | flops 960000000 | bytes 2097152 | tf_op jit(solution)/shard_map/pallas_call | solution.py:70
  54.1 3.2 %shard_map.61.base_ref = f32[48,128]{1,0:T(8,128)S(1)} custom-call(f32[48,128]{1,0:T(8,128)S(1)} %shard_map.59.base_ref, bf16[128,8,256]{2,1,0:T(8,128)(2,1)S(1)} %shard_map.60.early_ref, bf16[128,8,256]{2,1,0:T(8,128)(2,1)S(1)} %add.14.mid_ref, bf16[128,128,256]{2,1,0:T(8,128)(2,1)S(1)} %shard_map.58.grad_ref, s32[4]{0:T(128)S(1)} %copy-done.2), custom_call_target="tpu_custom_call" | custom-call | flops 1000 | bytes 1000 | tf_op jit(solution)/shard_map/pallas_call | solution.py:201
  58.0 1.9 %shard_map.62.far_0 = f32[8,128]{1,0:T(8,128)S(1)} custom-call(bf16[64,8,256]{2,1,0:T(8,128)(2,1)S(1)} %slice.17.far_in, bf16[64,8,256]{2,1,0:T(8,128)(2,1)S(1)} %collective-permute-done.12.far_out, bf16[128,128,256]{2,1,0:T(8,128)(2,1)S(1)} %shard_map.58.grad_ref, s32[4]{0:T(128)S(1)} %copy-done.2), custom_call_target="tpu_custom_call" | custom-call | flops 1000 | bytes 1000 | tf_op jit(solution)/shard_map/pallas_call | solution.py:201
  59.9 0.7 %collective-permute-done.13.far_out = bf16[32,8,256]{2,1,0:T(8,128)(2,1)S(1)} collective-permute-done((bf16[32,8,256]{2,1,0:T(8,128)(2,1)S(1)}, bf16[32,8,256]{2,1,0:T(8,128)(2,1)S(1)}, u32[]{:S(2)}, u32[]{:S(2)}) %collective-permute-start.13) | collective-permute-done | bytes 131104 | tf_op jit(solution)/shard_map/ppermute | solution.py:254
  60.6 1.2 %shard_map.63.far_1 = f32[8,128]{1,0:T(8,128)S(1)} custom-call(bf16[32,8,256]{2,1,0:T(8,128)(2,1)S(1)} %get-tuple-element.48.far_in, bf16[32,8,256]{2,1,0:T(8,128)(2,1)S(1)} %collective-permute-done.13.far_out, bf16[128,128,256]{2,1,0:T(8,128)(2,1)S(1)} %shard_map.58.grad_ref, s32[4]{0:T(128)S(1)} %copy-done.2), custom_call_target="tpu_custom_call" | custom-call | flops 1000 | bytes 1000 | tf_op jit(solution)/shard_map/pallas_call | solution.py:201
  62.0 1.2 %shard_map.64 = (f32[24,128]{1,0:T(8,128)S(1)}, f32[24,128]{1,0:T(8,128)S(1)}) custom-call(f32[48,128]{1,0:T(8,128)S(1)} %shard_map.61.base_ref, f32[8,128]{1,0:T(8,128)S(1)} %shard_map.62.far_0, f32[8,128]{1,0:T(8,128)S(1)} %shard_map.63.far_1, bf16[32,8,256]{2,1,0:T(8,128)(2,1)S(1)} %get-tuple-element.47.far_in, ...), custom_call_target="tpu_custom_call" | custom-call | flops 1000 | bytes 1000 | tf_op jit(solution)/shard_map/pallas_call | solution.py:201
  63.2 1.1 %collective-permute-start.15 = (f32[24,128]{1,0:T(8,128)S(1)}, f32[24,128]{1,0:T(8,128)S(1)}, u32[]{:S(2)}, u32[]{:S(2)}) collective-permute-start(f32[24,128]{1,0:T(8,128)S(1)} %get-tuple-element.46), channel_id=1, source_target_pairs={{0,2},{2,0},{1,3},{3,1},{4,6},{6,4},{5,7},{7,5},{8,10},{10,8},{9,1... | collective-permute-start | bytes 36872 | tf_op jit(solution)/shard_map/ppermute | solution.py:274
  64.3 2.7 %collective-permute-done.15 = f32[24,128]{1,0:T(8,128)S(1)} collective-permute-done((f32[24,128]{1,0:T(8,128)S(1)}, f32[24,128]{1,0:T(8,128)S(1)}, u32[]{:S(2)}, u32[]{:S(2)}) %collective-permute-start.15) | collective-permute-done | bytes 12320 | tf_op jit(solution)/shard_map/ppermute | solution.py:274
  (26 shorter events, 4.4 us)
Async XLA Ops:
  1.1 14.9 %collective-permute-start.2 = (bf16[8,128,256]{2,1,0:T(8,128)(2,1)S(1)}, bf16[8,128,256]{2,1,0:T(8,128)(2,1)S(1)}, u32[]{:S(2)}, u32[]{:S(2)}) collective-permute-start(bf16[8,128,256]{2,1,0:T(8,128)(2,1)S(1)} %slice_bitcast_fusion.own_ref), channel_id=1, source_target_pairs={{0,2},{2,0},{1,3},{3,1},{4,6},{6,4},{5,7},{7,5},{8,10},{10,8},{9,1... | collective-permute-start | bytes 1572872 | tf_op jit(solution)/shard_map/ppermute | solution.py:227
  5.1 7.1 %collective-permute-start.1 = (bf16[4,128,256]{2,1,0:T(8,128)(2,1)S(1)}, bf16[4,128,256]{2,1,0:T(8,128)(2,1)S(1)}, u32[]{:S(2)}, u32[]{:S(2)}) collective-permute-start(bf16[4,128,256]{2,1,0:T(8,128)(2,1)S(1)} %slice_bitcast_fusion.1), channel_id=1, source_target_pairs={{4,8},{8,4},{5,9},{9,5},{6,10},{10,6},{7,11},{11,7},{20,24},{24,20... | collective-permute-start | bytes 786440 | tf_op jit(solution)/shard_map/ppermute | solution.py:231
  5.7 10.2 %collective-permute-start = (bf16[4,128,256]{2,1,0:T(8,128)(2,1)S(1)}, bf16[4,128,256]{2,1,0:T(8,128)(2,1)S(1)}, u32[]{:S(2)}, u32[]{:S(2)}) collective-permute-start(bf16[4,128,256]{2,1,0:T(8,128)(2,1)S(1)} %slice_bitcast_fusion.1), channel_id=1, source_target_pairs={{0,4},{4,0},{8,12},{12,8},{1,5},{5,1},{9,13},{13,9},{2,6},{6,2},{1... | collective-permute-start | bytes 786440 | tf_op jit(solution)/shard_map/ppermute | solution.py:230
  10.2 0.9 %copy-start = (f32[256,256]{1,0:T(8,128)S(1)}, f32[256,256]{1,0:T(8,128)}, u32[]{:S(2)}) copy-start(f32[256,256]{1,0:T(8,128)} %left_ref.1) | copy-start | bytes 786436
  11.1 0.9 %copy-start.1 = (f32[256,256]{1,0:T(8,128)S(1)}, f32[256,256]{1,0:T(8,128)}, u32[]{:S(2)}) copy-start(f32[256,256]{1,0:T(8,128)} %right_ref) | copy-start | bytes 786436
  12.2 11.2 %collective-permute-start.5 = (bf16[4,128,256]{2,1,0:T(8,128)(2,1)S(1)}, bf16[4,128,256]{2,1,0:T(8,128)(2,1)S(1)}, u32[]{:S(2)}, u32[]{:S(2)}) collective-permute-start(bf16[4,128,256]{2,1,0:T(8,128)(2,1)S(1)} %collective-permute-done.1), channel_id=1, source_target_pairs={{4,0},{8,12},{5,1},{9,13},{6,2},{10,14},{7,3},{11,15},{20,16},{24,... | collective-permute-start | bytes 786440 | tf_op jit(solution)/shard_map/ppermute | solution.py:232
  16.0 8.9 %collective-permute-start.7 = (bf16[4,128,256]{2,1,0:T(8,128)(2,1)S(1)}, bf16[4,128,256]{2,1,0:T(8,128)(2,1)S(1)}, u32[]{:S(2)}, u32[]{:S(2)}) collective-permute-start(bf16[4,128,256]{2,1,0:T(8,128)(2,1)S(1)} %collective-permute-done), channel_id=1, source_target_pairs={{4,8},{8,4},{5,9},{9,5},{6,10},{10,6},{7,11},{11,7},{20,24},{24,20... | collective-permute-start | bytes 786440 | tf_op jit(solution)/shard_map/ppermute | solution.py:234
  17.9 24.0 %copy-start.2 = (s32[4]{0:T(128)S(1)}, s32[4]{0:T(128)}, u32[]{:S(2)}) copy-start(s32[4]{0:T(128)} %order_ref.9) | copy-start | bytes 52
  17.9 17.1 %collective-permute-start.3 = (bf16[128,8,256]{2,1,0:T(8,128)(2,1)S(1)}, bf16[128,8,256]{2,1,0:T(8,128)(2,1)S(1)}, u32[]{:S(2)}, u32[]{:S(2)}) collective-permute-start(bf16[128,8,256]{2,1,0:T(8,128)(2,1)S(1)} %shard_map.56.own_ref), channel_id=1, source_target_pairs={{0,4},{4,0},{8,12},{12,8},{1,5},{5,1},{9,13},{13,9},{2,6},{6,2},{1... | collective-permute-start | bytes 1572872 | tf_op jit(solution)/shard_map/ppermute | solution.py:237
  22.6 13.2 %collective-permute-start.4 = (bf16[128,8,256]{2,1,0:T(8,128)(2,1)S(1)}, bf16[128,8,256]{2,1,0:T(8,128)(2,1)S(1)}, u32[]{:S(2)}, u32[]{:S(2)}) collective-permute-start(bf16[128,8,256]{2,1,0:T(8,128)(2,1)S(1)} %shard_map.56.own_ref), channel_id=1, source_target_pairs={{4,8},{8,4},{5,9},{9,5},{6,10},{10,6},{7,11},{11,7},{20,24},{24,20... | collective-permute-start | bytes 1572872 | tf_op jit(solution)/shard_map/ppermute | solution.py:238
  23.3 16.6 %collective-permute-start.6 = (bf16[8,128,256]{2,1,0:T(8,128)(2,1)S(1)}, bf16[8,128,256]{2,1,0:T(8,128)(2,1)S(1)}, u32[]{:S(2)}, u32[]{:S(2)}) collective-permute-start(bf16[8,128,256]{2,1,0:T(8,128)(2,1)S(1)} %pad_maximum_fusion.own_ref), channel_id=1, source_target_pairs={{0,2},{2,0},{1,3},{3,1},{4,6},{6,4},{5,7},{7,5},{8,10},{10,8},{9,1... | collective-permute-start | bytes 1572872 | tf_op jit(solution)/shard_map/ppermute | solution.py:240
  30.1 9.8 %collective-permute-start.8 = (bf16[4,128,256]{2,1,0:T(8,128)(2,1)S(1)}, bf16[4,128,256]{2,1,0:T(8,128)(2,1)S(1)}, u32[]{:S(2)}, u32[]{:S(2)}) collective-permute-start(bf16[4,128,256]{2,1,0:T(8,128)(2,1)S(1)} %collective-permute-done.7), channel_id=1, source_target_pairs={{4,0},{8,12},{5,1},{9,13},{6,2},{10,14},{7,3},{11,15},{20,16},{24,... | collective-permute-start | bytes 786440 | tf_op jit(solution)/shard_map/ppermute | solution.py:241
  35.1 10.8 %collective-permute-start.9 = (bf16[128,8,256]{2,1,0:T(8,128)(2,1)S(1)}, bf16[128,8,256]{2,1,0:T(8,128)(2,1)S(1)}, u32[]{:S(2)}, u32[]{:S(2)}) collective-permute-start(bf16[128,8,256]{2,1,0:T(8,128)(2,1)S(1)} %collective-permute-done.3.near), channel_id=1, source_target_pairs={{4,8},{8,4},{5,9},{9,5},{6,10},{10,6},{7,11},{11,7},{20,24},{24,20... | collective-permute-start | bytes 1572872 | tf_op jit(solution)/shard_map/ppermute | solution.py:242
  35.8 16.5 %collective-permute-start.10 = (bf16[128,8,256]{2,1,0:T(8,128)(2,1)S(1)}, bf16[128,8,256]{2,1,0:T(8,128)(2,1)S(1)}, u32[]{:S(2)}, u32[]{:S(2)}) collective-permute-start(bf16[128,8,256]{2,1,0:T(8,128)(2,1)S(1)} %collective-permute-done.4), channel_id=1, source_target_pairs={{4,0},{8,12},{5,1},{9,13},{6,2},{10,14},{7,3},{11,15},{20,16},{24,... | collective-permute-start | bytes 1572872 | tf_op jit(solution)/shard_map/ppermute | solution.py:243
  41.3 11.4 %collective-permute-start.11 = (bf16[8,128,256]{2,1,0:T(8,128)(2,1)S(1)}, bf16[8,128,256]{2,1,0:T(8,128)(2,1)S(1)}, u32[]{:S(2)}, u32[]{:S(2)}) collective-permute-start(bf16[8,128,256]{2,1,0:T(8,128)(2,1)S(1)} %pad_maximum_fusion.1.own_ref), channel_id=1, source_target_pairs={{0,2},{2,0},{1,3},{3,1},{4,6},{6,4},{5,7},{7,5},{8,10},{10,8},{9,1... | collective-permute-start | bytes 1572872 | tf_op jit(solution)/shard_map/ppermute | solution.py:246
  45.9 12.1 %collective-permute-start.12 = (bf16[64,8,256]{2,1,0:T(8,128)(2,1)S(1)}, bf16[64,8,256]{2,1,0:T(8,128)(2,1)S(1)}, u32[]{:S(2)}, u32[]{:S(2)}) collective-permute-start(bf16[64,8,256]{2,1,0:T(8,128)(2,1)S(1)} %slice.17.far_in), channel_id=1, source_target_pairs={{4,0},{8,12},{5,1},{9,13},{6,2},{10,14},{7,3},{11,15},{20,16},{24,... | collective-permute-start | bytes 786440 | tf_op jit(solution)/shard_map/ppermute | solution.py:254
  47.2 13.4 %collective-permute-start.13 = (bf16[32,8,256]{2,1,0:T(8,128)(2,1)S(1)}, bf16[32,8,256]{2,1,0:T(8,128)(2,1)S(1)}, u32[]{:S(2)}, u32[]{:S(2)}) collective-permute-start(bf16[32,8,256]{2,1,0:T(8,128)(2,1)S(1)} %get-tuple-element.48.far_in), channel_id=1, source_target_pairs={{4,0},{8,12},{5,1},{9,13},{6,2},{10,14},{7,3},{11,15},{20,16},{24,... | collective-permute-start | bytes 393224 | tf_op jit(solution)/shard_map/ppermute | solution.py:254
  48.5 13.5 %collective-permute-start.14 = (bf16[32,8,256]{2,1,0:T(8,128)(2,1)S(1)}, bf16[32,8,256]{2,1,0:T(8,128)(2,1)S(1)}, u32[]{:S(2)}, u32[]{:S(2)}) collective-permute-start(bf16[32,8,256]{2,1,0:T(8,128)(2,1)S(1)} %get-tuple-element.47.far_in), channel_id=1, source_target_pairs={{4,0},{8,12},{5,1},{9,13},{6,2},{10,14},{7,3},{11,15},{20,16},{24,... | collective-permute-start | bytes 393224 | tf_op jit(solution)/shard_map/ppermute | solution.py:254
  63.2 3.8 %collective-permute-start.15 = (f32[24,128]{1,0:T(8,128)S(1)}, f32[24,128]{1,0:T(8,128)S(1)}, u32[]{:S(2)}, u32[]{:S(2)}) collective-permute-start(f32[24,128]{1,0:T(8,128)S(1)} %get-tuple-element.46), channel_id=1, source_target_pairs={{0,2},{2,0},{1,3},{3,1},{4,6},{6,4},{5,7},{7,5},{8,10},{10,8},{9,1... | collective-permute-start | bytes 36872 | tf_op jit(solution)/shard_map/ppermute | solution.py:274

commit v20 on v19

--- a/solution.py
+++ b/solution.py
@@ -11,7 +11,7 @@
 BF16 = jnp.bfloat16
 EARLY = 4
 TILE = 16
-EXAMPLES = 32
+EXAMPLES = 16
 DEEP = 32
 VMEM = pl.BlockSpec(memory_space=pltpu.VMEM)
 SMEM = pl.BlockSpec(memory_space=pltpu.SMEM)

time: 68 us -> 68 us (level)
    ppermute x1, waiting for transfers between devices: 3.67 us -> 4.36 us  [per_device_line(): near = lax.ppermute(late, 'ex', PAIRS)]
where the time goes in v20:
time: 68 us; the launch traced here: 67.5 us
  starting transfers between devices  25.9 us (38%)
  Pallas kernels  19.9 us (29%)
  waiting for transfers between devices  16.5 us (24%)
  local copies, waits for them, and re-layouts  3.99 us (6%)
  other arithmetic  0.97 us (1%)
    pallas_call x5, Pallas kernels, score_call(): pl.pallas_call(functools.partial(kernel, ex), out_shape=out_shape, in_spe...  11.3 us
    pallas_call x1, Pallas kernels, regroup(): pl.pallas_call(regroup_kernel, out_shape=jax.ShapeDtypeStruct((rows, n, w...  4.82 us
    ppermute x1, starting transfers between devices, per_device_line(): near = lax.ppermute(late, 'ex', PAIRS)  4.7 us
    ppermute x1, starting transfers between devices, per_device_line(): raw_near = lax.ppermute(raw, 'ex', PAIRS)  4.45 us
    ppermute x1, waiting for transfers between devices, per_device_line(): near = lax.ppermute(late, 'ex', PAIRS)  4.36 us
    ppermute x3, starting transfers between devices, per_device_line(): far_out = [lax.ppermute(x, 'ex', OUTWARD) for x in far_in]  3.88 us
    pallas_call x3, Pallas kernels, condition(): pl.pallas_call(condition_kernel, out_shape=jax.ShapeDtypeStruct((rows, co...  3.74 us
    ppermute x1, starting transfers between devices, per_device_line(): late_other = lax.ppermute(late_raw, 'feat', swap)  3 us
  transfers between devices with their start and end apart: 16, of which 9 were waited for; matrix products, arithmetic and copies ran while one was open for 2% of the time, Pallas kernels for 28%

profile of v20, /device:TPU:0, one launch (start us, length us, event | category | flops | bytes accessed | tf_op | source)
XLA Modules:
  0.0 67.5 jit_solution(3765121560473510856)
XLA Ops:
  0.0 1.1 %slice_bitcast_fusion.own_ref = bf16[8,128,256]{2,1,0:T(8,128)(2,1)S(1)} fusion(bf16[1,12,128,256]{3,2,1,0:T(8,128)(2,1)} %param.6), kind=kLoop, calls=%fused_computation.2 | loop fusion | bytes 1048576 | tf_op jit(solution)/shard_map/squeeze | solution.py:226
  1.1 3.0 %collective-permute-start.2 = (bf16[8,128,256]{2,1,0:T(8,128)(2,1)S(1)}, bf16[8,128,256]{2,1,0:T(8,128)(2,1)S(1)}, u32[]{:S(2)}, u32[]{:S(2)}) collective-permute-start(bf16[8,128,256]{2,1,0:T(8,128)(2,1)S(1)} %slice_bitcast_fusion.own_ref), channel_id=1, source_target_pairs={{0,2},{2,0},{1,3},{3,1},{4,6},{6,4},{5,7},{7,5},{8,10},{10,8},{9,1... | collective-permute-start | bytes 1572872 | tf_op jit(solution)/shard_map/ppermute | solution.py:227
  4.1 1.0 %slice_bitcast_fusion.1 = bf16[4,128,256]{2,1,0:T(8,128)(2,1)S(1)} fusion(bf16[1,12,128,256]{3,2,1,0:T(8,128)(2,1)} %param.6), kind=kLoop, calls=%fused_computation.3 | loop fusion | bytes 524288 | tf_op jit(solution)/shard_map/squeeze | solution.py:228
  5.7 4.4 %collective-permute-start = (bf16[4,128,256]{2,1,0:T(8,128)(2,1)S(1)}, bf16[4,128,256]{2,1,0:T(8,128)(2,1)S(1)}, u32[]{:S(2)}, u32[]{:S(2)}) collective-permute-start(bf16[4,128,256]{2,1,0:T(8,128)(2,1)S(1)} %slice_bitcast_fusion.1), channel_id=1, source_target_pairs={{0,4},{4,0},{8,12},{12,8},{1,5},{5,1},{9,13},{13,9},{2,6},{6,2},{1... | collective-permute-start | bytes 786440 | tf_op jit(solution)/shard_map/ppermute | solution.py:230
  10.2 0.9 %copy-done = f32[256,256]{1,0:T(8,128)S(1)} copy-done((f32[256,256]{1,0:T(8,128)S(1)}, f32[256,256]{1,0:T(8,128)}, u32[]{:S(2)}) %copy-start) | copy-done | bytes 262168
  11.1 0.9 %copy-done.1 = f32[256,256]{1,0:T(8,128)S(1)} copy-done((f32[256,256]{1,0:T(8,128)S(1)}, f32[256,256]{1,0:T(8,128)}, u32[]{:S(2)}) %copy-start.1) | copy-done | bytes 262168
  12.2 1.3 %collective-permute-start.5 = (bf16[4,128,256]{2,1,0:T(8,128)(2,1)S(1)}, bf16[4,128,256]{2,1,0:T(8,128)(2,1)S(1)}, u32[]{:S(2)}, u32[]{:S(2)}) collective-permute-start(bf16[4,128,256]{2,1,0:T(8,128)(2,1)S(1)} %collective-permute-done.1), channel_id=1, source_target_pairs={{4,0},{8,12},{5,1},{9,13},{6,2},{10,14},{7,3},{11,15},{20,16},{24,... | collective-permute-start | bytes 786440 | tf_op jit(solution)/shard_map/ppermute | solution.py:232
  13.5 2.5 %collective-permute-done = bf16[4,128,256]{2,1,0:T(8,128)(2,1)S(1)} collective-permute-done((bf16[4,128,256]{2,1,0:T(8,128)(2,1)S(1)}, bf16[4,128,256]{2,1,0:T(8,128)(2,1)S(1)}, u32[]{:S(2)}, u32[]{:S(2)}) %collective-permute-start) | collective-permute-done | bytes 262176 | tf_op jit(solution)/shard_map/ppermute | solution.py:230
  16.7 1.2 %shard_map.56.own_ref = bf16[128,8,256]{2,1,0:T(8,128)(2,1)S(1)} custom-call(bf16[8,128,256]{2,1,0:T(8,128)(2,1)S(1)} %slice_bitcast_fusion.own_ref, bf16[8,128,256]{2,1,0:T(8,128)(2,1)S(1)} %collective-permute-done.2.far_ref, bf16[384,256]{1,0:T(8,128)(2,1)S(1)} %get-tuple-element.29.left_ref, bf16[512,256]{1,0:T(8,128)(2,1)S(1)} %get-tuple-element.30.right_ref), custom_call_target="tpu_custom_call" | custom-call | flops 960000000 | bytes 2097152 | tf_op jit(solution)/shard_map/pallas_call | solution.py:70
  17.9 4.7 %collective-permute-start.3 = (bf16[128,8,256]{2,1,0:T(8,128)(2,1)S(1)}, bf16[128,8,256]{2,1,0:T(8,128)(2,1)S(1)}, u32[]{:S(2)}, u32[]{:S(2)}) collective-permute-start(bf16[128,8,256]{2,1,0:T(8,128)(2,1)S(1)} %shard_map.56.own_ref), channel_id=1, source_target_pairs={{0,4},{4,0},{8,12},{12,8},{1,5},{5,1},{9,13},{13,9},{2,6},{6,2},{1... | collective-permute-start | bytes 1572872 | tf_op jit(solution)/shard_map/ppermute | solution.py:237
  23.3 1.6 %collective-permute-start.6 = (bf16[8,128,256]{2,1,0:T(8,128)(2,1)S(1)}, bf16[8,128,256]{2,1,0:T(8,128)(2,1)S(1)}, u32[]{:S(2)}, u32[]{:S(2)}) collective-permute-start(bf16[8,128,256]{2,1,0:T(8,128)(2,1)S(1)} %pad_maximum_fusion.own_ref), channel_id=1, source_target_pairs={{0,2},{2,0},{1,3},{3,1},{4,6},{6,4},{5,7},{7,5},{8,10},{10,8},{9,1... | collective-permute-start | bytes 1572872 | tf_op jit(solution)/shard_map/ppermute | solution.py:240
  24.9 4.8 %shard_map.58.grad_ref = bf16[128,128,256]{2,1,0:T(8,128)(2,1)S(1)} custom-call(bf16[128,128,256]{2,1,0:T(8,128)(2,1)} %grads_ref), custom_call_target="tpu_custom_call" | custom-call | flops 6000000000 | bytes 16000000 | tf_op jit(solution)/shard_map/pallas_call | solution.py:106
  29.7 1.3 %collective-permute-start.8 = (bf16[4,128,256]{2,1,0:T(8,128)(2,1)S(1)}, bf16[4,128,256]{2,1,0:T(8,128)(2,1)S(1)}, u32[]{:S(2)}, u32[]{:S(2)}) collective-permute-start(bf16[4,128,256]{2,1,0:T(8,128)(2,1)S(1)} %collective-permute-done.7), channel_id=1, source_target_pairs={{4,0},{8,12},{5,1},{9,13},{6,2},{10,14},{7,3},{11,15},{20,16},{24,... | collective-permute-start | bytes 786440 | tf_op jit(solution)/shard_map/ppermute | solution.py:241
  31.0 4.4 %collective-permute-done.3.near = bf16[128,8,256]{2,1,0:T(8,128)(2,1)S(1)} collective-permute-done((bf16[128,8,256]{2,1,0:T(8,128)(2,1)S(1)}, bf16[128,8,256]{2,1,0:T(8,128)(2,1)S(1)}, u32[]{:S(2)}, u32[]{:S(2)}) %collective-permute-start.3) | collective-permute-done | bytes 524320 | tf_op jit(solution)/shard_map/ppermute | solution.py:237
  35.4 0.7 %collective-permute-start.9 = (bf16[128,8,256]{2,1,0:T(8,128)(2,1)S(1)}, bf16[128,8,256]{2,1,0:T(8,128)(2,1)S(1)}, u32[]{:S(2)}, u32[]{:S(2)}) collective-permute-start(bf16[128,8,256]{2,1,0:T(8,128)(2,1)S(1)} %collective-permute-done.3.near), channel_id=1, source_target_pairs={{4,8},{8,4},{5,9},{9,5},{6,10},{10,6},{7,11},{11,7},{20,24},{24,20... | collective-permute-start | bytes 1572872 | tf_op jit(solution)/shard_map/ppermute | solution.py:242
  36.2 1.3 %collective-permute-start.10 = (bf16[128,8,256]{2,1,0:T(8,128)(2,1)S(1)}, bf16[128,8,256]{2,1,0:T(8,128)(2,1)S(1)}, u32[]{:S(2)}, u32[]{:S(2)}) collective-permute-start(bf16[128,8,256]{2,1,0:T(8,128)(2,1)S(1)} %collective-permute-done.4), channel_id=1, source_target_pairs={{4,0},{8,12},{5,1},{9,13},{6,2},{10,14},{7,3},{11,15},{20,16},{24,... | collective-permute-start | bytes 1572872 | tf_op jit(solution)/shard_map/ppermute | solution.py:243
  37.5 2.4 %collective-permute-done.8 = bf16[4,128,256]{2,1,0:T(8,128)(2,1)S(1)} collective-permute-done((bf16[4,128,256]{2,1,0:T(8,128)(2,1)S(1)}, bf16[4,128,256]{2,1,0:T(8,128)(2,1)S(1)}, u32[]{:S(2)}, u32[]{:S(2)}) %collective-permute-start.8) | collective-permute-done | bytes 262176 | tf_op jit(solution)/shard_map/ppermute | solution.py:241
  40.0 1.2 %shard_map.57.early_ref = bf16[128,8,256]{2,1,0:T(8,128)(2,1)S(1)} custom-call(bf16[8,128,256]{2,1,0:T(8,128)(2,1)S(1)} %pad_maximum_fusion.own_ref, bf16[8,128,256]{2,1,0:T(8,128)(2,1)S(1)} %collective-permute-done.6.far_ref, bf16[384,256]{1,0:T(8,128)(2,1)S(1)} %get-tuple-element.29.left_ref, bf16[512,256]{1,0:T(8,128)(2,1)S(1)} %get-tuple-element.30.right_ref), custom_call_target="tpu_custom_call" | custom-call | flops 960000000 | bytes 2097152 | tf_op jit(solution)/shard_map/pallas_call | solution.py:70
  42.0 3.9 %shard_map.59.base_ref = f32[48,128]{1,0:T(8,128)S(1)} custom-call(bf16[128,8,256]{2,1,0:T(8,128)(2,1)S(1)} %shard_map.57.early_ref, bf16[128,8,256]{2,1,0:T(8,128)(2,1)S(1)} %shard_map.56.own_ref, bf16[128,8,256]{2,1,0:T(8,128)(2,1)S(1)} %collective-permute-done.3.near, bf16[128,128,256]{2,1,0:T(8,128)(2,1)S(1)} %shard_map.58.grad_ref, s32[4]{0:T(128)S(1)} %copy-done.2), custom_call_target="tpu_custom_call" | custom-call | flops 1000 | bytes 1000 | tf_op jit(solution)/shard_map/pallas_call | solution.py:201
  45.9 1.3 %collective-permute-start.12 = (bf16[64,8,256]{2,1,0:T(8,128)(2,1)S(1)}, bf16[64,8,256]{2,1,0:T(8,128)(2,1)S(1)}, u32[]{:S(2)}, u32[]{:S(2)}) collective-permute-start(bf16[64,8,256]{2,1,0:T(8,128)(2,1)S(1)} %slice.17.far_in), channel_id=1, source_target_pairs={{4,0},{8,12},{5,1},{9,13},{6,2},{10,14},{7,3},{11,15},{20,16},{24,... | collective-permute-start | bytes 786440 | tf_op jit(solution)/shard_map/ppermute | solution.py:254
  47.2 1.3 %collective-permute-start.13 = (bf16[32,8,256]{2,1,0:T(8,128)(2,1)S(1)}, bf16[32,8,256]{2,1,0:T(8,128)(2,1)S(1)}, u32[]{:S(2)}, u32[]{:S(2)}) collective-permute-start(bf16[32,8,256]{2,1,0:T(8,128)(2,1)S(1)} %get-tuple-element.48.far_in), channel_id=1, source_target_pairs={{4,0},{8,12},{5,1},{9,13},{6,2},{10,14},{7,3},{11,15},{20,16},{24,... | collective-permute-start | bytes 393224 | tf_op jit(solution)/shard_map/ppermute | solution.py:254
  48.5 1.3 %collective-permute-start.14 = (bf16[32,8,256]{2,1,0:T(8,128)(2,1)S(1)}, bf16[32,8,256]{2,1,0:T(8,128)(2,1)S(1)}, u32[]{:S(2)}, u32[]{:S(2)}) collective-permute-start(bf16[32,8,256]{2,1,0:T(8,128)(2,1)S(1)} %get-tuple-element.47.far_in), channel_id=1, source_target_pairs={{4,0},{8,12},{5,1},{9,13},{6,2},{10,14},{7,3},{11,15},{20,16},{24,... | collective-permute-start | bytes 393224 | tf_op jit(solution)/shard_map/ppermute | solution.py:254
  49.8 2.6 %collective-permute-done.10 = bf16[128,8,256]{2,1,0:T(8,128)(2,1)S(1)} collective-permute-done((bf16[128,8,256]{2,1,0:T(8,128)(2,1)S(1)}, bf16[128,8,256]{2,1,0:T(8,128)(2,1)S(1)}, u32[]{:S(2)}, u32[]{:S(2)}) %collective-permute-start.10) | collective-permute-done | bytes 524320 | tf_op jit(solution)/shard_map/ppermute | solution.py:243
  52.4 0.7 %collective-permute-done.11.far_ref = bf16[8,128,256]{2,1,0:T(8,128)(2,1)S(1)} collective-permute-done((bf16[8,128,256]{2,1,0:T(8,128)(2,1)S(1)}, bf16[8,128,256]{2,1,0:T(8,128)(2,1)S(1)}, u32[]{:S(2)}, u32[]{:S(2)}) %collective-permute-start.11) | collective-permute-done | bytes 524320 | tf_op jit(solution)/shard_map/ppermute | solution.py:246
  53.1 1.3 %shard_map.60.early_ref = bf16[128,8,256]{2,1,0:T(8,128)(2,1)S(1)} custom-call(bf16[8,128,256]{2,1,0:T(8,128)(2,1)S(1)} %pad_maximum_fusion.1.own_ref, bf16[8,128,256]{2,1,0:T(8,128)(2,1)S(1)} %collective-permute-done.11.far_ref, bf16[384,256]{1,0:T(8,128)(2,1)S(1)} %get-tuple-element.29.left_ref, bf16[512,256]{1,0:T(8,128)(2,1)S(1)} %get-tuple-element.30.right_ref), custom_call_target="tpu_custom_call" | custom-call | flops 960000000 | bytes 2097152 | tf_op jit(solution)/shard_map/pallas_call | solution.py:70
  54.4 3.2 %shard_map.61.base_ref = f32[48,128]{1,0:T(8,128)S(1)} custom-call(f32[48,128]{1,0:T(8,128)S(1)} %shard_map.59.base_ref, bf16[128,8,256]{2,1,0:T(8,128)(2,1)S(1)} %shard_map.60.early_ref, bf16[128,8,256]{2,1,0:T(8,128)(2,1)S(1)} %add.14.mid_ref, bf16[128,128,256]{2,1,0:T(8,128)(2,1)S(1)} %shard_map.58.grad_ref, s32[4]{0:T(128)S(1)} %copy-done.2), custom_call_target="tpu_custom_call" | custom-call | flops 1000 | bytes 1000 | tf_op jit(solution)/shard_map/pallas_call | solution.py:201
  58.0 1.9 %shard_map.62.far_0 = f32[8,128]{1,0:T(8,128)S(1)} custom-call(bf16[64,8,256]{2,1,0:T(8,128)(2,1)S(1)} %slice.17.far_in, bf16[64,8,256]{2,1,0:T(8,128)(2,1)S(1)} %collective-permute-done.12.far_out, bf16[128,128,256]{2,1,0:T(8,128)(2,1)S(1)} %shard_map.58.grad_ref, s32[4]{0:T(128)S(1)} %copy-done.2), custom_call_target="tpu_custom_call" | custom-call | flops 1000 | bytes 1000 | tf_op jit(solution)/shard_map/pallas_call | solution.py:201
  59.9 0.7 %collective-permute-done.13.far_out = bf16[32,8,256]{2,1,0:T(8,128)(2,1)S(1)} collective-permute-done((bf16[32,8,256]{2,1,0:T(8,128)(2,1)S(1)}, bf16[32,8,256]{2,1,0:T(8,128)(2,1)S(1)}, u32[]{:S(2)}, u32[]{:S(2)}) %collective-permute-start.13) | collective-permute-done | bytes 131104 | tf_op jit(solution)/shard_map/ppermute | solution.py:254
  60.6 1.2 %shard_map.63.far_1 = f32[8,128]{1,0:T(8,128)S(1)} custom-call(bf16[32,8,256]{2,1,0:T(8,128)(2,1)S(1)} %get-tuple-element.48.far_in, bf16[32,8,256]{2,1,0:T(8,128)(2,1)S(1)} %collective-permute-done.13.far_out, bf16[128,128,256]{2,1,0:T(8,128)(2,1)S(1)} %shard_map.58.grad_ref, s32[4]{0:T(128)S(1)} %copy-done.2), custom_call_target="tpu_custom_call" | custom-call | flops 1000 | bytes 1000 | tf_op jit(solution)/shard_map/pallas_call | solution.py:201
  62.0 1.2 %shard_map.64 = (f32[24,128]{1,0:T(8,128)S(1)}, f32[24,128]{1,0:T(8,128)S(1)}) custom-call(f32[48,128]{1,0:T(8,128)S(1)} %shard_map.61.base_ref, f32[8,128]{1,0:T(8,128)S(1)} %shard_map.62.far_0, f32[8,128]{1,0:T(8,128)S(1)} %shard_map.63.far_1, bf16[32,8,256]{2,1,0:T(8,128)(2,1)S(1)} %get-tuple-element.47.far_in, ...), custom_call_target="tpu_custom_call" | custom-call | flops 1000 | bytes 1000 | tf_op jit(solution)/shard_map/pallas_call | solution.py:201
  63.2 1.1 %collective-permute-start.15 = (f32[24,128]{1,0:T(8,128)S(1)}, f32[24,128]{1,0:T(8,128)S(1)}, u32[]{:S(2)}, u32[]{:S(2)}) collective-permute-start(f32[24,128]{1,0:T(8,128)S(1)} %get-tuple-element.46), channel_id=1, source_target_pairs={{0,2},{2,0},{1,3},{3,1},{4,6},{6,4},{5,7},{7,5},{8,10},{10,8},{9,1... | collective-permute-start | bytes 36872 | tf_op jit(solution)/shard_map/ppermute | solution.py:274
  64.3 2.7 %collective-permute-done.15 = f32[24,128]{1,0:T(8,128)S(1)} collective-permute-done((f32[24,128]{1,0:T(8,128)S(1)}, f32[24,128]{1,0:T(8,128)S(1)}, u32[]{:S(2)}, u32[]{:S(2)}) %collective-permute-start.15) | collective-permute-done | bytes 12320 | tf_op jit(solution)/shard_map/ppermute | solution.py:274
  (26 shorter events, 4.4 us)
Async XLA Ops:
  1.1 14.9 %collective-permute-start.2 = (bf16[8,128,256]{2,1,0:T(8,128)(2,1)S(1)}, bf16[8,128,256]{2,1,0:T(8,128)(2,1)S(1)}, u32[]{:S(2)}, u32[]{:S(2)}) collective-permute-start(bf16[8,128,256]{2,1,0:T(8,128)(2,1)S(1)} %slice_bitcast_fusion.own_ref), channel_id=1, source_target_pairs={{0,2},{2,0},{1,3},{3,1},{4,6},{6,4},{5,7},{7,5},{8,10},{10,8},{9,1... | collective-permute-start | bytes 1572872 | tf_op jit(solution)/shard_map/ppermute | solution.py:227
  5.1 7.1 %collective-permute-start.1 = (bf16[4,128,256]{2,1,0:T(8,128)(2,1)S(1)}, bf16[4,128,256]{2,1,0:T(8,128)(2,1)S(1)}, u32[]{:S(2)}, u32[]{:S(2)}) collective-permute-start(bf16[4,128,256]{2,1,0:T(8,128)(2,1)S(1)} %slice_bitcast_fusion.1), channel_id=1, source_target_pairs={{4,8},{8,4},{5,9},{9,5},{6,10},{10,6},{7,11},{11,7},{20,24},{24,20... | collective-permute-start | bytes 786440 | tf_op jit(solution)/shard_map/ppermute | solution.py:231
  5.7 10.2 %collective-permute-start = (bf16[4,128,256]{2,1,0:T(8,128)(2,1)S(1)}, bf16[4,128,256]{2,1,0:T(8,128)(2,1)S(1)}, u32[]{:S(2)}, u32[]{:S(2)}) collective-permute-start(bf16[4,128,256]{2,1,0:T(8,128)(2,1)S(1)} %slice_bitcast_fusion.1), channel_id=1, source_target_pairs={{0,4},{4,0},{8,12},{12,8},{1,5},{5,1},{9,13},{13,9},{2,6},{6,2},{1... | collective-permute-start | bytes 786440 | tf_op jit(solution)/shard_map/ppermute | solution.py:230
  10.2 0.9 %copy-start = (f32[256,256]{1,0:T(8,128)S(1)}, f32[256,256]{1,0:T(8,128)}, u32[]{:S(2)}) copy-start(f32[256,256]{1,0:T(8,128)} %left_ref.1) | copy-start | bytes 786436
  11.1 0.9 %copy-start.1 = (f32[256,256]{1,0:T(8,128)S(1)}, f32[256,256]{1,0:T(8,128)}, u32[]{:S(2)}) copy-start(f32[256,256]{1,0:T(8,128)} %right_ref) | copy-start | bytes 786436
  12.2 11.2 %collective-permute-start.5 = (bf16[4,128,256]{2,1,0:T(8,128)(2,1)S(1)}, bf16[4,128,256]{2,1,0:T(8,128)(2,1)S(1)}, u32[]{:S(2)}, u32[]{:S(2)}) collective-permute-start(bf16[4,128,256]{2,1,0:T(8,128)(2,1)S(1)} %collective-permute-done.1), channel_id=1, source_target_pairs={{4,0},{8,12},{5,1},{9,13},{6,2},{10,14},{7,3},{11,15},{20,16},{24,... | collective-permute-start | bytes 786440 | tf_op jit(solution)/shard_map/ppermute | solution.py:232
  16.0 8.9 %collective-permute-start.7 = (bf16[4,128,256]{2,1,0:T(8,128)(2,1)S(1)}, bf16[4,128,256]{2,1,0:T(8,128)(2,1)S(1)}, u32[]{:S(2)}, u32[]{:S(2)}) collective-permute-start(bf16[4,128,256]{2,1,0:T(8,128)(2,1)S(1)} %collective-permute-done), channel_id=1, source_target_pairs={{4,8},{8,4},{5,9},{9,5},{6,10},{10,6},{7,11},{11,7},{20,24},{24,20... | collective-permute-start | bytes 786440 | tf_op jit(solution)/shard_map/ppermute | solution.py:234
  17.9 24.0 %copy-start.2 = (s32[4]{0:T(128)S(1)}, s32[4]{0:T(128)}, u32[]{:S(2)}) copy-start(s32[4]{0:T(128)} %order_ref.9) | copy-start | bytes 52
  17.9 17.4 %collective-permute-start.3 = (bf16[128,8,256]{2,1,0:T(8,128)(2,1)S(1)}, bf16[128,8,256]{2,1,0:T(8,128)(2,1)S(1)}, u32[]{:S(2)}, u32[]{:S(2)}) collective-permute-start(bf16[128,8,256]{2,1,0:T(8,128)(2,1)S(1)} %shard_map.56.own_ref), channel_id=1, source_target_pairs={{0,4},{4,0},{8,12},{12,8},{1,5},{5,1},{9,13},{13,9},{2,6},{6,2},{1... | collective-permute-start | bytes 1572872 | tf_op jit(solution)/shard_map/ppermute | solution.py:237
  22.6 13.5 %collective-permute-start.4 = (bf16[128,8,256]{2,1,0:T(8,128)(2,1)S(1)}, bf16[128,8,256]{2,1,0:T(8,128)(2,1)S(1)}, u32[]{:S(2)}, u32[]{:S(2)}) collective-permute-start(bf16[128,8,256]{2,1,0:T(8,128)(2,1)S(1)} %shard_map.56.own_ref), channel_id=1, source_target_pairs={{4,8},{8,4},{5,9},{9,5},{6,10},{10,6},{7,11},{11,7},{20,24},{24,20... | collective-permute-start | bytes 1572872 | tf_op jit(solution)/shard_map/ppermute | solution.py:238
  23.3 16.6 %collective-permute-start.6 = (bf16[8,128,256]{2,1,0:T(8,128)(2,1)S(1)}, bf16[8,128,256]{2,1,0:T(8,128)(2,1)S(1)}, u32[]{:S(2)}, u32[]{:S(2)}) collective-permute-start(bf16[8,128,256]{2,1,0:T(8,128)(2,1)S(1)} %pad_maximum_fusion.own_ref), channel_id=1, source_target_pairs={{0,2},{2,0},{1,3},{3,1},{4,6},{6,4},{5,7},{7,5},{8,10},{10,8},{9,1... | collective-permute-start | bytes 1572872 | tf_op jit(solution)/shard_map/ppermute | solution.py:240
  29.7 10.2 %collective-permute-start.8 = (bf16[4,128,256]{2,1,0:T(8,128)(2,1)S(1)}, bf16[4,128,256]{2,1,0:T(8,128)(2,1)S(1)}, u32[]{:S(2)}, u32[]{:S(2)}) collective-permute-start(bf16[4,128,256]{2,1,0:T(8,128)(2,1)S(1)} %collective-permute-done.7), channel_id=1, source_target_pairs={{4,0},{8,12},{5,1},{9,13},{6,2},{10,14},{7,3},{11,15},{20,16},{24,... | collective-permute-start | bytes 786440 | tf_op jit(solution)/shard_map/ppermute | solution.py:241
  35.4 10.5 %collective-permute-start.9 = (bf16[128,8,256]{2,1,0:T(8,128)(2,1)S(1)}, bf16[128,8,256]{2,1,0:T(8,128)(2,1)S(1)}, u32[]{:S(2)}, u32[]{:S(2)}) collective-permute-start(bf16[128,8,256]{2,1,0:T(8,128)(2,1)S(1)} %collective-permute-done.3.near), channel_id=1, source_target_pairs={{4,8},{8,4},{5,9},{9,5},{6,10},{10,6},{7,11},{11,7},{20,24},{24,20... | collective-permute-start | bytes 1572872 | tf_op jit(solution)/shard_map/ppermute | solution.py:242
  36.2 16.2 %collective-permute-start.10 = (bf16[128,8,256]{2,1,0:T(8,128)(2,1)S(1)}, bf16[128,8,256]{2,1,0:T(8,128)(2,1)S(1)}, u32[]{:S(2)}, u32[]{:S(2)}) collective-permute-start(bf16[128,8,256]{2,1,0:T(8,128)(2,1)S(1)} %collective-permute-done.4), channel_id=1, source_target_pairs={{4,0},{8,12},{5,1},{9,13},{6,2},{10,14},{7,3},{11,15},{20,16},{24,... | collective-permute-start | bytes 1572872 | tf_op jit(solution)/shard_map/ppermute | solution.py:243
  41.3 11.8 %collective-permute-start.11 = (bf16[8,128,256]{2,1,0:T(8,128)(2,1)S(1)}, bf16[8,128,256]{2,1,0:T(8,128)(2,1)S(1)}, u32[]{:S(2)}, u32[]{:S(2)}) collective-permute-start(bf16[8,128,256]{2,1,0:T(8,128)(2,1)S(1)} %pad_maximum_fusion.1.own_ref), channel_id=1, source_target_pairs={{0,2},{2,0},{1,3},{3,1},{4,6},{6,4},{5,7},{7,5},{8,10},{10,8},{9,1... | collective-permute-start | bytes 1572872 | tf_op jit(solution)/shard_map/ppermute | solution.py:246
  45.9 12.1 %collective-permute-start.12 = (bf16[64,8,256]{2,1,0:T(8,128)(2,1)S(1)}, bf16[64,8,256]{2,1,0:T(8,128)(2,1)S(1)}, u32[]{:S(2)}, u32[]{:S(2)}) collective-permute-start(bf16[64,8,256]{2,1,0:T(8,128)(2,1)S(1)} %slice.17.far_in), channel_id=1, source_target_pairs={{4,0},{8,12},{5,1},{9,13},{6,2},{10,14},{7,3},{11,15},{20,16},{24,... | collective-permute-start | bytes 786440 | tf_op jit(solution)/shard_map/ppermute | solution.py:254
  47.2 13.4 %collective-permute-start.13 = (bf16[32,8,256]{2,1,0:T(8,128)(2,1)S(1)}, bf16[32,8,256]{2,1,0:T(8,128)(2,1)S(1)}, u32[]{:S(2)}, u32[]{:S(2)}) collective-permute-start(bf16[32,8,256]{2,1,0:T(8,128)(2,1)S(1)} %get-tuple-element.48.far_in), channel_id=1, source_target_pairs={{4,0},{8,12},{5,1},{9,13},{6,2},{10,14},{7,3},{11,15},{20,16},{24,... | collective-permute-start | bytes 393224 | tf_op jit(solution)/shard_map/ppermute | solution.py:254
  48.5 13.5 %collective-permute-start.14 = (bf16[32,8,256]{2,1,0:T(8,128)(2,1)S(1)}, bf16[32,8,256]{2,1,0:T(8,128)(2,1)S(1)}, u32[]{:S(2)}, u32[]{:S(2)}) collective-permute-start(bf16[32,8,256]{2,1,0:T(8,128)(2,1)S(1)} %get-tuple-element.47.far_in), channel_id=1, source_target_pairs={{4,0},{8,12},{5,1},{9,13},{6,2},{10,14},{7,3},{11,15},{20,16},{24,... | collective-permute-start | bytes 393224 | tf_op jit(solution)/shard_map/ppermute | solution.py:254
  63.2 3.8 %collective-permute-start.15 = (f32[24,128]{1,0:T(8,128)S(1)}, f32[24,128]{1,0:T(8,128)S(1)}, u32[]{:S(2)}, u32[]{:S(2)}) collective-permute-start(f32[24,128]{1,0:T(8,128)S(1)} %get-tuple-element.46), channel_id=1, source_target_pairs={{0,2},{2,0},{1,3},{3,1},{4,6},{6,4},{5,7},{7,5},{8,10},{10,8},{9,1... | collective-permute-start | bytes 36872 | tf_op jit(solution)/shard_map/ppermute | solution.py:274
